TPU v7x, 32 devices: a whole 2x2x4 slice. The times are simulated.
32 devices in a mesh: grp: 2 (over x), section: 16 (over z, y, core).
Axes of the slice: x: 2, y: 2, z: 4, core: 2. Of those that a mesh axis runs over, the one named last changes fastest.
Arguments:
- low_feat: bfloat16 [256, 8192], P(('grp', 'section')), parts along dimension 0, may hold values from -80 to 80
- mid_feat: bfloat16 [256, 8192], P(('grp', 'section')), parts along dimension 0, may hold values from -80 to 80
- high_feat: bfloat16 [256, 8192], P(('grp', 'section')), parts along dimension 0, may hold values from -80 to 80
- w_fc: bfloat16 [3, 8192, 8192], P(None, 'section'), may hold values from -0.0546875 to 0.0546875
- gain: float32 [8192], P('section'), may hold values from 0.1 to 1.9
- w_lm: bfloat16 [8192, 16384], P(None, 'section'), may hold values from -2.5 to 2.5
- targets: int32 [256], P('grp'), parts along dimension 0, may hold values from 0 to 16383
Outputs:
- token_loss: float32 [256], P('grp'), parts along dimension 0
- grad_fc: bfloat16 [6, 8192, 8192], P('grp', 'section'), parts along dimension 0
- grad_gain: float32 [16384], P(('grp', 'section')), parts along dimension 0
- grad_lm: bfloat16 [16384, 16384], P('grp', 'section'), parts along dimension 0
There are 2 independent parts, one for each index of `grp`. A program takes and returns all parts, laid end to end along the dimension named above; an argument that names none is the same for every part. Nothing has to cross between parts.
All inputs are finite; a program needn't handle non-finite values.
Results may differ from a plain program's by a relative error of at most 0.0049.
The roundings to bfloat16 on the way count: a program that leaves them out, or rounds other values in their place, can miss the bound.
Values may be sent and summed in bfloat16 or wider, within the bound.
No kernel may reach another device: no remote copies, remote signals or barrier semaphores. Data moves between devices by JAX's collectives and lax.ppermute only.
A program may use at most 192 MiB of HBM per device.

v0:
```python
import jax
import jax.numpy as jnp
from jax import lax
from jax.sharding import PartitionSpec as P

epsilon = 1e-06


def on_device(low_feat, mid_feat, high_feat, w_fc, gain, w_lm, targets):
    my_rank = lax.axis_index("section")
    full_width = w_fc.shape[2]
    tokens = targets.shape[0]
    pieces = (
        lax.all_to_all(low_feat, "section", split_axis=1, concat_axis=0, tiled=True),
        lax.all_to_all(mid_feat, "section", split_axis=1, concat_axis=0, tiled=True),
        lax.all_to_all(high_feat, "section", split_axis=1, concat_axis=0, tiled=True),
    )
    stacked = jnp.stack(pieces)
    w_block = w_fc
    joined_local = lax.psum_scatter(
        jnp.einsum("jsr,jts->rt", w_block, stacked, preferred_element_type=jnp.float32),
        "section",
        scatter_dimension=0,
        tiled=True,
    )
    squares = lax.psum(jnp.sum(joined_local * joined_local, axis=0), "section")
    inv_rms = lax.rsqrt(squares / full_width + epsilon)
    normed_local = (joined_local * inv_rms[None, :] * gain[:, None]).astype(jnp.bfloat16)
    normed_all = lax.all_gather(normed_local, "section", axis=0, tiled=True)
    logits = lax.dot_general(
        normed_all, w_lm, (((0,), (0,)), ((), ())), preferred_element_type=jnp.float32
    )
    vocab_share = w_lm.shape[1]
    column = my_rank * vocab_share + lax.iota(jnp.int32, vocab_share)
    is_target = column[None, :] == targets[:, None]
    picked_local = jnp.sum(jnp.where(is_target, logits, 0.0), axis=1)
    peak_local = jnp.max(logits, axis=1)
    row_peak = lax.pmax(peak_local, "section")
    local_total = jnp.sum(jnp.exp(logits - row_peak[:, None]), axis=1)
    exp_total, picked = lax.psum((local_total, picked_local), "section")
    log_total = row_peak + jnp.log(exp_total)
    token_loss = log_total - picked
    dlogits = (
        (jnp.exp(logits - log_total[:, None]) - is_target.astype(jnp.float32)) / tokens
    ).astype(jnp.bfloat16)
    grad_lm = jnp.dot(normed_all, dlogits, preferred_element_type=jnp.float32).astype(jnp.bfloat16)
    w_block = w_lm
    dnormed = lax.psum_scatter(
        lax.dot_general(
            w_block, dlogits, (((1,), (1,)), ((), ())), preferred_element_type=jnp.float32
        ),
        "section",
        scatter_dimension=0,
        tiled=True,
    )
    grad_gain = jnp.sum(dnormed * joined_local * inv_rms[None, :], axis=1)
    dscaled = dnormed * gain[:, None]
    rowdot = lax.psum(jnp.sum(dscaled * joined_local, axis=0), "section")
    inv_cube = inv_rms * inv_rms * inv_rms
    dfused = (
        inv_rms[None, :] * dscaled - joined_local * (inv_cube * rowdot / full_width)[None, :]
    ).astype(jnp.bfloat16)
    grad_fc = jnp.einsum(
        "jts,rt->jsr",
        stacked,
        lax.all_gather(dfused, "section", axis=0, tiled=True),
        preferred_element_type=jnp.float32,
    ).astype(jnp.bfloat16)
    return (token_loss, grad_fc, grad_gain, grad_lm)


def solution(mesh):
    return jax.shard_map(
        on_device,
        mesh=mesh,
        in_specs=(
            P(("grp", "section"), None),
            P(("grp", "section"), None),
            P(("grp", "section"), None),
            P(None, "section", None),
            P("section"),
            P(None, "section"),
            P("grp"),
        ),
        out_specs=(P("grp"), P("grp", "section", None), P(("grp", "section")), P("grp", "section")),
        check_vma=False,
    )
```

profile of v0, /device:TPU:1, one launch (start us, length us, event | category | flops | bytes accessed | tf_op | source)
XLA Modules:
  0.0 447.0 jit_solution(13795801103387590607)
XLA Ops:
  7.2 0.0 reduce-scatter.3.cloned.1.call-start
  7.2 14.2 %all_to_all.48 = bf16[8,16,512]{2,0,1:T(8,128)(2,1)S(1)} all-to-all(bf16[8,16,512]{2,0,1:T(8,128)(2,1)} %bitcast.32), channel_id=1, replica_groups=mesh['grp'=2,'section'=16] {'section'}, dimensions={1} | all-to-all | bytes 262144 | tf_op jit(solution)/shard_map/all_to_all | solution.py:14
  21.4 11.4 %all_to_all.49 = bf16[8,16,512]{2,0,1:T(8,128)(2,1)S(1)} all-to-all(bf16[8,16,512]{2,0,1:T(8,128)(2,1)} %bitcast.33), channel_id=1, replica_groups=mesh['grp'=2,'section'=16] {'section'}, dimensions={1} | all-to-all | bytes 262144 | tf_op jit(solution)/shard_map/all_to_all | solution.py:15
  32.8 11.4 %all_to_all.50 = bf16[8,16,512]{2,0,1:T(8,128)(2,1)S(1)} all-to-all(bf16[8,16,512]{2,0,1:T(8,128)(2,1)} %bitcast.34), channel_id=1, replica_groups=mesh['grp'=2,'section'=16] {'section'}, dimensions={1} | all-to-all | bytes 262144 | tf_op jit(solution)/shard_map/all_to_all | solution.py:16
  44.2 13.6 %convolution_bitcast_fusion.1 = f32[8192,128]{0,1:T(8,128)} fusion(bf16[3,512,8192]{2,1,0:T(8,128)(2,1)} %param.10, bf16[1,128,512]{2,1,0:T(8,128)(2,1)S(1)} %bitcast.30, bf16[1,128,512]{2,1,0:T(8,128)(2,1)S(1)} %bitcast.28, bf16[1,128,512]{2,1,0:T(8,128)(2,1)S(1)} %bitcast.26), kind=kOutput, calls=%fused_computation.3 | convolution fusion | flops 3221618688 | bytes 29753344 | tf_op jit(solution)/shard_map/jsr,jts->rt/dot_general | solution.py:21
  57.9 0.0 reduce-scatter.3.cloned.1.call-update
  57.9 0.0 all-gather.3.cloned.1.call-start
  57.9 68.9 %reduce-scatter.3.cloned.1.call-done = f32[512,128]{0,1:T(8,128)} async-done(((f32[8192,128]{0,1:T(8,128)}), f32[512,128]{0,1:T(8,128)}) %reduce-scatter.3.cloned.1.call-update) | async-done | bytes 262160 | tf_op jit(solution)/shard_map/reduce_scatter | solution.py:20
  126.8 1.1 multiply_reduce_fusion.2
  127.9 31.3 %psum.28 = f32[128]{0:T(128)S(1)} all-reduce(f32[128]{0:T(128)S(1)} %multiply_reduce_fusion.2), channel_id=1, replica_groups=mesh['grp'=2,'section'=16] {'section'}, use_global_device_ids=true, to_apply=%region_2.0 | all-reduce | flops 128 | bytes 1024 | tf_op jit(solution)/shard_map/psum | solution.py:26
  159.2 0.0 copy-done.2
  159.2 1.7 multiply_convert_fusion
  160.9 0.0 all-gather.3.cloned.1.call-update
  161.0 0.0 reduce-scatter.5.cloned.1.call-start
  161.0 39.5 %all-gather.3.cloned.1.call-done = bf16[8192,128]{0,1:T(8,128)(2,1)} async-done(((bf16[512,128]{0,1:T(8,128)(2,1)}), bf16[8192,128]{0,1:T(8,128)(2,1)}) %all-gather.3.cloned.1.call-update) | async-done | bytes 2097168 | tf_op jit(solution)/shard_map/all_gather | solution.py:29
  200.5 8.8 %fusion.11 = (f32[128]{0:T(128)S(1)}, f32[128,1024]{1,0:T(8,128)S(1)}) fusion(bf16[8192,128]{0,1:T(8,128)(2,1)} %all-gather.3.cloned.1.call-done, bf16[8192,1024]{1,0:T(8,128)(2,1)} %param.12), kind=kOutput, calls=%fused_computation.26 | convolution fusion | flops 2147614720 | bytes 19399168 | tf_op jit(solution)/shard_map/dot_general | solution.py:30
  209.3 29.1 %pmax.7 = f32[128]{0:T(128)S(1)} all-reduce(f32[128]{0:T(128)S(1)} %get-tuple-element.10), channel_id=1, replica_groups=mesh['grp'=2,'section'=16] {'section'}, use_global_device_ids=true, to_apply=%region_4.5 | all-reduce | flops 128 | bytes 1024 | tf_op jit(solution)/shard_map/pmax | solution.py:38
  238.4 0.3 fusion.1
  238.7 31.6 %psum.29 = f32[128]{0:T(128)S(1)} all-reduce(f32[128]{0:T(128)S(1)} %get-tuple-element.7), channel_id=1, replica_groups=mesh['grp'=2,'section'=16] {'section'}, use_global_device_ids=true, to_apply=%region_6.7 | all-reduce | flops 128 | bytes 1024 | tf_op jit(solution)/shard_map/psum | solution.py:40
  270.3 13.7 %convolution_bitcast_fusion = f32[8192,128]{0,1:T(8,128)} fusion(bf16[8192,1024]{1,0:T(8,128)(2,1)} %param.12, f32[128,1024]{1,0:T(8,128)S(1)} %get-tuple-element.11, f32[128]{0:T(128)S(1)} %log_add_fusion, s32[1024]{0:T(1024)S(1)} %iota_add_fusion, s32[128]{0:T(128)S(1)} %copy-done.3), kind=kOutput, calls=%fused_computation.2 | convolution fusion | flops 2148270080 | bytes 21500928 | tf_op jit(solution)/shard_map/dot_general | solution.py:49
  284.0 0.0 reduce-scatter.5.cloned.1.call-update
  284.0 0.0 all-gather.5.cloned.1.call-start
  284.1 67.9 %reduce-scatter.5.cloned.1.call-done = f32[512,128]{0,1:T(8,128)} async-done(((f32[8192,128]{0,1:T(8,128)}), f32[512,128]{0,1:T(8,128)}) %reduce-scatter.5.cloned.1.call-update) | async-done | bytes 262160 | tf_op jit(solution)/shard_map/reduce_scatter | solution.py:48
  352.0 1.7 multiply_reduce_fusion
  353.6 31.4 %all-reduce = (f32[128]{0:T(128)S(1)}, f32[128]{0:T(128)S(1)}) all-reduce(f32[128]{0:T(128)S(1)} %get-tuple-element.6, f32[128]{0:T(128)S(1)} %get-tuple-element.5), channel_id=1, replica_groups=mesh['grp'=2,'section'=16] {'section'}, use_global_device_ids=true, to_apply=%region_8.9 | all-reduce | flops 256 | bytes 2048 | tf_op jit(solution)/shard_map/psum | solution.py:40
  385.1 1.7 subtract_convert_fusion
  386.8 0.0 all-gather.5.cloned.1.call-update
  386.8 0.0 copy-done
  386.8 8.7 %convolution_convert_fusion.1 = bf16[8192,1024]{1,0:T(8,128)(2,1)} fusion(bf16[8192,128]{0,1:T(8,128)(2,1)S(1)} %copy-done, f32[128,1024]{1,0:T(8,128)S(1)} %get-tuple-element.11, f32[128]{0:T(128)S(1)} %log_add_fusion, s32[1024]{0:T(1024)S(1)} %iota_add_fusion, s32[128]{0:T(128)S(1)} %copy-done.3), kind=kOutput, calls=%fused_computation.1 | convolution fusion | flops 2156658688 | bytes 19403776 | tf_op jit(solution)/shard_map/dot_general | solution.py:46
  395.5 0.5 sub.27
  396.0 30.5 %all-gather.5.cloned.1.call-done = bf16[8192,128]{0,1:T(8,128)(2,1)} async-done(((bf16[512,128]{0,1:T(8,128)(2,1)}), bf16[8192,128]{0,1:T(8,128)(2,1)}) %all-gather.5.cloned.1.call-update) | async-done | bytes 2097168 | tf_op jit(solution)/shard_map/all_gather | solution.py:66
  426.5 14.0 %convolution_convert_fusion = bf16[3,512,8192]{2,1,0:T(8,128)(2,1)} fusion(bf16[8192,128]{0,1:T(8,128)(2,1)} %all-gather.5.cloned.1.call-done, bf16[1,128,512]{2,1,0:T(8,128)(2,1)S(1)} %bitcast.31, bf16[1,128,512]{2,1,0:T(8,128)(2,1)S(1)} %bitcast.29, bf16[1,128,512]{2,1,0:T(8,128)(2,1)S(1)} %bitcast.27), kind=kOutput, calls=%fused_computation | convolution fusion | flops 3234201600 | bytes 27656192 | tf_op jit(solution)/shard_map/jts,rt->jsr/dot_general | solution.py:63
  (10 shorter events, 0.0 us)
Async XLA Ops:
  7.2 119.7 %reduce-scatter.3.cloned.1.call-start = ((), (), s32[]{:S(2)}) async-start(), calls=%async_computation.5 | async-start | bytes 4456448 | tf_op jit(solution)/shard_map/reduce_scatter | solution.py:20
  44.2 115.0 %copy-start.2 = (f32[512]{0:T(512)S(1)}, f32[512]{0:T(512)}, u32[]{:S(2)}) copy-start(f32[512]{0:T(512)} %param.11) | copy-start | bytes 6148
  57.9 180.6 %copy-start.3 = (s32[128]{0:T(128)S(1)}, s32[128]{0:T(128)}, u32[]{:S(2)}) copy-start(s32[128]{0:T(128)} %param.13) | copy-start | bytes 1540
  57.9 142.6 %all-gather.3.cloned.1.call-start = ((), (), s32[]{:S(2)}) async-start(), calls=%async_computation.6 | async-start | bytes 2228224 | tf_op jit(solution)/shard_map/all_gather | solution.py:29
  161.0 191.0 %reduce-scatter.5.cloned.1.call-start = ((), (), s32[]{:S(2)}) async-start(), calls=%async_computation.7 | async-start | bytes 4456448 | tf_op jit(solution)/shard_map/reduce_scatter | solution.py:48
  270.3 81.7 %copy-start.1 = (f32[512,128]{0,1:T(8,128)S(1)}, f32[512,128]{0,1:T(8,128)}, u32[]{:S(2)}) copy-start(f32[512,128]{0,1:T(8,128)} %reduce-scatter.3.cloned.1.call-done) | copy-start | bytes 786436
  270.3 116.5 %copy-start = (bf16[8192,128]{0,1:T(8,128)(2,1)S(1)}, bf16[8192,128]{0,1:T(8,128)(2,1)}, u32[]{:S(2)}) copy-start(bf16[8192,128]{0,1:T(8,128)(2,1)} %all-gather.3.cloned.1.call-done) | copy-start | bytes 6291460
  284.0 142.5 %all-gather.5.cloned.1.call-start = ((), (), s32[]{:S(2)}) async-start(), calls=%async_computation.8 | async-start | bytes 2228224 | tf_op jit(solution)/shard_map/all_gather | solution.py:66
Sparse Core Ops, SparseCore 0:
  58.0 68.7 reduce-scatter.2
  161.1 39.3 all-gather.2
  284.1 67.7 reduce-scatter.4
  386.9 39.5 all-gather.4
where the time goes:
time: 448 us; the launch traced here: 447 us
  waiting for transfers between devices  207 us (46%)
  blocking collectives  160 us (36%)
  matrix products  58.8 us (13%)
  between operations  13.8 us (3%)
  other arithmetic  6.95 us (2%)
    reduce_scatter x1, waiting for transfers between devices, on_device(): lax.psum_scatter(jnp.einsum('jsr,jts->rt', w_block, stacked, preferred_el...  68.9 us
    reduce_scatter x1, waiting for transfers between devices, on_device(): lax.psum_scatter(lax.dot_general(w_block, dlogits, (((1,), (1,)), ((), ()...  67.9 us
    psum x2, blocking collectives, on_device(): exp_total, picked = lax.psum((local_total, picked_local), 'section')  63 us
    all_gather x1, waiting for transfers between devices, on_device(): normed_all = lax.all_gather(normed_local, 'section', axis=0, tiled=True)  39.5 us
    psum x1, blocking collectives, on_device(): squares = lax.psum(jnp.sum(joined_local * joined_local, axis=0), 'section')  31.3 us
    all_gather x1, waiting for transfers between devices, on_device(): lax.all_gather(dfused, 'section', axis=0, tiled=True)  30.5 us
    pmax x1, blocking collectives, on_device(): row_peak = lax.pmax(peak_local, 'section')  29.1 us
    all_to_all x1, blocking collectives, on_device(): lax.all_to_all(low_feat, 'section', split_axis=1, concat_axis=0, tiled=True)  14.2 us
  transfers between devices with their start and end apart: 4, of which 4 were waited for; matrix products, arithmetic and copies ran while one was open for 2% of the time, Pallas kernels for 0%

commit v1 on v0

v1 whole, which is shorter than its diff:
```python
import functools

import jax
import jax.numpy as jnp
import numpy as np
from jax import lax
from jax.experimental import pallas as pl
from jax.experimental.pallas import tpu as pltpu
from jax.sharding import PartitionSpec as P

epsilon = 1e-06
VMEM_LIMIT = 48 * 1024 * 1024


def places(order):
    count = len(order)
    out = []
    for q in range(1 << count):
        out.append(sum(((q >> (count - 1 - k)) & 1) << bit for k, bit in enumerate(order)))
    return np.array(out, np.int32)


def exchange(x, bit, size):
    return lax.ppermute(x, "section", [(i, i ^ (1 << bit)) for i in range(size)])


def reduce_halves(low, high, order, size):
    received = exchange(high, order[0], size)
    for bit in order[1:]:
        half = low.shape[0] // 2
        high = low[half:] + received[half:]
        fresh = exchange(high, bit, size)
        low = low[:half] + received[:half]
        received = fresh
    return low[0] + received[0]


def gather_halves(own, order, size):
    held = own[None]
    for bit in order[:0:-1]:
        held = jnp.concatenate([held, exchange(held, bit, size)], axis=0)
    return held, exchange(held, order[0], size)


def params(steps_flops, steps_bytes):
    return dict(
        compiler_params=pltpu.CompilerParams(vmem_limit_bytes=VMEM_LIMIT),
        cost_estimate=pl.CostEstimate(flops=steps_flops, bytes_accessed=steps_bytes, transcendentals=0),
    )


def join_kernel(table, x_ref, w_ref, first_ref, second_ref):
    rows = w_ref.shape[1]
    total = jnp.dot(x_ref[:, :rows], w_ref[0], preferred_element_type=jnp.float32)
    total += jnp.dot(x_ref[:, rows : 2 * rows], w_ref[1], preferred_element_type=jnp.float32)
    total += jnp.dot(x_ref[:, 2 * rows :], w_ref[2], preferred_element_type=jnp.float32)
    half = total.shape[0] // 2
    first_ref[0] = total[:half]
    second_ref[0] = total[half:]


def join(table, x, w_fc):
    count = table.shape[1]
    tokens = x.shape[0]
    rows = w_fc.shape[1]
    shape = jax.ShapeDtypeStruct((count, tokens // 2, rows), jnp.float32)
    if rows % 128:
        total = jnp.dot(x, w_fc.reshape(-1, w_fc.shape[2]), preferred_element_type=jnp.float32)
        total = total.reshape(2, tokens // 2, -1, rows).transpose(0, 2, 1, 3)
        chosen = jnp.take(total, table[0], axis=1)
        return jnp.take(chosen[0], table[1], axis=0), jnp.take(chosen[1], table[2], axis=0)
    return pl.pallas_call(
        join_kernel,
        out_shape=(shape, shape),
        grid_spec=pltpu.PrefetchScalarGridSpec(
            num_scalar_prefetch=1,
            grid=(count,),
            in_specs=[
                pl.BlockSpec(x.shape, lambda g, t: (0, 0)),
                pl.BlockSpec((3, rows, rows), lambda g, t: (0, 0, t[0, g])),
            ],
            out_specs=(
                pl.BlockSpec((1, tokens // 2, rows), lambda g, t: (t[1, g], 0, 0)),
                pl.BlockSpec((1, tokens // 2, rows), lambda g, t: (t[2, g], 0, 0)),
            ),
        ),
        name="join",
        **params(6 * tokens * rows * rows * count, count * (6 * rows * rows + 4 * tokens * rows)),
    )(table, x, w_fc)


def logits_kernel(table, first_ref, second_ref, w_ref, out_ref):
    block = jnp.concatenate([first_ref[0], second_ref[0]], axis=0)
    part = jnp.dot(block, w_ref[...], preferred_element_type=jnp.float32)

    @pl.when(pl.program_id(0) == 0)
    def _():
        out_ref[...] = part

    @pl.when(pl.program_id(0) != 0)
    def _():
        out_ref[...] += part


def natural(table, first, second):
    chosen = jnp.concatenate([jnp.take(first, table[1], axis=0), jnp.take(second, table[2], axis=0)], axis=1)
    return chosen


def head(table, first, second, w_lm):
    count, half, rows = first.shape
    share = w_lm.shape[1]
    if rows % 128:
        block = natural(table, first, second)
        weights = jnp.take(w_lm.reshape(-1, rows, share), table[0], axis=0)
        return jnp.einsum("ctr,crv->tv", block, weights, preferred_element_type=jnp.float32)
    return pl.pallas_call(
        logits_kernel,
        out_shape=jax.ShapeDtypeStruct((2 * half, share), jnp.float32),
        grid_spec=pltpu.PrefetchScalarGridSpec(
            num_scalar_prefetch=1,
            grid=(count,),
            in_specs=[
                pl.BlockSpec((1, half, rows), lambda g, t: (t[1, g], 0, 0)),
                pl.BlockSpec((1, half, rows), lambda g, t: (t[2, g], 0, 0)),
                pl.BlockSpec((rows, share), lambda g, t: (t[0, g], 0)),
            ],
            out_specs=pl.BlockSpec((2 * half, share), lambda g, t: (0, 0)),
        ),
        name="head",
        **params(4 * half * rows * share * count, count * rows * (2 * share + 4 * half)),
    )(table, first, second, w_lm)


def back_kernel(table, d_ref, w_ref, first_ref, second_ref):
    total = lax.dot_general(
        d_ref[...], w_ref[...], (((1,), (1,)), ((), ())), preferred_element_type=jnp.float32
    )
    half = total.shape[0] // 2
    first_ref[0] = total[:half]
    second_ref[0] = total[half:]


def back(table, dlogits, w_lm, rows):
    count = table.shape[1]
    tokens, share = dlogits.shape
    shape = jax.ShapeDtypeStruct((count, tokens // 2, rows), jnp.float32)
    if rows % 128:
        total = lax.dot_general(
            dlogits, w_lm, (((1,), (1,)), ((), ())), preferred_element_type=jnp.float32
        )
        total = total.reshape(2, tokens // 2, -1, rows).transpose(0, 2, 1, 3)
        chosen = jnp.take(total, table[0], axis=1)
        return jnp.take(chosen[0], table[1], axis=0), jnp.take(chosen[1], table[2], axis=0)
    return pl.pallas_call(
        back_kernel,
        out_shape=(shape, shape),
        grid_spec=pltpu.PrefetchScalarGridSpec(
            num_scalar_prefetch=1,
            grid=(count,),
            in_specs=[
                pl.BlockSpec(dlogits.shape, lambda g, t: (0, 0)),
                pl.BlockSpec((rows, share), lambda g, t: (t[0, g], 0)),
            ],
            out_specs=(
                pl.BlockSpec((1, tokens // 2, rows), lambda g, t: (t[1, g], 0, 0)),
                pl.BlockSpec((1, tokens // 2, rows), lambda g, t: (t[2, g], 0, 0)),
            ),
        ),
        name="back",
        **params(2 * tokens * rows * share * count, count * rows * (2 * share + 4 * tokens)),
    )(table, dlogits, w_lm)


def head_grad_kernel(table, fl_ref, sl_ref, fh_ref, sh_ref, d_ref, out_ref):
    step = pl.program_id(0)
    half_steps = pl.num_programs(0) // 2

    def fill(first_ref, second_ref):
        block = jnp.concatenate([first_ref[0], second_ref[0]], axis=0)
        out_ref[...] = lax.dot_general(
            block, d_ref[...], (((0,), (0,)), ((), ())), preferred_element_type=jnp.float32
        ).astype(out_ref.dtype)

    @pl.when(step < half_steps)
    def _():
        fill(fl_ref, sl_ref)

    @pl.when(step >= half_steps)
    def _():
        fill(fh_ref, sh_ref)


def paired_specs(count, half, rows):
    low = lambda row: lambda g, t: (t[row, jnp.minimum(g, count - 1)], 0, 0)
    high = lambda row: lambda g, t: (t[row, jnp.maximum(g - count, 0)], 0, 0)
    shape = (1, half, rows)
    return [pl.BlockSpec(shape, low(1)), pl.BlockSpec(shape, low(2)), pl.BlockSpec(shape, high(1)), pl.BlockSpec(shape, high(2))]


def head_grad(table, low, high, dlogits):
    count, half, rows = low[0].shape
    tokens, share = dlogits.shape
    if rows % 128:
        block = jnp.concatenate(
            [natural(table[:, :count], *low), natural(table[:, :count], *high)], axis=0
        )
        block = jnp.take(block, jnp.argsort(table[0]), axis=0)
        return jnp.einsum("ctr,tv->crv", block, dlogits, preferred_element_type=jnp.float32).astype(
            jnp.bfloat16
        ).reshape(-1, share)
    return pl.pallas_call(
        head_grad_kernel,
        out_shape=jax.ShapeDtypeStruct((2 * count * rows, share), jnp.bfloat16),
        grid_spec=pltpu.PrefetchScalarGridSpec(
            num_scalar_prefetch=1,
            grid=(2 * count,),
            in_specs=paired_specs(count, half, rows) + [pl.BlockSpec(dlogits.shape, lambda g, t: (0, 0))],
            out_specs=pl.BlockSpec((rows, share), lambda g, t: (t[0, g], 0)),
        ),
        name="head_grad",
        **params(4 * tokens * rows * share * count, 2 * count * rows * (2 * share + 2 * tokens)),
    )(table, low[0], low[1], high[0], high[1], dlogits)


def join_grad_kernel(table, fl_ref, sl_ref, fh_ref, sh_ref, x_ref, out_ref):
    step = pl.program_id(0)
    half_steps = pl.num_programs(0) // 2
    rows = out_ref.shape[1]

    def fill(first_ref, second_ref):
        block = jnp.concatenate([first_ref[0], second_ref[0]], axis=0)
        for j in range(3):
            out_ref[j] = jnp.dot(
                x_ref[j * rows : (j + 1) * rows, :], block, preferred_element_type=jnp.float32
            ).astype(out_ref.dtype)

    @pl.when(step < half_steps)
    def _():
        fill(fl_ref, sl_ref)

    @pl.when(step >= half_steps)
    def _():
        fill(fh_ref, sh_ref)


def join_grad(table, low, high, x_turned):
    count, half, rows = low[0].shape
    tokens = 2 * half
    if rows % 128:
        block = jnp.concatenate(
            [natural(table[:, :count], *low), natural(table[:, :count], *high)], axis=0
        )
        block = jnp.take(block, jnp.argsort(table[0]), axis=0)
        return jnp.einsum(
            "jrt,cts->jrcs", x_turned.reshape(3, rows, tokens), block, preferred_element_type=jnp.float32
        ).astype(jnp.bfloat16).reshape(3, rows, -1)
    return pl.pallas_call(
        join_grad_kernel,
        out_shape=jax.ShapeDtypeStruct((3, rows, 2 * count * rows), jnp.bfloat16),
        grid_spec=pltpu.PrefetchScalarGridSpec(
            num_scalar_prefetch=1,
            grid=(2 * count,),
            in_specs=paired_specs(count, half, rows) + [pl.BlockSpec(x_turned.shape, lambda g, t: (0, 0))],
            out_specs=pl.BlockSpec((3, rows, rows), lambda g, t: (0, 0, t[0, g])),
        ),
        name="join_grad",
        **params(12 * tokens * rows * rows * count, 2 * count * rows * (6 * rows + 2 * tokens)),
    )(table, low[0], low[1], high[0], high[1], x_turned)


def merge_sums(a, b):
    peak = jnp.maximum(a[0], b[0])
    shift_a, shift_b = a[0] - peak, b[0] - peak
    scale_a, scale_b = jnp.exp(shift_a), jnp.exp(shift_b)
    return jnp.stack(
        [
            peak,
            a[1] * scale_a + b[1] * scale_b,
            (a[2] + a[1] * shift_a) * scale_a + (b[2] + b[1] * shift_b) * scale_b,
            a[3] + b[3],
        ]
    )


def on_device(size, low_feat, mid_feat, high_feat, w_fc, gain, w_lm, targets):
    me = lax.axis_index("section")
    rows, full_width = w_fc.shape[1], w_fc.shape[2]
    tokens = targets.shape[0]
    half = tokens // 2
    bits = size.bit_length() - 1
    orders = (list(range(bits)), [0, 2, 1] + list(range(3, bits)))

    place_first, place_second = places(orders[0]), places(orders[1])
    where_second = np.argsort(place_second)[place_first]
    count = size // 2
    within = np.stack([np.arange(size) % count, where_second % count])
    chunk = jnp.asarray(place_first) ^ me
    table = jnp.concatenate([chunk[None], jnp.asarray(within, jnp.int32)], axis=0).astype(jnp.int32)
    table_low, table_high = table[:, :count], table[:, count:]

    sent = jnp.concatenate(
        [f.reshape(-1, size, rows) for f in (low_feat, mid_feat, high_feat)], axis=2
    ).transpose(1, 0, 2)
    x = lax.all_to_all(sent, "section", split_axis=0, concat_axis=0, tiled=True).reshape(tokens, 3 * rows)

    joined_high = join(table_high, x, w_fc)
    joined_low = join(table_low, x, w_fc)
    joined = jnp.concatenate(
        [reduce_halves(joined_low[s], joined_high[s], orders[s], size) for s in range(2)], axis=0
    )

    squares_own = jnp.sum(joined * joined, axis=1)
    squares = jnp.sum(
        lax.all_to_all(
            jnp.broadcast_to(squares_own[None], (size, tokens)), "section", split_axis=0, concat_axis=0, tiled=True
        ),
        axis=0,
    )
    inv_rms = lax.rsqrt(squares / full_width + epsilon)[:, None]
    normed = (joined * inv_rms * gain[None, :]).astype(jnp.bfloat16)
    parts = [gather_halves(normed[s * half : (s + 1) * half], orders[s], size) for s in range(2)]
    normed_low = [p[0] for p in parts]
    normed_high = [p[1] for p in parts]

    logits = head(table_low, *normed_low, w_lm) + head(table_high, *normed_high, w_lm)
    share = w_lm.shape[1]
    column = me * share + lax.iota(jnp.int32, share)
    is_target = column[None, :] == targets[:, None]
    peak = jnp.max(logits, axis=1)
    shifted = logits - peak[:, None]
    weight = jnp.exp(shifted)
    sums = jnp.stack(
        [
            peak,
            jnp.sum(weight, axis=1),
            jnp.sum(weight * shifted, axis=1),
            jnp.sum(jnp.where(is_target, logits, 0.0), axis=1),
        ]
    )
    for bit in range(bits):
        sums = merge_sums(sums, exchange(sums, bit, size))
    peak, exp_total, exp_moment, picked = sums
    log_total = peak + jnp.log(exp_total)
    token_loss = log_total - picked
    dlogits = (
        (jnp.exp(logits - log_total[:, None]) - is_target.astype(jnp.float32)) / tokens
    ).astype(jnp.bfloat16)
    rowdot = ((exp_moment / exp_total - (picked - peak)) / tokens)[:, None] / inv_rms

    back_high = back(table_high, dlogits, w_lm, rows)
    back_low = back(table_low, dlogits, w_lm, rows)
    grad_lm = head_grad(table, normed_low, normed_high, dlogits)
    dnormed = jnp.concatenate(
        [reduce_halves(back_low[s], back_high[s], orders[s], size) for s in range(2)], axis=0
    )

    grad_gain = jnp.sum(dnormed * joined * inv_rms, axis=0)
    dfused = (
        inv_rms * (dnormed * gain[None, :]) - joined * (inv_rms * inv_rms * inv_rms * rowdot / full_width)
    ).astype(jnp.bfloat16)
    parts = [gather_halves(dfused[s * half : (s + 1) * half], orders[s], size) for s in range(2)]
    grad_fc = join_grad(table, [p[0] for p in parts], [p[1] for p in parts], x.T)
    return (token_loss, grad_fc, grad_gain, grad_lm)


def solution(mesh):
    return jax.shard_map(
        functools.partial(on_device, mesh.shape["section"]),
        mesh=mesh,
        in_specs=(
            P(("grp", "section"), None),
            P(("grp", "section"), None),
            P(("grp", "section"), None),
            P(None, "section", None),
            P("section"),
            P(None, "section"),
            P("grp"),
        ),
        out_specs=(P("grp"), P("grp", "section", None), P(("grp", "section")), P("grp", "section")),
        check_vma=False,
    )
```

time: 448 us -> 244 us (0.54)
  blocking collectives: 160 us -> 11.5 us
  waiting for transfers between devices: 207 us -> 104 us
  Pallas kernels: 0 us -> 77.7 us
  matrix products: 58.8 us -> 0 us
  starting transfers between devices: 0.16 us -> 37.6 us
  between operations: 13.8 us -> 1.01 us
    reduce_scatter x2 -> x0, waiting for transfers between devices: 137 us -> none  [the longest x1 68.9 us: on_device(): lax.psum_scatter(jnp.einsum('jsr,jts->rt', w_block, stacked, preferred_el...]
    psum x3 -> x0, blocking collectives: 94.3 us -> none  [the longest x2 63 us: on_device(): exp_total, picked = lax.psum((local_total, picked_local), 'section')]
    ppermute x0 -> x36, waiting for transfers between devices: none -> 93.5 us  [exchange(): return lax.ppermute(x, 'section', [(i, i ^ 1 << bit) for i in range(size)])]
    pallas_call x0 -> x8, Pallas kernels: none -> 77.7 us  [the longest x2 17.1 us: join(): pl.pallas_call(join_kernel, out_shape=(shape, shape), grid_spec=pltpu.Pre...]
    all_gather x2 -> x0, waiting for transfers between devices: 69.9 us -> none  [the longest x1 39.5 us: on_device(): normed_all = lax.all_gather(normed_local, 'section', axis=0, tiled=True)]
    dot_general x5 -> x0, matrix products: 58.8 us -> none  [the longest x1 14 us: on_device(): jnp.einsum('jts,rt->jsr', stacked, lax.all_gather(dfused, 'section', axis...]
    ppermute x0 -> x36, starting transfers between devices: none -> 30.3 us  [exchange(): return lax.ppermute(x, 'section', [(i, i ^ 1 << bit) for i in range(size)])]
    pmax x1 -> x0, blocking collectives: 29.1 us -> none  [on_device(): row_peak = lax.pmax(peak_local, 'section')]
  transfers between devices with their start and end apart: 4 -> 37, of which waited for: 4 -> 25; matrix products, arithmetic and copies ran while one was open for 2% -> 2% of each run, Pallas kernels for 0% -> 15%
where the time goes in v1:
time: 244 us; the launch traced here: 242 us
  waiting for transfers between devices  104 us (43%)
  Pallas kernels  77.7 us (32%)
  starting transfers between devices  37.6 us (15%)
  blocking collectives  11.5 us (5%)
  other arithmetic  7.94 us (3%)
    ppermute x36, waiting for transfers between devices, exchange(): return lax.ppermute(x, 'section', [(i, i ^ 1 << bit) for i in range(size)])  93.5 us
    ppermute x36, starting transfers between devices, exchange(): return lax.ppermute(x, 'section', [(i, i ^ 1 << bit) for i in range(size)])  30.3 us
    pallas_call x2, Pallas kernels, join(): pl.pallas_call(join_kernel, out_shape=(shape, shape), grid_spec=pltpu.Pre...  17.1 us
    pallas_call x1, Pallas kernels, join_grad(): pl.pallas_call(join_grad_kernel, out_shape=jax.ShapeDtypeStruct((3, rows,...  16.5 us
    pallas_call x2, Pallas kernels, back(): pl.pallas_call(back_kernel, out_shape=(shape, shape), grid_spec=pltpu.Pre...  16.4 us
    pallas_call x2, Pallas kernels, head(): pl.pallas_call(logits_kernel, out_shape=jax.ShapeDtypeStruct((2 * half, s...  15.1 us
    pallas_call x1, Pallas kernels, head_grad(): pl.pallas_call(head_grad_kernel, out_shape=jax.ShapeDtypeStruct((2 * coun...  12.5 us
    all_to_all x1, blocking collectives, on_device(): lax.all_to_all(jnp.broadcast_to(squares_own[None], (size, tokens)), 'sect...  11.5 us
  transfers between devices with their start and end apart: 37, of which 25 were waited for; matrix products, arithmetic and copies ran while one was open for 2% of the time, Pallas kernels for 15%

profile of v1, /device:TPU:1, one launch (start us, length us, event | category | flops | bytes accessed | tf_op | source)
XLA Modules:
  0.0 241.8 jit_solution(10663488259707113223)
XLA Ops:
  2.4 7.3 %all-to-all-start = ((bf16[16,8,1536]{2,1,0:T(8,128)(2,1)}), bf16[16,8,1536]{2,1,0:T(8,128)(2,1)S(1)}, u32[]{:S(2)}, u32[]{:S(2)}) async-start(bf16[16,8,1536]{2,1,0:T(8,128)(2,1)} %maximum_bitcast_fusion), calls=%async_computation | async-start | bytes 786432 | tf_op jit(solution)/shard_map/all_to_all | solution.py:305
  11.2 10.5 %all-to-all-done = bf16[16,8,1536]{2,1,0:T(8,128)(2,1)S(1)} async-done(((bf16[16,8,1536]{2,1,0:T(8,128)(2,1)}), bf16[16,8,1536]{2,1,0:T(8,128)(2,1)S(1)}, u32[]{:S(2)}, u32[]{:S(2)}) %all-to-all-start) | async-done | bytes 393248 | tf_op jit(solution)/shard_map/all_to_all | solution.py:305
  21.7 8.6 %join.3 = (f32[8,64,512]{2,1,0:T(8,128)S(1)}, f32[8,64,512]{2,1,0:T(8,128)S(1)}) custom-call(s32[3,8]{1,0:T(4,128)S(1)} %get-tuple-element.63.table, bf16[128,1536]{1,0:T(8,128)(2,1)S(1)} %bitcast.258, bf16[3,512,8192]{2,1,0:T(8,128)(2,1)} %w_ref.7), custom_call_target="tpu_custom_call" | custom-call | flops 1610612736 | bytes 14680064 | tf_op jit(solution)/shard_map/join/pallas_call | solution.py:72
  30.8 8.6 %join.2 = (f32[8,64,512]{2,1,0:T(8,128)S(1)}, f32[8,64,512]{2,1,0:T(8,128)S(1)}) custom-call(s32[3,8]{1,0:T(4,128)S(1)} %get-tuple-element.64.table, bf16[128,1536]{1,0:T(8,128)(2,1)S(1)} %bitcast.259, bf16[3,512,8192]{2,1,0:T(8,128)(2,1)} %w_ref.7), custom_call_target="tpu_custom_call" | custom-call | flops 1610612736 | bytes 14680064 | tf_op jit(solution)/shard_map/join/pallas_call | solution.py:72
  41.4 11.4 %collective-permute-done.5 = f32[4,64,512]{2,1,0:T(8,128)S(1)} collective-permute-done((f32[4,64,512]{2,1,0:T(8,128)S(1)}, f32[4,64,512]{2,1,0:T(8,128)S(1)}, u32[]{:S(2)}, u32[]{:S(2)}) %collective-permute-start.5) | collective-permute-done | bytes 524320 | tf_op jit(solution)/shard_map/ppermute | solution.py:24
  54.8 4.8 %collective-permute-done.6 = f32[2,64,512]{2,1,0:T(8,128)S(1)} collective-permute-done((f32[2,64,512]{2,1,0:T(8,128)S(1)}, f32[2,64,512]{2,1,0:T(8,128)S(1)}, u32[]{:S(2)}, u32[]{:S(2)}) %collective-permute-start.6) | collective-permute-done | bytes 262176 | tf_op jit(solution)/shard_map/ppermute | solution.py:24
  62.1 2.3 collective-permute-done.7
  64.4 8.6 %collective-permute-done.3 = f32[1,64,512]{2,1,0:T(8,128)S(1)} collective-permute-done((f32[1,64,512]{2,1,0:T(8,128)S(1)}, f32[1,64,512]{2,1,0:T(8,128)S(1)}, u32[]{:S(2)}, u32[]{:S(2)}) %collective-permute-start.3) | collective-permute-done | bytes 131104 | tf_op jit(solution)/shard_map/ppermute | solution.py:24
  73.1 11.5 %all_to_all.11 = f32[16,1,128]{2,1,0:T(1,128)S(1)} all-to-all(f32[16,1,128]{2,1,0:T(1,128)S(1)} %broadcast_in_dim.17), channel_id=1, replica_groups=mesh['grp'=2,'section'=16] {'section'}, dimensions={0} | all-to-all | bytes 16384 | tf_op jit(solution)/shard_map/all_to_all | solution.py:315
  87.2 5.3 %collective-permute-done.8 = bf16[1,64,512]{2,1,0:T(8,128)(2,1)S(1)} collective-permute-done((bf16[1,64,512]{2,1,0:T(8,128)(2,1)S(1)}, bf16[1,64,512]{2,1,0:T(8,128)(2,1)S(1)}, u32[]{:S(2)}, u32[]{:S(2)}) %collective-permute-start.8) | collective-permute-done | bytes 65568 | tf_op jit(solution)/shard_map/ppermute | solution.py:24
  94.3 2.7 %collective-permute-done.9 = bf16[2,64,512]{2,1,0:T(8,128)(2,1)S(1)} collective-permute-done((bf16[2,64,512]{2,1,0:T(8,128)(2,1)S(1)}, bf16[2,64,512]{2,1,0:T(8,128)(2,1)S(1)}, u32[]{:S(2)}, u32[]{:S(2)}) %collective-permute-start.9) | collective-permute-done | bytes 131104 | tf_op jit(solution)/shard_map/ppermute | solution.py:24
  98.7 4.8 %collective-permute-done.10 = bf16[4,64,512]{2,1,0:T(8,128)(2,1)S(1)} collective-permute-done((bf16[4,64,512]{2,1,0:T(8,128)(2,1)S(1)}, bf16[4,64,512]{2,1,0:T(8,128)(2,1)S(1)}, u32[]{:S(2)}, u32[]{:S(2)}) %collective-permute-start.10) | collective-permute-done | bytes 262176 | tf_op jit(solution)/shard_map/ppermute | solution.py:24
  103.5 2.5 %collective-permute-start.14 = (bf16[8,64,512]{2,1,0:T(8,128)(2,1)S(1)}, bf16[8,64,512]{2,1,0:T(8,128)(2,1)S(1)}, u32[]{:S(2)}, u32[]{:S(2)}) collective-permute-start(bf16[8,64,512]{2,1,0:T(8,128)(2,1)S(1)} %pad_maximum_fusion.first_ref.fl_ref), channel_id=1, source_target_pairs={{0,1},{1,0},{2,3},{3,2},{4,5},{5,4},{6,7},{7,6},{8,9},{9,8},{10,11... | collective-permute-start | bytes 1572872 | tf_op jit(solution)/shard_map/ppermute | solution.py:24
  107.5 7.6 %head.2 = f32[128,1024]{1,0:T(8,128)S(1)} custom-call(s32[3,8]{1,0:T(4,128)S(1)} %get-tuple-element.64.table, bf16[8,64,512]{2,1,0:T(8,128)(2,1)S(1)} %pad_maximum_fusion.first_ref.fl_ref, bf16[8,64,512]{2,1,0:T(8,128)(2,1)S(1)} %pad_maximum_fusion.1.second_ref.sl_ref, bf16[8192,1024]{1,0:T(8,128)(2,1)} %w_ref.11), custom_call_target="tpu_custom_call" | custom-call | flops 1073741824 | bytes 9437184 | tf_op jit(solution)/shard_map/head/pallas_call | solution.py:117
  115.1 7.6 %head.3 = f32[128,1024]{1,0:T(8,128)S(1)} custom-call(s32[3,8]{1,0:T(4,128)S(1)} %get-tuple-element.63.table, bf16[8,64,512]{2,1,0:T(8,128)(2,1)S(1)} %collective-permute-done.14.first_ref.fh_ref, bf16[8,64,512]{2,1,0:T(8,128)(2,1)S(1)} %collective-permute-done.15.second_ref.sh_ref, bf16[8192,1024]{1,0:T(8,128)(2,1)} %w_ref.11), custom_call_target="tpu_custom_call" | custom-call | flops 1073741824 | bytes 9437184 | tf_op jit(solution)/shard_map/head/pallas_call | solution.py:117
  124.8 2.1 collective-permute-done.17
  127.1 2.4 %collective-permute-done.18 = f32[4,128]{1,0:T(4,128)S(1)} collective-permute-done((f32[4,128]{1,0:T(4,128)S(1)}, f32[4,128]{1,0:T(4,128)S(1)}, u32[]{:S(2)}, u32[]{:S(2)}) %collective-permute-start.18) | collective-permute-done | bytes 2080 | tf_op jit(solution)/shard_map/ppermute | solution.py:24
  129.6 3.3 %collective-permute-done.19 = f32[4,128]{1,0:T(4,128)S(1)} collective-permute-done((f32[4,128]{1,0:T(4,128)S(1)}, f32[4,128]{1,0:T(4,128)S(1)}, u32[]{:S(2)}, u32[]{:S(2)}) %collective-permute-start.19) | collective-permute-done | bytes 2080 | tf_op jit(solution)/shard_map/ppermute | solution.py:24
  133.7 8.2 %back.3 = (f32[8,64,512]{2,1,0:T(8,128)S(1)}, f32[8,64,512]{2,1,0:T(8,128)S(1)}) custom-call(s32[3,8]{1,0:T(4,128)S(1)} %get-tuple-element.63.table, bf16[128,1024]{1,0:T(8,128)(2,1)S(1)} %fusion.3.d_ref, bf16[8192,1024]{1,0:T(8,128)(2,1)} %w_ref.11), custom_call_target="tpu_custom_call" | custom-call | flops 1073741824 | bytes 10485760 | tf_op jit(solution)/shard_map/back/pallas_call | solution.py:155
  141.9 3.7 %collective-permute-start.24 = (f32[8,64,512]{2,1,0:T(8,128)S(1)}, f32[8,64,512]{2,1,0:T(8,128)S(1)}, u32[]{:S(2)}, u32[]{:S(2)}) collective-permute-start(f32[8,64,512]{2,1,0:T(8,128)S(1)} %get-tuple-element.19), channel_id=1, source_target_pairs={{0,1},{1,0},{2,3},{3,2},{4,5},{5,4},{6,7},{7,6},{8,9},{9,8},{10,11... | collective-permute-start | bytes 3145736 | tf_op jit(solution)/shard_map/ppermute | solution.py:24
  145.7 8.2 %back.2 = (f32[8,64,512]{2,1,0:T(8,128)S(1)}, f32[8,64,512]{2,1,0:T(8,128)S(1)}) custom-call(s32[3,8]{1,0:T(4,128)S(1)} %get-tuple-element.64.table, bf16[128,1024]{1,0:T(8,128)(2,1)S(1)} %fusion.3.d_ref, bf16[8192,1024]{1,0:T(8,128)(2,1)} %w_ref.11), custom_call_target="tpu_custom_call" | custom-call | flops 1073741824 | bytes 10485760 | tf_op jit(solution)/shard_map/back/pallas_call | solution.py:155
  154.8 12.4 %collective-permute-done.25 = f32[4,64,512]{2,1,0:T(8,128)S(1)} collective-permute-done((f32[4,64,512]{2,1,0:T(8,128)S(1)}, f32[4,64,512]{2,1,0:T(8,128)S(1)}, u32[]{:S(2)}, u32[]{:S(2)}) %collective-permute-start.25) | collective-permute-done | bytes 524320 | tf_op jit(solution)/shard_map/ppermute | solution.py:24
  168.8 5.1 %collective-permute-done.26 = f32[2,64,512]{2,1,0:T(8,128)S(1)} collective-permute-done((f32[2,64,512]{2,1,0:T(8,128)S(1)}, f32[2,64,512]{2,1,0:T(8,128)S(1)}, u32[]{:S(2)}, u32[]{:S(2)}) %collective-permute-start.26) | collective-permute-done | bytes 262176 | tf_op jit(solution)/shard_map/ppermute | solution.py:24
  174.1 2.4 collective-permute-start.23
  176.4 9.2 %collective-permute-done.27 = f32[1,64,512]{2,1,0:T(8,128)S(1)} collective-permute-done((f32[1,64,512]{2,1,0:T(8,128)S(1)}, f32[1,64,512]{2,1,0:T(8,128)S(1)}, u32[]{:S(2)}, u32[]{:S(2)}) %collective-permute-start.27) | collective-permute-done | bytes 131104 | tf_op jit(solution)/shard_map/ppermute | solution.py:24
  185.7 2.8 %collective-permute-done.23 = f32[1,64,512]{2,1,0:T(8,128)S(1)} collective-permute-done((f32[1,64,512]{2,1,0:T(8,128)S(1)}, f32[1,64,512]{2,1,0:T(8,128)S(1)}, u32[]{:S(2)}, u32[]{:S(2)}) %collective-permute-start.23) | collective-permute-done | bytes 131104 | tf_op jit(solution)/shard_map/ppermute | solution.py:24
  189.3 2.4 collective-permute-start.31
  191.7 2.7 %collective-permute-done.28 = bf16[1,64,512]{2,1,0:T(8,128)(2,1)S(1)} collective-permute-done((bf16[1,64,512]{2,1,0:T(8,128)(2,1)S(1)}, bf16[1,64,512]{2,1,0:T(8,128)(2,1)S(1)}, u32[]{:S(2)}, u32[]{:S(2)}) %collective-permute-start.28) | collective-permute-done | bytes 65568 | tf_op jit(solution)/shard_map/ppermute | solution.py:24
  200.9 4.2 %collective-permute-done.30 = bf16[4,64,512]{2,1,0:T(8,128)(2,1)S(1)} collective-permute-done((bf16[4,64,512]{2,1,0:T(8,128)(2,1)S(1)}, bf16[4,64,512]{2,1,0:T(8,128)(2,1)S(1)}, u32[]{:S(2)}, u32[]{:S(2)}) %collective-permute-start.30) | collective-permute-done | bytes 262176 | tf_op jit(solution)/shard_map/ppermute | solution.py:24
  205.1 3.1 %collective-permute-start.34 = (bf16[8,64,512]{2,1,0:T(8,128)(2,1)S(1)}, bf16[8,64,512]{2,1,0:T(8,128)(2,1)}, u32[]{:S(2)}, u32[]{:S(2)}) collective-permute-start(bf16[8,64,512]{2,1,0:T(8,128)(2,1)S(1)} %pad_maximum_fusion.2.fl_ref), channel_id=1, source_target_pairs={{0,1},{1,0},{2,3},{3,2},{4,5},{5,4},{6,7},{7,6},{8,9},{9,8},{10,11... | collective-permute-start | bytes 1572872 | tf_op jit(solution)/shard_map/ppermute | solution.py:24
  211.8 12.5 %head_grad.1 = bf16[8192,1024]{1,0:T(8,128)(2,1)} custom-call(s32[3,16]{1,0:T(4,128)S(1)} %pad_add_fusion.table, bf16[8,64,512]{2,1,0:T(8,128)(2,1)S(1)} %pad_maximum_fusion.first_ref.fl_ref, bf16[8,64,512]{2,1,0:T(8,128)(2,1)S(1)} %pad_maximum_fusion.1.second_ref.sl_ref, bf16[8,64,512]{2,1,0:T(8,128)(2,1)S(1)} %collective-permute-done.14.first_ref.fh_ref, ...), custom_call_target="tpu_custom_call" | custom-call | flops 2147483648 | bytes 18874368 | tf_op jit(solution)/shard_map/head_grad/pallas_call | solution.py:212
  225.3 16.5 %join_grad.1 = bf16[3,512,8192]{2,1,0:T(8,128)(2,1)} custom-call(s32[3,16]{1,0:T(4,128)S(1)} %pad_add_fusion.table, bf16[8,64,512]{2,1,0:T(8,128)(2,1)S(1)} %pad_maximum_fusion.2.fl_ref, bf16[8,64,512]{2,1,0:T(8,128)(2,1)} %pad_maximum_fusion.3.sl_ref, bf16[8,64,512]{2,1,0:T(8,128)(2,1)} %collective-permute-done.34.fh_ref, ...), custom_call_target="tpu_custom_call" | custom-call | flops 3221225472 | bytes 27262976 | tf_op jit(solution)/shard_map/join_grad/pallas_call | solution.py:258
  (113 shorter events, 35.6 us)
Async XLA Ops:
  2.4 19.3 %all-to-all-start = ((bf16[16,8,1536]{2,1,0:T(8,128)(2,1)}), bf16[16,8,1536]{2,1,0:T(8,128)(2,1)S(1)}, u32[]{:S(2)}, u32[]{:S(2)}) async-start(bf16[16,8,1536]{2,1,0:T(8,128)(2,1)} %maximum_bitcast_fusion), calls=%async_computation | async-start | bytes 786432 | tf_op jit(solution)/shard_map/all_to_all | solution.py:305
  30.3 9.2 %collective-permute-start.4 = (f32[8,64,512]{2,1,0:T(8,128)S(1)}, f32[8,64,512]{2,1,0:T(8,128)S(1)}, u32[]{:S(2)}, u32[]{:S(2)}) collective-permute-start(f32[8,64,512]{2,1,0:T(8,128)S(1)} %get-tuple-element.15), channel_id=1, source_target_pairs={{0,1},{1,0},{2,3},{3,2},{4,5},{5,4},{6,7},{7,6},{8,9},{9,8},{10,11... | collective-permute-start | bytes 3145736 | tf_op jit(solution)/shard_map/ppermute | solution.py:24
  30.7 9.9 %collective-permute-start = (f32[8,64,512]{2,1,0:T(8,128)S(1)}, f32[8,64,512]{2,1,0:T(8,128)S(1)}, u32[]{:S(2)}, u32[]{:S(2)}) collective-permute-start(f32[8,64,512]{2,1,0:T(8,128)S(1)} %get-tuple-element.13), channel_id=1, source_target_pairs={{0,1},{1,0},{2,3},{3,2},{4,5},{5,4},{6,7},{7,6},{8,9},{9,8},{10,11... | collective-permute-start | bytes 3145736 | tf_op jit(solution)/shard_map/ppermute | solution.py:24
  39.7 13.2 %collective-permute-start.5 = (f32[4,64,512]{2,1,0:T(8,128)S(1)}, f32[4,64,512]{2,1,0:T(8,128)S(1)}, u32[]{:S(2)}, u32[]{:S(2)}) collective-permute-start(f32[4,64,512]{2,1,0:T(8,128)S(1)} %get-tuple-element.40), channel_id=1, source_target_pairs={{0,4},{1,5},{2,6},{3,7},{4,0},{5,1},{6,2},{7,3},{8,12},{9,13},{10,... | collective-permute-start | bytes 1572872 | tf_op jit(solution)/shard_map/ppermute | solution.py:24
  40.8 13.2 %collective-permute-start.1 = (f32[4,64,512]{2,1,0:T(8,128)S(1)}, f32[4,64,512]{2,1,0:T(8,128)S(1)}, u32[]{:S(2)}, u32[]{:S(2)}) collective-permute-start(f32[4,64,512]{2,1,0:T(8,128)S(1)} %get-tuple-element.38), channel_id=1, source_target_pairs={{0,2},{1,3},{2,0},{3,1},{4,6},{5,7},{6,4},{7,5},{8,10},{9,11},{10,... | collective-permute-start | bytes 1572872 | tf_op jit(solution)/shard_map/ppermute | solution.py:24
  52.9 6.6 %collective-permute-start.6 = (f32[2,64,512]{2,1,0:T(8,128)S(1)}, f32[2,64,512]{2,1,0:T(8,128)S(1)}, u32[]{:S(2)}, u32[]{:S(2)}) collective-permute-start(f32[2,64,512]{2,1,0:T(8,128)S(1)} %get-tuple-element.48), channel_id=1, source_target_pairs={{0,2},{1,3},{2,0},{3,1},{4,6},{5,7},{6,4},{7,5},{8,10},{9,11},{10,... | collective-permute-start | bytes 786440 | tf_op jit(solution)/shard_map/ppermute | solution.py:24
  54.1 6.8 %collective-permute-start.2 = (f32[2,64,512]{2,1,0:T(8,128)S(1)}, f32[2,64,512]{2,1,0:T(8,128)S(1)}, u32[]{:S(2)}, u32[]{:S(2)}) collective-permute-start(f32[2,64,512]{2,1,0:T(8,128)S(1)} %get-tuple-element.46), channel_id=1, source_target_pairs={{0,4},{1,5},{2,6},{3,7},{4,0},{5,1},{6,2},{7,3},{8,12},{9,13},{10,... | collective-permute-start | bytes 786440 | tf_op jit(solution)/shard_map/ppermute | solution.py:24
  59.6 4.8 %collective-permute-start.7 = (f32[1,64,512]{2,1,0:T(8,128)S(1)}, f32[1,64,512]{2,1,0:T(8,128)S(1)}, u32[]{:S(2)}, u32[]{:S(2)}) collective-permute-start(f32[1,64,512]{2,1,0:T(8,128)S(1)} %slice_add_fusion.20), channel_id=1, source_target_pairs={{0,8},{1,9},{2,10},{3,11},{4,12},{5,13},{6,14},{7,15},{8,0},{9,1},... | collective-permute-start | bytes 393224 | tf_op jit(solution)/shard_map/ppermute | solution.py:24
  61.0 12.0 %collective-permute-start.3 = (f32[1,64,512]{2,1,0:T(8,128)S(1)}, f32[1,64,512]{2,1,0:T(8,128)S(1)}, u32[]{:S(2)}, u32[]{:S(2)}) collective-permute-start(f32[1,64,512]{2,1,0:T(8,128)S(1)} %slice_add_fusion.22), channel_id=1, source_target_pairs={{0,8},{1,9},{2,10},{3,11},{4,12},{5,13},{6,14},{7,15},{8,0},{9,1},... | collective-permute-start | bytes 393224 | tf_op jit(solution)/shard_map/ppermute | solution.py:24
  84.8 7.8 %collective-permute-start.8 = (bf16[1,64,512]{2,1,0:T(8,128)(2,1)S(1)}, bf16[1,64,512]{2,1,0:T(8,128)(2,1)S(1)}, u32[]{:S(2)}, u32[]{:S(2)}) collective-permute-start(bf16[1,64,512]{2,1,0:T(8,128)(2,1)S(1)} %get-tuple-element.54), channel_id=1, source_target_pairs={{0,8},{1,9},{2,10},{3,11},{4,12},{5,13},{6,14},{7,15},{8,0},{9,1},... | collective-permute-start | bytes 196616 | tf_op jit(solution)/shard_map/ppermute | solution.py:24
  85.2 8.8 %collective-permute-start.11 = (bf16[1,64,512]{2,1,0:T(8,128)(2,1)S(1)}, bf16[1,64,512]{2,1,0:T(8,128)(2,1)S(1)}, u32[]{:S(2)}, u32[]{:S(2)}) collective-permute-start(bf16[1,64,512]{2,1,0:T(8,128)(2,1)S(1)} %get-tuple-element.53), channel_id=1, source_target_pairs={{0,8},{1,9},{2,10},{3,11},{4,12},{5,13},{6,14},{7,15},{8,0},{9,1},... | collective-permute-start | bytes 196616 | tf_op jit(solution)/shard_map/ppermute | solution.py:24
  92.6 4.5 %collective-permute-start.9 = (bf16[2,64,512]{2,1,0:T(8,128)(2,1)S(1)}, bf16[2,64,512]{2,1,0:T(8,128)(2,1)S(1)}, u32[]{:S(2)}, u32[]{:S(2)}) collective-permute-start(bf16[2,64,512]{2,1,0:T(8,128)(2,1)S(1)} %pad_maximum_fusion.10), channel_id=1, source_target_pairs={{0,4},{1,5},{2,6},{3,7},{4,0},{5,1},{6,2},{7,3},{8,12},{9,13},{10,... | collective-permute-start | bytes 393224 | tf_op jit(solution)/shard_map/ppermute | solution.py:24
  94.0 4.6 %collective-permute-start.12 = (bf16[2,64,512]{2,1,0:T(8,128)(2,1)S(1)}, bf16[2,64,512]{2,1,0:T(8,128)(2,1)S(1)}, u32[]{:S(2)}, u32[]{:S(2)}) collective-permute-start(bf16[2,64,512]{2,1,0:T(8,128)(2,1)S(1)} %pad_maximum_fusion.11), channel_id=1, source_target_pairs={{0,2},{1,3},{2,0},{3,1},{4,6},{5,7},{6,4},{7,5},{8,10},{9,11},{10,... | collective-permute-start | bytes 393224 | tf_op jit(solution)/shard_map/ppermute | solution.py:24
  97.1 6.4 %collective-permute-start.10 = (bf16[4,64,512]{2,1,0:T(8,128)(2,1)S(1)}, bf16[4,64,512]{2,1,0:T(8,128)(2,1)S(1)}, u32[]{:S(2)}, u32[]{:S(2)}) collective-permute-start(bf16[4,64,512]{2,1,0:T(8,128)(2,1)S(1)} %pad_maximum_fusion.5), channel_id=1, source_target_pairs={{0,2},{1,3},{2,0},{3,1},{4,6},{5,7},{6,4},{7,5},{8,10},{9,11},{10,... | collective-permute-start | bytes 786440 | tf_op jit(solution)/shard_map/ppermute | solution.py:24
  98.6 7.4 %collective-permute-start.13 = (bf16[4,64,512]{2,1,0:T(8,128)(2,1)S(1)}, bf16[4,64,512]{2,1,0:T(8,128)(2,1)S(1)}, u32[]{:S(2)}, u32[]{:S(2)}) collective-permute-start(bf16[4,64,512]{2,1,0:T(8,128)(2,1)S(1)} %pad_maximum_fusion.6), channel_id=1, source_target_pairs={{0,4},{1,5},{2,6},{3,7},{4,0},{5,1},{6,2},{7,3},{8,12},{9,13},{10,... | collective-permute-start | bytes 786440 | tf_op jit(solution)/shard_map/ppermute | solution.py:24
  103.5 11.6 %collective-permute-start.14 = (bf16[8,64,512]{2,1,0:T(8,128)(2,1)S(1)}, bf16[8,64,512]{2,1,0:T(8,128)(2,1)S(1)}, u32[]{:S(2)}, u32[]{:S(2)}) collective-permute-start(bf16[8,64,512]{2,1,0:T(8,128)(2,1)S(1)} %pad_maximum_fusion.first_ref.fl_ref), channel_id=1, source_target_pairs={{0,1},{1,0},{2,3},{3,2},{4,5},{5,4},{6,7},{7,6},{8,9},{9,8},{10,11... | collective-permute-start | bytes 1572872 | tf_op jit(solution)/shard_map/ppermute | solution.py:24
  106.1 9.1 %collective-permute-start.15 = (bf16[8,64,512]{2,1,0:T(8,128)(2,1)S(1)}, bf16[8,64,512]{2,1,0:T(8,128)(2,1)S(1)}, u32[]{:S(2)}, u32[]{:S(2)}) collective-permute-start(bf16[8,64,512]{2,1,0:T(8,128)(2,1)S(1)} %pad_maximum_fusion.1.second_ref.sl_ref), channel_id=1, source_target_pairs={{0,1},{1,0},{2,3},{3,2},{4,5},{5,4},{6,7},{7,6},{8,9},{9,8},{10,11... | collective-permute-start | bytes 1572872 | tf_op jit(solution)/shard_map/ppermute | solution.py:24
  141.9 12.0 %collective-permute-start.24 = (f32[8,64,512]{2,1,0:T(8,128)S(1)}, f32[8,64,512]{2,1,0:T(8,128)S(1)}, u32[]{:S(2)}, u32[]{:S(2)}) collective-permute-start(f32[8,64,512]{2,1,0:T(8,128)S(1)} %get-tuple-element.19), channel_id=1, source_target_pairs={{0,1},{1,0},{2,3},{3,2},{4,5},{5,4},{6,7},{7,6},{8,9},{9,8},{10,11... | collective-permute-start | bytes 3145736 | tf_op jit(solution)/shard_map/ppermute | solution.py:24
  145.6 8.6 %collective-permute-start.20 = (f32[8,64,512]{2,1,0:T(8,128)S(1)}, f32[8,64,512]{2,1,0:T(8,128)S(1)}, u32[]{:S(2)}, u32[]{:S(2)}) collective-permute-start(f32[8,64,512]{2,1,0:T(8,128)S(1)} %get-tuple-element.17), channel_id=1, source_target_pairs={{0,1},{1,0},{2,3},{3,2},{4,5},{5,4},{6,7},{7,6},{8,9},{9,8},{10,11... | collective-permute-start | bytes 3145736 | tf_op jit(solution)/shard_map/ppermute | solution.py:24
  154.1 13.1 %collective-permute-start.25 = (f32[4,64,512]{2,1,0:T(8,128)S(1)}, f32[4,64,512]{2,1,0:T(8,128)S(1)}, u32[]{:S(2)}, u32[]{:S(2)}) collective-permute-start(f32[4,64,512]{2,1,0:T(8,128)S(1)} %get-tuple-element.36), channel_id=1, source_target_pairs={{0,4},{1,5},{2,6},{3,7},{4,0},{5,1},{6,2},{7,3},{8,12},{9,13},{10,... | collective-permute-start | bytes 1572872 | tf_op jit(solution)/shard_map/ppermute | solution.py:24
  154.4 13.3 %collective-permute-start.21 = (f32[4,64,512]{2,1,0:T(8,128)S(1)}, f32[4,64,512]{2,1,0:T(8,128)S(1)}, u32[]{:S(2)}, u32[]{:S(2)}) collective-permute-start(f32[4,64,512]{2,1,0:T(8,128)S(1)} %get-tuple-element.34), channel_id=1, source_target_pairs={{0,2},{1,3},{2,0},{3,1},{4,6},{5,7},{6,4},{7,5},{8,10},{9,11},{10,... | collective-permute-start | bytes 1572872 | tf_op jit(solution)/shard_map/ppermute | solution.py:24
  167.3 6.6 %collective-permute-start.26 = (f32[2,64,512]{2,1,0:T(8,128)S(1)}, f32[2,64,512]{2,1,0:T(8,128)S(1)}, u32[]{:S(2)}, u32[]{:S(2)}) collective-permute-start(f32[2,64,512]{2,1,0:T(8,128)S(1)} %get-tuple-element.44), channel_id=1, source_target_pairs={{0,2},{1,3},{2,0},{3,1},{4,6},{5,7},{6,4},{7,5},{8,10},{9,11},{10,... | collective-permute-start | bytes 786440 | tf_op jit(solution)/shard_map/ppermute | solution.py:24
  167.7 6.3 %collective-permute-start.22 = (f32[2,64,512]{2,1,0:T(8,128)S(1)}, f32[2,64,512]{2,1,0:T(8,128)S(1)}, u32[]{:S(2)}, u32[]{:S(2)}) collective-permute-start(f32[2,64,512]{2,1,0:T(8,128)S(1)} %get-tuple-element.42), channel_id=1, source_target_pairs={{0,4},{1,5},{2,6},{3,7},{4,0},{5,1},{6,2},{7,3},{8,12},{9,13},{10,... | collective-permute-start | bytes 786440 | tf_op jit(solution)/shard_map/ppermute | solution.py:24
  173.9 11.7 %collective-permute-start.27 = (f32[1,64,512]{2,1,0:T(8,128)S(1)}, f32[1,64,512]{2,1,0:T(8,128)S(1)}, u32[]{:S(2)}, u32[]{:S(2)}) collective-permute-start(f32[1,64,512]{2,1,0:T(8,128)S(1)} %slice_add_fusion.16), channel_id=1, source_target_pairs={{0,8},{1,9},{2,10},{3,11},{4,12},{5,13},{6,14},{7,15},{8,0},{9,1},... | collective-permute-start | bytes 393224 | tf_op jit(solution)/shard_map/ppermute | solution.py:24
  174.1 14.4 %collective-permute-start.23 = (f32[1,64,512]{2,1,0:T(8,128)S(1)}, f32[1,64,512]{2,1,0:T(8,128)S(1)}, u32[]{:S(2)}, u32[]{:S(2)}) collective-permute-start(f32[1,64,512]{2,1,0:T(8,128)S(1)} %slice_add_fusion.18), channel_id=1, source_target_pairs={{0,8},{1,9},{2,10},{3,11},{4,12},{5,13},{6,14},{7,15},{8,0},{9,1},... | collective-permute-start | bytes 393224 | tf_op jit(solution)/shard_map/ppermute | solution.py:24
  189.2 5.2 %collective-permute-start.28 = (bf16[1,64,512]{2,1,0:T(8,128)(2,1)S(1)}, bf16[1,64,512]{2,1,0:T(8,128)(2,1)S(1)}, u32[]{:S(2)}, u32[]{:S(2)}) collective-permute-start(bf16[1,64,512]{2,1,0:T(8,128)(2,1)S(1)} %get-tuple-element.52), channel_id=1, source_target_pairs={{0,8},{1,9},{2,10},{3,11},{4,12},{5,13},{6,14},{7,15},{8,0},{9,1},... | collective-permute-start | bytes 196616 | tf_op jit(solution)/shard_map/ppermute | solution.py:24
  189.3 7.2 %collective-permute-start.31 = (bf16[1,64,512]{2,1,0:T(8,128)(2,1)S(1)}, bf16[1,64,512]{2,1,0:T(8,128)(2,1)S(1)}, u32[]{:S(2)}, u32[]{:S(2)}) collective-permute-start(bf16[1,64,512]{2,1,0:T(8,128)(2,1)S(1)} %get-tuple-element.51), channel_id=1, source_target_pairs={{0,8},{1,9},{2,10},{3,11},{4,12},{5,13},{6,14},{7,15},{8,0},{9,1},... | collective-permute-start | bytes 196616 | tf_op jit(solution)/shard_map/ppermute | solution.py:24
  196.5 4.3 %collective-permute-start.32 = (bf16[2,64,512]{2,1,0:T(8,128)(2,1)S(1)}, bf16[2,64,512]{2,1,0:T(8,128)(2,1)S(1)}, u32[]{:S(2)}, u32[]{:S(2)}) collective-permute-start(bf16[2,64,512]{2,1,0:T(8,128)(2,1)S(1)} %pad_maximum_fusion.13), channel_id=1, source_target_pairs={{0,2},{1,3},{2,0},{3,1},{4,6},{5,7},{6,4},{7,5},{8,10},{9,11},{10,... | collective-permute-start | bytes 393224 | tf_op jit(solution)/shard_map/ppermute | solution.py:24
  198.3 6.8 %collective-permute-start.30 = (bf16[4,64,512]{2,1,0:T(8,128)(2,1)S(1)}, bf16[4,64,512]{2,1,0:T(8,128)(2,1)S(1)}, u32[]{:S(2)}, u32[]{:S(2)}) collective-permute-start(bf16[4,64,512]{2,1,0:T(8,128)(2,1)S(1)} %pad_maximum_fusion.8), channel_id=1, source_target_pairs={{0,2},{1,3},{2,0},{3,1},{4,6},{5,7},{6,4},{7,5},{8,10},{9,11},{10,... | collective-permute-start | bytes 786440 | tf_op jit(solution)/shard_map/ppermute | solution.py:24
  200.8 7.4 %collective-permute-start.33 = (bf16[4,64,512]{2,1,0:T(8,128)(2,1)S(1)}, bf16[4,64,512]{2,1,0:T(8,128)(2,1)S(1)}, u32[]{:S(2)}, u32[]{:S(2)}) collective-permute-start(bf16[4,64,512]{2,1,0:T(8,128)(2,1)S(1)} %pad_maximum_fusion.9), channel_id=1, source_target_pairs={{0,4},{1,5},{2,6},{3,7},{4,0},{5,1},{6,2},{7,3},{8,12},{9,13},{10,... | collective-permute-start | bytes 786440 | tf_op jit(solution)/shard_map/ppermute | solution.py:24
  205.1 19.2 %collective-permute-start.34 = (bf16[8,64,512]{2,1,0:T(8,128)(2,1)S(1)}, bf16[8,64,512]{2,1,0:T(8,128)(2,1)}, u32[]{:S(2)}, u32[]{:S(2)}) collective-permute-start(bf16[8,64,512]{2,1,0:T(8,128)(2,1)S(1)} %pad_maximum_fusion.2.fl_ref), channel_id=1, source_target_pairs={{0,1},{1,0},{2,3},{3,2},{4,5},{5,4},{6,7},{7,6},{8,9},{9,8},{10,11... | collective-permute-start | bytes 1572872 | tf_op jit(solution)/shard_map/ppermute | solution.py:24
  209.1 15.2 %collective-permute-start.35 = (bf16[8,64,512]{2,1,0:T(8,128)(2,1)}, bf16[8,64,512]{2,1,0:T(8,128)(2,1)}, u32[]{:S(2)}, u32[]{:S(2)}) collective-permute-start(bf16[8,64,512]{2,1,0:T(8,128)(2,1)} %pad_maximum_fusion.3.sl_ref), channel_id=1, source_target_pairs={{0,1},{1,0},{2,3},{3,2},{4,5},{5,4},{6,7},{7,6},{8,9},{9,8},{10,11... | collective-permute-start | bytes 1572872 | tf_op jit(solution)/shard_map/ppermute | solution.py:24
  (8 other events, 159.7 us)

commit v2 on v0

v2 whole, which is shorter than its diff:
```python
import functools

import jax
import jax.numpy as jnp
import numpy as np
from jax import lax
from jax.experimental import pallas as pl
from jax.experimental.pallas import tpu as pltpu
from jax.sharding import PartitionSpec as P

epsilon = 1e-06
MIB = 1024 * 1024
SMALL_LIMIT = 12 * MIB
SLOTS = 6


def places(order):
    count = len(order)
    out = []
    for q in range(1 << count):
        out.append(sum(((q >> (count - 1 - k)) & 1) << bit for k, bit in enumerate(order)))
    return np.array(out, np.int32)


def exchange(x, mask, size):
    return lax.ppermute(x, "section", [(i, i ^ mask) for i in range(size)])


def settings(flops, bytes_moved, limit=SMALL_LIMIT):
    return dict(
        compiler_params=pltpu.CompilerParams(vmem_limit_bytes=limit),
        cost_estimate=pl.CostEstimate(flops=flops, bytes_accessed=bytes_moved, transcendentals=0),
    )


ANYWHERE = pl.BlockSpec(memory_space=pl.ANY)
IN_VMEM = pl.BlockSpec(memory_space=pltpu.VMEM)
IN_SMEM = pl.BlockSpec(memory_space=pltpu.SMEM)


vmem_out = pltpu.VMEM


def near(x):
    return pltpu.with_memory_space_constraint(x, pltpu.VMEM)


def stage_kernel(pieces, w_ref, after_ref, out_ref, token_ref, sems):
    copies = []
    for k, piece in enumerate(pieces):
        copies.append(pltpu.make_async_copy(w_ref.at[piece], out_ref.at[piece], sems.at[k]))
    for copy in copies:
        copy.start()
    token_ref[...] = jnp.ones_like(token_ref)
    for copy in copies:
        copy.wait()


def stage(w, after, half):
    pieces = []
    if w.ndim == 3:
        step = w.shape[1] // 8
        pieces = [(j, pl.ds(k * step, step)) for j in range(w.shape[0]) for k in range(8)]
    else:
        step = w.shape[0] // 16
        pieces = [pl.ds(k * step, step) for k in range(16)]
    return pl.pallas_call(
        functools.partial(stage_kernel, pieces),
        out_shape=(vmem_out(w.shape, w.dtype), jax.ShapeDtypeStruct((1, half), jnp.float32)),
        in_specs=[ANYWHERE, ANYWHERE],
        out_specs=(IN_VMEM, IN_VMEM),
        scratch_shapes=[pltpu.SemaphoreType.DMA((len(pieces),))],
        name="stage",
        **settings(0, w.size * 2),
    )(w, after)


def join_kernel(first, count, chunks, x_ref, w_ref, a_ref, b_ref):
    rows = w_ref.shape[1]
    half = rows // 2

    @pl.loop(0, count)
    def _(q):
        for s, out in enumerate((a_ref, b_ref)):
            column = pl.multiple_of(chunks[s, first + q] * rows + s * half, 128)
            total = jnp.dot(x_ref[:, :rows], w_ref[0, :, pl.ds(column, half)], preferred_element_type=jnp.float32)
            for j in (1, 2):
                total += jnp.dot(
                    x_ref[:, j * rows : (j + 1) * rows],
                    w_ref[j, :, pl.ds(column, half)],
                    preferred_element_type=jnp.float32,
                )
            out[q] = total


def join(chunks, first, count, x, w_fc):
    tokens = x.shape[0]
    rows = w_fc.shape[1]
    half = rows // 2
    out = vmem_out((count, tokens, half), jnp.float32)
    return pl.pallas_call(
        functools.partial(join_kernel, first, count),
        out_shape=(out, out),
        in_specs=[IN_SMEM, IN_VMEM, IN_VMEM],
        out_specs=(IN_VMEM, IN_VMEM),
        name="join",
        **settings(6 * tokens * rows * rows * count, 4 * tokens * rows * count),
    )(chunks, near(x), near(w_fc))


def head_kernel(first, count, chunks, a_ref, b_ref, w_ref, before_ref, out_ref, token_ref):
    half = a_ref.shape[2]
    out_ref[...] = before_ref[...]
    token_ref[...] = jnp.ones_like(token_ref)

    @pl.loop(0, count)
    def _(q):
        total = out_ref[...]
        for s, piece in enumerate((a_ref, b_ref)):
            row = pl.multiple_of(chunks[s, first + q] * (2 * half) + s * half, 128)
            total += jnp.dot(piece[q], w_ref[pl.ds(row, half), :], preferred_element_type=jnp.float32)
        out_ref[...] = total


def head(chunks, first, pieces, w_lm, before):
    count, tokens, half = pieces[0].shape
    share = w_lm.shape[1]
    return pl.pallas_call(
        functools.partial(head_kernel, first, count),
        out_shape=(vmem_out(before.shape, jnp.float32), vmem_out((1, half), jnp.float32)),
        in_specs=[IN_SMEM, IN_VMEM, IN_VMEM, IN_VMEM, IN_VMEM],
        out_specs=(IN_VMEM, IN_VMEM),
        name="head",
        **settings(4 * tokens * half * share * count, 8 * tokens * share),
    )(chunks, near(pieces[0]), near(pieces[1]), near(w_lm), near(before))


def back_kernel(first, count, chunks, d_ref, w_ref, a_ref, b_ref):
    half = a_ref.shape[2]

    @pl.loop(0, count)
    def _(q):
        for s, out in enumerate((a_ref, b_ref)):
            row = pl.multiple_of(chunks[s, first + q] * (2 * half) + s * half, 128)
            out[q] = lax.dot_general(
                d_ref[...],
                w_ref[pl.ds(row, half), :],
                (((1,), (1,)), ((), ())),
                preferred_element_type=jnp.float32,
            )


def back(chunks, first, count, dlogits, w_lm, half):
    tokens, share = dlogits.shape
    out = vmem_out((count, tokens, half), jnp.float32)
    return pl.pallas_call(
        functools.partial(back_kernel, first, count),
        out_shape=(out, out),
        in_specs=[IN_SMEM, IN_VMEM, IN_VMEM],
        out_specs=(IN_VMEM, IN_VMEM),
        name="back",
        **settings(4 * tokens * half * share * count, 8 * tokens * half * count),
    )(chunks, near(dlogits), near(w_lm))


def head_grad_kernel(first, count, aliased, chunks, a_ref, b_ref, d_ref, *rest):
    out_ref, token_ref, slots, sems = rest[1 + aliased :]
    half = a_ref.shape[2]
    token_ref[...] = jnp.ones_like(token_ref)
    started = []
    for q in range(count):
        for s, piece in enumerate((a_ref, b_ref)):
            slot = len(started) % SLOTS
            if len(started) >= SLOTS:
                started[-SLOTS].wait()
            row = pl.multiple_of(chunks[s, first + q] * (2 * half) + s * half, 128)
            slots[slot] = lax.dot_general(
                piece[q], d_ref[...], (((0,), (0,)), ((), ())), preferred_element_type=jnp.float32
            ).astype(slots.dtype)
            copy = pltpu.make_async_copy(slots.at[slot], out_ref.at[pl.ds(row, half), :], sems.at[slot])
            copy.start()
            started.append(copy)
    for copy in started[-SLOTS:]:
        copy.wait()


def head_grad(chunks, first, pieces, dlogits, width, after, into=None):
    count, tokens, half = pieces[0].shape
    share = dlogits.shape[1]
    aliased = into is not None
    extra = (into,) if aliased else ()
    return pl.pallas_call(
        functools.partial(head_grad_kernel, first, count, aliased),
        out_shape=(
            jax.ShapeDtypeStruct((width, share), jnp.bfloat16),
            jax.ShapeDtypeStruct((1, half), jnp.float32),
        ),
        in_specs=[IN_SMEM, IN_VMEM, IN_VMEM, IN_VMEM, ANYWHERE] + [ANYWHERE] * len(extra),
        out_specs=(ANYWHERE, IN_VMEM),
        scratch_shapes=[pltpu.VMEM((SLOTS, half, share), jnp.bfloat16), pltpu.SemaphoreType.DMA((SLOTS,))],
        input_output_aliases={5: 0} if aliased else {},
        name="head_grad",
        **settings(4 * tokens * half * share * count, 4 * half * share * count),
    )(chunks, near(pieces[0]), near(pieces[1]), near(dlogits), after, *extra)


def join_grad_kernel(first, count, aliased, chunks, a_ref, b_ref, x_ref, *rest):
    out_ref, token_ref, slots, sems = rest[aliased:]
    half = a_ref.shape[2]
    rows = 2 * half
    token_ref[...] = jnp.ones_like(token_ref)
    started = []
    for q in range(count):
        for s, piece in enumerate((a_ref, b_ref)):
            slot = len(started) % SLOTS
            if len(started) >= SLOTS:
                started[-SLOTS].wait()
            column = pl.multiple_of(chunks[s, first + q] * rows + s * half, 128)
            for j in range(3):
                slots[slot, j] = jnp.dot(
                    x_ref[j * rows : (j + 1) * rows, :], piece[q], preferred_element_type=jnp.float32
                ).astype(slots.dtype)
            copy = pltpu.make_async_copy(slots.at[slot], out_ref.at[:, :, pl.ds(column, half)], sems.at[slot])
            copy.start()
            started.append(copy)
    for copy in started[-SLOTS:]:
        copy.wait()


def join_grad(chunks, first, pieces, x_turned, width, into=None):
    count, tokens, half = pieces[0].shape
    rows = 2 * half
    aliased = into is not None
    extra = (into,) if aliased else ()
    return pl.pallas_call(
        functools.partial(join_grad_kernel, first, count, aliased),
        out_shape=(
            jax.ShapeDtypeStruct((3, rows, width), jnp.bfloat16),
            jax.ShapeDtypeStruct((1, half), jnp.float32),
        ),
        in_specs=[IN_SMEM, IN_VMEM, IN_VMEM, IN_VMEM] + [ANYWHERE] * len(extra),
        out_specs=(ANYWHERE, IN_VMEM),
        scratch_shapes=[pltpu.VMEM((SLOTS, 3, rows, half), jnp.bfloat16), pltpu.SemaphoreType.DMA((SLOTS,))],
        input_output_aliases={4: 0} if aliased else {},
        name="join_grad",
        **settings(12 * tokens * rows * rows * count, 6 * rows * rows * count),
    )(chunks, near(pieces[0]), near(pieces[1]), near(x_turned), *extra)


def cut(total, chunks, rows):
    tokens = total.shape[0]
    blocks = total.reshape(tokens, -1, 2, rows // 2).transpose(2, 1, 0, 3)
    parts = [jnp.take(blocks[s], chunks[s], axis=0) for s in range(2)]
    count = chunks.shape[1] // 2
    return [p[:count] for p in parts], [p[count:] for p in parts]


def whole(pieces, chunks):
    parts = [jnp.take(pieces[s], jnp.argsort(chunks[s]), axis=0) for s in range(2)]
    return jnp.concatenate(parts, axis=2).transpose(1, 0, 2).reshape(pieces[0].shape[1], -1)


def groups_of(bits):
    later = [list(range(at, min(at + 3, bits))) for at in range(1, bits, 3)]
    return later + [[0]]


def contributions(x, group, size):
    masks = [sum(1 << b for k, b in enumerate(group) if (m >> k) & 1) for m in range(1 << len(group))]
    return [x] + [exchange(x, m, size) for m in masks[1:]]


def tree_sum(items):
    while len(items) > 1:
        items = [items[k] + items[k + 1] for k in range(0, len(items), 2)]
    return items[0]


def merge_sums(items):
    peak = functools.reduce(jnp.maximum, [i[0] for i in items])
    shifts = [i[0] - peak for i in items]
    scales = [jnp.exp(s) for s in shifts]
    return jnp.stack(
        [
            peak,
            tree_sum([i[1] * c for i, c in zip(items, scales)]),
            tree_sum([(i[2] + i[1] * s) * c for i, s, c in zip(items, shifts, scales)]),
            tree_sum([i[3] for i in items]),
        ]
    )


def reduce_halves(low, high, orders, size, pack, unpack, work):
    received = [exchange(pack(high[s]), 1 << orders[s][0], size) for s in range(2)]
    token = None
    for k in range(1, len(orders[0])):
        half = low[0].shape[0] // 2
        arrived = [unpack(r, token) for r in received]
        high = [low[s][half:] + arrived[s][half:] for s in range(2)]
        received = [exchange(pack(high[s]), 1 << orders[s][k], size) for s in range(2)]
        low = [low[s][:half] + arrived[s][:half] for s in range(2)]
        token = work(k, high[0])
    return [low[s][0] + unpack(received[s], token)[0] for s in range(2)]


def gather_doubling(own, orders, size, work):
    held = [o[None] for o in own]
    fresh = held
    first = 0
    for k in range(len(orders[0]) - 1, -1, -1):
        arrived = [exchange(held[s], 1 << orders[s][k], size) for s in range(2)]
        token = work(first, fresh)
        first = held[0].shape[0]
        if k:
            if token is not None:
                arrived = [(a.astype(jnp.float32) * token[None]).astype(a.dtype) for a in arrived]
            held = [jnp.concatenate([held[s], arrived[s]], axis=0) for s in range(2)]
        fresh = arrived
    work(first, fresh)
    return held, fresh


HALF_SCALE = 2.0**20


def on_device(size, low_feat, mid_feat, high_feat, w_fc, gain, w_lm, targets):
    me = lax.axis_index("section")
    rows, full_width = w_fc.shape[1], w_fc.shape[2]
    share = w_lm.shape[1]
    tokens = targets.shape[0]
    half = rows // 2
    bits = size.bit_length() - 1
    count = size // 2
    orders = (list(range(bits)), [0, 2, 1] + list(range(3, bits)))
    chunks = jnp.asarray(np.stack([places(o) for o in orders])) ^ me
    kernels = half % 128 == 0

    sent = jnp.concatenate(
        [f.reshape(-1, size, rows) for f in (low_feat, mid_feat, high_feat)], axis=2
    ).transpose(1, 0, 2)
    x = lax.all_to_all(sent, "section", split_axis=0, concat_axis=0, tiled=True).reshape(tokens, 3 * rows)
    x_turned = x.T

    held = {}
    if kernels:
        near_fc, _ = stage(w_fc, sent, half)
        high = join(chunks, count, count, x, near_fc)
        low = join(chunks, 0, count, x, near_fc)
    else:
        total = jnp.dot(x, w_fc.reshape(3 * rows, full_width), preferred_element_type=jnp.float32)
        low, high = cut(total, chunks, rows)

    def bring_head(k, sent):
        if kernels and k == 1:
            held["lm"], token = stage(w_lm, sent, half)
            return token

    def plain(x, token):
        return x if token is None else x * token[None]

    joined = jnp.concatenate(
        reduce_halves(low, high, orders, size, lambda x: x, plain, bring_head), axis=1
    )

    squares = jnp.sum(joined * joined, axis=1)
    for group in groups_of(bits):
        squares = tree_sum(contributions(squares, group, size))
    inv_rms = lax.rsqrt(squares / full_width + epsilon)[:, None]
    normed = (joined * inv_rms * gain[None, :]).astype(jnp.bfloat16)

    held["logits"] = jnp.zeros((tokens, share), jnp.float32)

    def add_logits(first, pieces):
        if kernels:
            held["logits"], token = head(chunks, first, pieces, held["lm"], held["logits"])
            return token

    normed_low, normed_high = gather_doubling(
        [normed[:, :half], normed[:, half:]], orders, size, add_logits
    )
    if kernels:
        logits = held["logits"]
    else:
        normed_all = whole(
            [jnp.concatenate([normed_low[s], normed_high[s]], axis=0) for s in range(2)], chunks
        )
        logits = jnp.dot(normed_all, w_lm, preferred_element_type=jnp.float32)

    column = me * share + lax.iota(jnp.int32, share)
    is_target = column[None, :] == targets[:, None]
    peak = jnp.max(logits, axis=1)
    shifted = logits - peak[:, None]
    weight = jnp.exp(shifted)
    sums = jnp.stack(
        [
            peak,
            jnp.sum(weight, axis=1),
            jnp.sum(weight * shifted, axis=1),
            jnp.sum(jnp.where(is_target, logits, 0.0), axis=1),
        ]
    )
    for group in groups_of(bits):
        sums = merge_sums(contributions(sums, group, size))
    peak, exp_total, exp_moment, picked = sums
    log_total = peak + jnp.log(exp_total)
    token_loss = log_total - picked
    dlogits = (
        (jnp.exp(logits - log_total[:, None]) - is_target.astype(jnp.float32)) / tokens
    ).astype(jnp.bfloat16)
    rowdot = ((exp_moment / exp_total - (picked - peak)) / tokens)[:, None] / inv_rms

    if kernels:
        high = back(chunks, count, count, dlogits, held["lm"], half)
        low = back(chunks, 0, count, dlogits, held["lm"], half)
    else:
        total = lax.dot_general(
            dlogits, w_lm, (((1,), (1,)), ((), ())), preferred_element_type=jnp.float32
        )
        low, high = cut(total, chunks, rows)

    def fill_grad_lm(k, sent):
        if not kernels:
            return None
        if k == 1:
            held["grad_lm"], token = head_grad(chunks, 0, normed_low, dlogits, full_width, sent)
            return token
        if k == bits - 1:
            held["grad_lm"], token = head_grad(
                chunks, count, normed_high, dlogits, full_width, sent, held["grad_lm"]
            )
            return token

    scale = HALF_SCALE * (tokens / 128)

    def pack_half(x):
        return (x * scale).astype(jnp.float16)

    def unpack_half(x, token):
        wide = x.astype(jnp.float32) * (1.0 / scale)
        return wide if token is None else wide * token[None]

    dnormed = jnp.concatenate(
        reduce_halves(low, high, orders, size, pack_half, unpack_half, fill_grad_lm), axis=1
    )
    if kernels:
        grad_lm = held["grad_lm"]
    else:
        grad_lm = lax.dot_general(
            normed_all, dlogits, (((0,), (0,)), ((), ())), preferred_element_type=jnp.float32
        ).astype(jnp.bfloat16)

    grad_gain = jnp.sum(dnormed * joined * inv_rms, axis=0)
    dfused = (
        inv_rms * (dnormed * gain[None, :]) - joined * (inv_rms * inv_rms * inv_rms * rowdot / full_width)
    ).astype(jnp.bfloat16)

    held["grad_fc"] = None

    def fill_grad_fc(first, pieces):
        if kernels:
            held["grad_fc"], token = join_grad(chunks, first, pieces, x_turned, full_width, held["grad_fc"])
            return token

    dfused_low, dfused_high = gather_doubling(
        [dfused[:, :half], dfused[:, half:]], orders, size, fill_grad_fc
    )
    if kernels:
        grad_fc = held["grad_fc"]
    else:
        dfused_all = whole(
            [jnp.concatenate([dfused_low[s], dfused_high[s]], axis=0) for s in range(2)], chunks
        )
        grad_fc = jnp.dot(x_turned, dfused_all, preferred_element_type=jnp.float32).astype(jnp.bfloat16)
        grad_fc = grad_fc.reshape(3, rows, full_width)
    return (token_loss, grad_fc, grad_gain, grad_lm)


def solution(mesh):
    return jax.shard_map(
        functools.partial(on_device, mesh.shape["section"]),
        mesh=mesh,
        in_specs=(
            P(("grp", "section"), None),
            P(("grp", "section"), None),
            P(("grp", "section"), None),
            P(None, "section", None),
            P("section"),
            P(None, "section"),
            P("grp"),
        ),
        out_specs=(P("grp"), P("grp", "section", None), P(("grp", "section")), P("grp", "section")),
        check_vma=False,
    )
```

time: 448 us -> 230 us (0.51)
  waiting for transfers between devices: 207 us -> 45.8 us
  blocking collectives: 160 us -> 0 us
  starting transfers between devices: 0.16 us -> 68.1 us
  Pallas kernels: 0 us -> 66.4 us
  matrix products: 58.8 us -> 0 us
  local copies, waits for them, and re-layouts: 0.01 us -> 40.4 us
  between operations: 13.8 us -> 1.46 us
    reduce_scatter x2 -> x0, waiting for transfers between devices: 137 us -> none  [the longest x1 68.9 us: on_device(): lax.psum_scatter(jnp.einsum('jsr,jts->rt', w_block, stacked, preferred_el...]
    psum x3 -> x0, blocking collectives: 94.3 us -> none  [the longest x2 63 us: on_device(): exp_total, picked = lax.psum((local_total, picked_local), 'section')]
    all_gather x2 -> x0, waiting for transfers between devices: 69.9 us -> none  [the longest x1 39.5 us: on_device(): normed_all = lax.all_gather(normed_local, 'section', axis=0, tiled=True)]
    pallas_call x0 -> x18, Pallas kernels: none -> 66.4 us  [the longest x5 19.3 us: join_grad(): pl.pallas_call(functools.partial(join_grad_kernel, first, count, aliased)...]
    ppermute x0 -> x48, starting transfers between devices: none -> 60.8 us  [exchange(): return lax.ppermute(x, 'section', [(i, i ^ mask) for i in range(size)])]
    dot_general x5 -> x0, matrix products: 58.8 us -> none  [the longest x1 14 us: on_device(): jnp.einsum('jts,rt->jsr', stacked, lax.all_gather(dfused, 'section', axis...]
    ppermute x0 -> x48, waiting for transfers between devices: none -> 45.8 us  [exchange(): return lax.ppermute(x, 'section', [(i, i ^ mask) for i in range(size)])]
    unnamed x8 -> x24, local copies, waits for them, and re-layouts: 0.01 us -> 40.2 us
  transfers between devices with their start and end apart: 4 -> 49, of which waited for: 4 -> 23; matrix products, arithmetic and copies ran while one was open for 2% -> 1% of each run, Pallas kernels for 0% -> 20%
where the time goes in v2:
time: 230 us
  starting transfers between devices  68.1 us (30%)
  Pallas kernels  66.4 us (29%)
  waiting for transfers between devices  45.8 us (20%)
  local copies, waits for them, and re-layouts  40.4 us (18%)
  other arithmetic  7.31 us (3%)
    ppermute x48, starting transfers between devices, exchange(): return lax.ppermute(x, 'section', [(i, i ^ mask) for i in range(size)])  60.8 us
    ppermute x48, waiting for transfers between devices, exchange(): return lax.ppermute(x, 'section', [(i, i ^ mask) for i in range(size)])  45.8 us
    unnamed x24, local copies, waits for them, and re-layouts  40.2 us
    pallas_call x5, Pallas kernels, join_grad(): pl.pallas_call(functools.partial(join_grad_kernel, first, count, aliased)...  19.3 us
    pallas_call x2, Pallas kernels, head_grad(): pl.pallas_call(functools.partial(head_grad_kernel, first, count, aliased)...  12 us
    pallas_call x2, Pallas kernels, stage(): pl.pallas_call(functools.partial(stage_kernel, pieces), out_shape=(vmem_o...  10.2 us
    pallas_call x2, Pallas kernels, back(): pl.pallas_call(functools.partial(back_kernel, first, count), out_shape=(o...  8.96 us
    pallas_call x5, Pallas kernels, head(): pl.pallas_call(functools.partial(head_kernel, first, count), out_shape=(v...  8.55 us
  transfers between devices with their start and end apart: 49, of which 23 were waited for; matrix products, arithmetic and copies ran while one was open for 1% of the time, Pallas kernels for 20%

profile of v2, /device:TPU:1, one launch (start us, length us, event | category | flops | bytes accessed | tf_op | source)
XLA Modules:
  0.0 229.5 jit_solution(14127716188375830593)
XLA Ops:
  2.5 7.3 %all-to-all-start = ((bf16[16,8,1536]{2,1,0:T(8,128)(2,1)}), bf16[16,8,1536]{2,1,0:T(8,128)(2,1)S(1)}, u32[]{:S(2)}, u32[]{:S(2)}) async-start(bf16[16,8,1536]{2,1,0:T(8,128)(2,1)} %maximum_bitcast_fusion.after_ref), calls=%async_computation | async-start | bytes 786432 | tf_op jit(solution)/shard_map/all_to_all | solution.py:341
  9.8 8.9 %stage.2 = (bf16[3,512,8192]{2,1,0:T(8,128)(2,1)S(1)}, f32[1,256]{1,0:T(1,128)}) custom-call(bf16[3,512,8192]{2,1,0:T(8,128)(2,1)} %w_ref.2, bf16[16,8,1536]{2,1,0:T(8,128)(2,1)} %maximum_bitcast_fusion.after_ref), custom_call_target="tpu_custom_call" | custom-call | bytes 25165824 | tf_op jit(solution)/shard_map/stage/pallas_call | solution.py:67
  18.8 8.9 %copy-done.4 = bf16[3,512,8192]{2,1,0:T(8,128)(2,1)} copy-done((bf16[3,512,8192]{2,1,0:T(8,128)(2,1)}, bf16[3,512,8192]{2,1,0:T(8,128)(2,1)S(1)}, u32[]{:S(2)}) %copy-start.4) | copy-done | bytes 25165848
  27.7 8.1 %copy-done.5 = bf16[3,512,8192]{2,1,0:T(8,128)(2,1)S(1)} copy-done((bf16[3,512,8192]{2,1,0:T(8,128)(2,1)S(1)}, bf16[3,512,8192]{2,1,0:T(8,128)(2,1)}, u32[]{:S(2)}) %copy-start.5) | copy-done | bytes 25165848
  35.9 3.7 %join.3 = (f32[8,128,256]{2,1,0:T(8,128)S(1)}, f32[8,128,256]{2,1,0:T(8,128)S(1)}) custom-call(s32[2,16]{1,0:T(2,128)S(1)} %broadcast_xor_fusion.chunks, bf16[128,1536]{1,0:T(8,128)(2,1)S(1)} %bitcast.352, bf16[3,512,8192]{2,1,0:T(8,128)(2,1)S(1)} %copy-done.5), custom_call_target="tpu_custom_call" | custom-call | flops 1610612736 | bytes 2097152 | tf_op jit(solution)/shard_map/join/pallas_call | solution.py:101
  40.1 3.7 %join.2 = (f32[8,128,256]{2,1,0:T(8,128)S(1)}, f32[8,128,256]{2,1,0:T(8,128)S(1)}) custom-call(s32[2,16]{1,0:T(2,128)S(1)} %broadcast_xor_fusion.chunks, bf16[128,1536]{1,0:T(8,128)(2,1)S(1)} %bitcast.353, bf16[3,512,8192]{2,1,0:T(8,128)(2,1)S(1)} %copy-done.5), custom_call_target="tpu_custom_call" | custom-call | flops 1610612736 | bytes 2097152 | tf_op jit(solution)/shard_map/join/pallas_call | solution.py:101
  46.8 5.8 %copy-done.6 = bf16[8192,1024]{1,0:T(8,128)(2,1)S(1)} copy-done((bf16[8192,1024]{1,0:T(8,128)(2,1)S(1)}, bf16[8192,1024]{1,0:T(8,128)(2,1)}, u32[]{:S(2)}) %copy-start.6) | copy-done | bytes 16777240
  53.9 3.6 %collective-permute-done.1 = f32[4,128,256]{2,1,0:T(8,128)S(1)} collective-permute-done((f32[4,128,256]{2,1,0:T(8,128)S(1)}, f32[4,128,256]{2,1,0:T(8,128)S(1)}, u32[]{:S(2)}, u32[]{:S(2)}) %collective-permute-start.1) | collective-permute-done | bytes 524320 | tf_op jit(solution)/shard_map/ppermute | solution.py:26
  60.3 4.7 %collective-permute-done.6 = f32[2,128,256]{2,1,0:T(8,128)S(1)} collective-permute-done((f32[2,128,256]{2,1,0:T(8,128)S(1)}, f32[2,128,256]{2,1,0:T(8,128)S(1)}, u32[]{:S(2)}, u32[]{:S(2)}) %collective-permute-start.6) | collective-permute-done | bytes 262176 | tf_op jit(solution)/shard_map/ppermute | solution.py:26
  67.5 3.7 %collective-permute-done.7 = f32[1,128,256]{2,1,0:T(8,128)S(1)} collective-permute-done((f32[1,128,256]{2,1,0:T(8,128)S(1)}, f32[1,128,256]{2,1,0:T(8,128)S(1)}, u32[]{:S(2)}, u32[]{:S(2)}) %collective-permute-start.7) | collective-permute-done | bytes 131104 | tf_op jit(solution)/shard_map/ppermute | solution.py:26
  71.2 7.1 %collective-permute-done.3 = f32[1,128,256]{2,1,0:T(8,128)S(1)} collective-permute-done((f32[1,128,256]{2,1,0:T(8,128)S(1)}, f32[1,128,256]{2,1,0:T(8,128)S(1)}, u32[]{:S(2)}, u32[]{:S(2)}) %collective-permute-start.3) | collective-permute-done | bytes 131104 | tf_op jit(solution)/shard_map/ppermute | solution.py:26
  78.5 4.5 %collective-permute-start.14 = (f32[128]{0:T(128)S(1)}, f32[128]{0:T(128)S(1)}, u32[]{:S(2)}, u32[]{:S(2)}) collective-permute-start(f32[128]{0:T(128)S(1)} %multiply_reduce_fusion.1), channel_id=1, source_target_pairs={{0,14},{1,15},{2,12},{3,13},{4,10},{5,11},{6,8},{7,9},{8,6},{9,7},... | collective-permute-start | bytes 1544 | tf_op jit(solution)/shard_map/ppermute | solution.py:26
  83.1 3.2 %collective-permute-start.11 = (f32[128]{0:T(128)S(1)}, f32[128]{0:T(128)S(1)}, u32[]{:S(2)}, u32[]{:S(2)}) collective-permute-start(f32[128]{0:T(128)S(1)} %multiply_reduce_fusion.1), channel_id=1, source_target_pairs={{0,8},{1,9},{2,10},{3,11},{4,12},{5,13},{6,14},{7,15},{8,0},{9,1},... | collective-permute-start | bytes 1544 | tf_op jit(solution)/shard_map/ppermute | solution.py:26
  90.2 4.0 %collective-permute-start.15 = (f32[128]{0:T(128)S(1)}, f32[128]{0:T(128)S(1)}, u32[]{:S(2)}, u32[]{:S(2)}) collective-permute-start(f32[128]{0:T(128)S(1)} %add_add_fusion.4), channel_id=1, source_target_pairs={{0,1},{1,0},{2,3},{3,2},{4,5},{5,4},{6,7},{7,6},{8,9},{9,8},{10,11... | collective-permute-start | bytes 1544 | tf_op jit(solution)/shard_map/ppermute | solution.py:26
  98.6 2.9 %collective-permute-done.18 = bf16[1,128,256]{2,1,0:T(8,128)(2,1)S(1)} collective-permute-done((bf16[1,128,256]{2,1,0:T(8,128)(2,1)S(1)}, bf16[1,128,256]{2,1,0:T(8,128)(2,1)S(1)}, u32[]{:S(2)}, u32[]{:S(2)}) %collective-permute-start.18) | collective-permute-done | bytes 65568 | tf_op jit(solution)/shard_map/ppermute | solution.py:26
  101.5 2.8 %collective-permute-done.16 = bf16[1,128,256]{2,1,0:T(8,128)(2,1)S(1)} collective-permute-done((bf16[1,128,256]{2,1,0:T(8,128)(2,1)S(1)}, bf16[1,128,256]{2,1,0:T(8,128)(2,1)S(1)}, u32[]{:S(2)}, u32[]{:S(2)}) %collective-permute-start.16) | collective-permute-done | bytes 65568 | tf_op jit(solution)/shard_map/ppermute | solution.py:26
  105.8 3.0 %collective-permute-done.17 = bf16[2,128,256]{2,1,0:T(8,128)(2,1)S(1)} collective-permute-done((bf16[2,128,256]{2,1,0:T(8,128)(2,1)S(1)}, bf16[2,128,256]{2,1,0:T(8,128)(2,1)S(1)}, u32[]{:S(2)}, u32[]{:S(2)}) %collective-permute-start.17) | collective-permute-done | bytes 131104 | tf_op jit(solution)/shard_map/ppermute | solution.py:26
  111.7 3.6 %collective-permute-done.19 = bf16[4,128,256]{2,1,0:T(8,128)(2,1)S(1)} collective-permute-done((bf16[4,128,256]{2,1,0:T(8,128)(2,1)S(1)}, bf16[4,128,256]{2,1,0:T(8,128)(2,1)S(1)}, u32[]{:S(2)}, u32[]{:S(2)}) %collective-permute-start.19) | collective-permute-done | bytes 262176 | tf_op jit(solution)/shard_map/ppermute | solution.py:26
  119.0 5.8 %copy-done.1 = bf16[8192,1024]{1,0:T(8,128)(2,1)S(1)} copy-done((bf16[8192,1024]{1,0:T(8,128)(2,1)S(1)}, bf16[8192,1024]{1,0:T(8,128)(2,1)}, u32[]{:S(2)}) %copy-start.1) | copy-done | bytes 16777240
  126.9 3.4 %head.9 = (f32[128,1024]{1,0:T(8,128)S(1)}, f32[1,256]{1,0:T(1,128)}) custom-call(s32[2,16]{1,0:T(2,128)S(1)} %broadcast_xor_fusion.chunks, bf16[8,128,256]{2,1,0:T(8,128)(2,1)S(1)} %collective-permute-done.21.a_ref, bf16[8,128,256]{2,1,0:T(8,128)(2,1)S(1)} %collective-permute-done.23.b_ref, bf16[8192,1024]{1,0:T(8,128)(2,1)S(1)} %copy-done.1, ...), custom_call_target="tpu_custom_call" | custom-call | flops 1073741824 | bytes 1048576 | tf_op jit(solution)/shard_map/head/pallas_call | solution.py:128
  130.8 3.4 %collective-permute-start.30 = (f32[4,128]{1,0:T(4,128)S(1)}, f32[4,128]{1,0:T(4,128)S(1)}, u32[]{:S(2)}, u32[]{:S(2)}) collective-permute-start(f32[4,128]{1,0:T(4,128)S(1)} %pad_maximum_fusion.14), channel_id=1, source_target_pairs={{0,14},{1,15},{2,12},{3,13},{4,10},{5,11},{6,8},{7,9},{8,6},{9,7},... | collective-permute-start | bytes 6152 | tf_op jit(solution)/shard_map/ppermute | solution.py:26
  142.4 3.4 %collective-permute-start.31 = (f32[4,128]{1,0:T(4,128)S(1)}, f32[4,128]{1,0:T(4,128)S(1)}, u32[]{:S(2)}, u32[]{:S(2)}) collective-permute-start(f32[4,128]{1,0:T(4,128)S(1)} %pad_maximum_fusion.15), channel_id=1, source_target_pairs={{0,1},{1,0},{2,3},{3,2},{4,5},{5,4},{6,7},{7,6},{8,9},{9,8},{10,11... | collective-permute-start | bytes 6152 | tf_op jit(solution)/shard_map/ppermute | solution.py:26
  147.4 5.8 %copy-done.2 = bf16[8192,1024]{1,0:T(8,128)(2,1)S(1)} copy-done((bf16[8192,1024]{1,0:T(8,128)(2,1)S(1)}, bf16[8192,1024]{1,0:T(8,128)(2,1)}, u32[]{:S(2)}) %copy-start.2) | copy-done | bytes 16777240
  153.2 4.4 %back.3 = (f32[8,128,256]{2,1,0:T(8,128)S(1)}, f32[8,128,256]{2,1,0:T(8,128)S(1)}) custom-call(s32[2,16]{1,0:T(2,128)S(1)} %broadcast_xor_fusion.chunks, bf16[128,1024]{1,0:T(8,128)(2,1)S(1)} %fusion.3.d_ref, bf16[8192,1024]{1,0:T(8,128)(2,1)S(1)} %copy-done.2), custom_call_target="tpu_custom_call" | custom-call | flops 1073741824 | bytes 2097152 | tf_op jit(solution)/shard_map/back/pallas_call | solution.py:156
  158.5 5.8 %copy-done.3 = bf16[8192,1024]{1,0:T(8,128)(2,1)S(1)} copy-done((bf16[8192,1024]{1,0:T(8,128)(2,1)S(1)}, bf16[8192,1024]{1,0:T(8,128)(2,1)}, u32[]{:S(2)}) %copy-start.3) | copy-done | bytes 16777240
  164.2 4.6 %back.2 = (f32[8,128,256]{2,1,0:T(8,128)S(1)}, f32[8,128,256]{2,1,0:T(8,128)S(1)}) custom-call(s32[2,16]{1,0:T(2,128)S(1)} %broadcast_xor_fusion.chunks, bf16[128,1024]{1,0:T(8,128)(2,1)S(1)} %fusion.3.d_ref, bf16[8192,1024]{1,0:T(8,128)(2,1)S(1)} %copy-done.3), custom_call_target="tpu_custom_call" | custom-call | flops 1073741824 | bytes 2097152 | tf_op jit(solution)/shard_map/back/pallas_call | solution.py:156
  170.7 6.2 %head_grad.2 = (bf16[8192,1024]{1,0:T(8,128)(2,1)}, f32[1,256]{1,0:T(1,128)S(1)}) custom-call(s32[2,16]{1,0:T(2,128)S(1)} %broadcast_xor_fusion.chunks, bf16[8,128,256]{2,1,0:T(8,128)(2,1)} %pad_maximum_fusion.a_ref, bf16[8,128,256]{2,1,0:T(8,128)(2,1)S(1)} %pad_maximum_fusion.1.b_ref, bf16[128,1024]{1,0:T(8,128)(2,1)S(1)} %fusion.3.d_ref, ...), custom_call_target="tpu_custom_call" | custom-call | flops 1073741824 | bytes 8388608 | tf_op jit(solution)/shard_map/head_grad/pallas_call | solution.py:192
  185.2 5.7 %head_grad.3 = (bf16[8192,1024]{1,0:T(8,128)(2,1)}, f32[1,256]{1,0:T(1,128)S(1)}) custom-call(s32[2,16]{1,0:T(2,128)S(1)} %broadcast_xor_fusion.chunks, bf16[8,128,256]{2,1,0:T(8,128)(2,1)S(1)} %collective-permute-done.21.a_ref, bf16[8,128,256]{2,1,0:T(8,128)(2,1)S(1)} %collective-permute-done.23.b_ref, ...), custom_call_target="tpu_custom_call", output_to_operand_aliasing={{0}: (5, {})} | custom-call | flops 1073741824 | bytes 8388608 | tf_op jit(solution)/shard_map/head_grad/pallas_call | solution.py:192
  206.9 2.9 %collective-permute-done.43 = bf16[4,128,256]{2,1,0:T(8,128)(2,1)S(1)} collective-permute-done((bf16[4,128,256]{2,1,0:T(8,128)(2,1)S(1)}, bf16[4,128,256]{2,1,0:T(8,128)(2,1)S(1)}, u32[]{:S(2)}, u32[]{:S(2)}) %collective-permute-start.43) | collective-permute-done | bytes 262176 | tf_op jit(solution)/shard_map/ppermute | solution.py:26
  210.0 6.9 %collective-permute-start.45 = (bf16[8,128,256]{2,1,0:T(8,128)(2,1)S(1)}, bf16[8,128,256]{2,1,0:T(8,128)(2,1)S(1)}, u32[]{:S(2)}, u32[]{:S(2)}) collective-permute-start(bf16[8,128,256]{2,1,0:T(8,128)(2,1)S(1)} %pad_maximum_fusion.2), channel_id=1, source_target_pairs={{0,1},{1,0},{2,3},{3,2},{4,5},{5,4},{6,7},{7,6},{8,9},{9,8},{10,11... | collective-permute-start | bytes 1572872 | tf_op jit(solution)/shard_map/ppermute | solution.py:26
  217.0 4.4 %join_grad.8 = (bf16[3,512,8192]{2,1,0:T(8,128)(2,1)}, f32[1,256]{1,0:T(1,128)}) custom-call(s32[2,16]{1,0:T(2,128)S(1)} %broadcast_xor_fusion.chunks, bf16[4,128,256]{2,1,0:T(8,128)(2,1)S(1)} %get-tuple-element.105.a_ref, bf16[4,128,256]{2,1,0:T(8,128)(2,1)S(1)} %get-tuple-element.104.b_ref, ...), custom_call_target="tpu_custom_call", output_to_operand_aliasing={{0}: (4, {})} | custom-call | flops 1610612736 | bytes 6291456 | tf_op jit(solution)/shard_map/join_grad/pallas_call | solution.py:235
  221.4 8.0 %join_grad.9 = (bf16[3,512,8192]{2,1,0:T(8,128)(2,1)}, f32[1,256]{1,0:T(1,128)}) custom-call(s32[2,16]{1,0:T(2,128)S(1)} %broadcast_xor_fusion.chunks, bf16[8,128,256]{2,1,0:T(8,128)(2,1)S(1)} %collective-permute-done.45.a_ref, bf16[8,128,256]{2,1,0:T(8,128)(2,1)S(1)} %collective-permute-done.47.b_ref, ...), custom_call_target="tpu_custom_call", output_to_operand_aliasing={{0}: (4, {})} | custom-call | flops 3221225472 | bytes 12582912 | tf_op jit(solution)/shard_map/join_grad/pallas_call | solution.py:235
  (173 shorter events, 67.9 us)
Async XLA Ops:
  2.5 25.2 %all-to-all-start = ((bf16[16,8,1536]{2,1,0:T(8,128)(2,1)}), bf16[16,8,1536]{2,1,0:T(8,128)(2,1)S(1)}, u32[]{:S(2)}, u32[]{:S(2)}) async-start(bf16[16,8,1536]{2,1,0:T(8,128)(2,1)} %maximum_bitcast_fusion.after_ref), calls=%async_computation | async-start | bytes 786432 | tf_op jit(solution)/shard_map/all_to_all | solution.py:341
  39.7 5.7 %collective-permute-start.4 = (f32[8,128,256]{2,1,0:T(8,128)S(1)}, f32[8,128,256]{2,1,0:T(8,128)S(1)}, u32[]{:S(2)}, u32[]{:S(2)}) collective-permute-start(f32[8,128,256]{2,1,0:T(8,128)S(1)} %get-tuple-element.40), channel_id=1, source_target_pairs={{0,1},{1,0},{2,3},{3,2},{4,5},{5,4},{6,7},{7,6},{8,9},{9,8},{10,11... | collective-permute-start | bytes 3145736 | tf_op jit(solution)/shard_map/ppermute | solution.py:26
  44.0 13.6 %collective-permute-start.1 = (f32[4,128,256]{2,1,0:T(8,128)S(1)}, f32[4,128,256]{2,1,0:T(8,128)S(1)}, u32[]{:S(2)}, u32[]{:S(2)}) collective-permute-start(f32[4,128,256]{2,1,0:T(8,128)S(1)} %get-tuple-element.87.after_ref), channel_id=1, source_target_pairs={{0,2},{1,3},{2,0},{3,1},{4,6},{5,7},{6,4},{7,5},{8,10},{9,11},{10,... | collective-permute-start | bytes 1572872 | tf_op jit(solution)/shard_map/ppermute | solution.py:26
  45.6 12.9 %collective-permute-start.5 = (f32[4,128,256]{2,1,0:T(8,128)S(1)}, f32[4,128,256]{2,1,0:T(8,128)S(1)}, u32[]{:S(2)}, u32[]{:S(2)}) collective-permute-start(f32[4,128,256]{2,1,0:T(8,128)S(1)} %get-tuple-element.89), channel_id=1, source_target_pairs={{0,4},{1,5},{2,6},{3,7},{4,0},{5,1},{6,2},{7,3},{8,12},{9,13},{10,... | collective-permute-start | bytes 1572872 | tf_op jit(solution)/shard_map/ppermute | solution.py:26
  58.6 6.4 %collective-permute-start.6 = (f32[2,128,256]{2,1,0:T(8,128)S(1)}, f32[2,128,256]{2,1,0:T(8,128)S(1)}, u32[]{:S(2)}, u32[]{:S(2)}) collective-permute-start(f32[2,128,256]{2,1,0:T(8,128)S(1)} %get-tuple-element.97), channel_id=1, source_target_pairs={{0,2},{1,3},{2,0},{3,1},{4,6},{5,7},{6,4},{7,5},{8,10},{9,11},{10,... | collective-permute-start | bytes 786440 | tf_op jit(solution)/shard_map/ppermute | solution.py:26
  59.2 8.0 %collective-permute-start.2 = (f32[2,128,256]{2,1,0:T(8,128)S(1)}, f32[2,128,256]{2,1,0:T(8,128)S(1)}, u32[]{:S(2)}, u32[]{:S(2)}) collective-permute-start(f32[2,128,256]{2,1,0:T(8,128)S(1)} %get-tuple-element.95), channel_id=1, source_target_pairs={{0,4},{1,5},{2,6},{3,7},{4,0},{5,1},{6,2},{7,3},{8,12},{9,13},{10,... | collective-permute-start | bytes 786440 | tf_op jit(solution)/shard_map/ppermute | solution.py:26
  65.0 6.2 %collective-permute-start.7 = (f32[1,128,256]{2,1,0:T(8,128)S(1)}, f32[1,128,256]{2,1,0:T(8,128)S(1)}, u32[]{:S(2)}, u32[]{:S(2)}) collective-permute-start(f32[1,128,256]{2,1,0:T(8,128)S(1)} %slice_add_fusion.20), channel_id=1, source_target_pairs={{0,8},{1,9},{2,10},{3,11},{4,12},{5,13},{6,14},{7,15},{8,0},{9,1},... | collective-permute-start | bytes 393224 | tf_op jit(solution)/shard_map/ppermute | solution.py:26
  67.2 11.2 %collective-permute-start.3 = (f32[1,128,256]{2,1,0:T(8,128)S(1)}, f32[1,128,256]{2,1,0:T(8,128)S(1)}, u32[]{:S(2)}, u32[]{:S(2)}) collective-permute-start(f32[1,128,256]{2,1,0:T(8,128)S(1)} %slice_add_fusion.22), channel_id=1, source_target_pairs={{0,8},{1,9},{2,10},{3,11},{4,12},{5,13},{6,14},{7,15},{8,0},{9,1},... | collective-permute-start | bytes 393224 | tf_op jit(solution)/shard_map/ppermute | solution.py:26
  78.5 9.0 %collective-permute-start.14 = (f32[128]{0:T(128)S(1)}, f32[128]{0:T(128)S(1)}, u32[]{:S(2)}, u32[]{:S(2)}) collective-permute-start(f32[128]{0:T(128)S(1)} %multiply_reduce_fusion.1), channel_id=1, source_target_pairs={{0,14},{1,15},{2,12},{3,13},{4,10},{5,11},{6,8},{7,9},{8,6},{9,7},... | collective-permute-start | bytes 1544 | tf_op jit(solution)/shard_map/ppermute | solution.py:26
  83.1 5.8 %collective-permute-start.12 = (f32[128]{0:T(128)S(1)}, f32[128]{0:T(128)S(1)}, u32[]{:S(2)}, u32[]{:S(2)}) collective-permute-start(f32[128]{0:T(128)S(1)} %multiply_reduce_fusion.1), channel_id=1, source_target_pairs={{0,10},{1,11},{2,8},{3,9},{4,14},{5,15},{6,12},{7,13},{8,2},{9,3},... | collective-permute-start | bytes 1544 | tf_op jit(solution)/shard_map/ppermute | solution.py:26
  83.1 5.8 %collective-permute-start.11 = (f32[128]{0:T(128)S(1)}, f32[128]{0:T(128)S(1)}, u32[]{:S(2)}, u32[]{:S(2)}) collective-permute-start(f32[128]{0:T(128)S(1)} %multiply_reduce_fusion.1), channel_id=1, source_target_pairs={{0,8},{1,9},{2,10},{3,11},{4,12},{5,13},{6,14},{7,15},{8,0},{9,1},... | collective-permute-start | bytes 1544 | tf_op jit(solution)/shard_map/ppermute | solution.py:26
  95.2 6.2 %collective-permute-start.18 = (bf16[1,128,256]{2,1,0:T(8,128)(2,1)S(1)}, bf16[1,128,256]{2,1,0:T(8,128)(2,1)S(1)}, u32[]{:S(2)}, u32[]{:S(2)}) collective-permute-start(bf16[1,128,256]{2,1,0:T(8,128)(2,1)S(1)} %get-tuple-element.102.b_ref), channel_id=1, source_target_pairs={{0,8},{1,9},{2,10},{3,11},{4,12},{5,13},{6,14},{7,15},{8,0},{9,1},... | collective-permute-start | bytes 196616 | tf_op jit(solution)/shard_map/ppermute | solution.py:26
  96.4 7.9 %collective-permute-start.16 = (bf16[1,128,256]{2,1,0:T(8,128)(2,1)S(1)}, bf16[1,128,256]{2,1,0:T(8,128)(2,1)S(1)}, u32[]{:S(2)}, u32[]{:S(2)}) collective-permute-start(bf16[1,128,256]{2,1,0:T(8,128)(2,1)S(1)} %get-tuple-element.103.a_ref), channel_id=1, source_target_pairs={{0,8},{1,9},{2,10},{3,11},{4,12},{5,13},{6,14},{7,15},{8,0},{9,1},... | collective-permute-start | bytes 196616 | tf_op jit(solution)/shard_map/ppermute | solution.py:26
  109.0 6.4 %collective-permute-start.19 = (bf16[4,128,256]{2,1,0:T(8,128)(2,1)S(1)}, bf16[4,128,256]{2,1,0:T(8,128)(2,1)S(1)}, u32[]{:S(2)}, u32[]{:S(2)}) collective-permute-start(bf16[4,128,256]{2,1,0:T(8,128)(2,1)S(1)} %pad_maximum_fusion.5), channel_id=1, source_target_pairs={{0,2},{1,3},{2,0},{3,1},{4,6},{5,7},{6,4},{7,5},{8,10},{9,11},{10,... | collective-permute-start | bytes 786440 | tf_op jit(solution)/shard_map/ppermute | solution.py:26
  109.3 6.1 %collective-permute-start.22 = (bf16[4,128,256]{2,1,0:T(8,128)(2,1)S(1)}, bf16[4,128,256]{2,1,0:T(8,128)(2,1)S(1)}, u32[]{:S(2)}, u32[]{:S(2)}) collective-permute-start(bf16[4,128,256]{2,1,0:T(8,128)(2,1)S(1)} %pad_maximum_fusion.6), channel_id=1, source_target_pairs={{0,4},{1,5},{2,6},{3,7},{4,0},{5,1},{6,2},{7,3},{8,12},{9,13},{10,... | collective-permute-start | bytes 786440 | tf_op jit(solution)/shard_map/ppermute | solution.py:26
  116.4 10.5 %collective-permute-start.21 = (bf16[8,128,256]{2,1,0:T(8,128)(2,1)}, bf16[8,128,256]{2,1,0:T(8,128)(2,1)S(1)}, u32[]{:S(2)}, u32[]{:S(2)}) collective-permute-start(bf16[8,128,256]{2,1,0:T(8,128)(2,1)} %pad_maximum_fusion.a_ref), channel_id=1, source_target_pairs={{0,1},{1,0},{2,3},{3,2},{4,5},{5,4},{6,7},{7,6},{8,9},{9,8},{10,11... | collective-permute-start | bytes 1572872 | tf_op jit(solution)/shard_map/ppermute | solution.py:26
  119.0 7.9 %collective-permute-start.23 = (bf16[8,128,256]{2,1,0:T(8,128)(2,1)S(1)}, bf16[8,128,256]{2,1,0:T(8,128)(2,1)S(1)}, u32[]{:S(2)}, u32[]{:S(2)}) collective-permute-start(bf16[8,128,256]{2,1,0:T(8,128)(2,1)S(1)} %pad_maximum_fusion.1.b_ref), channel_id=1, source_target_pairs={{0,1},{1,0},{2,3},{3,2},{4,5},{5,4},{6,7},{7,6},{8,9},{9,8},{10,11... | collective-permute-start | bytes 1572872 | tf_op jit(solution)/shard_map/ppermute | solution.py:26
  130.8 7.9 %collective-permute-start.30 = (f32[4,128]{1,0:T(4,128)S(1)}, f32[4,128]{1,0:T(4,128)S(1)}, u32[]{:S(2)}, u32[]{:S(2)}) collective-permute-start(f32[4,128]{1,0:T(4,128)S(1)} %pad_maximum_fusion.14), channel_id=1, source_target_pairs={{0,14},{1,15},{2,12},{3,13},{4,10},{5,11},{6,8},{7,9},{8,6},{9,7},... | collective-permute-start | bytes 6152 | tf_op jit(solution)/shard_map/ppermute | solution.py:26
  134.2 5.7 %collective-permute-start.29 = (f32[4,128]{1,0:T(4,128)S(1)}, f32[4,128]{1,0:T(4,128)S(1)}, u32[]{:S(2)}, u32[]{:S(2)}) collective-permute-start(f32[4,128]{1,0:T(4,128)S(1)} %pad_maximum_fusion.14), channel_id=1, source_target_pairs={{0,12},{1,13},{2,14},{3,15},{4,8},{5,9},{6,10},{7,11},{8,4},{9,5},... | collective-permute-start | bytes 6152 | tf_op jit(solution)/shard_map/ppermute | solution.py:26
  135.1 5.0 %collective-permute-start.28 = (f32[4,128]{1,0:T(4,128)S(1)}, f32[4,128]{1,0:T(4,128)S(1)}, u32[]{:S(2)}, u32[]{:S(2)}) collective-permute-start(f32[4,128]{1,0:T(4,128)S(1)} %pad_maximum_fusion.14), channel_id=1, source_target_pairs={{0,10},{1,11},{2,8},{3,9},{4,14},{5,15},{6,12},{7,13},{8,2},{9,3},... | collective-permute-start | bytes 6152 | tf_op jit(solution)/shard_map/ppermute | solution.py:26
  157.7 11.1 %collective-permute-start.36 = (f16[8,128,256]{2,1,0:T(8,128)(2,1)S(1)}, f16[8,128,256]{2,1,0:T(8,128)(2,1)S(1)}, u32[]{:S(2)}, u32[]{:S(2)}) collective-permute-start(f16[8,128,256]{2,1,0:T(8,128)(2,1)S(1)} %multiply_convert_fusion), channel_id=1, source_target_pairs={{0,1},{1,0},{2,3},{3,2},{4,5},{5,4},{6,7},{7,6},{8,9},{9,8},{10,11... | collective-permute-start | bytes 1572872 | tf_op jit(solution)/shard_map/ppermute | solution.py:26
  158.2 11.0 %collective-permute-start.32 = (f16[8,128,256]{2,1,0:T(8,128)(2,1)S(1)}, f16[8,128,256]{2,1,0:T(8,128)(2,1)S(1)}, u32[]{:S(2)}, u32[]{:S(2)}) collective-permute-start(f16[8,128,256]{2,1,0:T(8,128)(2,1)S(1)} %multiply_convert_fusion.1), channel_id=1, source_target_pairs={{0,1},{1,0},{2,3},{3,2},{4,5},{5,4},{6,7},{7,6},{8,9},{9,8},{10,11... | collective-permute-start | bytes 1572872 | tf_op jit(solution)/shard_map/ppermute | solution.py:26
  169.1 7.9 %collective-permute-start.37 = (f16[4,128,256]{2,1,0:T(8,128)(2,1)S(1)}, f16[4,128,256]{2,1,0:T(8,128)(2,1)S(1)}, u32[]{:S(2)}, u32[]{:S(2)}) collective-permute-start(f16[4,128,256]{2,1,0:T(8,128)(2,1)S(1)} %get-tuple-element.85), channel_id=1, source_target_pairs={{0,4},{1,5},{2,6},{3,7},{4,0},{5,1},{6,2},{7,3},{8,12},{9,13},{10,... | collective-permute-start | bytes 786440 | tf_op jit(solution)/shard_map/ppermute | solution.py:26
  169.5 7.5 %collective-permute-start.33 = (f16[4,128,256]{2,1,0:T(8,128)(2,1)S(1)}, f16[4,128,256]{2,1,0:T(8,128)(2,1)S(1)}, u32[]{:S(2)}, u32[]{:S(2)}) collective-permute-start(f16[4,128,256]{2,1,0:T(8,128)(2,1)S(1)} %get-tuple-element.75), channel_id=1, source_target_pairs={{0,2},{1,3},{2,0},{3,1},{4,6},{5,7},{6,4},{7,5},{8,10},{9,11},{10,... | collective-permute-start | bytes 786440 | tf_op jit(solution)/shard_map/ppermute | solution.py:26
  178.3 5.5 %collective-permute-start.34 = (f16[2,128,256]{2,1,0:T(8,128)(2,1)S(1)}, f16[2,128,256]{2,1,0:T(8,128)(2,1)S(1)}, u32[]{:S(2)}, u32[]{:S(2)}) collective-permute-start(f16[2,128,256]{2,1,0:T(8,128)(2,1)S(1)} %get-tuple-element.91), channel_id=1, source_target_pairs={{0,4},{1,5},{2,6},{3,7},{4,0},{5,1},{6,2},{7,3},{8,12},{9,13},{10,... | collective-permute-start | bytes 393224 | tf_op jit(solution)/shard_map/ppermute | solution.py:26
  181.1 9.8 %collective-permute-start.39 = (f16[1,128,256]{2,1,0:T(8,128)(2,1)S(1)}, f16[1,128,256]{2,1,0:T(8,128)(2,1)S(1)}, u32[]{:S(2)}, u32[]{:S(2)}) collective-permute-start(f16[1,128,256]{2,1,0:T(8,128)(2,1)S(1)} %fusion.12), channel_id=1, source_target_pairs={{0,8},{1,9},{2,10},{3,11},{4,12},{5,13},{6,14},{7,15},{8,0},{9,1},... | collective-permute-start | bytes 196616 | tf_op jit(solution)/shard_map/ppermute | solution.py:26
  183.9 7.1 %collective-permute-start.35 = (f16[1,128,256]{2,1,0:T(8,128)(2,1)S(1)}, f16[1,128,256]{2,1,0:T(8,128)(2,1)S(1)}, u32[]{:S(2)}, u32[]{:S(2)}) collective-permute-start(f16[1,128,256]{2,1,0:T(8,128)(2,1)S(1)} %get-tuple-element.73), channel_id=1, source_target_pairs={{0,8},{1,9},{2,10},{3,11},{4,12},{5,13},{6,14},{7,15},{8,0},{9,1},... | collective-permute-start | bytes 196616 | tf_op jit(solution)/shard_map/ppermute | solution.py:26
  191.8 5.5 %collective-permute-start.42 = (bf16[1,128,256]{2,1,0:T(8,128)(2,1)S(1)}, bf16[1,128,256]{2,1,0:T(8,128)(2,1)S(1)}, u32[]{:S(2)}, u32[]{:S(2)}) collective-permute-start(bf16[1,128,256]{2,1,0:T(8,128)(2,1)S(1)} %get-tuple-element.100.b_ref), channel_id=1, source_target_pairs={{0,8},{1,9},{2,10},{3,11},{4,12},{5,13},{6,14},{7,15},{8,0},{9,1},... | collective-permute-start | bytes 196616 | tf_op jit(solution)/shard_map/ppermute | solution.py:26
  198.0 5.1 %collective-permute-start.41 = (bf16[2,128,256]{2,1,0:T(8,128)(2,1)S(1)}, bf16[2,128,256]{2,1,0:T(8,128)(2,1)S(1)}, u32[]{:S(2)}, u32[]{:S(2)}) collective-permute-start(bf16[2,128,256]{2,1,0:T(8,128)(2,1)S(1)} %pad_maximum_fusion.12), channel_id=1, source_target_pairs={{0,4},{1,5},{2,6},{3,7},{4,0},{5,1},{6,2},{7,3},{8,12},{9,13},{10,... | collective-permute-start | bytes 393224 | tf_op jit(solution)/shard_map/ppermute | solution.py:26
  203.2 6.6 %collective-permute-start.43 = (bf16[4,128,256]{2,1,0:T(8,128)(2,1)S(1)}, bf16[4,128,256]{2,1,0:T(8,128)(2,1)S(1)}, u32[]{:S(2)}, u32[]{:S(2)}) collective-permute-start(bf16[4,128,256]{2,1,0:T(8,128)(2,1)S(1)} %pad_maximum_fusion.8), channel_id=1, source_target_pairs={{0,2},{1,3},{2,0},{3,1},{4,6},{5,7},{6,4},{7,5},{8,10},{9,11},{10,... | collective-permute-start | bytes 786440 | tf_op jit(solution)/shard_map/ppermute | solution.py:26
  203.5 6.3 %collective-permute-start.46 = (bf16[4,128,256]{2,1,0:T(8,128)(2,1)S(1)}, bf16[4,128,256]{2,1,0:T(8,128)(2,1)S(1)}, u32[]{:S(2)}, u32[]{:S(2)}) collective-permute-start(bf16[4,128,256]{2,1,0:T(8,128)(2,1)S(1)} %pad_maximum_fusion.9), channel_id=1, source_target_pairs={{0,4},{1,5},{2,6},{3,7},{4,0},{5,1},{6,2},{7,3},{8,12},{9,13},{10,... | collective-permute-start | bytes 786440 | tf_op jit(solution)/shard_map/ppermute | solution.py:26
  210.0 11.3 %collective-permute-start.45 = (bf16[8,128,256]{2,1,0:T(8,128)(2,1)S(1)}, bf16[8,128,256]{2,1,0:T(8,128)(2,1)S(1)}, u32[]{:S(2)}, u32[]{:S(2)}) collective-permute-start(bf16[8,128,256]{2,1,0:T(8,128)(2,1)S(1)} %pad_maximum_fusion.2), channel_id=1, source_target_pairs={{0,1},{1,0},{2,3},{3,2},{4,5},{5,4},{6,7},{7,6},{8,9},{9,8},{10,11... | collective-permute-start | bytes 1572872 | tf_op jit(solution)/shard_map/ppermute | solution.py:26
  (29 other events, 325.1 us)

commit v3 on v0

v3 whole, which is shorter than its diff:
```python
import functools

import jax
import jax.numpy as jnp
import numpy as np
from jax import lax
from jax.experimental import pallas as pl
from jax.experimental.pallas import tpu as pltpu
from jax.sharding import PartitionSpec as P

epsilon = 1e-06
MIB = 1024 * 1024
HALF_SCALE = 2.0**20
TILE = 256


def reduce_places(bits):
    later = range(1, bits)
    low = [
        sum(((q >> (bits - 2 - k)) & 1) << bit for k, bit in enumerate(later)) for q in range(1 << (bits - 1))
    ]
    return low + [p + 1 for p in low]


def gather_rounds(bits):
    later = [[1, 2]] if bits > 2 else [[1]]
    at = 3
    while at < bits:
        later.append([at, at + 1] if at + 1 < bits and (bits - at) % 2 == 0 else [at])
        at += len(later[-1])
    return later[::-1]


def masks_of(group):
    return [sum(1 << b for k, b in enumerate(group) if (m >> k) & 1) for m in range(1, 1 << len(group))]


def gather_places(bits):
    held = [0]
    for group in gather_rounds(bits):
        held = held + [p ^ m for m in masks_of(group) for p in held]
    return held


def exchange(x, mask, size):
    return lax.ppermute(x, "section", [(i, i ^ mask) for i in range(size)])


def settings(flops, bytes_moved, limit):
    return dict(
        compiler_params=pltpu.CompilerParams(vmem_limit_bytes=limit),
        cost_estimate=pl.CostEstimate(flops=flops, bytes_accessed=bytes_moved, transcendentals=0),
    )


ANYWHERE = pl.BlockSpec(memory_space=pl.ANY)
IN_VMEM = pl.BlockSpec(memory_space=pltpu.VMEM)
IN_SMEM = pl.BlockSpec(memory_space=pltpu.SMEM)
vmem_out = pltpu.VMEM


def near(x):
    return pltpu.with_memory_space_constraint(x, pltpu.VMEM)


def far(x):
    return pltpu.with_memory_space_constraint(x, pltpu.HBM)


def stage_kernel(pieces, table, w_ref, after_ref, out_ref, token_ref, sems):
    copies = []
    for k, piece in enumerate(pieces):
        copies.append(pltpu.make_async_copy(w_ref.at[piece], out_ref.at[piece], sems.at[k]))
    for copy in copies:
        copy.start()
    token_ref[...] = jnp.ones_like(token_ref)
    for copy in copies:
        copy.wait()


def stage(table, w, after, rows):
    step = w.shape[0] // 16
    pieces = [pl.ds(k * step, step) for k in range(16)]
    return pl.pallas_call(
        functools.partial(stage_kernel, pieces),
        out_shape=(vmem_out(w.shape, w.dtype), vmem_out((1, rows), jnp.float32)),
        in_specs=[IN_SMEM, ANYWHERE, ANYWHERE],
        out_specs=(IN_VMEM, IN_VMEM),
        scratch_shapes=[pltpu.SemaphoreType.DMA((len(pieces),))],
        name="stage",
        **settings(0, w.size * 2, 2 * MIB),
    )(table, far(w), after)


def join_kernel(first, count, table, x_ref, w_ref, *rest):
    out_ref, slots, sems = rest[0], rest[-2], rest[-1]
    rows = w_ref.shape[1]

    def copy(q):
        column = pl.multiple_of(table[0, first + q] * rows, 128)
        return pltpu.make_async_copy(w_ref.at[:, :, pl.ds(column, rows)], slots.at[q], sems.at[q])

    for q in range(count):
        copy(q).start()
    if len(rest) == 4:
        rest[1][...] = x_ref[...].T

    @pl.loop(0, count)
    def _(q):
        copy(q).wait()
        for column in range(0, rows, TILE):
            total = jnp.dot(
                x_ref[:, :rows], slots[q, 0, :, column : column + TILE], preferred_element_type=jnp.float32
            )
            for j in (1, 2):
                total += jnp.dot(
                    x_ref[:, j * rows : (j + 1) * rows],
                    slots[q, j, :, column : column + TILE],
                    preferred_element_type=jnp.float32,
                )
            out_ref[q, :, column : column + TILE] = total


def join(table, first, count, x, w_fc, turn):
    tokens = x.shape[0]
    rows = w_fc.shape[1]
    shapes = [vmem_out((count, tokens, rows), jnp.float32)]
    if turn:
        shapes.append(jax.ShapeDtypeStruct(x.shape[::-1], x.dtype))
    return pl.pallas_call(
        functools.partial(join_kernel, first, count),
        out_shape=tuple(shapes),
        in_specs=[IN_SMEM, IN_VMEM, ANYWHERE],
        out_specs=(IN_VMEM,) * len(shapes),
        scratch_shapes=[pltpu.VMEM((count, 3, rows, rows), jnp.bfloat16), pltpu.SemaphoreType.DMA((count,))],
        name="join",
        **settings(6 * tokens * rows * rows * count, 6 * rows * rows * count, 20 * MIB),
    )(table, near(x), far(w_fc))


def columns_of(rows_of_stats):
    count, tokens = rows_of_stats.shape
    padded = jnp.concatenate([rows_of_stats, jnp.zeros((tokens - count, tokens), jnp.float32)], axis=0)
    return padded.T


def target_mask(table, targets_ref, share):
    column = table[0, 0] * share + lax.broadcasted_iota(jnp.int32, (targets_ref.shape[1], share), 1)
    return column == columns_of(targets_ref[...].astype(jnp.float32))[:, :1].astype(jnp.int32)


def head_kernel(first, count, last, table, piece_ref, w_ref, before_ref, targets_ref, out_ref, extra_ref):
    rows = piece_ref.shape[2]
    out_ref[...] = before_ref[...]

    @pl.loop(0, count)
    def _(q):
        row = pl.multiple_of(table[1, first + q] * rows, 128)
        out_ref[...] += jnp.dot(piece_ref[q], w_ref[pl.ds(row, rows), :], preferred_element_type=jnp.float32)

    if not last:
        extra_ref[...] = jnp.ones_like(extra_ref)
        return
    logits = out_ref[...]
    tokens, share = logits.shape
    peak = jnp.max(logits, axis=1, keepdims=True)
    shifted = logits - peak
    weight = jnp.exp(shifted)
    picked = jnp.where(target_mask(table, targets_ref, share), logits, 0.0)
    lane = lax.broadcasted_iota(jnp.int32, (tokens, tokens), 1)
    stats = jnp.where(lane == 0, peak, 0.0)
    for k, part in enumerate((weight, weight * shifted, picked)):
        stats = jnp.where(lane == k + 1, jnp.sum(part, axis=1, keepdims=True), stats)
    extra_ref[...] = stats.T[: extra_ref.shape[0]]


def head(table, first, piece, w_lm, before, targets, last):
    count, tokens, rows = piece.shape
    share = w_lm.shape[1]
    extra = (8, tokens) if last else (1, rows)
    return pl.pallas_call(
        functools.partial(head_kernel, first, count, last),
        out_shape=(vmem_out(before.shape, jnp.float32), vmem_out(extra, jnp.float32)),
        in_specs=[IN_SMEM] + [IN_VMEM] * 4,
        out_specs=(IN_VMEM, IN_VMEM),
        name="head",
        **settings(2 * tokens * rows * share * count, 8 * tokens * share, 6 * MIB),
    )(table, near(piece), near(w_lm), near(before), near(targets))


def back_products(first, count, table, d_ref, w_ref, out_ref):
    rows = out_ref.shape[2]

    @pl.loop(0, count)
    def _(q):
        row = pl.multiple_of(table[0, first + q] * rows, 128)
        for step in range(0, rows, TILE):
            out_ref[q, :, step : step + TILE] = lax.dot_general(
                d_ref[...],
                w_ref[pl.ds(row + step, TILE), :],
                (((1,), (1,)), ((), ())),
                preferred_element_type=jnp.float32,
            )


def back_first_kernel(first, count, table, logits_ref, stats_ref, targets_ref, w_ref, out_ref, d_ref):
    logits = logits_ref[...]
    tokens, share = logits.shape
    log_total = columns_of(stats_ref[...])[:, :1]
    hit = jnp.where(target_mask(table, targets_ref, share), 1.0, 0.0)
    d_ref[...] = ((jnp.exp(logits - log_total) - hit) / tokens).astype(d_ref.dtype)
    back_products(first, count, table, d_ref, w_ref, out_ref)


def back_first(table, first, count, logits, stats, targets, w_lm, rows):
    tokens, share = logits.shape
    return pl.pallas_call(
        functools.partial(back_first_kernel, first, count),
        out_shape=(vmem_out((count, tokens, rows), jnp.float32), vmem_out((tokens, share), jnp.bfloat16)),
        in_specs=[IN_SMEM] + [IN_VMEM] * 4,
        out_specs=(IN_VMEM, IN_VMEM),
        name="back_first",
        **settings(2 * tokens * rows * share * count, 4 * tokens * rows * count, 6 * MIB),
    )(table, near(logits), near(stats), near(targets), near(w_lm))


def back_rest_kernel(first, count, table, d_ref, w_ref, out_ref):
    back_products(first, count, table, d_ref, w_ref, out_ref)


def back_rest(table, first, count, dlogits, w_lm, rows):
    tokens, share = dlogits.shape
    return pl.pallas_call(
        functools.partial(back_rest_kernel, first, count),
        out_shape=vmem_out((count, tokens, rows), jnp.float32),
        in_specs=[IN_SMEM, IN_VMEM, IN_VMEM],
        out_specs=IN_VMEM,
        name="back_rest",
        **settings(2 * tokens * rows * share * count, 4 * tokens * rows * count, 6 * MIB),
    )(table, near(dlogits), near(w_lm))


def head_grad_kernel(first, counts, aliased, table, a_ref, b_ref, d_ref, *rest):
    out_ref, token_ref, slots, sems = rest[1 + aliased :]
    rows = a_ref.shape[2]
    share = d_ref.shape[1]
    token_ref[...] = jnp.ones_like(token_ref)

    def copy(at):
        row = pl.multiple_of(table[1, first + at] * rows, 128)
        return pltpu.make_async_copy(slots.at[at], out_ref.at[pl.ds(row, rows), :], sems.at[at])

    for piece, offset, count in ((a_ref, 0, counts[0]), (b_ref, counts[0], counts[1])):

        @pl.loop(0, count)
        def _(q):
            turned = piece[q].T
            for column in range(0, share, TILE):
                for row in range(0, rows, TILE):
                    slots[offset + q, row : row + TILE, column : column + TILE] = jnp.dot(
                        turned[row : row + TILE],
                        d_ref[:, column : column + TILE],
                        preferred_element_type=jnp.float32,
                    ).astype(slots.dtype)
            copy(offset + q).start()

    for at in range(sum(counts)):
        copy(at).wait()


def head_grad(table, first, a, b, dlogits, width, after, into=None):
    tokens, rows = a.shape[1:]
    counts = (a.shape[0], b.shape[0])
    share = dlogits.shape[1]
    aliased = into is not None
    extra = (into,) if aliased else ()
    blocks = sum(counts)
    return pl.pallas_call(
        functools.partial(head_grad_kernel, first, counts, aliased),
        out_shape=(
            jax.ShapeDtypeStruct((width, share), jnp.bfloat16),
            vmem_out((1, rows), jnp.float32),
        ),
        in_specs=[IN_SMEM, IN_VMEM, IN_VMEM, IN_VMEM, ANYWHERE] + [ANYWHERE] * len(extra),
        out_specs=(ANYWHERE, IN_VMEM),
        scratch_shapes=[pltpu.VMEM((blocks, rows, share), jnp.bfloat16), pltpu.SemaphoreType.DMA((blocks,))],
        input_output_aliases={5: 0} if aliased else {},
        name="head_grad",
        **settings(2 * tokens * rows * share * blocks, 2 * rows * share * blocks, 16 * MIB),
    )(table, near(a), near(b), near(dlogits), after, *extra)


def join_grad_kernel(first, count, aliased, table, piece_ref, x_ref, *rest):
    out_ref, token_ref, slots, sems = rest[aliased:]
    rows = piece_ref.shape[2]
    token_ref[...] = jnp.ones_like(token_ref)

    def copy(at):
        column = pl.multiple_of(table[1, first + at] * rows, 128)
        return pltpu.make_async_copy(slots.at[at], out_ref.at[:, :, pl.ds(column, rows)], sems.at[at])

    @pl.loop(0, count)
    def _(q):
        for column in range(0, rows, TILE):
            for j in range(3):
                for row in range(0, rows, TILE):
                    slots[q, j, row : row + TILE, column : column + TILE] = jnp.dot(
                        x_ref[j * rows + row : j * rows + row + TILE, :],
                        piece_ref[q, :, column : column + TILE],
                        preferred_element_type=jnp.float32,
                    ).astype(slots.dtype)
        copy(q).start()

    for at in range(count):
        copy(at).wait()


def join_grad(table, first, piece, x_turned, width, into=None):
    count, tokens, rows = piece.shape
    aliased = into is not None
    extra = (into,) if aliased else ()
    return pl.pallas_call(
        functools.partial(join_grad_kernel, first, count, aliased),
        out_shape=(
            jax.ShapeDtypeStruct((3, rows, width), jnp.bfloat16),
            vmem_out((1, rows), jnp.float32),
        ),
        in_specs=[IN_SMEM, IN_VMEM, IN_VMEM] + [ANYWHERE] * len(extra),
        out_specs=(ANYWHERE, IN_VMEM),
        scratch_shapes=[pltpu.VMEM((count, 3, rows, rows), jnp.bfloat16), pltpu.SemaphoreType.DMA((count,))],
        input_output_aliases={3: 0} if aliased else {},
        name="join_grad",
        **settings(6 * tokens * rows * rows * count, 6 * rows * rows * count, 20 * MIB),
    )(table, near(piece), near(x_turned), *extra)


def cut(total, chunks, rows):
    tokens = total.shape[0]
    blocks = jnp.take(total.reshape(tokens, -1, rows).transpose(1, 0, 2), chunks, axis=0)
    count = chunks.shape[0] // 2
    return blocks[:count], blocks[count:]


def whole(pieces, chunks):
    blocks = jnp.take(jnp.concatenate(pieces, axis=0), jnp.argsort(chunks), axis=0)
    return blocks.transpose(1, 0, 2).reshape(blocks.shape[1], -1)


def contributions(x, group, size):
    return [x] + [exchange(x, m, size) for m in masks_of(group)]


def tree_sum(items):
    while len(items) > 1:
        items = [items[k] + items[k + 1] for k in range(0, len(items), 2)]
    return items[0]


def merge_sums(items):
    peak = functools.reduce(jnp.maximum, [i[0:1] for i in items])
    shifts = [i[0:1] - peak for i in items]
    scales = [jnp.exp(s) for s in shifts]
    return jnp.concatenate(
        [
            peak,
            tree_sum([i[1:2] * c for i, c in zip(items, scales)]),
            tree_sum([(i[2:3] + i[1:2] * s) * c for i, s, c in zip(items, shifts, scales)]),
            tree_sum([i[3:4] for i in items]),
        ],
        axis=0,
    )


def with_token(x, token):
    return x if token is None else (x.astype(jnp.float32) * token).astype(x.dtype)


def reduce_halves(low, high, bits, size, pack, unpack, work):
    received = exchange(pack(high), 1, size)
    total = low + unpack(received)
    count, tokens, rows = total.shape
    half = rows // 2
    total = total.reshape(2, 2, count // 4, tokens, rows)
    a, b = total[..., :half], total[..., half:]
    send_a, send_b = a[1], b[:, 1]
    got_a, got_b = exchange(pack(send_a), 2, size), exchange(pack(send_b), 4, size)
    token = work(1, send_a)
    a = a[0] + with_token(unpack(got_a), None if token is None else token[:, :half])
    b = b[:, 0] + unpack(got_b)
    got_a, got_b = exchange(pack(a[1]), 4, size), exchange(pack(b[1]), 2, size)
    a, b = a[0] + unpack(got_a), b[0] + unpack(got_b)
    total = jnp.concatenate([a, b], axis=-1)
    for bit in range(3, bits):
        half_count = total.shape[0] // 2
        send = total[half_count:]
        got = exchange(pack(send), 1 << bit, size)
        token = work(bit, send)
        total = total[:half_count] + with_token(unpack(got), token)
    return total[0]


def gather(own, bits, size, work):
    held = own[None]
    rounds = gather_rounds(bits)
    token = None
    first = 0
    fresh = held
    across = []
    for at, group in enumerate(rounds):
        pieces = [exchange(held, m, size) for m in masks_of(group)]
        token = work(first, fresh, False)
        if at == len(rounds) - 1 and at > 0:
            across.append(exchange(held, 1, size))
            token = work(size // 2, across[0], False)
        first += fresh.shape[0]
        fresh = with_token(pieces[0] if len(pieces) == 1 else jnp.concatenate(pieces, axis=0), token)
        if at < len(rounds) - 1:
            held = jnp.concatenate([held, fresh], axis=0)
    across.append(exchange(fresh, 1, size))
    work(first, fresh, False)
    work(size // 2 + first, across[-1], True)
    return [held, fresh], across


def on_device(size, low_feat, mid_feat, high_feat, w_fc, gain, w_lm, targets):
    me = lax.axis_index("section")
    rows, full_width = w_fc.shape[1], w_fc.shape[2]
    share = w_lm.shape[1]
    tokens = targets.shape[0]
    bits = size.bit_length() - 1
    count = size // 2
    gather_list = gather_places(bits)
    gather_list = gather_list + [p + 1 for p in gather_list]
    table = jnp.asarray(np.array([reduce_places(bits), gather_list], np.int32)) ^ me
    kernels = rows % TILE == 0
    target_row = targets.reshape(1, tokens)

    sent = jnp.concatenate(
        [f.reshape(-1, size, rows) for f in (low_feat, mid_feat, high_feat)], axis=2
    ).transpose(1, 0, 2)
    x = lax.all_to_all(sent, "section", split_axis=0, concat_axis=0, tiled=True).reshape(tokens, 3 * rows)

    held = {"logits": jnp.zeros((tokens, share), jnp.float32), "grad_lm": None, "grad_fc": None}
    if kernels:
        high, x_turned = join(table, count, count, x, w_fc, True)
        (low,) = join(table, 0, count, x, w_fc, False)
    else:
        total = jnp.dot(x, w_fc.reshape(3 * rows, full_width), preferred_element_type=jnp.float32)
        low, high = cut(total, table[0], rows)

    def bring_head(k, after):
        if kernels and k == 1:
            held["lm"], token = stage(table, w_lm, after, rows)
            return token

    joined = reduce_halves(low, high, bits, size, lambda x: x, lambda x: x, bring_head)

    squares = jnp.sum(joined * joined, axis=1)
    for group in gather_rounds(bits) + [[0]]:
        squares = tree_sum(contributions(squares, group, size))
    inv_rms = lax.rsqrt(squares / full_width + epsilon)[:, None]
    normed = (joined * inv_rms * gain[None, :]).astype(jnp.bfloat16)

    def add_logits(first, piece, last):
        if kernels:
            held["logits"], extra = head(table, first, piece, held["lm"], held["logits"], target_row, last)
            if last:
                held["stats"] = extra
            return extra

    normed_near, normed_across = gather(normed, bits, size, add_logits)
    logits = held["logits"]
    if kernels:
        stats = held["stats"][:4]
    else:
        normed_all = whole(normed_near + normed_across, table[1])
        logits = jnp.dot(normed_all, w_lm, preferred_element_type=jnp.float32)
        is_target = (me * share + lax.iota(jnp.int32, share))[None, :] == targets[:, None]
        peak = jnp.max(logits, axis=1)
        shifted = logits - peak[:, None]
        weight = jnp.exp(shifted)
        stats = jnp.stack(
            [
                peak,
                jnp.sum(weight, axis=1),
                jnp.sum(weight * shifted, axis=1),
                jnp.sum(jnp.where(is_target, logits, 0.0), axis=1),
            ]
        )
    for group in gather_rounds(bits) + [[0]]:
        stats = merge_sums(contributions(stats, group, size))
    peak, exp_total, exp_moment, picked = stats[0], stats[1], stats[2], stats[3]
    log_total = peak + jnp.log(exp_total)
    token_loss = log_total - picked
    rowdot = ((exp_moment / exp_total - (picked - peak)) / tokens)[:, None] / inv_rms

    if kernels:
        spread = jnp.broadcast_to(log_total[None], (8, tokens))
        high, dlogits = back_first(table, count, count, logits, spread, target_row, held["lm"], rows)
        low = back_rest(table, 0, count, dlogits, held["lm"], rows)
    else:
        dlogits = (
            (jnp.exp(logits - log_total[:, None]) - is_target.astype(jnp.float32)) / tokens
        ).astype(jnp.bfloat16)
        total = lax.dot_general(
            dlogits, w_lm, (((1,), (1,)), ((), ())), preferred_element_type=jnp.float32
        )
        low, high = cut(total, table[0], rows)

    def fill_grad_lm(k, after):
        if kernels and k in (1, bits - 1):
            at, pieces = (0, normed_near) if k == 1 else (count, normed_across)
            held["grad_lm"], token = head_grad(
                table, at, *pieces, dlogits, full_width, after, held["grad_lm"]
            )
            return token

    scale = HALF_SCALE * (tokens / 128)

    def pack_half(x):
        return (x * scale).astype(jnp.float16)

    def unpack_half(x):
        return x.astype(jnp.float32) * (1.0 / scale)

    dnormed = reduce_halves(low, high, bits, size, pack_half, unpack_half, fill_grad_lm)
    if kernels:
        grad_lm = held["grad_lm"]
    else:
        grad_lm = lax.dot_general(
            normed_all, dlogits, (((0,), (0,)), ((), ())), preferred_element_type=jnp.float32
        ).astype(jnp.bfloat16)

    grad_gain = jnp.sum(dnormed * joined * inv_rms, axis=0)
    dfused = (
        inv_rms * (dnormed * gain[None, :]) - joined * (inv_rms * inv_rms * inv_rms * rowdot / full_width)
    ).astype(jnp.bfloat16)

    def fill_grad_fc(first, piece, last):
        if kernels:
            held["grad_fc"], token = join_grad(table, first, piece, x_turned, full_width, held["grad_fc"])
            return token

    dfused_near, dfused_across = gather(dfused, bits, size, fill_grad_fc)
    if kernels:
        grad_fc = held["grad_fc"]
    else:
        dfused_all = whole(dfused_near + dfused_across, table[1])
        grad_fc = jnp.dot(x.T, dfused_all, preferred_element_type=jnp.float32).astype(jnp.bfloat16)
        grad_fc = grad_fc.reshape(3, rows, full_width)
    return (token_loss, grad_fc, grad_gain, grad_lm)


def solution(mesh):
    return jax.shard_map(
        functools.partial(on_device, mesh.shape["section"]),
        mesh=mesh,
        in_specs=(
            P(("grp", "section"), None),
            P(("grp", "section"), None),
            P(("grp", "section"), None),
            P(None, "section", None),
            P("section"),
            P(None, "section"),
            P("grp"),
        ),
        out_specs=(P("grp"), P("grp", "section", None), P(("grp", "section")), P("grp", "section")),
        check_vma=False,
    )
```

time: 448 us -> 194 us (0.43)
  blocking collectives: 160 us -> 0 us
  waiting for transfers between devices: 207 us -> 76.7 us
  Pallas kernels: 0 us -> 66.4 us
  matrix products: 58.8 us -> 0 us
  starting transfers between devices: 0.16 us -> 43.3 us
  between operations: 13.8 us -> 1.07 us
    reduce_scatter x2 -> x0, waiting for transfers between devices: 137 us -> none  [the longest x1 68.9 us: on_device(): lax.psum_scatter(jnp.einsum('jsr,jts->rt', w_block, stacked, preferred_el...]
    psum x3 -> x0, blocking collectives: 94.3 us -> none  [the longest x2 63 us: on_device(): exp_total, picked = lax.psum((local_total, picked_local), 'section')]
    all_gather x2 -> x0, waiting for transfers between devices: 69.9 us -> none  [the longest x1 39.5 us: on_device(): normed_all = lax.all_gather(normed_local, 'section', axis=0, tiled=True)]
    pallas_call x0 -> x17, Pallas kernels: none -> 66.4 us  [the longest x5 19.3 us: join_grad(): pl.pallas_call(functools.partial(join_grad_kernel, first, count, aliased)...]
    ppermute x0 -> x34, waiting for transfers between devices: none -> 65.5 us  [exchange(): return lax.ppermute(x, 'section', [(i, i ^ mask) for i in range(size)])]
    dot_general x5 -> x0, matrix products: 58.8 us -> none  [the longest x1 14 us: on_device(): jnp.einsum('jts,rt->jsr', stacked, lax.all_gather(dfused, 'section', axis...]
    all_to_all x3 -> x0, blocking collectives: 37 us -> none  [the longest x1 14.2 us: on_device(): lax.all_to_all(low_feat, 'section', split_axis=1, concat_axis=0, tiled=True)]
    ppermute x0 -> x34, starting transfers between devices: none -> 36 us  [exchange(): return lax.ppermute(x, 'section', [(i, i ^ mask) for i in range(size)])]
  transfers between devices with their start and end apart: 4 -> 35, of which waited for: 4 -> 26; matrix products, arithmetic and copies ran while one was open for 2% -> 1% of each run, Pallas kernels for 0% -> 24%
where the time goes in v3:
time: 194 us
  waiting for transfers between devices  76.7 us (40%)
  Pallas kernels  66.4 us (34%)
  starting transfers between devices  43.3 us (22%)
  other arithmetic  6.39 us (3%)
    ppermute x34, waiting for transfers between devices, exchange(): return lax.ppermute(x, 'section', [(i, i ^ mask) for i in range(size)])  65.5 us
    ppermute x34, starting transfers between devices, exchange(): return lax.ppermute(x, 'section', [(i, i ^ mask) for i in range(size)])  36 us
    pallas_call x5, Pallas kernels, join_grad(): pl.pallas_call(functools.partial(join_grad_kernel, first, count, aliased)...  19.3 us
    pallas_call x2, Pallas kernels, join(): pl.pallas_call(functools.partial(join_kernel, first, count), out_shape=tu...  11.4 us
    all_to_all x1, waiting for transfers between devices, on_device(): lax.all_to_all(sent, 'section', split_axis=0, concat_axis=0, tiled=True)  11.2 us
    pallas_call x2, Pallas kernels, head_grad(): pl.pallas_call(functools.partial(head_grad_kernel, first, counts, aliased...  10.6 us
    pallas_call x5, Pallas kernels, head(): pl.pallas_call(functools.partial(head_kernel, first, count, last), out_sh...  9.44 us
    all_to_all x1, starting transfers between devices, on_device(): lax.all_to_all(sent, 'section', split_axis=0, concat_axis=0, tiled=True)  7.35 us
  transfers between devices with their start and end apart: 35, of which 26 were waited for; matrix products, arithmetic and copies ran while one was open for 1% of the time, Pallas kernels for 24%

profile of v3, /device:TPU:1, one launch (start us, length us, event | category | flops | bytes accessed | tf_op | source)
XLA Modules:
  0.0 194.1 jit_solution(12949776688114284064)
XLA Ops:
  0.6 1.8 maximum_bitcast_fusion
  2.4 7.3 %all-to-all-start = ((bf16[16,8,1536]{2,1,0:T(8,128)(2,1)}), bf16[16,8,1536]{2,1,0:T(8,128)(2,1)S(1)}, u32[]{:S(2)}, u32[]{:S(2)}) async-start(bf16[16,8,1536]{2,1,0:T(8,128)(2,1)} %maximum_bitcast_fusion), calls=%async_computation | async-start | bytes 786432 | tf_op jit(solution)/shard_map/all_to_all | solution.py:441
  10.5 11.2 %all-to-all-done = bf16[16,8,1536]{2,1,0:T(8,128)(2,1)S(1)} async-done(((bf16[16,8,1536]{2,1,0:T(8,128)(2,1)}), bf16[16,8,1536]{2,1,0:T(8,128)(2,1)S(1)}, u32[]{:S(2)}, u32[]{:S(2)}) %all-to-all-start) | async-done | bytes 393248 | tf_op jit(solution)/shard_map/all_to_all | solution.py:441
  21.7 5.7 %join.3 = (f32[8,128,512]{2,1,0:T(8,128)S(1)}, bf16[1536,128]{1,0:T(8,128)(2,1)S(1)}) custom-call(s32[2,16]{1,0:T(2,128)S(1)} %broadcast_xor_fusion.table, bf16[128,1536]{1,0:T(8,128)(2,1)S(1)} %bitcast.112, bf16[3,512,8192]{2,1,0:T(8,128)(2,1)} %w_ref.4), custom_call_target="tpu_custom_call" | custom-call | flops 1610612736 | bytes 12582912 | tf_op jit(solution)/shard_map/join/pallas_call | solution.py:130
  27.9 5.7 %join.2 = f32[8,128,512]{2,1,0:T(8,128)S(1)} custom-call(s32[2,16]{1,0:T(2,128)S(1)} %broadcast_xor_fusion.table, bf16[128,1536]{1,0:T(8,128)(2,1)S(1)} %bitcast.113, bf16[3,512,8192]{2,1,0:T(8,128)(2,1)} %w_ref.4), custom_call_target="tpu_custom_call" | custom-call | flops 1610612736 | bytes 12582912 | tf_op jit(solution)/shard_map/join/pallas_call | solution.py:130
  35.5 6.5 %stage.1 = (bf16[8192,1024]{1,0:T(8,128)(2,1)S(1)}, f32[1,512]{1,0:T(1,128)S(1)}) custom-call(s32[2,16]{1,0:T(2,128)S(1)} %broadcast_xor_fusion.table, bf16[8192,1024]{1,0:T(8,128)(2,1)} %w_ref.5, f32[2,2,128,256]{3,2,1,0:T(8,128)S(1)} %slice_bitcast_fusion.6.after_ref), custom_call_target="tpu_custom_call" | custom-call | bytes 16777216 | tf_op jit(solution)/shard_map/stage/pallas_call | solution.py:84
  42.0 5.7 %collective-permute-done.3 = f32[2,2,128,256]{3,2,1,0:T(8,128)S(1)} collective-permute-done((f32[2,2,128,256]{3,2,1,0:T(8,128)S(1)}, f32[2,2,128,256]{3,2,1,0:T(8,128)S(1)}, u32[]{:S(2)}, u32[]{:S(2)}) %collective-permute-start.3) | collective-permute-done | bytes 524320 | tf_op jit(solution)/shard_map/ppermute | solution.py:46
  49.3 5.2 %collective-permute-done.4 = f32[2,128,256]{2,1,0:T(8,128)S(1)} collective-permute-done((f32[2,128,256]{2,1,0:T(8,128)S(1)}, f32[2,128,256]{2,1,0:T(8,128)S(1)}, u32[]{:S(2)}, u32[]{:S(2)}) %collective-permute-start.4) | collective-permute-done | bytes 262176 | tf_op jit(solution)/shard_map/ppermute | solution.py:46
  56.6 12.4 %collective-permute-done.5 = f32[1,128,512]{2,1,0:T(8,128)S(1)} collective-permute-done((f32[1,128,512]{2,1,0:T(8,128)S(1)}, f32[1,128,512]{2,1,0:T(8,128)S(1)}, u32[]{:S(2)}, u32[]{:S(2)}) %collective-permute-start.5) | collective-permute-done | bytes 262176 | tf_op jit(solution)/shard_map/ppermute | solution.py:46
  69.2 3.3 %collective-permute-done.6 = f32[128]{0:T(128)S(1)} collective-permute-done((f32[128]{0:T(128)S(1)}, f32[128]{0:T(128)S(1)}, u32[]{:S(2)}, u32[]{:S(2)}) %collective-permute-start.6) | collective-permute-done | bytes 544 | tf_op jit(solution)/shard_map/ppermute | solution.py:46
  76.6 4.4 %collective-permute-start.10 = (f32[128]{0:T(128)S(1)}, f32[128]{0:T(128)S(1)}, u32[]{:S(2)}, u32[]{:S(2)}) collective-permute-start(f32[128]{0:T(128)S(1)} %add_add_fusion.3), channel_id=1, source_target_pairs={{0,1},{1,0},{2,3},{3,2},{4,5},{5,4},{6,7},{7,6},{8,9},{9,8},{10,11... | collective-permute-start | bytes 1544 | tf_op jit(solution)/shard_map/ppermute | solution.py:46
  84.2 6.8 %collective-permute-done.11 = bf16[1,128,512]{2,1,0:T(8,128)(2,1)S(1)} collective-permute-done((bf16[1,128,512]{2,1,0:T(8,128)(2,1)S(1)}, bf16[1,128,512]{2,1,0:T(8,128)(2,1)S(1)}, u32[]{:S(2)}, u32[]{:S(2)}) %collective-permute-start.11) | collective-permute-done | bytes 131104 | tf_op jit(solution)/shard_map/ppermute | solution.py:46
  91.8 1.8 collective-permute-start.13
  97.1 3.5 %collective-permute-done.14 = bf16[2,128,512]{2,1,0:T(8,128)(2,1)S(1)} collective-permute-done((bf16[2,128,512]{2,1,0:T(8,128)(2,1)S(1)}, bf16[2,128,512]{2,1,0:T(8,128)(2,1)S(1)}, u32[]{:S(2)}, u32[]{:S(2)}) %collective-permute-start.14) | collective-permute-done | bytes 262176 | tf_op jit(solution)/shard_map/ppermute | solution.py:46
  100.6 5.0 %collective-permute-done.13 = bf16[2,128,512]{2,1,0:T(8,128)(2,1)S(1)} collective-permute-done((bf16[2,128,512]{2,1,0:T(8,128)(2,1)S(1)}, bf16[2,128,512]{2,1,0:T(8,128)(2,1)S(1)}, u32[]{:S(2)}, u32[]{:S(2)}) %collective-permute-start.13) | collective-permute-done | bytes 262176 | tf_op jit(solution)/shard_map/ppermute | solution.py:46
  107.3 3.1 %head.8 = (f32[128,1024]{1,0:T(8,128)S(1)}, f32[1,512]{1,0:T(1,128)}) custom-call(s32[2,16]{1,0:T(2,128)S(1)} %broadcast_xor_fusion.table, bf16[6,128,512]{2,1,0:T(8,128)(2,1)S(1)} %multiply_convert_fusion.2.piece_ref.b_ref, bf16[8192,1024]{1,0:T(8,128)(2,1)S(1)} %get-tuple-element.31.w_ref, f32[128,1024]{1,0:T(8,128)S(1)} %get-tuple-element.36.before_ref, ...), custom_call_target="tpu_custom_call" | custom-call | flops 805306368 | bytes 1048576 | tf_op jit(solution)/shard_map/head/pallas_call | solution.py:181
  110.4 2.9 %head.9 = (f32[128,1024]{1,0:T(8,128)S(1)}, f32[8,128]{1,0:T(8,128)S(1)}) custom-call(s32[2,16]{1,0:T(2,128)S(1)} %broadcast_xor_fusion.table, bf16[6,128,512]{2,1,0:T(8,128)(2,1)S(1)} %collective-permute-done.16.piece_ref.b_ref, bf16[8192,1024]{1,0:T(8,128)(2,1)S(1)} %get-tuple-element.31.w_ref, f32[128,1024]{1,0:T(8,128)S(1)} %get-tuple-element.37.before_ref, ...), custom_call_target="tpu_custom_call" | custom-call | flops 805306368 | bytes 1048576 | tf_op jit(solution)/shard_map/head/pallas_call | solution.py:181
  113.5 3.1 %collective-permute-done.17 = f32[4,128]{1,0:T(4,128)S(1)} collective-permute-done((f32[4,128]{1,0:T(4,128)S(1)}, f32[4,128]{1,0:T(4,128)S(1)}, u32[]{:S(2)}, u32[]{:S(2)}) %collective-permute-start.17) | collective-permute-done | bytes 2080 | tf_op jit(solution)/shard_map/ppermute | solution.py:46
  121.0 2.9 %collective-permute-start.21 = (f32[4,128]{1,0:T(4,128)S(1)}, f32[4,128]{1,0:T(4,128)S(1)}, u32[]{:S(2)}, u32[]{:S(2)}) collective-permute-start(f32[4,128]{1,0:T(4,128)S(1)} %pad_maximum_fusion.5), channel_id=1, source_target_pairs={{0,1},{1,0},{2,3},{3,2},{4,5},{5,4},{6,7},{7,6},{8,9},{9,8},{10,11... | collective-permute-start | bytes 6152 | tf_op jit(solution)/shard_map/ppermute | solution.py:46
  124.8 4.7 %back_first.1 = (f32[8,128,512]{2,1,0:T(8,128)S(1)}, bf16[128,1024]{1,0:T(8,128)(2,1)S(1)}) custom-call(s32[2,16]{1,0:T(2,128)S(1)} %broadcast_xor_fusion.table, f32[128,1024]{1,0:T(8,128)S(1)} %get-tuple-element.39.logits_ref, f32[8,128]{1,0:T(8,128)S(1)} %broadcast_in_dim.8.stats_ref, s32[1,128]{1,0:T(1,128)S(1)} %bitcast.119, ...), custom_call_target="tpu_custom_call" | custom-call | flops 1073741824 | bytes 2097152 | tf_op jit(solution)/shard_map/back_first/pallas_call | solution.py:217
  130.2 4.4 %back_rest.1 = f32[8,128,512]{2,1,0:T(8,128)S(1)} custom-call(s32[2,16]{1,0:T(2,128)S(1)} %broadcast_xor_fusion.table, bf16[128,1024]{1,0:T(8,128)(2,1)S(1)} %get-tuple-element.40.d_ref, bf16[8192,1024]{1,0:T(8,128)(2,1)S(1)} %get-tuple-element.31.w_ref), custom_call_target="tpu_custom_call" | custom-call | flops 1073741824 | bytes 2097152 | tf_op jit(solution)/shard_map/back_rest/pallas_call | solution.py:233
  136.8 5.3 %head_grad.2 = (bf16[8192,1024]{1,0:T(8,128)(2,1)}, f32[1,512]{1,0:T(1,128)S(1)}) custom-call(s32[2,16]{1,0:T(2,128)S(1)} %broadcast_xor_fusion.table, bf16[2,128,512]{2,1,0:T(8,128)(2,1)S(1)} %pad_maximum_fusion.2.a_ref, bf16[6,128,512]{2,1,0:T(8,128)(2,1)S(1)} %multiply_convert_fusion.2.piece_ref.b_ref, bf16[128,1024]{1,0:T(8,128)(2,1)S(1)} %get-tuple-element.40.d_ref, ...), custom_call_target="tpu_custom_call" | custom-call | flops 1073741824 | bytes 8388608 | tf_op jit(solution)/shard_map/head_grad/pallas_call | solution.py:278
  149.1 2.0 %collective-permute-start.27 = (f16[1,128,512]{2,1,0:T(8,128)(2,1)S(1)}, f16[1,128,512]{2,1,0:T(8,128)(2,1)S(1)}, u32[]{:S(2)}, u32[]{:S(2)}) collective-permute-start(f16[1,128,512]{2,1,0:T(8,128)(2,1)S(1)} %get-tuple-element.54), channel_id=1, source_target_pairs={{0,8},{1,9},{2,10},{3,11},{4,12},{5,13},{6,14},{7,15},{8,0},{9,1},... | collective-permute-start | bytes 393224 | tf_op jit(solution)/shard_map/ppermute | solution.py:46
  151.1 5.3 %head_grad.3 = (bf16[8192,1024]{1,0:T(8,128)(2,1)}, f32[1,512]{1,0:T(1,128)S(1)}) custom-call(s32[2,16]{1,0:T(2,128)S(1)} %broadcast_xor_fusion.table, bf16[2,128,512]{2,1,0:T(8,128)(2,1)S(1)} %collective-permute-done.15.piece_ref.a_ref, bf16[6,128,512]{2,1,0:T(8,128)(2,1)S(1)} %collective-permute-done.16.piece_ref.b_ref, ...), custom_call_target="tpu_custom_call", output_to_operand_aliasing={{0}: (5, {})} | custom-call | flops 1073741824 | bytes 8388608 | tf_op jit(solution)/shard_map/head_grad/pallas_call | solution.py:278
  157.1 2.2 %join_grad.5 = (bf16[3,512,8192]{2,1,0:T(8,128)(2,1)}, f32[1,512]{1,0:T(1,128)S(1)}) custom-call(s32[2,16]{1,0:T(2,128)S(1)} %broadcast_xor_fusion.table, bf16[1,128,512]{2,1,0:T(8,128)(2,1)S(1)} %subtract_convert_fusion.piece_ref, bf16[1536,128]{1,0:T(8,128)(2,1)S(1)} %get-tuple-element.45.x_ref), custom_call_target="tpu_custom_call" | custom-call | flops 201326592 | bytes 1572864 | tf_op jit(solution)/shard_map/join_grad/pallas_call | solution.py:322
  159.3 3.5 %collective-permute-done.28 = bf16[1,128,512]{2,1,0:T(8,128)(2,1)S(1)} collective-permute-done((bf16[1,128,512]{2,1,0:T(8,128)(2,1)S(1)}, bf16[1,128,512]{2,1,0:T(8,128)(2,1)S(1)}, u32[]{:S(2)}, u32[]{:S(2)}) %collective-permute-start.28) | collective-permute-done | bytes 131104 | tf_op jit(solution)/shard_map/ppermute | solution.py:46
  162.8 3.7 %collective-permute-start.32 = (bf16[2,128,512]{2,1,0:T(8,128)(2,1)S(1)}, bf16[2,128,512]{2,1,0:T(8,128)(2,1)S(1)}, u32[]{:S(2)}, u32[]{:S(2)}) collective-permute-start(bf16[2,128,512]{2,1,0:T(8,128)(2,1)S(1)} %pad_maximum_fusion.3), channel_id=1, source_target_pairs={{0,1},{1,0},{2,3},{3,2},{4,5},{5,4},{6,7},{7,6},{8,9},{9,8},{10,11... | collective-permute-start | bytes 786440 | tf_op jit(solution)/shard_map/ppermute | solution.py:46
  169.2 2.8 %join_grad.6 = (bf16[3,512,8192]{2,1,0:T(8,128)(2,1)}, f32[1,512]{1,0:T(1,128)}) custom-call(s32[2,16]{1,0:T(2,128)S(1)} %broadcast_xor_fusion.table, bf16[1,128,512]{2,1,0:T(8,128)(2,1)S(1)} %multiply_convert_fusion.4.piece_ref, bf16[1536,128]{1,0:T(8,128)(2,1)S(1)} %get-tuple-element.45.x_ref, ...), custom_call_target="tpu_custom_call", output_to_operand_aliasing={{0}: (3, {})} | custom-call | flops 201326592 | bytes 1572864 | tf_op jit(solution)/shard_map/join_grad/pallas_call | solution.py:322
  172.1 2.8 %join_grad.7 = (bf16[3,512,8192]{2,1,0:T(8,128)(2,1)}, f32[1,512]{1,0:T(1,128)S(1)}) custom-call(s32[2,16]{1,0:T(2,128)S(1)} %broadcast_xor_fusion.table, bf16[2,128,512]{2,1,0:T(8,128)(2,1)S(1)} %collective-permute-done.32.piece_ref, bf16[1536,128]{1,0:T(8,128)(2,1)S(1)} %get-tuple-element.45.x_ref, ...), custom_call_target="tpu_custom_call", output_to_operand_aliasing={{0}: (3, {})} | custom-call | flops 402653184 | bytes 3145728 | tf_op jit(solution)/shard_map/join_grad/pallas_call | solution.py:322
  175.4 5.0 %collective-permute-done.30 = bf16[2,128,512]{2,1,0:T(8,128)(2,1)S(1)} collective-permute-done((bf16[2,128,512]{2,1,0:T(8,128)(2,1)S(1)}, bf16[2,128,512]{2,1,0:T(8,128)(2,1)S(1)}, u32[]{:S(2)}, u32[]{:S(2)}) %collective-permute-start.30) | collective-permute-done | bytes 262176 | tf_op jit(solution)/shard_map/ppermute | solution.py:46
  182.7 5.7 %join_grad.8 = (bf16[3,512,8192]{2,1,0:T(8,128)(2,1)}, f32[1,512]{1,0:T(1,128)}) custom-call(s32[2,16]{1,0:T(2,128)S(1)} %broadcast_xor_fusion.table, bf16[6,128,512]{2,1,0:T(8,128)(2,1)S(1)} %multiply_convert_fusion.1.piece_ref, bf16[1536,128]{1,0:T(8,128)(2,1)S(1)} %get-tuple-element.45.x_ref, ...), custom_call_target="tpu_custom_call", output_to_operand_aliasing={{0}: (3, {})} | custom-call | flops 1207959552 | bytes 9437184 | tf_op jit(solution)/shard_map/join_grad/pallas_call | solution.py:322
  188.4 5.7 %join_grad.9 = (bf16[3,512,8192]{2,1,0:T(8,128)(2,1)}, f32[1,512]{1,0:T(1,128)}) custom-call(s32[2,16]{1,0:T(2,128)S(1)} %broadcast_xor_fusion.table, bf16[6,128,512]{2,1,0:T(8,128)(2,1)S(1)} %collective-permute-done.33.piece_ref, bf16[1536,128]{1,0:T(8,128)(2,1)S(1)} %get-tuple-element.45.x_ref, ...), custom_call_target="tpu_custom_call", output_to_operand_aliasing={{0}: (3, {})} | custom-call | flops 1207959552 | bytes 9437184 | tf_op jit(solution)/shard_map/join_grad/pallas_call | solution.py:322
  (108 shorter events, 41.3 us)
Async XLA Ops:
  2.4 19.3 %all-to-all-start = ((bf16[16,8,1536]{2,1,0:T(8,128)(2,1)}), bf16[16,8,1536]{2,1,0:T(8,128)(2,1)S(1)}, u32[]{:S(2)}, u32[]{:S(2)}) async-start(bf16[16,8,1536]{2,1,0:T(8,128)(2,1)} %maximum_bitcast_fusion), calls=%async_computation | async-start | bytes 786432 | tf_op jit(solution)/shard_map/all_to_all | solution.py:441
  27.4 6.2 %collective-permute-start = (f32[8,128,512]{2,1,0:T(8,128)S(1)}, f32[8,128,512]{2,1,0:T(8,128)S(1)}, u32[]{:S(2)}, u32[]{:S(2)}) collective-permute-start(f32[8,128,512]{2,1,0:T(8,128)S(1)} %get-tuple-element.29), channel_id=1, source_target_pairs={{0,1},{1,0},{2,3},{3,2},{4,5},{5,4},{6,7},{7,6},{8,9},{9,8},{10,11... | collective-permute-start | bytes 6291464 | tf_op jit(solution)/shard_map/ppermute | solution.py:46
  34.2 13.6 %collective-permute-start.3 = (f32[2,2,128,256]{3,2,1,0:T(8,128)S(1)}, f32[2,2,128,256]{3,2,1,0:T(8,128)S(1)}, u32[]{:S(2)}, u32[]{:S(2)}) collective-permute-start(f32[2,2,128,256]{3,2,1,0:T(8,128)S(1)} %slice_bitcast_fusion.4), channel_id=1, source_target_pairs={{0,4},{1,5},{2,6},{3,7},{4,0},{5,1},{6,2},{7,3},{8,12},{9,13},{10,... | collective-permute-start | bytes 1572872 | tf_op jit(solution)/shard_map/ppermute | solution.py:46
  34.8 13.0 %collective-permute-start.1 = (f32[2,2,128,256]{3,2,1,0:T(8,128)S(1)}, f32[2,2,128,256]{3,2,1,0:T(8,128)S(1)}, u32[]{:S(2)}, u32[]{:S(2)}) collective-permute-start(f32[2,2,128,256]{3,2,1,0:T(8,128)S(1)} %slice_bitcast_fusion.6.after_ref), channel_id=1, source_target_pairs={{0,2},{1,3},{2,0},{3,1},{4,6},{5,7},{6,4},{7,5},{8,10},{9,11},{10,... | collective-permute-start | bytes 1572872 | tf_op jit(solution)/shard_map/ppermute | solution.py:46
  48.0 6.5 %collective-permute-start.4 = (f32[2,128,256]{2,1,0:T(8,128)S(1)}, f32[2,128,256]{2,1,0:T(8,128)S(1)}, u32[]{:S(2)}, u32[]{:S(2)}) collective-permute-start(f32[2,128,256]{2,1,0:T(8,128)S(1)} %slice_bitcast_fusion.10), channel_id=1, source_target_pairs={{0,2},{1,3},{2,0},{3,1},{4,6},{5,7},{6,4},{7,5},{8,10},{9,11},{10,... | collective-permute-start | bytes 786440 | tf_op jit(solution)/shard_map/ppermute | solution.py:46
  48.7 6.2 %collective-permute-start.2 = (f32[2,128,256]{2,1,0:T(8,128)S(1)}, f32[2,128,256]{2,1,0:T(8,128)S(1)}, u32[]{:S(2)}, u32[]{:S(2)}) collective-permute-start(f32[2,128,256]{2,1,0:T(8,128)S(1)} %slice_bitcast_fusion.12), channel_id=1, source_target_pairs={{0,4},{1,5},{2,6},{3,7},{4,0},{5,1},{6,2},{7,3},{8,12},{9,13},{10,... | collective-permute-start | bytes 786440 | tf_op jit(solution)/shard_map/ppermute | solution.py:46
  55.0 14.1 %collective-permute-start.5 = (f32[1,128,512]{2,1,0:T(8,128)S(1)}, f32[1,128,512]{2,1,0:T(8,128)S(1)}, u32[]{:S(2)}, u32[]{:S(2)}) collective-permute-start(f32[1,128,512]{2,1,0:T(8,128)S(1)} %pad_maximum_fusion.1), channel_id=1, source_target_pairs={{0,8},{1,9},{2,10},{3,11},{4,12},{5,13},{6,14},{7,15},{8,0},{9,1},... | collective-permute-start | bytes 786440 | tf_op jit(solution)/shard_map/ppermute | solution.py:46
  69.2 3.4 %collective-permute-start.6 = (f32[128]{0:T(128)S(1)}, f32[128]{0:T(128)S(1)}, u32[]{:S(2)}, u32[]{:S(2)}) collective-permute-start(f32[128]{0:T(128)S(1)} %get-tuple-element.62), channel_id=1, source_target_pairs={{0,8},{1,9},{2,10},{3,11},{4,12},{5,13},{6,14},{7,15},{8,0},{9,1},... | collective-permute-start | bytes 1544 | tf_op jit(solution)/shard_map/ppermute | solution.py:46
  72.5 3.3 %collective-permute-start.9 = (f32[128]{0:T(128)S(1)}, f32[128]{0:T(128)S(1)}, u32[]{:S(2)}, u32[]{:S(2)}) collective-permute-start(f32[128]{0:T(128)S(1)} %add.138), channel_id=1, source_target_pairs={{0,6},{1,7},{2,4},{3,5},{4,2},{5,3},{6,0},{7,1},{8,14},{9,15},{10,... | collective-permute-start | bytes 1544 | tf_op jit(solution)/shard_map/ppermute | solution.py:46
  76.6 5.3 %collective-permute-start.10 = (f32[128]{0:T(128)S(1)}, f32[128]{0:T(128)S(1)}, u32[]{:S(2)}, u32[]{:S(2)}) collective-permute-start(f32[128]{0:T(128)S(1)} %add_add_fusion.3), channel_id=1, source_target_pairs={{0,1},{1,0},{2,3},{3,2},{4,5},{5,4},{6,7},{7,6},{8,9},{9,8},{10,11... | collective-permute-start | bytes 1544 | tf_op jit(solution)/shard_map/ppermute | solution.py:46
  82.0 9.0 %collective-permute-start.11 = (bf16[1,128,512]{2,1,0:T(8,128)(2,1)S(1)}, bf16[1,128,512]{2,1,0:T(8,128)(2,1)S(1)}, u32[]{:S(2)}, u32[]{:S(2)}) collective-permute-start(bf16[1,128,512]{2,1,0:T(8,128)(2,1)S(1)} %multiply_convert_fusion.7.piece_ref), channel_id=1, source_target_pairs={{0,8},{1,9},{2,10},{3,11},{4,12},{5,13},{6,14},{7,15},{8,0},{9,1},... | collective-permute-start | bytes 393224 | tf_op jit(solution)/shard_map/ppermute | solution.py:46
  91.0 4.8 %collective-permute-start.15 = (bf16[2,128,512]{2,1,0:T(8,128)(2,1)S(1)}, bf16[2,128,512]{2,1,0:T(8,128)(2,1)S(1)}, u32[]{:S(2)}, u32[]{:S(2)}) collective-permute-start(bf16[2,128,512]{2,1,0:T(8,128)(2,1)S(1)} %pad_maximum_fusion.2.a_ref), channel_id=1, source_target_pairs={{0,1},{1,0},{2,3},{3,2},{4,5},{5,4},{6,7},{7,6},{8,9},{9,8},{10,11... | collective-permute-start | bytes 786440 | tf_op jit(solution)/shard_map/ppermute | solution.py:46
  91.8 8.8 %collective-permute-start.14 = (bf16[2,128,512]{2,1,0:T(8,128)(2,1)S(1)}, bf16[2,128,512]{2,1,0:T(8,128)(2,1)S(1)}, u32[]{:S(2)}, u32[]{:S(2)}) collective-permute-start(bf16[2,128,512]{2,1,0:T(8,128)(2,1)S(1)} %pad_maximum_fusion.2.a_ref), channel_id=1, source_target_pairs={{0,6},{1,7},{2,4},{3,5},{4,2},{5,3},{6,0},{7,1},{8,14},{9,15},{10,... | collective-permute-start | bytes 786440 | tf_op jit(solution)/shard_map/ppermute | solution.py:46
  91.8 13.9 %collective-permute-start.13 = (bf16[2,128,512]{2,1,0:T(8,128)(2,1)S(1)}, bf16[2,128,512]{2,1,0:T(8,128)(2,1)S(1)}, u32[]{:S(2)}, u32[]{:S(2)}) collective-permute-start(bf16[2,128,512]{2,1,0:T(8,128)(2,1)S(1)} %pad_maximum_fusion.2.a_ref), channel_id=1, source_target_pairs={{0,4},{1,5},{2,6},{3,7},{4,0},{5,1},{6,2},{7,3},{8,12},{9,13},{10,... | collective-permute-start | bytes 786440 | tf_op jit(solution)/shard_map/ppermute | solution.py:46
  93.6 13.0 %collective-permute-start.12 = (bf16[2,128,512]{2,1,0:T(8,128)(2,1)S(1)}, bf16[2,128,512]{2,1,0:T(8,128)(2,1)S(1)}, u32[]{:S(2)}, u32[]{:S(2)}) collective-permute-start(bf16[2,128,512]{2,1,0:T(8,128)(2,1)S(1)} %pad_maximum_fusion.2.a_ref), channel_id=1, source_target_pairs={{0,2},{1,3},{2,0},{3,1},{4,6},{5,7},{6,4},{7,5},{8,10},{9,11},{10,... | collective-permute-start | bytes 786440 | tf_op jit(solution)/shard_map/ppermute | solution.py:46
  106.7 3.7 %collective-permute-start.16 = (bf16[6,128,512]{2,1,0:T(8,128)(2,1)S(1)}, bf16[6,128,512]{2,1,0:T(8,128)(2,1)S(1)}, u32[]{:S(2)}, u32[]{:S(2)}) collective-permute-start(bf16[6,128,512]{2,1,0:T(8,128)(2,1)S(1)} %multiply_convert_fusion.2.piece_ref.b_ref), channel_id=1, source_target_pairs={{0,1},{1,0},{2,3},{3,2},{4,5},{5,4},{6,7},{7,6},{8,9},{9,8},{10,11... | collective-permute-start | bytes 2359304 | tf_op jit(solution)/shard_map/ppermute | solution.py:46
  113.2 3.4 %collective-permute-start.17 = (f32[4,128]{1,0:T(4,128)S(1)}, f32[4,128]{1,0:T(4,128)S(1)}, u32[]{:S(2)}, u32[]{:S(2)}) collective-permute-start(f32[4,128]{1,0:T(4,128)S(1)} %slice.181), channel_id=1, source_target_pairs={{0,8},{1,9},{2,10},{3,11},{4,12},{5,13},{6,14},{7,15},{8,0},{9,1},... | collective-permute-start | bytes 6152 | tf_op jit(solution)/shard_map/ppermute | solution.py:46
  116.7 3.4 %collective-permute-start.20 = (f32[4,128]{1,0:T(4,128)S(1)}, f32[4,128]{1,0:T(4,128)S(1)}, u32[]{:S(2)}, u32[]{:S(2)}) collective-permute-start(f32[4,128]{1,0:T(4,128)S(1)} %pad_maximum_fusion.4), channel_id=1, source_target_pairs={{0,6},{1,7},{2,4},{3,5},{4,2},{5,3},{6,0},{7,1},{8,14},{9,15},{10,... | collective-permute-start | bytes 6152 | tf_op jit(solution)/shard_map/ppermute | solution.py:46
  117.0 3.1 %collective-permute-start.19 = (f32[4,128]{1,0:T(4,128)S(1)}, f32[4,128]{1,0:T(4,128)S(1)}, u32[]{:S(2)}, u32[]{:S(2)}) collective-permute-start(f32[4,128]{1,0:T(4,128)S(1)} %pad_maximum_fusion.4), channel_id=1, source_target_pairs={{0,4},{1,5},{2,6},{3,7},{4,0},{5,1},{6,2},{7,3},{8,12},{9,13},{10,... | collective-permute-start | bytes 6152 | tf_op jit(solution)/shard_map/ppermute | solution.py:46
  121.0 3.8 %collective-permute-start.21 = (f32[4,128]{1,0:T(4,128)S(1)}, f32[4,128]{1,0:T(4,128)S(1)}, u32[]{:S(2)}, u32[]{:S(2)}) collective-permute-start(f32[4,128]{1,0:T(4,128)S(1)} %pad_maximum_fusion.5), channel_id=1, source_target_pairs={{0,1},{1,0},{2,3},{3,2},{4,5},{5,4},{6,7},{7,6},{8,9},{9,8},{10,11... | collective-permute-start | bytes 6152 | tf_op jit(solution)/shard_map/ppermute | solution.py:46
  129.8 5.4 %collective-permute-start.22 = (f16[8,128,512]{2,1,0:T(8,128)(2,1)S(1)}, f16[8,128,512]{2,1,0:T(8,128)(2,1)S(1)}, u32[]{:S(2)}, u32[]{:S(2)}) collective-permute-start(f16[8,128,512]{2,1,0:T(8,128)(2,1)S(1)} %multiply_convert_fusion), channel_id=1, source_target_pairs={{0,1},{1,0},{2,3},{3,2},{4,5},{5,4},{6,7},{7,6},{8,9},{9,8},{10,11... | collective-permute-start | bytes 3145736 | tf_op jit(solution)/shard_map/ppermute | solution.py:46
  135.8 7.8 %collective-permute-start.25 = (f16[2,2,128,256]{3,2,1,0:T(8,128)(2,1)S(1)}, f16[2,2,128,256]{3,2,1,0:T(8,128)(2,1)S(1)}, u32[]{:S(2)}, u32[]{:S(2)}) collective-permute-start(f16[2,2,128,256]{3,2,1,0:T(8,128)(2,1)S(1)} %fusion.10), channel_id=1, source_target_pairs={{0,4},{1,5},{2,6},{3,7},{4,0},{5,1},{6,2},{7,3},{8,12},{9,13},{10,... | collective-permute-start | bytes 786440 | tf_op jit(solution)/shard_map/ppermute | solution.py:46
  135.9 7.8 %collective-permute-start.23 = (f16[2,2,128,256]{3,2,1,0:T(8,128)(2,1)S(1)}, f16[2,2,128,256]{3,2,1,0:T(8,128)(2,1)S(1)}, u32[]{:S(2)}, u32[]{:S(2)}) collective-permute-start(f16[2,2,128,256]{3,2,1,0:T(8,128)(2,1)S(1)} %multiply_convert_fusion.3), channel_id=1, source_target_pairs={{0,2},{1,3},{2,0},{3,1},{4,6},{5,7},{6,4},{7,5},{8,10},{9,11},{10,... | collective-permute-start | bytes 786440 | tf_op jit(solution)/shard_map/ppermute | solution.py:46
  143.9 3.9 %collective-permute-start.26 = (f16[2,128,256]{2,1,0:T(8,128)(2,1)S(1)}, f16[2,128,256]{2,1,0:T(8,128)(2,1)S(1)}, u32[]{:S(2)}, u32[]{:S(2)}) collective-permute-start(f16[2,128,256]{2,1,0:T(8,128)(2,1)S(1)} %fusion.19), channel_id=1, source_target_pairs={{0,2},{1,3},{2,0},{3,1},{4,6},{5,7},{6,4},{7,5},{8,10},{9,11},{10,... | collective-permute-start | bytes 393224 | tf_op jit(solution)/shard_map/ppermute | solution.py:46
  144.9 4.2 %collective-permute-start.24 = (f16[2,128,256]{2,1,0:T(8,128)(2,1)S(1)}, f16[2,128,256]{2,1,0:T(8,128)(2,1)S(1)}, u32[]{:S(2)}, u32[]{:S(2)}) collective-permute-start(f16[2,128,256]{2,1,0:T(8,128)(2,1)S(1)} %fusion.18), channel_id=1, source_target_pairs={{0,4},{1,5},{2,6},{3,7},{4,0},{5,1},{6,2},{7,3},{8,12},{9,13},{10,... | collective-permute-start | bytes 393224 | tf_op jit(solution)/shard_map/ppermute | solution.py:46
  149.1 7.4 %collective-permute-start.27 = (f16[1,128,512]{2,1,0:T(8,128)(2,1)S(1)}, f16[1,128,512]{2,1,0:T(8,128)(2,1)S(1)}, u32[]{:S(2)}, u32[]{:S(2)}) collective-permute-start(f16[1,128,512]{2,1,0:T(8,128)(2,1)S(1)} %get-tuple-element.54), channel_id=1, source_target_pairs={{0,8},{1,9},{2,10},{3,11},{4,12},{5,13},{6,14},{7,15},{8,0},{9,1},... | collective-permute-start | bytes 393224 | tf_op jit(solution)/shard_map/ppermute | solution.py:46
  156.6 6.2 %collective-permute-start.28 = (bf16[1,128,512]{2,1,0:T(8,128)(2,1)S(1)}, bf16[1,128,512]{2,1,0:T(8,128)(2,1)S(1)}, u32[]{:S(2)}, u32[]{:S(2)}) collective-permute-start(bf16[1,128,512]{2,1,0:T(8,128)(2,1)S(1)} %subtract_convert_fusion.piece_ref), channel_id=1, source_target_pairs={{0,8},{1,9},{2,10},{3,11},{4,12},{5,13},{6,14},{7,15},{8,0},{9,1},... | collective-permute-start | bytes 393224 | tf_op jit(solution)/shard_map/ppermute | solution.py:46
  162.8 9.2 %collective-permute-start.32 = (bf16[2,128,512]{2,1,0:T(8,128)(2,1)S(1)}, bf16[2,128,512]{2,1,0:T(8,128)(2,1)S(1)}, u32[]{:S(2)}, u32[]{:S(2)}) collective-permute-start(bf16[2,128,512]{2,1,0:T(8,128)(2,1)S(1)} %pad_maximum_fusion.3), channel_id=1, source_target_pairs={{0,1},{1,0},{2,3},{3,2},{4,5},{5,4},{6,7},{7,6},{8,9},{9,8},{10,11... | collective-permute-start | bytes 786440 | tf_op jit(solution)/shard_map/ppermute | solution.py:46
  166.6 8.8 %collective-permute-start.31 = (bf16[2,128,512]{2,1,0:T(8,128)(2,1)S(1)}, bf16[2,128,512]{2,1,0:T(8,128)(2,1)S(1)}, u32[]{:S(2)}, u32[]{:S(2)}) collective-permute-start(bf16[2,128,512]{2,1,0:T(8,128)(2,1)S(1)} %pad_maximum_fusion.3), channel_id=1, source_target_pairs={{0,6},{1,7},{2,4},{3,5},{4,2},{5,3},{6,0},{7,1},{8,14},{9,15},{10,... | collective-permute-start | bytes 786440 | tf_op jit(solution)/shard_map/ppermute | solution.py:46
  166.6 13.8 %collective-permute-start.30 = (bf16[2,128,512]{2,1,0:T(8,128)(2,1)S(1)}, bf16[2,128,512]{2,1,0:T(8,128)(2,1)S(1)}, u32[]{:S(2)}, u32[]{:S(2)}) collective-permute-start(bf16[2,128,512]{2,1,0:T(8,128)(2,1)S(1)} %pad_maximum_fusion.3), channel_id=1, source_target_pairs={{0,4},{1,5},{2,6},{3,7},{4,0},{5,1},{6,2},{7,3},{8,12},{9,13},{10,... | collective-permute-start | bytes 786440 | tf_op jit(solution)/shard_map/ppermute | solution.py:46
  168.3 13.0 %collective-permute-start.29 = (bf16[2,128,512]{2,1,0:T(8,128)(2,1)S(1)}, bf16[2,128,512]{2,1,0:T(8,128)(2,1)S(1)}, u32[]{:S(2)}, u32[]{:S(2)}) collective-permute-start(bf16[2,128,512]{2,1,0:T(8,128)(2,1)S(1)} %pad_maximum_fusion.3), channel_id=1, source_target_pairs={{0,2},{1,3},{2,0},{3,1},{4,6},{5,7},{6,4},{7,5},{8,10},{9,11},{10,... | collective-permute-start | bytes 786440 | tf_op jit(solution)/shard_map/ppermute | solution.py:46
  181.5 6.9 %collective-permute-start.33 = (bf16[6,128,512]{2,1,0:T(8,128)(2,1)S(1)}, bf16[6,128,512]{2,1,0:T(8,128)(2,1)S(1)}, u32[]{:S(2)}, u32[]{:S(2)}) collective-permute-start(bf16[6,128,512]{2,1,0:T(8,128)(2,1)S(1)} %multiply_convert_fusion.1.piece_ref), channel_id=1, source_target_pairs={{0,1},{1,0},{2,3},{3,2},{4,5},{5,4},{6,7},{7,6},{8,9},{9,8},{10,11... | collective-permute-start | bytes 2359304 | tf_op jit(solution)/shard_map/ppermute | solution.py:46
  (5 other events, 75.7 us)

commit v4 on v3

v4 whole, which is shorter than its diff:
```python
import functools

import jax
import jax.numpy as jnp
import numpy as np
from jax import lax
from jax.experimental import pallas as pl
from jax.experimental.pallas import tpu as pltpu
from jax.sharding import PartitionSpec as P

epsilon = 1e-06
MIB = 1024 * 1024
HALF_SCALE = 2.0**20
TILE = 256
DEPTH = 4


def reduce_places(bits, order):
    return [
        sum(((q >> (bits - 2 - k)) & 1) << bit for k, bit in enumerate(order)) for q in range(1 << (bits - 1))
    ]


def gather_places(bits):
    held = fresh = np.zeros((2, 1), np.int32)
    out, across = [], [fresh ^ 1]
    for bit in range(bits - 1, 2, -1):
        out.append(fresh)
        fresh = held ^ (1 << bit)
        across.append(fresh ^ 1)
        held = np.concatenate([held, fresh], axis=1)
    first = held ^ np.array([[4], [2]], np.int32)
    second = np.concatenate([held, first], axis=1) ^ np.array([[2], [4]], np.int32)
    out += [fresh, *across, first, first ^ 1, second, second ^ 1]
    places = np.concatenate([p.reshape(-1) for p in out])
    streams = np.concatenate([np.repeat(np.arange(2), p.shape[1]) for p in out])
    return places.astype(np.int32), streams.astype(np.int32)


def masks_of(group):
    return [sum(1 << b for k, b in enumerate(group) if (m >> k) & 1) for m in range(1, 1 << len(group))]


def sum_rounds(bits):
    return [[bit] for bit in range(bits - 1, 2, -1)] + [[1, 2], [0]]


def exchange(x, mask, size):
    return lax.ppermute(x, "section", [(i, i ^ mask) for i in range(size)])


def settings(flops, bytes_moved, limit):
    return dict(
        compiler_params=pltpu.CompilerParams(vmem_limit_bytes=limit),
        cost_estimate=pl.CostEstimate(flops=flops, bytes_accessed=bytes_moved, transcendentals=0),
    )


ANYWHERE = pl.BlockSpec(memory_space=pl.ANY)
IN_VMEM = pl.BlockSpec(memory_space=pltpu.VMEM)
IN_SMEM = pl.BlockSpec(memory_space=pltpu.SMEM)
vmem_out = pltpu.VMEM


def near(x):
    return pltpu.with_memory_space_constraint(x, pltpu.VMEM)


def far(x):
    return pltpu.with_memory_space_constraint(x, pltpu.HBM)


def stage_kernel(pieces, table, w_ref, after_ref, out_ref, token_ref, sems):
    copies = []
    for k, piece in enumerate(pieces):
        copies.append(pltpu.make_async_copy(w_ref.at[piece], out_ref.at[piece], sems.at[k]))
    for copy in copies:
        copy.start()
    token_ref[...] = jnp.ones_like(token_ref)
    for copy in copies:
        copy.wait()


def stage(table, w, after, rows):
    step = w.shape[0] // 16
    pieces = [pl.ds(k * step, step) for k in range(16)]
    return pl.pallas_call(
        functools.partial(stage_kernel, pieces),
        out_shape=(vmem_out(w.shape, w.dtype), vmem_out((1, rows), jnp.float32)),
        in_specs=[IN_SMEM, ANYWHERE, ANYWHERE],
        out_specs=(IN_VMEM, IN_VMEM),
        scratch_shapes=[pltpu.SemaphoreType.DMA((len(pieces),))],
        name="stage",
        **settings(0, w.size * 2, 2 * MIB),
    )(table, far(w), after)


def join_kernel(first, count, offset, table, x_ref, w_ref, after_ref, *rest):
    out_ref, token_ref, slots, sems = rest[0], rest[1], rest[-2], rest[-1]
    rows = w_ref.shape[1]
    width = slots.shape[3]
    half = width // 2
    middle = table.shape[1] // 2

    def copy(q):
        column = pl.multiple_of(table[0, first + q] * rows + offset, 128)
        return pltpu.make_async_copy(w_ref.at[:, :, pl.ds(column, width)], slots.at[q], sems.at[q])

    for q in range(min(DEPTH, count)):
        copy(q).start()
    token_ref[...] = jnp.ones_like(token_ref)
    if len(rest) == 5:
        rest[2][...] = x_ref[...].T

    @pl.loop(0, count)
    def _(q):
        copy(q).wait()

        @pl.when(q + DEPTH < count)
        def _():
            copy(q + DEPTH).start()

        total = jnp.dot(x_ref[:, :rows], slots[q, 0], preferred_element_type=jnp.float32)
        for j in (1, 2):
            total += jnp.dot(
                x_ref[:, j * rows : (j + 1) * rows], slots[q, j], preferred_element_type=jnp.float32
            )
        out_ref[0, q] = total[:, :half]
        out_ref[1, table[1, first + q] + (q // middle) * middle] = total[:, half:]


def join(table, first, count, offset, width, x, w_fc, after, turn):
    tokens = x.shape[0]
    rows = w_fc.shape[1]
    shapes = [vmem_out((2, count, tokens, width // 2), jnp.float32), vmem_out((1, width // 2), jnp.float32)]
    if turn:
        shapes.append(jax.ShapeDtypeStruct(x.shape[::-1], x.dtype))
    return pl.pallas_call(
        functools.partial(join_kernel, first, count, offset),
        out_shape=tuple(shapes),
        in_specs=[IN_SMEM, IN_VMEM, ANYWHERE, ANYWHERE],
        out_specs=(IN_VMEM,) * len(shapes),
        scratch_shapes=[pltpu.VMEM((count, 3, rows, width), jnp.bfloat16), pltpu.SemaphoreType.DMA((count,))],
        name="join",
        **settings(6 * tokens * rows * width * count, 6 * rows * width * count, 20 * MIB),
    )(table, near(x), far(w_fc), after)


def columns_of(rows_of_stats):
    count, tokens = rows_of_stats.shape
    padded = jnp.concatenate([rows_of_stats, jnp.zeros((tokens - count, tokens), jnp.float32)], axis=0)
    return padded.T


def target_mask(me, targets_ref, share):
    column = me * share + lax.broadcasted_iota(jnp.int32, (targets_ref.shape[1], share), 1)
    return column == columns_of(targets_ref[...].astype(jnp.float32))[:, :1].astype(jnp.int32)


def head_kernel(first, counts, last, starts, w_ref, before_ref, targets_ref, *rest):
    pieces, (out_ref, extra_ref) = rest[:-2], rest[-2:]
    width = pieces[0].shape[2]
    out_ref[...] = before_ref[...]
    at = first
    for piece_ref, count in zip(pieces, counts):

        @pl.loop(0, count)
        def _(q):
            row = pl.multiple_of(starts[at + q], 128)
            out_ref[...] += jnp.dot(piece_ref[q], w_ref[pl.ds(row, width), :], preferred_element_type=jnp.float32)

        at += count
    if not last:
        extra_ref[...] = jnp.ones_like(extra_ref)
        return
    logits = out_ref[...]
    tokens, share = logits.shape
    peak = jnp.max(logits, axis=1, keepdims=True)
    shifted = logits - peak
    weight = jnp.exp(shifted)
    picked = jnp.where(target_mask(starts[starts.shape[0] - 1], targets_ref, share), logits, 0.0)
    lane = lax.broadcasted_iota(jnp.int32, (tokens, tokens), 1)
    stats = jnp.where(lane == 0, peak, 0.0)
    for k, part in enumerate((weight, weight * shifted, picked)):
        stats = jnp.where(lane == k + 1, jnp.sum(part, axis=1, keepdims=True), stats)
    extra_ref[...] = stats.T[: extra_ref.shape[0]]


def head(starts, first, pieces, w_lm, before, targets, last):
    tokens, width = pieces[0].shape[1:]
    counts = tuple(p.shape[0] for p in pieces)
    share = w_lm.shape[1]
    extra = (8, tokens) if last else (1, width)
    return pl.pallas_call(
        functools.partial(head_kernel, first, counts, last),
        out_shape=(vmem_out(before.shape, jnp.float32), vmem_out(extra, jnp.float32)),
        in_specs=[IN_SMEM] + [IN_VMEM] * (3 + len(pieces)),
        out_specs=(IN_VMEM, IN_VMEM),
        name="head",
        **settings(2 * tokens * width * share * sum(counts), 8 * tokens * share, 6 * MIB),
    )(starts, near(w_lm), near(before), near(targets), *[near(p) for p in pieces])


def back_products(first, count, table, d_ref, w_ref, out_ref):
    width = out_ref.shape[3]

    @pl.loop(0, count)
    def _(q):
        row = pl.multiple_of(table[0, first + q] * (2 * width), 128)
        for stream, at in ((0, q), (1, table[1, first + q])):
            out_ref[stream, at] = lax.dot_general(
                d_ref[...],
                w_ref[pl.ds(row + stream * width, width), :],
                (((1,), (1,)), ((), ())),
                preferred_element_type=jnp.float32,
            )


def back_first_kernel(first, count, table, logits_ref, stats_ref, targets_ref, w_ref, out_ref, d_ref):
    logits = logits_ref[...]
    tokens, share = logits.shape
    log_total = columns_of(stats_ref[...])[:, :1]
    hit = jnp.where(target_mask(table[0, 0], targets_ref, share), 1.0, 0.0)
    d_ref[...] = ((jnp.exp(logits - log_total) - hit) / tokens).astype(d_ref.dtype)
    back_products(first, count, table, d_ref, w_ref, out_ref)


def back_first(table, first, count, logits, stats, targets, w_lm, width):
    tokens, share = logits.shape
    return pl.pallas_call(
        functools.partial(back_first_kernel, first, count),
        out_shape=(vmem_out((2, count, tokens, width), jnp.float32), vmem_out((tokens, share), jnp.bfloat16)),
        in_specs=[IN_SMEM] + [IN_VMEM] * 4,
        out_specs=(IN_VMEM, IN_VMEM),
        name="back_first",
        **settings(4 * tokens * width * share * count, 8 * tokens * width * count, 6 * MIB),
    )(table, near(logits), near(stats), near(targets), near(w_lm))


def back_rest_kernel(first, count, table, d_ref, w_ref, out_ref):
    back_products(first, count, table, d_ref, w_ref, out_ref)


def back_rest(table, first, count, dlogits, w_lm, width):
    tokens, share = dlogits.shape
    return pl.pallas_call(
        functools.partial(back_rest_kernel, first, count),
        out_shape=vmem_out((2, count, tokens, width), jnp.float32),
        in_specs=[IN_SMEM, IN_VMEM, IN_VMEM],
        out_specs=IN_VMEM,
        name="back_rest",
        **settings(4 * tokens * width * share * count, 8 * tokens * width * count, 6 * MIB),
    )(table, near(dlogits), near(w_lm))


def head_grad_kernel(first, counts, aliased, starts, d_ref, after_ref, *rest):
    pieces = rest[aliased : aliased + len(counts)]
    out_ref, token_ref, slots, sems = rest[-4:]
    width = pieces[0].shape[2]
    share = d_ref.shape[1]
    token_ref[...] = jnp.ones_like(token_ref)

    def copy(at):
        row = pl.multiple_of(starts[first + at], 128)
        return pltpu.make_async_copy(slots.at[at], out_ref.at[pl.ds(row, width), :], sems.at[at])

    offset = 0
    for piece_ref, count in zip(pieces, counts):

        @pl.loop(0, count)
        def _(q):
            turned = piece_ref[q].T
            for column in range(0, share, TILE):
                slots[offset + q, :, column : column + TILE] = jnp.dot(
                    turned, d_ref[:, column : column + TILE], preferred_element_type=jnp.float32
                ).astype(slots.dtype)
            copy(offset + q).start()

        offset += count

    for at in range(sum(counts)):
        copy(at).wait()


def head_grad(starts, first, pieces, dlogits, full_width, after, into):
    tokens, width = pieces[0].shape[1:]
    counts = tuple(p.shape[0] for p in pieces)
    share = dlogits.shape[1]
    extra = () if into is None else (into,)
    blocks = sum(counts)
    return pl.pallas_call(
        functools.partial(head_grad_kernel, first, counts, len(extra)),
        out_shape=(
            jax.ShapeDtypeStruct((full_width, share), jnp.bfloat16),
            vmem_out((1, width), jnp.float32),
        ),
        in_specs=[IN_SMEM, IN_VMEM, ANYWHERE] + [ANYWHERE] * len(extra) + [IN_VMEM] * len(pieces),
        out_specs=(ANYWHERE, IN_VMEM),
        scratch_shapes=[pltpu.VMEM((blocks, width, share), jnp.bfloat16), pltpu.SemaphoreType.DMA((blocks,))],
        input_output_aliases={3: 0} if extra else {},
        name="head_grad",
        **settings(2 * tokens * width * share * blocks, 2 * width * share * blocks, 14 * MIB),
    )(starts, near(dlogits), after, *extra, *[near(p) for p in pieces])


def join_grad_kernel(first, counts, aliased, starts, x_ref, *rest):
    pieces = rest[aliased : aliased + len(counts)]
    out_ref, token_ref, slots, sems = rest[-4:]
    rows, width = slots.shape[2:]
    token_ref[...] = jnp.ones_like(token_ref)

    def copy(at):
        column = pl.multiple_of(starts[first + at], 128)
        return pltpu.make_async_copy(slots.at[at], out_ref.at[:, :, pl.ds(column, width)], sems.at[at])

    offset = 0
    for piece_ref, count in zip(pieces, counts):

        @pl.loop(0, count)
        def _(q):
            for j in range(3):
                for row in range(0, rows, TILE):
                    slots[offset + q, j, row : row + TILE, :] = jnp.dot(
                        x_ref[j * rows + row : j * rows + row + TILE, :],
                        piece_ref[q],
                        preferred_element_type=jnp.float32,
                    ).astype(slots.dtype)
            copy(offset + q).start()

        offset += count

    for at in range(sum(counts)):
        copy(at).wait()


def join_grad(starts, first, pieces, x_turned, full_width, into):
    tokens, width = pieces[0].shape[1:]
    rows = x_turned.shape[0] // 3
    counts = tuple(p.shape[0] for p in pieces)
    extra = () if into is None else (into,)
    blocks = sum(counts)
    return pl.pallas_call(
        functools.partial(join_grad_kernel, first, counts, len(extra)),
        out_shape=(
            jax.ShapeDtypeStruct((3, rows, full_width), jnp.bfloat16),
            vmem_out((1, width), jnp.float32),
        ),
        in_specs=[IN_SMEM, IN_VMEM] + [ANYWHERE] * len(extra) + [IN_VMEM] * len(pieces),
        out_specs=(ANYWHERE, IN_VMEM),
        scratch_shapes=[pltpu.VMEM((blocks, 3, rows, width), jnp.bfloat16), pltpu.SemaphoreType.DMA((blocks,))],
        input_output_aliases={2: 0} if extra else {},
        name="join_grad",
        **settings(6 * tokens * rows * width * blocks, 6 * rows * width * blocks, 14 * MIB),
    )(starts, near(x_turned), *extra, *[near(p) for p in pieces])


def cut(total, table, rows, offset, width):
    tokens = total.shape[0]
    blocks = jnp.take(total.reshape(tokens, -1, rows).transpose(1, 0, 2), table[0], axis=0)
    count = table.shape[1] // 2
    blocks = blocks[:, :, offset : offset + width].reshape(2, count, tokens, 2, width // 2)
    out = []
    for side in range(2):
        second = jnp.take(blocks[side, :, :, 1], jnp.argsort(table[1, side * count : (side + 1) * count]), axis=0)
        out.append(jnp.stack([blocks[side, :, :, 0], second]))
    return out


def whole(pieces, starts):
    blocks = jnp.take(jnp.concatenate(pieces, axis=0), jnp.argsort(starts[:-1]), axis=0)
    return blocks.transpose(1, 0, 2).reshape(blocks.shape[1], -1)


def contributions(x, group, size):
    return [x] + [exchange(x, m, size) for m in masks_of(group)]


def tree_sum(items):
    while len(items) > 1:
        items = [items[k] + items[k + 1] for k in range(0, len(items), 2)]
    return items[0]


def merge_sums(items):
    peak = functools.reduce(jnp.maximum, [i[0:1] for i in items])
    shifts = [i[0:1] - peak for i in items]
    scales = [jnp.exp(s) for s in shifts]
    return jnp.concatenate(
        [
            peak,
            tree_sum([i[1:2] * c for i, c in zip(items, scales)]),
            tree_sum([(i[2:3] + i[1:2] * s) * c for i, s, c in zip(items, shifts, scales)]),
            tree_sum([i[3:4] for i in items]),
        ],
        axis=0,
    )


def with_token(x, token):
    return x if token is None else (x.astype(jnp.float32) * token).astype(x.dtype)


def reduce_halves(low, high, bits, size, pack, unpack, work):
    total = low + unpack(exchange(pack(high), 1, size))
    streams = [total[0], total[1]]
    for k, order in ((1, (1, 2)), (2, (2, 1))):
        half = streams[0].shape[0] // 2
        sent = [t[half:] for t in streams]
        got = [exchange(pack(t), 1 << bit, size) for t, bit in zip(sent, order)]
        token = work(k, sent[0])
        streams = [t[:half] + with_token(unpack(g), token) for t, g in zip(streams, got)]
    total = jnp.stack(streams)
    for bit in range(3, bits):
        half = total.shape[1] // 2
        sent = total[:, half:]
        got = exchange(pack(sent), 1 << bit, size)
        token = work(bit, sent)
        total = total[:, :half] + with_token(unpack(got), token)
    return [total[0, 0], total[1, 0]]


def gather(own, bits, size, work):
    def flat(x):
        return x.reshape((-1,) + x.shape[2:])

    held = fresh = jnp.stack(own)[:, None]
    across = [exchange(fresh, 1, size)]
    for bit in range(bits - 1, 2, -1):
        arrived = exchange(held, 1 << bit, size)
        token = work([flat(fresh)], False)
        fresh = with_token(arrived, token)
        across.append(exchange(fresh, 1, size))
        held = jnp.concatenate([held, fresh], axis=1)
    first = [exchange(held[0], 4, size), exchange(held[1], 2, size)]
    token = work([flat(fresh)] + [flat(a) for a in across], False)
    first = with_token(jnp.stack(first), token)
    across = exchange(first, 1, size)
    both = jnp.concatenate([held, first], axis=1)
    second = [exchange(both[0], 2, size), exchange(both[1], 4, size)]
    token = work([flat(first), flat(across)], False)
    second = with_token(jnp.stack(second), token)
    across = exchange(second, 1, size)
    work([flat(second)], False)
    work([flat(across)], True)


def on_device(size, low_feat, mid_feat, high_feat, w_fc, gain, w_lm, targets):
    me = lax.axis_index("section")
    rows, full_width = w_fc.shape[1], w_fc.shape[2]
    share = w_lm.shape[1]
    tokens = targets.shape[0]
    half = rows // 2
    bits = size.bit_length() - 1
    count = size // 2
    first_order = reduce_places(bits, [1, 2] + list(range(3, bits)))
    second_order = reduce_places(bits, [2, 1] + list(range(3, bits)))
    where = [second_order.index(p) for p in first_order]
    chunks = jnp.asarray(np.array(first_order + [p + 1 for p in first_order], np.int32)) ^ me
    table = jnp.stack([chunks, jnp.asarray(np.array(where + where, np.int32))])
    places, streams = gather_places(bits)
    starts = jnp.concatenate([(jnp.asarray(places) ^ me) * rows + jnp.asarray(streams * half), me[None]])
    kernels = half % TILE == 0
    target_row = targets.reshape(1, tokens)

    sent = jnp.concatenate(
        [f.reshape(-1, size, rows) for f in (low_feat, mid_feat, high_feat)], axis=2
    ).transpose(1, 0, 2)
    x = lax.all_to_all(sent, "section", split_axis=0, concat_axis=0, tiled=True).reshape(tokens, 3 * rows)

    held = {"logits": jnp.zeros((tokens, share), jnp.float32), "grad_lm": None, "grad_fc": None}
    if not kernels:
        total = jnp.dot(x, w_fc.reshape(3 * rows, full_width), preferred_element_type=jnp.float32)

    if kernels:
        high, _, held["x"] = join(table, count, count, 0, rows, x, w_fc, sent, True)
        low, _ = join(table, 0, count, 0, rows, x, w_fc, sent, False)
    else:
        low, high = cut(total, table, rows, 0, rows)

    def bring_head(k, after):
        if kernels and k == 1:
            held["lm"], token = stage(table, w_lm, after, half)
            return token

    joined = jnp.concatenate(
        reduce_halves(low, high, bits, size, lambda x: x, lambda x: x, bring_head), axis=1
    )

    squares = jnp.sum(joined * joined, axis=1)
    for group in sum_rounds(bits):
        squares = tree_sum(contributions(squares, group, size))
    inv_rms = lax.rsqrt(squares / full_width + epsilon)[:, None]
    normed = (joined * inv_rms * gain[None, :]).astype(jnp.bfloat16)

    all_normed, all_dfused = [], []

    def add_logits(pieces, last):
        first = sum(p.shape[0] for p in all_normed)
        all_normed.extend(pieces)
        if kernels:
            held["logits"], extra = head(starts, first, pieces, held["lm"], held["logits"], target_row, last)
            if last:
                held["stats"] = extra
            return extra

    gather([normed[:, :half], normed[:, half:]], bits, size, add_logits)
    logits = held["logits"]
    if kernels:
        stats = held["stats"][:4]
    else:
        normed_all = whole(all_normed, starts)
        logits = jnp.dot(normed_all, w_lm, preferred_element_type=jnp.float32)
        is_target = (me * share + lax.iota(jnp.int32, share))[None, :] == targets[:, None]
        peak = jnp.max(logits, axis=1)
        shifted = logits - peak[:, None]
        weight = jnp.exp(shifted)
        stats = jnp.stack(
            [
                peak,
                jnp.sum(weight, axis=1),
                jnp.sum(weight * shifted, axis=1),
                jnp.sum(jnp.where(is_target, logits, 0.0), axis=1),
            ]
        )
    for group in sum_rounds(bits):
        stats = merge_sums(contributions(stats, group, size))
    peak, exp_total, exp_moment, picked = stats[0], stats[1], stats[2], stats[3]
    log_total = peak + jnp.log(exp_total)
    token_loss = log_total - picked
    rowdot = ((exp_moment / exp_total - (picked - peak)) / tokens)[:, None] / inv_rms

    if kernels:
        spread = jnp.broadcast_to(log_total[None], (8, tokens))
        high, dlogits = back_first(table, count, count, logits, spread, target_row, held["lm"], half)
        low = back_rest(table, 0, count, dlogits, held["lm"], half)
    else:
        dlogits = (
            (jnp.exp(logits - log_total[:, None]) - is_target.astype(jnp.float32)) / tokens
        ).astype(jnp.bfloat16)
        total = lax.dot_general(
            dlogits, w_lm, (((1,), (1,)), ((), ())), preferred_element_type=jnp.float32
        )
        low, high = cut(total, table, rows, 0, rows)

    def fill_grad_lm(k, after):
        if kernels and k in (1, bits - 1):
            middle = len(all_normed) - 2
            pieces = all_normed[:middle] if k == 1 else all_normed[middle:]
            first = 0 if k == 1 else sum(p.shape[0] for p in all_normed[:middle])
            held["grad_lm"], token = head_grad(
                starts, first, pieces, dlogits, full_width, after, held["grad_lm"]
            )
            return token

    scale = HALF_SCALE * (tokens / 128)

    def pack_half(x):
        return (x * scale).astype(jnp.float16)

    def unpack_half(x):
        return x.astype(jnp.float32) * (1.0 / scale)

    dnormed = jnp.concatenate(
        reduce_halves(low, high, bits, size, pack_half, unpack_half, fill_grad_lm), axis=1
    )
    if kernels:
        grad_lm = held["grad_lm"]
    else:
        grad_lm = lax.dot_general(
            normed_all, dlogits, (((0,), (0,)), ((), ())), preferred_element_type=jnp.float32
        ).astype(jnp.bfloat16)

    grad_gain = jnp.sum(dnormed * joined * inv_rms, axis=0)
    dfused = (
        inv_rms * (dnormed * gain[None, :]) - joined * (inv_rms * inv_rms * inv_rms * rowdot / full_width)
    ).astype(jnp.bfloat16)

    def fill_grad_fc(pieces, last):
        first = sum(p.shape[0] for p in all_dfused)
        all_dfused.extend(pieces)
        if kernels:
            held["grad_fc"], token = join_grad(starts, first, pieces, held["x"], full_width, held["grad_fc"])
            return token

    gather([dfused[:, :half], dfused[:, half:]], bits, size, fill_grad_fc)
    if kernels:
        grad_fc = held["grad_fc"]
    else:
        grad_fc = jnp.dot(x.T, whole(all_dfused, starts), preferred_element_type=jnp.float32)
        grad_fc = grad_fc.astype(jnp.bfloat16).reshape(3, rows, full_width)
    return (token_loss, grad_fc, grad_gain, grad_lm)


def solution(mesh):
    return jax.shard_map(
        functools.partial(on_device, mesh.shape["section"]),
        mesh=mesh,
        in_specs=(
            P(("grp", "section"), None),
            P(("grp", "section"), None),
            P(("grp", "section"), None),
            P(None, "section", None),
            P("section"),
            P(None, "section"),
            P("grp"),
        ),
        out_specs=(P("grp"), P("grp", "section", None), P(("grp", "section")), P("grp", "section")),
        check_vma=False,
    )
```

time: 194 us -> 196 us (1.010)
  waiting for transfers between devices: 76.7 us -> 60.7 us
  starting transfers between devices: 43.3 us -> 53.6 us
  Pallas kernels: 66.4 us -> 72.5 us
    ppermute x34 -> x40, waiting for transfers between devices: 65.5 us -> 50.1 us  [exchange(): return lax.ppermute(x, 'section', [(i, i ^ mask) for i in range(size)])]
    ppermute x34 -> x40, starting transfers between devices: 36 us -> 46.2 us  [exchange(): return lax.ppermute(x, 'section', [(i, i ^ mask) for i in range(size)])]
    pallas_call x14, Pallas kernels: 50.7 us -> 56.7 us  [the longest x5 19.9 us: join_grad(): pl.pallas_call(functools.partial(join_grad_kernel, first, counts, len(ext...]
  transfers between devices with their start and end apart: 35 -> 41, of which waited for: 26 -> 26; matrix products, arithmetic and copies ran while one was open for 1% -> 1% of each run, Pallas kernels for 24% -> 27%
where the time goes in v4:
time: 196 us
  Pallas kernels  72.5 us (37%)
  waiting for transfers between devices  60.7 us (31%)
  starting transfers between devices  53.6 us (27%)
  other arithmetic  7.58 us (4%)
    ppermute x40, waiting for transfers between devices, exchange(): return lax.ppermute(x, 'section', [(i, i ^ mask) for i in range(size)])  50.1 us
    ppermute x40, starting transfers between devices, exchange(): return lax.ppermute(x, 'section', [(i, i ^ mask) for i in range(size)])  46.2 us
    pallas_call x5, Pallas kernels, join_grad(): pl.pallas_call(functools.partial(join_grad_kernel, first, counts, len(ext...  19.9 us
    pallas_call x2, Pallas kernels, head_grad(): pl.pallas_call(functools.partial(head_grad_kernel, first, counts, len(ext...  13.2 us
    pallas_call x2, Pallas kernels, join(): pl.pallas_call(functools.partial(join_kernel, first, count, offset), out_...  12.2 us
    pallas_call x5, Pallas kernels, head(): pl.pallas_call(functools.partial(head_kernel, first, counts, last), out_s...  11.4 us
    all_to_all x1, waiting for transfers between devices, on_device(): lax.all_to_all(sent, 'section', split_axis=0, concat_axis=0, tiled=True)  10.6 us
    all_to_all x1, starting transfers between devices, on_device(): lax.all_to_all(sent, 'section', split_axis=0, concat_axis=0, tiled=True)  7.35 us
  transfers between devices with their start and end apart: 41, of which 26 were waited for; matrix products, arithmetic and copies ran while one was open for 1% of the time, Pallas kernels for 27%

profile of v4, /device:TPU:1, one launch (start us, length us, event | category | flops | bytes accessed | tf_op | source)
XLA Modules:
  0.0 195.8 jit_solution(4356194686454674319)
XLA Ops:
  2.4 7.3 %all-to-all-start = ((bf16[16,8,1536]{2,1,0:T(8,128)(2,1)}), bf16[16,8,1536]{2,1,0:T(8,128)(2,1)S(1)}, u32[]{:S(2)}, u32[]{:S(2)}) async-start(bf16[16,8,1536]{2,1,0:T(8,128)(2,1)} %maximum_bitcast_fusion.after_ref), calls=%async_computation | async-start | bytes 786432 | tf_op jit(solution)/shard_map/all_to_all | solution.py:468
  11.1 10.6 %all-to-all-done = bf16[16,8,1536]{2,1,0:T(8,128)(2,1)S(1)} async-done(((bf16[16,8,1536]{2,1,0:T(8,128)(2,1)}), bf16[16,8,1536]{2,1,0:T(8,128)(2,1)S(1)}, u32[]{:S(2)}, u32[]{:S(2)}) %all-to-all-start) | async-done | bytes 393248 | tf_op jit(solution)/shard_map/all_to_all | solution.py:468
  21.7 6.1 %join.3 = (f32[2,8,128,256]{3,2,1,0:T(8,128)S(1)}, f32[1,256]{1,0:T(1,128)}, bf16[1536,128]{1,0:T(8,128)(2,1)S(1)}) custom-call(s32[2,16]{1,0:T(2,128)S(1)} %pad_add_fusion.table, bf16[128,1536]{1,0:T(8,128)(2,1)S(1)} %bitcast.173, bf16[3,512,8192]{2,1,0:T(8,128)(2,1)} %w_ref.4, bf16[16,8,1536]{2,1,0:T(8,128)(2,1)} %maximum_bitcast_fusion.after_ref), custom_call_target="tpu_custom_call" | custom-call | flops 1610612736 | bytes 12582912 | tf_op jit(solution)/shard_map/join/pallas_call | solution.py:138
  28.3 6.1 %join.2 = (f32[2,8,128,256]{3,2,1,0:T(8,128)S(1)}, f32[1,256]{1,0:T(1,128)}) custom-call(s32[2,16]{1,0:T(2,128)S(1)} %pad_add_fusion.table, bf16[128,1536]{1,0:T(8,128)(2,1)S(1)} %bitcast.174, bf16[3,512,8192]{2,1,0:T(8,128)(2,1)} %w_ref.4, bf16[16,8,1536]{2,1,0:T(8,128)(2,1)} %maximum_bitcast_fusion.after_ref), custom_call_target="tpu_custom_call" | custom-call | flops 1610612736 | bytes 12582912 | tf_op jit(solution)/shard_map/join/pallas_call | solution.py:138
  36.1 6.5 %stage.1 = (bf16[8192,1024]{1,0:T(8,128)(2,1)S(1)}, f32[1,256]{1,0:T(1,128)S(1)}) custom-call(s32[2,16]{1,0:T(2,128)S(1)} %pad_add_fusion.table, bf16[8192,1024]{1,0:T(8,128)(2,1)} %w_ref.5, f32[4,128,256]{2,1,0:T(8,128)S(1)} %get-tuple-element.74.after_ref), custom_call_target="tpu_custom_call" | custom-call | bytes 16777216 | tf_op jit(solution)/shard_map/stage/pallas_call | solution.py:87
  42.6 5.8 %collective-permute-done.3 = f32[4,128,256]{2,1,0:T(8,128)S(1)} collective-permute-done((f32[4,128,256]{2,1,0:T(8,128)S(1)}, f32[4,128,256]{2,1,0:T(8,128)S(1)}, u32[]{:S(2)}, u32[]{:S(2)}) %collective-permute-start.3) | collective-permute-done | bytes 524320 | tf_op jit(solution)/shard_map/ppermute | solution.py:49
  49.8 5.2 %collective-permute-done.4 = f32[2,128,256]{2,1,0:T(8,128)S(1)} collective-permute-done((f32[2,128,256]{2,1,0:T(8,128)S(1)}, f32[2,128,256]{2,1,0:T(8,128)S(1)}, u32[]{:S(2)}, u32[]{:S(2)}) %collective-permute-start.4) | collective-permute-done | bytes 262176 | tf_op jit(solution)/shard_map/ppermute | solution.py:49
  57.2 12.3 %collective-permute-done.5 = f32[2,1,128,256]{3,2,1,0:T(8,128)S(1)} collective-permute-done((f32[2,1,128,256]{3,2,1,0:T(8,128)S(1)}, f32[2,1,128,256]{3,2,1,0:T(8,128)S(1)}, u32[]{:S(2)}, u32[]{:S(2)}) %collective-permute-start.5) | collective-permute-done | bytes 262176 | tf_op jit(solution)/shard_map/ppermute | solution.py:49
  69.8 3.3 %collective-permute-done.6 = f32[128]{0:T(128)S(1)} collective-permute-done((f32[128]{0:T(128)S(1)}, f32[128]{0:T(128)S(1)}, u32[]{:S(2)}, u32[]{:S(2)}) %collective-permute-start.6) | collective-permute-done | bytes 544 | tf_op jit(solution)/shard_map/ppermute | solution.py:49
  77.3 4.4 %collective-permute-start.10 = (f32[128]{0:T(128)S(1)}, f32[128]{0:T(128)S(1)}, u32[]{:S(2)}, u32[]{:S(2)}) collective-permute-start(f32[128]{0:T(128)S(1)} %add_add_fusion.3), channel_id=1, source_target_pairs={{0,1},{1,0},{2,3},{3,2},{4,5},{5,4},{6,7},{7,6},{8,9},{9,8},{10,11... | collective-permute-start | bytes 1544 | tf_op jit(solution)/shard_map/ppermute | solution.py:49
  85.7 5.9 %collective-permute-done.11 = bf16[2,1,128,256]{3,2,1,0:T(8,128)(2,1)S(1)} collective-permute-done((bf16[2,1,128,256]{3,2,1,0:T(8,128)(2,1)S(1)}, bf16[2,1,128,256]{3,2,1,0:T(8,128)(2,1)S(1)}, u32[]{:S(2)}, u32[]{:S(2)}) %collective-permute-start.11) | collective-permute-done | bytes 131104 | tf_op jit(solution)/shard_map/ppermute | solution.py:49
  94.5 2.0 %head.6 = (f32[128,1024]{1,0:T(8,128)S(1)}, f32[1,256]{1,0:T(1,128)S(1)}) custom-call(s32[33]{0:T(128)S(1)} %pad_add_fusion.1.starts, bf16[8192,1024]{1,0:T(8,128)(2,1)S(1)} %get-tuple-element.34.w_ref, f32[128,1024]{1,0:T(8,128)S(1)} %get-tuple-element.36.before_ref, s32[1,128]{1,0:T(1,128)S(1)} %bitcast.188, ...), custom_call_target="tpu_custom_call" | custom-call | flops 402653184 | bytes 1048576 | tf_op jit(solution)/shard_map/head/pallas_call | solution.py:194
  100.1 2.5 %head.7 = (f32[128,1024]{1,0:T(8,128)S(1)}, f32[1,256]{1,0:T(1,128)S(1)}) custom-call(s32[33]{0:T(128)S(1)} %pad_add_fusion.1.starts, bf16[8192,1024]{1,0:T(8,128)(2,1)S(1)} %get-tuple-element.34.w_ref, f32[128,1024]{1,0:T(8,128)S(1)} %get-tuple-element.38.before_ref, s32[1,128]{1,0:T(1,128)S(1)} %bitcast.189, ...), custom_call_target="tpu_custom_call" | custom-call | flops 536870912 | bytes 1048576 | tf_op jit(solution)/shard_map/head/pallas_call | solution.py:194
  102.6 3.4 %collective-permute-done.17 = bf16[4,128,256]{2,1,0:T(8,128)(2,1)S(1)} collective-permute-done((bf16[4,128,256]{2,1,0:T(8,128)(2,1)S(1)}, bf16[4,128,256]{2,1,0:T(8,128)(2,1)S(1)}, u32[]{:S(2)}, u32[]{:S(2)}) %collective-permute-start.17) | collective-permute-done | bytes 262176 | tf_op jit(solution)/shard_map/ppermute | solution.py:49
  107.7 3.0 %head.8 = (f32[128,1024]{1,0:T(8,128)S(1)}, f32[1,256]{1,0:T(1,128)}) custom-call(s32[33]{0:T(128)S(1)} %pad_add_fusion.1.starts, bf16[8192,1024]{1,0:T(8,128)(2,1)S(1)} %get-tuple-element.34.w_ref, f32[128,1024]{1,0:T(8,128)S(1)} %get-tuple-element.40.before_ref, s32[1,128]{1,0:T(1,128)S(1)} %bitcast.190, bf16[8,128,256]{2,1,0:T(8,128)(2,1)S(1)} %fusion.1.rest_0_.rest_1_), custom_call_target="tpu_custom_call" | custom-call | flops 536870912 | bytes 1048576 | tf_op jit(solution)/shard_map/head/pallas_call | solution.py:194
  110.8 2.8 %head.9 = (f32[128,1024]{1,0:T(8,128)S(1)}, f32[8,128]{1,0:T(8,128)S(1)}) custom-call(s32[33]{0:T(128)S(1)} %pad_add_fusion.1.starts, bf16[8192,1024]{1,0:T(8,128)(2,1)S(1)} %get-tuple-element.34.w_ref, f32[128,1024]{1,0:T(8,128)S(1)} %get-tuple-element.42.before_ref, s32[1,128]{1,0:T(1,128)S(1)} %bitcast.191, bf16[8,128,256]{2,1,0:T(8,128)(2,1)S(1)} %bitcast.175), custom_call_target="tpu_custom_call" | custom-call | flops 536870912 | bytes 1048576 | tf_op jit(solution)/shard_map/head/pallas_call | solution.py:194
  113.6 2.6 %collective-permute-start.20 = (f32[4,128]{1,0:T(4,128)S(1)}, f32[4,128]{1,0:T(4,128)S(1)}, u32[]{:S(2)}, u32[]{:S(2)}) collective-permute-start(f32[4,128]{1,0:T(4,128)S(1)} %slice.256), channel_id=1, source_target_pairs={{0,8},{1,9},{2,10},{3,11},{4,12},{5,13},{6,14},{7,15},{8,0},{9,1},... | collective-permute-start | bytes 6152 | tf_op jit(solution)/shard_map/ppermute | solution.py:49
  117.2 2.0 %collective-permute-start.23 = (f32[4,128]{1,0:T(4,128)S(1)}, f32[4,128]{1,0:T(4,128)S(1)}, u32[]{:S(2)}, u32[]{:S(2)}) collective-permute-start(f32[4,128]{1,0:T(4,128)S(1)} %pad_maximum_fusion.10), channel_id=1, source_target_pairs={{0,6},{1,7},{2,4},{3,5},{4,2},{5,3},{6,0},{7,1},{8,14},{9,15},{10,... | collective-permute-start | bytes 6152 | tf_op jit(solution)/shard_map/ppermute | solution.py:49
  122.2 2.5 %collective-permute-start.24 = (f32[4,128]{1,0:T(4,128)S(1)}, f32[4,128]{1,0:T(4,128)S(1)}, u32[]{:S(2)}, u32[]{:S(2)}) collective-permute-start(f32[4,128]{1,0:T(4,128)S(1)} %pad_maximum_fusion.11), channel_id=1, source_target_pairs={{0,1},{1,0},{2,3},{3,2},{4,5},{5,4},{6,7},{7,6},{8,9},{9,8},{10,11... | collective-permute-start | bytes 6152 | tf_op jit(solution)/shard_map/ppermute | solution.py:49
  125.5 4.8 %back_first.1 = (f32[2,8,128,256]{3,2,1,0:T(8,128)S(1)}, bf16[128,1024]{1,0:T(8,128)(2,1)S(1)}) custom-call(s32[2,16]{1,0:T(2,128)S(1)} %pad_add_fusion.table, f32[128,1024]{1,0:T(8,128)S(1)} %get-tuple-element.45.logits_ref, f32[8,128]{1,0:T(8,128)S(1)} %broadcast_in_dim.16.stats_ref, s32[1,128]{1,0:T(1,128)S(1)} %bitcast.192, ...), custom_call_target="tpu_custom_call" | custom-call | flops 1073741824 | bytes 2097152 | tf_op jit(solution)/shard_map/back_first/pallas_call | solution.py:230
  131.0 4.5 %back_rest.1 = f32[2,8,128,256]{3,2,1,0:T(8,128)S(1)} custom-call(s32[2,16]{1,0:T(2,128)S(1)} %pad_add_fusion.table, bf16[128,1024]{1,0:T(8,128)(2,1)S(1)} %get-tuple-element.46.d_ref, bf16[8192,1024]{1,0:T(8,128)(2,1)S(1)} %get-tuple-element.34.w_ref), custom_call_target="tpu_custom_call" | custom-call | flops 1073741824 | bytes 2097152 | tf_op jit(solution)/shard_map/back_rest/pallas_call | solution.py:246
  138.0 6.6 %head_grad.2 = (bf16[8192,1024]{1,0:T(8,128)(2,1)}, f32[1,256]{1,0:T(1,128)S(1)}) custom-call(s32[33]{0:T(128)S(1)} %pad_add_fusion.1.starts, bf16[128,1024]{1,0:T(8,128)(2,1)S(1)} %get-tuple-element.46.d_ref, f32[4,128,256]{2,1,0:T(8,128)S(1)} %get-tuple-element.73.after_ref, bf16[2,128,256]{2,1,0:T(8,128)(2,1)S(1)} %get-tuple-element.97.rest_0_, ...), custom_call_target="tpu_custom_call" | custom-call | flops 1073741824 | bytes 8388608 | tf_op jit(solution)/shard_map/head_grad/pallas_call | solution.py:291
  146.7 2.5 %collective-permute-done.27 = f16[2,128,256]{2,1,0:T(8,128)(2,1)S(1)} collective-permute-done((f16[2,128,256]{2,1,0:T(8,128)(2,1)S(1)}, f16[2,128,256]{2,1,0:T(8,128)(2,1)S(1)}, u32[]{:S(2)}, u32[]{:S(2)}) %collective-permute-start.27) | collective-permute-done | bytes 131104 | tf_op jit(solution)/shard_map/ppermute | solution.py:49
  150.0 1.9 collective-permute-start.30
  151.8 6.6 %head_grad.3 = (bf16[8192,1024]{1,0:T(8,128)(2,1)}, f32[1,256]{1,0:T(1,128)S(1)}) custom-call(s32[33]{0:T(128)S(1)} %pad_add_fusion.1.starts, bf16[128,1024]{1,0:T(8,128)(2,1)S(1)} %get-tuple-element.46.d_ref, f32[2,1,128,256]{3,2,1,0:T(8,128)S(1)} %get-tuple-element.63.after_ref, ...), custom_call_target="tpu_custom_call", output_to_operand_aliasing={{0}: (3, {})} | custom-call | flops 1073741824 | bytes 8388608 | tf_op jit(solution)/shard_map/head_grad/pallas_call | solution.py:291
  159.9 3.0 %collective-permute-start.32 = (bf16[2,1,128,256]{3,2,1,0:T(8,128)(2,1)S(1)}, bf16[2,1,128,256]{3,2,1,0:T(8,128)(2,1)S(1)}, u32[]{:S(2)}, u32[]{:S(2)}) collective-permute-start(bf16[2,1,128,256]{3,2,1,0:T(8,128)(2,1)S(1)} %get-tuple-element.91), channel_id=1, source_target_pairs={{0,1},{1,0},{2,3},{3,2},{4,5},{5,4},{6,7},{7,6},{8,9},{9,8},{10,11... | collective-permute-start | bytes 393224 | tf_op jit(solution)/shard_map/ppermute | solution.py:49
  162.9 2.1 %join_grad.5 = (bf16[3,512,8192]{2,1,0:T(8,128)(2,1)}, f32[1,256]{1,0:T(1,128)S(1)}) custom-call(s32[33]{0:T(128)S(1)} %pad_add_fusion.1.starts, bf16[1536,128]{1,0:T(8,128)(2,1)S(1)} %get-tuple-element.44.x_ref, bf16[2,128,256]{2,1,0:T(8,128)(2,1)S(1)} %get-tuple-element.92.rest_0_), custom_call_target="tpu_custom_call" | custom-call | flops 201326592 | bytes 1572864 | tf_op jit(solution)/shard_map/join_grad/pallas_call | solution.py:342
  165.9 3.1 %collective-permute-start.33 = (bf16[2,1,128,256]{3,2,0,1:T(8,128)(2,1)S(1)}, bf16[2,1,128,256]{3,2,0,1:T(8,128)(2,1)S(1)}, u32[]{:S(2)}, u32[]{:S(2)}) collective-permute-start(bf16[2,1,128,256]{3,2,0,1:T(8,128)(2,1)S(1)} %bitcast_convert_fusion), channel_id=1, source_target_pairs={{0,1},{1,0},{2,3},{3,2},{4,5},{5,4},{6,7},{7,6},{8,9},{9,8},{10,11... | collective-permute-start | bytes 393224 | tf_op jit(solution)/shard_map/ppermute | solution.py:49
  170.3 3.6 %join_grad.6 = (bf16[3,512,8192]{2,1,0:T(8,128)(2,1)}, f32[1,256]{1,0:T(1,128)S(1)}) custom-call(s32[33]{0:T(128)S(1)} %pad_add_fusion.1.starts, bf16[1536,128]{1,0:T(8,128)(2,1)S(1)} %get-tuple-element.44.x_ref, bf16[3,512,8192]{2,1,0:T(8,128)(2,1)} %get-tuple-element.51.rest_0_, ...), custom_call_target="tpu_custom_call", output_to_operand_aliasing={{0}: (2, {})} | custom-call | flops 603979776 | bytes 4718592 | tf_op jit(solution)/shard_map/join_grad/pallas_call | solution.py:342
  177.9 4.3 %join_grad.7 = (bf16[3,512,8192]{2,1,0:T(8,128)(2,1)}, f32[1,256]{1,0:T(1,128)S(1)}) custom-call(s32[33]{0:T(128)S(1)} %pad_add_fusion.1.starts, bf16[1536,128]{1,0:T(8,128)(2,1)S(1)} %get-tuple-element.44.x_ref, bf16[3,512,8192]{2,1,0:T(8,128)(2,1)} %get-tuple-element.53.rest_0_, ...), custom_call_target="tpu_custom_call", output_to_operand_aliasing={{0}: (2, {})} | custom-call | flops 805306368 | bytes 6291456 | tf_op jit(solution)/shard_map/join_grad/pallas_call | solution.py:342
  186.0 4.9 %join_grad.8 = (bf16[3,512,8192]{2,1,0:T(8,128)(2,1)}, f32[1,256]{1,0:T(1,128)}) custom-call(s32[33]{0:T(128)S(1)} %pad_add_fusion.1.starts, bf16[1536,128]{1,0:T(8,128)(2,1)S(1)} %get-tuple-element.44.x_ref, bf16[3,512,8192]{2,1,0:T(8,128)(2,1)} %get-tuple-element.55.rest_0_, bf16[8,128,256]{2,1,0:T(8,128)(2,1)S(1)} %fusion.rest_1_), custom_call_target="tpu_custom_call", output_to_operand_aliasing={{0}: (2, {})} | custom-call | flops 805306368 | bytes 6291456 | tf_op jit(solution)/shard_map/join_grad/pallas_call | solution.py:342
  190.9 4.9 %join_grad.9 = (bf16[3,512,8192]{2,1,0:T(8,128)(2,1)}, f32[1,256]{1,0:T(1,128)}) custom-call(s32[33]{0:T(128)S(1)} %pad_add_fusion.1.starts, bf16[1536,128]{1,0:T(8,128)(2,1)S(1)} %get-tuple-element.44.x_ref, bf16[3,512,8192]{2,1,0:T(8,128)(2,1)} %get-tuple-element.57.rest_0_, bf16[8,128,256]{2,1,0:T(8,128)(2,1)S(1)} %bitcast.177), custom_call_target="tpu_custom_call", output_to_operand_aliasing={{0}: (2, {})} | custom-call | flops 805306368 | bytes 6291456 | tf_op jit(solution)/shard_map/join_grad/pallas_call | solution.py:342
  (150 shorter events, 47.4 us)
Async XLA Ops:
  2.4 19.3 %all-to-all-start = ((bf16[16,8,1536]{2,1,0:T(8,128)(2,1)}), bf16[16,8,1536]{2,1,0:T(8,128)(2,1)S(1)}, u32[]{:S(2)}, u32[]{:S(2)}) async-start(bf16[16,8,1536]{2,1,0:T(8,128)(2,1)} %maximum_bitcast_fusion.after_ref), calls=%async_computation | async-start | bytes 786432 | tf_op jit(solution)/shard_map/all_to_all | solution.py:468
  27.8 6.6 %collective-permute-start = (f32[2,8,128,256]{3,2,1,0:T(8,128)S(1)}, f32[2,8,128,256]{3,2,1,0:T(8,128)S(1)}, u32[]{:S(2)}, u32[]{:S(2)}) collective-permute-start(f32[2,8,128,256]{3,2,1,0:T(8,128)S(1)} %get-tuple-element.33), channel_id=1, source_target_pairs={{0,1},{1,0},{2,3},{3,2},{4,5},{5,4},{6,7},{7,6},{8,9},{9,8},{10,11... | collective-permute-start | bytes 6291464 | tf_op jit(solution)/shard_map/ppermute | solution.py:49
  34.8 13.6 %collective-permute-start.3 = (f32[4,128,256]{2,1,0:T(8,128)S(1)}, f32[4,128,256]{2,1,0:T(8,128)S(1)}, u32[]{:S(2)}, u32[]{:S(2)}) collective-permute-start(f32[4,128,256]{2,1,0:T(8,128)S(1)} %get-tuple-element.75), channel_id=1, source_target_pairs={{0,4},{1,5},{2,6},{3,7},{4,0},{5,1},{6,2},{7,3},{8,12},{9,13},{10,... | collective-permute-start | bytes 1572872 | tf_op jit(solution)/shard_map/ppermute | solution.py:49
  35.3 13.0 %collective-permute-start.1 = (f32[4,128,256]{2,1,0:T(8,128)S(1)}, f32[4,128,256]{2,1,0:T(8,128)S(1)}, u32[]{:S(2)}, u32[]{:S(2)}) collective-permute-start(f32[4,128,256]{2,1,0:T(8,128)S(1)} %get-tuple-element.74.after_ref), channel_id=1, source_target_pairs={{0,2},{1,3},{2,0},{3,1},{4,6},{5,7},{6,4},{7,5},{8,10},{9,11},{10,... | collective-permute-start | bytes 1572872 | tf_op jit(solution)/shard_map/ppermute | solution.py:49
  48.5 6.5 %collective-permute-start.4 = (f32[2,128,256]{2,1,0:T(8,128)S(1)}, f32[2,128,256]{2,1,0:T(8,128)S(1)}, u32[]{:S(2)}, u32[]{:S(2)}) collective-permute-start(f32[2,128,256]{2,1,0:T(8,128)S(1)} %slice.308), channel_id=1, source_target_pairs={{0,2},{1,3},{2,0},{3,1},{4,6},{5,7},{6,4},{7,5},{8,10},{9,11},{10,... | collective-permute-start | bytes 786440 | tf_op jit(solution)/shard_map/ppermute | solution.py:49
  49.2 6.1 %collective-permute-start.2 = (f32[2,128,256]{2,1,0:T(8,128)S(1)}, f32[2,128,256]{2,1,0:T(8,128)S(1)}, u32[]{:S(2)}, u32[]{:S(2)}) collective-permute-start(f32[2,128,256]{2,1,0:T(8,128)S(1)} %slice.304), channel_id=1, source_target_pairs={{0,4},{1,5},{2,6},{3,7},{4,0},{5,1},{6,2},{7,3},{8,12},{9,13},{10,... | collective-permute-start | bytes 786440 | tf_op jit(solution)/shard_map/ppermute | solution.py:49
  55.5 14.0 %collective-permute-start.5 = (f32[2,1,128,256]{3,2,1,0:T(8,128)S(1)}, f32[2,1,128,256]{3,2,1,0:T(8,128)S(1)}, u32[]{:S(2)}, u32[]{:S(2)}) collective-permute-start(f32[2,1,128,256]{3,2,1,0:T(8,128)S(1)} %pad_maximum_fusion.3), channel_id=1, source_target_pairs={{0,8},{1,9},{2,10},{3,11},{4,12},{5,13},{6,14},{7,15},{8,0},{9,1},... | collective-permute-start | bytes 786440 | tf_op jit(solution)/shard_map/ppermute | solution.py:49
  77.3 5.3 %collective-permute-start.10 = (f32[128]{0:T(128)S(1)}, f32[128]{0:T(128)S(1)}, u32[]{:S(2)}, u32[]{:S(2)}) collective-permute-start(f32[128]{0:T(128)S(1)} %add_add_fusion.3), channel_id=1, source_target_pairs={{0,1},{1,0},{2,3},{3,2},{4,5},{5,4},{6,7},{7,6},{8,9},{9,8},{10,11... | collective-permute-start | bytes 1544 | tf_op jit(solution)/shard_map/ppermute | solution.py:49
  82.7 9.0 %collective-permute-start.11 = (bf16[2,1,128,256]{3,2,1,0:T(8,128)(2,1)S(1)}, bf16[2,1,128,256]{3,2,1,0:T(8,128)(2,1)S(1)}, u32[]{:S(2)}, u32[]{:S(2)}) collective-permute-start(bf16[2,1,128,256]{3,2,1,0:T(8,128)(2,1)S(1)} %get-tuple-element.96), channel_id=1, source_target_pairs={{0,8},{1,9},{2,10},{3,11},{4,12},{5,13},{6,14},{7,15},{8,0},{9,1},... | collective-permute-start | bytes 393224 | tf_op jit(solution)/shard_map/ppermute | solution.py:49
  84.0 9.5 %collective-permute-start.12 = (bf16[2,1,128,256]{3,2,0,1:T(8,128)(2,1)S(1)}, bf16[2,1,128,256]{3,2,0,1:T(8,128)(2,1)S(1)}, u32[]{:S(2)}, u32[]{:S(2)}) collective-permute-start(bf16[2,1,128,256]{3,2,0,1:T(8,128)(2,1)S(1)} %get-tuple-element.95), channel_id=1, source_target_pairs={{0,1},{1,0},{2,3},{3,2},{4,5},{5,4},{6,7},{7,6},{8,9},{9,8},{10,11... | collective-permute-start | bytes 393224 | tf_op jit(solution)/shard_map/ppermute | solution.py:49
  91.7 4.8 %collective-permute-start.14 = (bf16[2,128,256]{2,1,0:T(8,128)(2,1)S(1)}, bf16[2,128,256]{2,1,0:T(8,128)(2,1)S(1)}, u32[]{:S(2)}, u32[]{:S(2)}) collective-permute-start(bf16[2,128,256]{2,1,0:T(8,128)(2,1)S(1)} %get-tuple-element.86), channel_id=1, source_target_pairs={{0,4},{1,5},{2,6},{3,7},{4,0},{5,1},{6,2},{7,3},{8,12},{9,13},{10,... | collective-permute-start | bytes 393224 | tf_op jit(solution)/shard_map/ppermute | solution.py:49
  91.8 4.7 %collective-permute-start.15 = (bf16[2,128,256]{2,1,0:T(8,128)(2,1)S(1)}, bf16[2,128,256]{2,1,0:T(8,128)(2,1)S(1)}, u32[]{:S(2)}, u32[]{:S(2)}) collective-permute-start(bf16[2,128,256]{2,1,0:T(8,128)(2,1)S(1)} %get-tuple-element.87), channel_id=1, source_target_pairs={{0,2},{1,3},{2,0},{3,1},{4,6},{5,7},{6,4},{7,5},{8,10},{9,11},{10,... | collective-permute-start | bytes 393224 | tf_op jit(solution)/shard_map/ppermute | solution.py:49
  96.6 3.5 %collective-permute-start.16 = (bf16[2,2,128,256]{3,2,1,0:T(8,128)(2,1)S(1)}, bf16[2,2,128,256]{3,2,1,0:T(8,128)(2,1)S(1)}, u32[]{:S(2)}, u32[]{:S(2)}) collective-permute-start(bf16[2,2,128,256]{3,2,1,0:T(8,128)(2,1)S(1)} %multiply_convert_fusion.5), channel_id=1, source_target_pairs={{0,1},{1,0},{2,3},{3,2},{4,5},{5,4},{6,7},{7,6},{8,9},{9,8},{10,11... | collective-permute-start | bytes 786440 | tf_op jit(solution)/shard_map/ppermute | solution.py:49
  98.0 8.0 %collective-permute-start.17 = (bf16[4,128,256]{2,1,0:T(8,128)(2,1)S(1)}, bf16[4,128,256]{2,1,0:T(8,128)(2,1)S(1)}, u32[]{:S(2)}, u32[]{:S(2)}) collective-permute-start(bf16[4,128,256]{2,1,0:T(8,128)(2,1)S(1)} %get-tuple-element.80), channel_id=1, source_target_pairs={{0,2},{1,3},{2,0},{3,1},{4,6},{5,7},{6,4},{7,5},{8,10},{9,11},{10,... | collective-permute-start | bytes 786440 | tf_op jit(solution)/shard_map/ppermute | solution.py:49
  98.6 7.6 %collective-permute-start.18 = (bf16[4,128,256]{2,1,0:T(8,128)(2,1)S(1)}, bf16[4,128,256]{2,1,0:T(8,128)(2,1)S(1)}, u32[]{:S(2)}, u32[]{:S(2)}) collective-permute-start(bf16[4,128,256]{2,1,0:T(8,128)(2,1)S(1)} %get-tuple-element.81), channel_id=1, source_target_pairs={{0,4},{1,5},{2,6},{3,7},{4,0},{5,1},{6,2},{7,3},{8,12},{9,13},{10,... | collective-permute-start | bytes 786440 | tf_op jit(solution)/shard_map/ppermute | solution.py:49
  106.4 4.4 %collective-permute-start.19 = (bf16[2,4,128,256]{3,2,1,0:T(8,128)(2,1)S(1)}, bf16[2,4,128,256]{3,2,1,0:T(8,128)(2,1)S(1)}, u32[]{:S(2)}, u32[]{:S(2)}) collective-permute-start(bf16[2,4,128,256]{3,2,1,0:T(8,128)(2,1)S(1)} %multiply_convert_fusion.2), channel_id=1, source_target_pairs={{0,1},{1,0},{2,3},{3,2},{4,5},{5,4},{6,7},{7,6},{8,9},{9,8},{10,11... | collective-permute-start | bytes 1572872 | tf_op jit(solution)/shard_map/ppermute | solution.py:49
  113.6 3.5 %collective-permute-start.20 = (f32[4,128]{1,0:T(4,128)S(1)}, f32[4,128]{1,0:T(4,128)S(1)}, u32[]{:S(2)}, u32[]{:S(2)}) collective-permute-start(f32[4,128]{1,0:T(4,128)S(1)} %slice.256), channel_id=1, source_target_pairs={{0,8},{1,9},{2,10},{3,11},{4,12},{5,13},{6,14},{7,15},{8,0},{9,1},... | collective-permute-start | bytes 6152 | tf_op jit(solution)/shard_map/ppermute | solution.py:49
  130.6 4.9 %collective-permute-start.25 = (f16[2,8,128,256]{3,2,1,0:T(8,128)(2,1)S(1)}, f16[2,8,128,256]{3,2,1,0:T(8,128)(2,1)S(1)}, u32[]{:S(2)}, u32[]{:S(2)}) collective-permute-start(f16[2,8,128,256]{3,2,1,0:T(8,128)(2,1)S(1)} %multiply_convert_fusion), channel_id=1, source_target_pairs={{0,1},{1,0},{2,3},{3,2},{4,5},{5,4},{6,7},{7,6},{8,9},{9,8},{10,11... | collective-permute-start | bytes 3145736 | tf_op jit(solution)/shard_map/ppermute | solution.py:49
  136.0 8.7 %collective-permute-start.26 = (f16[4,128,256]{2,1,0:T(8,128)(2,1)S(1)}, f16[4,128,256]{2,1,0:T(8,128)(2,1)S(1)}, u32[]{:S(2)}, u32[]{:S(2)}) collective-permute-start(f16[4,128,256]{2,1,0:T(8,128)(2,1)S(1)} %multiply_convert_fusion.4), channel_id=1, source_target_pairs={{0,2},{1,3},{2,0},{3,1},{4,6},{5,7},{6,4},{7,5},{8,10},{9,11},{10,... | collective-permute-start | bytes 786440 | tf_op jit(solution)/shard_map/ppermute | solution.py:49
  136.6 8.1 %collective-permute-start.28 = (f16[4,128,256]{2,1,0:T(8,128)(2,1)S(1)}, f16[4,128,256]{2,1,0:T(8,128)(2,1)S(1)}, u32[]{:S(2)}, u32[]{:S(2)}) collective-permute-start(f16[4,128,256]{2,1,0:T(8,128)(2,1)S(1)} %get-tuple-element.72), channel_id=1, source_target_pairs={{0,4},{1,5},{2,6},{3,7},{4,0},{5,1},{6,2},{7,3},{8,12},{9,13},{10,... | collective-permute-start | bytes 786440 | tf_op jit(solution)/shard_map/ppermute | solution.py:49
  144.9 4.4 %collective-permute-start.27 = (f16[2,128,256]{2,1,0:T(8,128)(2,1)S(1)}, f16[2,128,256]{2,1,0:T(8,128)(2,1)S(1)}, u32[]{:S(2)}, u32[]{:S(2)}) collective-permute-start(f16[2,128,256]{2,1,0:T(8,128)(2,1)S(1)} %fusion.16), channel_id=1, source_target_pairs={{0,4},{1,5},{2,6},{3,7},{4,0},{5,1},{6,2},{7,3},{8,12},{9,13},{10,... | collective-permute-start | bytes 393224 | tf_op jit(solution)/shard_map/ppermute | solution.py:49
  145.7 4.2 %collective-permute-start.29 = (f16[2,128,256]{2,1,0:T(8,128)(2,1)S(1)}, f16[2,128,256]{2,1,0:T(8,128)(2,1)S(1)}, u32[]{:S(2)}, u32[]{:S(2)}) collective-permute-start(f16[2,128,256]{2,1,0:T(8,128)(2,1)S(1)} %fusion.14), channel_id=1, source_target_pairs={{0,2},{1,3},{2,0},{3,1},{4,6},{5,7},{6,4},{7,5},{8,10},{9,11},{10,... | collective-permute-start | bytes 393224 | tf_op jit(solution)/shard_map/ppermute | solution.py:49
  150.0 8.5 %collective-permute-start.30 = (f16[2,1,128,256]{3,2,1,0:T(8,128)(2,1)S(1)}, f16[2,1,128,256]{3,2,1,0:T(8,128)(2,1)S(1)}, u32[]{:S(2)}, u32[]{:S(2)}) collective-permute-start(f16[2,1,128,256]{3,2,1,0:T(8,128)(2,1)S(1)} %get-tuple-element.62), channel_id=1, source_target_pairs={{0,8},{1,9},{2,10},{3,11},{4,12},{5,13},{6,14},{7,15},{8,0},{9,1},... | collective-permute-start | bytes 393224 | tf_op jit(solution)/shard_map/ppermute | solution.py:49
  159.3 6.6 %collective-permute-start.31 = (bf16[2,1,128,256]{3,2,1,0:T(8,128)(2,1)S(1)}, bf16[2,1,128,256]{3,2,1,0:T(8,128)(2,1)S(1)}, u32[]{:S(2)}, u32[]{:S(2)}) collective-permute-start(bf16[2,1,128,256]{3,2,1,0:T(8,128)(2,1)S(1)} %get-tuple-element.91), channel_id=1, source_target_pairs={{0,8},{1,9},{2,10},{3,11},{4,12},{5,13},{6,14},{7,15},{8,0},{9,1},... | collective-permute-start | bytes 393224 | tf_op jit(solution)/shard_map/ppermute | solution.py:49
  159.9 10.3 %collective-permute-start.32 = (bf16[2,1,128,256]{3,2,1,0:T(8,128)(2,1)S(1)}, bf16[2,1,128,256]{3,2,1,0:T(8,128)(2,1)S(1)}, u32[]{:S(2)}, u32[]{:S(2)}) collective-permute-start(bf16[2,1,128,256]{3,2,1,0:T(8,128)(2,1)S(1)} %get-tuple-element.91), channel_id=1, source_target_pairs={{0,1},{1,0},{2,3},{3,2},{4,5},{5,4},{6,7},{7,6},{8,9},{9,8},{10,11... | collective-permute-start | bytes 393224 | tf_op jit(solution)/shard_map/ppermute | solution.py:49
  165.9 4.3 %collective-permute-start.33 = (bf16[2,1,128,256]{3,2,0,1:T(8,128)(2,1)S(1)}, bf16[2,1,128,256]{3,2,0,1:T(8,128)(2,1)S(1)}, u32[]{:S(2)}, u32[]{:S(2)}) collective-permute-start(bf16[2,1,128,256]{3,2,0,1:T(8,128)(2,1)S(1)} %bitcast_convert_fusion), channel_id=1, source_target_pairs={{0,1},{1,0},{2,3},{3,2},{4,5},{5,4},{6,7},{7,6},{8,9},{9,8},{10,11... | collective-permute-start | bytes 393224 | tf_op jit(solution)/shard_map/ppermute | solution.py:49
  169.1 5.2 %collective-permute-start.34 = (bf16[2,128,256]{2,1,0:T(8,128)(2,1)S(1)}, bf16[2,128,256]{2,1,0:T(8,128)(2,1)S(1)}, u32[]{:S(2)}, u32[]{:S(2)}) collective-permute-start(bf16[2,128,256]{2,1,0:T(8,128)(2,1)S(1)} %get-tuple-element.82), channel_id=1, source_target_pairs={{0,4},{1,5},{2,6},{3,7},{4,0},{5,1},{6,2},{7,3},{8,12},{9,13},{10,... | collective-permute-start | bytes 393224 | tf_op jit(solution)/shard_map/ppermute | solution.py:49
  169.2 5.2 %collective-permute-start.35 = (bf16[2,128,256]{2,1,0:T(8,128)(2,1)S(1)}, bf16[2,128,256]{2,1,0:T(8,128)(2,1)S(1)}, u32[]{:S(2)}, u32[]{:S(2)}) collective-permute-start(bf16[2,128,256]{2,1,0:T(8,128)(2,1)S(1)} %get-tuple-element.83), channel_id=1, source_target_pairs={{0,2},{1,3},{2,0},{3,1},{4,6},{5,7},{6,4},{7,5},{8,10},{9,11},{10,... | collective-permute-start | bytes 393224 | tf_op jit(solution)/shard_map/ppermute | solution.py:49
  174.4 3.5 %collective-permute-start.36 = (bf16[2,2,128,256]{3,2,1,0:T(8,128)(2,1)S(1)}, bf16[2,2,128,256]{3,2,1,0:T(8,128)(2,1)S(1)}, u32[]{:S(2)}, u32[]{:S(2)}) collective-permute-start(bf16[2,2,128,256]{3,2,1,0:T(8,128)(2,1)S(1)} %multiply_convert_fusion.3), channel_id=1, source_target_pairs={{0,1},{1,0},{2,3},{3,2},{4,5},{5,4},{6,7},{7,6},{8,9},{9,8},{10,11... | collective-permute-start | bytes 786440 | tf_op jit(solution)/shard_map/ppermute | solution.py:49
  175.4 8.0 %collective-permute-start.37 = (bf16[4,128,256]{2,1,0:T(8,128)(2,1)S(1)}, bf16[4,128,256]{2,1,0:T(8,128)(2,1)S(1)}, u32[]{:S(2)}, u32[]{:S(2)}) collective-permute-start(bf16[4,128,256]{2,1,0:T(8,128)(2,1)S(1)} %get-tuple-element.78), channel_id=1, source_target_pairs={{0,2},{1,3},{2,0},{3,1},{4,6},{5,7},{6,4},{7,5},{8,10},{9,11},{10,... | collective-permute-start | bytes 786440 | tf_op jit(solution)/shard_map/ppermute | solution.py:49
  176.4 7.6 %collective-permute-start.38 = (bf16[4,128,256]{2,1,0:T(8,128)(2,1)S(1)}, bf16[4,128,256]{2,1,0:T(8,128)(2,1)S(1)}, u32[]{:S(2)}, u32[]{:S(2)}) collective-permute-start(bf16[4,128,256]{2,1,0:T(8,128)(2,1)S(1)} %get-tuple-element.79), channel_id=1, source_target_pairs={{0,4},{1,5},{2,6},{3,7},{4,0},{5,1},{6,2},{7,3},{8,12},{9,13},{10,... | collective-permute-start | bytes 786440 | tf_op jit(solution)/shard_map/ppermute | solution.py:49
  184.1 6.8 %collective-permute-start.39 = (bf16[2,4,128,256]{3,2,1,0:T(8,128)(2,1)S(1)}, bf16[2,4,128,256]{3,2,1,0:T(8,128)(2,1)S(1)}, u32[]{:S(2)}, u32[]{:S(2)}) collective-permute-start(bf16[2,4,128,256]{3,2,1,0:T(8,128)(2,1)S(1)} %multiply_convert_fusion.1), channel_id=1, source_target_pairs={{0,1},{1,0},{2,3},{3,2},{4,5},{5,4},{6,7},{7,6},{8,9},{9,8},{10,11... | collective-permute-start | bytes 1572872 | tf_op jit(solution)/shard_map/ppermute | solution.py:49
  (13 other events, 144.8 us)

commit v5 on v4

--- a/solution.py
+++ b/solution.py
@@ -12,7 +12,6 @@
 MIB = 1024 * 1024
 HALF_SCALE = 2.0**20
 TILE = 256
-DEPTH = 4
 
 
 def reduce_places(bits, order):
@@ -22,16 +21,16 @@
 
 
 def gather_places(bits):
-    held = fresh = np.zeros((2, 1), np.int32)
-    out, across = [], [fresh ^ 1]
-    for bit in range(bits - 1, 2, -1):
+    held = fresh = np.array([[0, 1 << (bits - 1)]] * 2, np.int32)
+    out, across = [held], []
+    for bit in range(bits - 2, 2, -1):
+        across.append(fresh ^ 1)
+        fresh = held ^ (1 << bit)
+        held = np.concatenate([held, fresh], axis=1)
         out.append(fresh)
-        fresh = held ^ (1 << bit)
-        across.append(fresh ^ 1)
-        held = np.concatenate([held, fresh], axis=1)
     first = held ^ np.array([[4], [2]], np.int32)
     second = np.concatenate([held, first], axis=1) ^ np.array([[2], [4]], np.int32)
-    out += [fresh, *across, first, first ^ 1, second, second ^ 1]
+    out += [*across, fresh ^ 1, first, first ^ 1, second, second ^ 1]
     places = np.concatenate([p.reshape(-1) for p in out])
     streams = np.concatenate([np.repeat(np.arange(2), p.shape[1]) for p in out])
     return places.astype(np.int32), streams.astype(np.int32)
@@ -41,8 +40,8 @@
     return [sum(1 << b for k, b in enumerate(group) if (m >> k) & 1) for m in range(1, 1 << len(group))]
 
 
-def sum_rounds(bits):
-    return [[bit] for bit in range(bits - 1, 2, -1)] + [[1, 2], [0]]
+def sum_rounds(top):
+    return [[bit] for bit in range(top - 1, 2, -1)] + [[1, 2], [0]]
 
 
 def exchange(x, mask, size):
@@ -70,7 +69,7 @@
     return pltpu.with_memory_space_constraint(x, pltpu.HBM)
 
 
-def stage_kernel(pieces, table, w_ref, after_ref, out_ref, token_ref, sems):
+def stage_kernel(pieces, w_ref, after_ref, out_ref, token_ref, sems):
     copies = []
     for k, piece in enumerate(pieces):
         copies.append(pltpu.make_async_copy(w_ref.at[piece], out_ref.at[piece], sems.at[k]))
@@ -81,69 +80,68 @@
         copy.wait()
 
 
-def stage(table, w, after, rows):
+def stage(w, after, rows):
     step = w.shape[0] // 16
     pieces = [pl.ds(k * step, step) for k in range(16)]
     return pl.pallas_call(
         functools.partial(stage_kernel, pieces),
         out_shape=(vmem_out(w.shape, w.dtype), vmem_out((1, rows), jnp.float32)),
-        in_specs=[IN_SMEM, ANYWHERE, ANYWHERE],
+        in_specs=[ANYWHERE, ANYWHERE],
         out_specs=(IN_VMEM, IN_VMEM),
         scratch_shapes=[pltpu.SemaphoreType.DMA((len(pieces),))],
         name="stage",
         **settings(0, w.size * 2, 2 * MIB),
-    )(table, far(w), after)
-
-
-def join_kernel(first, count, offset, table, x_ref, w_ref, after_ref, *rest):
+    )(far(w), after)
+
+
+def join_kernel(first, count, order, x_ref, w_ref, after_ref, *rest):
     out_ref, token_ref, slots, sems = rest[0], rest[1], rest[-2], rest[-1]
     rows = w_ref.shape[1]
     width = slots.shape[3]
-    half = width // 2
-    middle = table.shape[1] // 2
-
-    def copy(q):
-        column = pl.multiple_of(table[0, first + q] * rows + offset, 128)
-        return pltpu.make_async_copy(w_ref.at[:, :, pl.ds(column, width)], slots.at[q], sems.at[q])
-
-    for q in range(min(DEPTH, count)):
-        copy(q).start()
+
+    def copy(q, s):
+        column = pl.multiple_of(order[s, first + q], 128)
+        at = 2 * q + s
+        return pltpu.make_async_copy(w_ref.at[:, :, pl.ds(column, width)], slots.at[at], sems.at[at])
+
+    for q in range(count):
+        for s in range(2):
+            copy(q, s).start()
     token_ref[...] = jnp.ones_like(token_ref)
     if len(rest) == 5:
         rest[2][...] = x_ref[...].T
 
     @pl.loop(0, count)
     def _(q):
-        copy(q).wait()
-
-        @pl.when(q + DEPTH < count)
-        def _():
-            copy(q + DEPTH).start()
-
-        total = jnp.dot(x_ref[:, :rows], slots[q, 0], preferred_element_type=jnp.float32)
-        for j in (1, 2):
-            total += jnp.dot(
-                x_ref[:, j * rows : (j + 1) * rows], slots[q, j], preferred_element_type=jnp.float32
-            )
-        out_ref[0, q] = total[:, :half]
-        out_ref[1, table[1, first + q] + (q // middle) * middle] = total[:, half:]
-
-
-def join(table, first, count, offset, width, x, w_fc, after, turn):
+        for s in range(2):
+            copy(q, s).wait()
+            total = jnp.dot(x_ref[:, :rows], slots[2 * q + s, 0], preferred_element_type=jnp.float32)
+            for j in (1, 2):
+                total += jnp.dot(
+                    x_ref[:, j * rows : (j + 1) * rows], slots[2 * q + s, j], preferred_element_type=jnp.float32
+                )
+            out_ref[s, q] = total
+
+
+def join(order, first, count, x, w_fc, after, turn):
     tokens = x.shape[0]
     rows = w_fc.shape[1]
-    shapes = [vmem_out((2, count, tokens, width // 2), jnp.float32), vmem_out((1, width // 2), jnp.float32)]
+    width = rows // 2
+    shapes = [vmem_out((2, count, tokens, width), jnp.float32), vmem_out((1, width), jnp.float32)]
     if turn:
         shapes.append(jax.ShapeDtypeStruct(x.shape[::-1], x.dtype))
     return pl.pallas_call(
-        functools.partial(join_kernel, first, count, offset),
+        functools.partial(join_kernel, first, count),
         out_shape=tuple(shapes),
         in_specs=[IN_SMEM, IN_VMEM, ANYWHERE, ANYWHERE],
         out_specs=(IN_VMEM,) * len(shapes),
-        scratch_shapes=[pltpu.VMEM((count, 3, rows, width), jnp.bfloat16), pltpu.SemaphoreType.DMA((count,))],
+        scratch_shapes=[
+            pltpu.VMEM((2 * count, 3, rows, width), jnp.bfloat16),
+            pltpu.SemaphoreType.DMA((2 * count,)),
+        ],
         name="join",
-        **settings(6 * tokens * rows * width * count, 6 * rows * width * count, 20 * MIB),
-    )(table, near(x), far(w_fc), after)
+        **settings(6 * tokens * rows * rows * count, 6 * rows * rows * count, 20 * MIB),
+    )(order, near(x), far(w_fc), after)
 
 
 def columns_of(rows_of_stats):
@@ -201,56 +199,57 @@
     )(starts, near(w_lm), near(before), near(targets), *[near(p) for p in pieces])
 
 
-def back_products(first, count, table, d_ref, w_ref, out_ref):
+def back_products(first, count, order, d_ref, w_ref, out_ref):
     width = out_ref.shape[3]
 
     @pl.loop(0, count)
     def _(q):
-        row = pl.multiple_of(table[0, first + q] * (2 * width), 128)
-        for stream, at in ((0, q), (1, table[1, first + q])):
-            out_ref[stream, at] = lax.dot_general(
+        for s in range(2):
+            row = pl.multiple_of(order[s, first + q], 128)
+            out_ref[s, q] = lax.dot_general(
                 d_ref[...],
-                w_ref[pl.ds(row + stream * width, width), :],
+                w_ref[pl.ds(row, width), :],
                 (((1,), (1,)), ((), ())),
                 preferred_element_type=jnp.float32,
             )
 
 
-def back_first_kernel(first, count, table, logits_ref, stats_ref, targets_ref, w_ref, out_ref, d_ref):
+def back_first_kernel(first, count, order, starts, logits_ref, stats_ref, targets_ref, w_ref, out_ref, d_ref):
     logits = logits_ref[...]
     tokens, share = logits.shape
     log_total = columns_of(stats_ref[...])[:, :1]
-    hit = jnp.where(target_mask(table[0, 0], targets_ref, share), 1.0, 0.0)
+    hit = jnp.where(target_mask(starts[starts.shape[0] - 1], targets_ref, share), 1.0, 0.0)
     d_ref[...] = ((jnp.exp(logits - log_total) - hit) / tokens).astype(d_ref.dtype)
-    back_products(first, count, table, d_ref, w_ref, out_ref)
-
-
-def back_first(table, first, count, logits, stats, targets, w_lm, width):
+    back_products(first, count, order, d_ref, w_ref, out_ref)
+
+
+def back_first(order, starts, first, count, logits, stats, targets, w_lm, width):
     tokens, share = logits.shape
     return pl.pallas_call(
         functools.partial(back_first_kernel, first, count),
         out_shape=(vmem_out((2, count, tokens, width), jnp.float32), vmem_out((tokens, share), jnp.bfloat16)),
-        in_specs=[IN_SMEM] + [IN_VMEM] * 4,
+        in_specs=[IN_SMEM] * 2 + [IN_VMEM] * 4,
         out_specs=(IN_VMEM, IN_VMEM),
         name="back_first",
         **settings(4 * tokens * width * share * count, 8 * tokens * width * count, 6 * MIB),
-    )(table, near(logits), near(stats), near(targets), near(w_lm))
-
-
-def back_rest_kernel(first, count, table, d_ref, w_ref, out_ref):
-    back_products(first, count, table, d_ref, w_ref, out_ref)
-
-
-def back_rest(table, first, count, dlogits, w_lm, width):
+    )(order, starts, near(logits), near(stats), near(targets), near(w_lm))
+
+
+def back_rest_kernel(first, count, order, d_ref, w_ref, after_ref, out_ref, token_ref):
+    token_ref[...] = jnp.ones_like(token_ref)
+    back_products(first, count, order, d_ref, w_ref, out_ref)
+
+
+def back_rest(order, first, count, dlogits, w_lm, width, after):
     tokens, share = dlogits.shape
     return pl.pallas_call(
         functools.partial(back_rest_kernel, first, count),
-        out_shape=vmem_out((2, count, tokens, width), jnp.float32),
-        in_specs=[IN_SMEM, IN_VMEM, IN_VMEM],
-        out_specs=IN_VMEM,
+        out_shape=(vmem_out((2, count, tokens, width), jnp.float32), vmem_out((1, width), jnp.float32)),
+        in_specs=[IN_SMEM, IN_VMEM, IN_VMEM, ANYWHERE],
+        out_specs=(IN_VMEM, IN_VMEM),
         name="back_rest",
         **settings(4 * tokens * width * share * count, 8 * tokens * width * count, 6 * MIB),
-    )(table, near(dlogits), near(w_lm))
+    )(order, near(dlogits), near(w_lm), after)
 
 
 def head_grad_kernel(first, counts, aliased, starts, d_ref, after_ref, *rest):
@@ -271,9 +270,12 @@
         def _(q):
             turned = piece_ref[q].T
             for column in range(0, share, TILE):
-                slots[offset + q, :, column : column + TILE] = jnp.dot(
-                    turned, d_ref[:, column : column + TILE], preferred_element_type=jnp.float32
-                ).astype(slots.dtype)
+                for row in range(0, width, TILE):
+                    slots[offset + q, row : row + TILE, column : column + TILE] = jnp.dot(
+                        turned[row : row + TILE],
+                        d_ref[:, column : column + TILE],
+                        preferred_element_type=jnp.float32,
+                    ).astype(slots.dtype)
             copy(offset + q).start()
 
         offset += count
@@ -299,7 +301,7 @@
         scratch_shapes=[pltpu.VMEM((blocks, width, share), jnp.bfloat16), pltpu.SemaphoreType.DMA((blocks,))],
         input_output_aliases={3: 0} if extra else {},
         name="head_grad",
-        **settings(2 * tokens * width * share * blocks, 2 * width * share * blocks, 14 * MIB),
+        **settings(1024, 1024, 14 * MIB),
     )(starts, near(dlogits), after, *extra, *[near(p) for p in pieces])
 
 
@@ -354,16 +356,12 @@
     )(starts, near(x_turned), *extra, *[near(p) for p in pieces])
 
 
-def cut(total, table, rows, offset, width):
+def cut(total, order, width):
     tokens = total.shape[0]
-    blocks = jnp.take(total.reshape(tokens, -1, rows).transpose(1, 0, 2), table[0], axis=0)
-    count = table.shape[1] // 2
-    blocks = blocks[:, :, offset : offset + width].reshape(2, count, tokens, 2, width // 2)
-    out = []
-    for side in range(2):
-        second = jnp.take(blocks[side, :, :, 1], jnp.argsort(table[1, side * count : (side + 1) * count]), axis=0)
-        out.append(jnp.stack([blocks[side, :, :, 0], second]))
-    return out
+    blocks = total.reshape(tokens, -1, width).transpose(1, 0, 2)
+    blocks = jnp.take(blocks, order // width, axis=0)
+    quarter = order.shape[1] // 4
+    return blocks[:, :quarter], blocks[:, quarter : 2 * quarter], blocks[:, 2 * quarter :]
 
 
 def whole(pieces, starts):
@@ -400,44 +398,48 @@
     return x if token is None else (x.astype(jnp.float32) * token).astype(x.dtype)
 
 
-def reduce_halves(low, high, bits, size, pack, unpack, work):
-    total = low + unpack(exchange(pack(high), 1, size))
-    streams = [total[0], total[1]]
-    for k, order in ((1, (1, 2)), (2, (2, 1))):
-        half = streams[0].shape[0] // 2
-        sent = [t[half:] for t in streams]
-        got = [exchange(pack(t), 1 << bit, size) for t, bit in zip(sent, order)]
-        token = work(k, sent[0])
-        streams = [t[:half] + with_token(unpack(g), token) for t, g in zip(streams, got)]
-    total = jnp.stack(streams)
-    for bit in range(3, bits):
+def reduce_halves(low, high, rest, bits, size, pack, unpack, work):
+    got = unpack(exchange(pack(high), 1, size))
+    quarter = low.shape[1]
+    sent = low + got[:, quarter:]
+    passed = [exchange(pack(sent[0]), 2, size), exchange(pack(sent[1]), 4, size)]
+    remaining, token = rest(sent)
+    token = work(1, remaining, token)
+    total = remaining + got[:, :quarter]
+    total = total + with_token(unpack(jnp.stack(passed)), token)
+    half = quarter // 2
+    sent = total[:, half:]
+    passed = [exchange(pack(sent[0]), 4, size), exchange(pack(sent[1]), 2, size)]
+    token = work(2, sent, None)
+    total = total[:, :half] + with_token(unpack(jnp.stack(passed)), token)
+    for bit in range(3, bits - 1):
         half = total.shape[1] // 2
-        sent = total[:, half:]
-        got = exchange(pack(sent), 1 << bit, size)
-        token = work(bit, sent)
-        total = total[:, :half] + with_token(unpack(got), token)
-    return [total[0, 0], total[1, 0]]
-
-
-def gather(own, bits, size, work):
+        total = total[:, :half] + unpack(exchange(pack(total[:, half:]), 1 << bit, size))
+    passed = exchange(pack(total), 1 << (bits - 1), size)
+    token = work(bits - 1, total, None)
+    return total + with_token(unpack(jnp.stack([passed[:, 1], passed[:, 0]], axis=1)), token)
+
+
+def gather(held, bits, size, work):
     def flat(x):
         return x.reshape((-1,) + x.shape[2:])
 
-    held = fresh = jnp.stack(own)[:, None]
-    across = [exchange(fresh, 1, size)]
-    for bit in range(bits - 1, 2, -1):
+    fresh = held
+    across = []
+    for bit in range(bits - 2, 2, -1):
         arrived = exchange(held, 1 << bit, size)
+        across.append(exchange(fresh, 1, size))
         token = work([flat(fresh)], False)
         fresh = with_token(arrived, token)
-        across.append(exchange(fresh, 1, size))
         held = jnp.concatenate([held, fresh], axis=1)
     first = [exchange(held[0], 4, size), exchange(held[1], 2, size)]
-    token = work([flat(fresh)] + [flat(a) for a in across], False)
+    across.append(exchange(fresh, 1, size))
+    token = work([flat(fresh)], False)
     first = with_token(jnp.stack(first), token)
-    across = exchange(first, 1, size)
+    across += [first, exchange(first, 1, size)]
     both = jnp.concatenate([held, first], axis=1)
     second = [exchange(both[0], 2, size), exchange(both[1], 4, size)]
-    token = work([flat(first), flat(across)], False)
+    token = work([flat(a) for a in across], False)
     second = with_token(jnp.stack(second), token)
     across = exchange(second, 1, size)
     work([flat(second)], False)
@@ -452,11 +454,10 @@
     half = rows // 2
     bits = size.bit_length() - 1
     count = size // 2
-    first_order = reduce_places(bits, [1, 2] + list(range(3, bits)))
-    second_order = reduce_places(bits, [2, 1] + list(range(3, bits)))
-    where = [second_order.index(p) for p in first_order]
-    chunks = jnp.asarray(np.array(first_order + [p + 1 for p in first_order], np.int32)) ^ me
-    table = jnp.stack([chunks, jnp.asarray(np.array(where + where, np.int32))])
+    last = list(range(3, bits))
+    orders = np.array([reduce_places(bits, [1, 2] + last), reduce_places(bits, [2, 1] + last)], np.int32)
+    orders = np.concatenate([orders, orders + 1], axis=1)
+    order = (jnp.asarray(orders) ^ me) * rows + jnp.asarray(np.array([[0], [half]], np.int32))
     places, streams = gather_places(bits)
     starts = jnp.concatenate([(jnp.asarray(places) ^ me) * rows + jnp.asarray(streams * half), me[None]])
     kernels = half % TILE == 0
@@ -468,29 +469,32 @@
     x = lax.all_to_all(sent, "section", split_axis=0, concat_axis=0, tiled=True).reshape(tokens, 3 * rows)
 
     held = {"logits": jnp.zeros((tokens, share), jnp.float32), "grad_lm": None, "grad_fc": None}
-    if not kernels:
+    quarter = size // 4
+    if kernels:
+        high, _, held["x"] = join(order, count, count, x, w_fc, sent, True)
+        low, _ = join(order, quarter, quarter, x, w_fc, sent, False)
+    else:
         total = jnp.dot(x, w_fc.reshape(3 * rows, full_width), preferred_element_type=jnp.float32)
-
-    if kernels:
-        high, _, held["x"] = join(table, count, count, 0, rows, x, w_fc, sent, True)
-        low, _ = join(table, 0, count, 0, rows, x, w_fc, sent, False)
-    else:
-        low, high = cut(total, table, rows, 0, rows)
-
-    def bring_head(k, after):
+        remaining, low, high = cut(total, order, half)
+
+    def join_rest(after):
+        return join(order, 0, quarter, x, w_fc, after, False) if kernels else (remaining, None)
+
+    def bring_head(k, after, token):
         if kernels and k == 1:
-            held["lm"], token = stage(table, w_lm, after, half)
-            return token
-
-    joined = jnp.concatenate(
-        reduce_halves(low, high, bits, size, lambda x: x, lambda x: x, bring_head), axis=1
-    )
-
-    squares = jnp.sum(joined * joined, axis=1)
-    for group in sum_rounds(bits):
+            held["lm"], token = stage(w_lm, after, half)
+        return token
+
+    joined = reduce_halves(low, high, join_rest, bits, size, lambda x: x, lambda x: x, bring_head)
+
+    squares = jnp.sum(joined * joined, axis=(0, 3))
+    squares = squares[0] + squares[1]
+    for group in sum_rounds(bits - 1):
         squares = tree_sum(contributions(squares, group, size))
     inv_rms = lax.rsqrt(squares / full_width + epsilon)[:, None]
-    normed = (joined * inv_rms * gain[None, :]).astype(jnp.bfloat16)
+    gains = gain.reshape(2, 1, 1, half)
+    gains = jnp.concatenate([gains, exchange(gain, 1 << (bits - 1), size).reshape(2, 1, 1, half)], axis=1)
+    normed = (joined * inv_rms * gains).astype(jnp.bfloat16)
 
     all_normed, all_dfused = [], []
 
@@ -503,7 +507,7 @@
                 held["stats"] = extra
             return extra
 
-    gather([normed[:, :half], normed[:, half:]], bits, size, add_logits)
+    gather(normed, bits, size, add_logits)
     logits = held["logits"]
     if kernels:
         stats = held["stats"][:4]
@@ -531,8 +535,8 @@
 
     if kernels:
         spread = jnp.broadcast_to(log_total[None], (8, tokens))
-        high, dlogits = back_first(table, count, count, logits, spread, target_row, held["lm"], half)
-        low = back_rest(table, 0, count, dlogits, held["lm"], half)
+        high, dlogits = back_first(order, starts, count, count, logits, spread, target_row, held["lm"], half)
+        low, _ = back_rest(order, quarter, quarter, dlogits, held["lm"], half, high)
     else:
         dlogits = (
             (jnp.exp(logits - log_total[:, None]) - is_target.astype(jnp.float32)) / tokens
@@ -540,17 +544,20 @@
         total = lax.dot_general(
             dlogits, w_lm, (((1,), (1,)), ((), ())), preferred_element_type=jnp.float32
         )
-        low, high = cut(total, table, rows, 0, rows)
-
-    def fill_grad_lm(k, after):
-        if kernels and k in (1, bits - 1):
-            middle = len(all_normed) - 2
+        left, low, high = cut(total, order, half)
+
+    def back_last(after):
+        return back_rest(order, 0, quarter, dlogits, held["lm"], half, after) if kernels else (left, None)
+
+    def fill_grad_lm(k, after, token):
+        if kernels and k != 2:
+            middle = len(all_normed) - 3
             pieces = all_normed[:middle] if k == 1 else all_normed[middle:]
             first = 0 if k == 1 else sum(p.shape[0] for p in all_normed[:middle])
             held["grad_lm"], token = head_grad(
                 starts, first, pieces, dlogits, full_width, after, held["grad_lm"]
             )
-            return token
+        return token
 
     scale = HALF_SCALE * (tokens / 128)
 
@@ -560,9 +567,7 @@
     def unpack_half(x):
         return x.astype(jnp.float32) * (1.0 / scale)
 
-    dnormed = jnp.concatenate(
-        reduce_halves(low, high, bits, size, pack_half, unpack_half, fill_grad_lm), axis=1
-    )
+    dnormed = reduce_halves(low, high, back_last, bits, size, pack_half, unpack_half, fill_grad_lm)
     if kernels:
         grad_lm = held["grad_lm"]
     else:
@@ -570,9 +575,9 @@
             normed_all, dlogits, (((0,), (0,)), ((), ())), preferred_element_type=jnp.float32
         ).astype(jnp.bfloat16)
 
-    grad_gain = jnp.sum(dnormed * joined * inv_rms, axis=0)
+    grad_gain = jnp.sum(dnormed[:, 0] * joined[:, 0] * inv_rms, axis=1).reshape(rows)
     dfused = (
-        inv_rms * (dnormed * gain[None, :]) - joined * (inv_rms * inv_rms * inv_rms * rowdot / full_width)
+        inv_rms * (dnormed * gains) - joined * (inv_rms * inv_rms * inv_rms * rowdot / full_width)
     ).astype(jnp.bfloat16)
 
     def fill_grad_fc(pieces, last):
@@ -582,7 +587,7 @@
             held["grad_fc"], token = join_grad(starts, first, pieces, held["x"], full_width, held["grad_fc"])
             return token
 
-    gather([dfused[:, :half], dfused[:, half:]], bits, size, fill_grad_fc)
+    gather(dfused, bits, size, fill_grad_fc)
     if kernels:
         grad_fc = held["grad_fc"]
     else:

time: 196 us -> 189 us (0.964)
  starting transfers between devices: 53.6 us -> 45.3 us
  Pallas kernels: 72.5 us -> 76.3 us
    ppermute x40 -> x36, starting transfers between devices: 46.2 us -> 37.9 us  [exchange(): return lax.ppermute(x, 'section', [(i, i ^ mask) for i in range(size)])]
    pallas_call x2 -> x3, Pallas kernels: 12.2 us -> 17.3 us  [join(): pl.pallas_call(functools.partial(join_kernel, first, count), out_shape=tu...]
    ppermute x40 -> x36, waiting for transfers between devices: 50.1 us -> 48 us  [exchange(): return lax.ppermute(x, 'section', [(i, i ^ mask) for i in range(size)])]
    pallas_call x5 -> x4, Pallas kernels: 19.9 us -> 18.4 us  [join_grad(): pl.pallas_call(functools.partial(join_grad_kernel, first, counts, len(ext...]
    pallas_call x1 -> x2, Pallas kernels: 4.48 us -> 5.67 us  [back_rest(): pl.pallas_call(functools.partial(back_rest_kernel, first, count), out_sha...]
    pallas_call x5 -> x4, Pallas kernels: 11.4 us -> 10.8 us  [head(): pl.pallas_call(functools.partial(head_kernel, first, counts, last), out_s...]
  transfers between devices with their start and end apart: 41 -> 37, of which waited for: 26 -> 19; matrix products, arithmetic and copies ran while one was open for 1% -> 2% of each run, Pallas kernels for 27% -> 30%
where the time goes in v5:
time: 189 us
  Pallas kernels  76.3 us (40%)
  waiting for transfers between devices  59.2 us (31%)
  starting transfers between devices  45.3 us (24%)
  other arithmetic  6.39 us (3%)
    ppermute x36, waiting for transfers between devices, exchange(): return lax.ppermute(x, 'section', [(i, i ^ mask) for i in range(size)])  48 us
    ppermute x36, starting transfers between devices, exchange(): return lax.ppermute(x, 'section', [(i, i ^ mask) for i in range(size)])  37.9 us
    pallas_call x4, Pallas kernels, join_grad(): pl.pallas_call(functools.partial(join_grad_kernel, first, counts, len(ext...  18.4 us
    pallas_call x3, Pallas kernels, join(): pl.pallas_call(functools.partial(join_kernel, first, count), out_shape=tu...  17.3 us
    pallas_call x2, Pallas kernels, head_grad(): pl.pallas_call(functools.partial(head_grad_kernel, first, counts, len(ext...  13.4 us
    all_to_all x1, waiting for transfers between devices, on_device(): lax.all_to_all(sent, 'section', split_axis=0, concat_axis=0, tiled=True)  11.1 us
    pallas_call x4, Pallas kernels, head(): pl.pallas_call(functools.partial(head_kernel, first, counts, last), out_s...  10.8 us
    all_to_all x1, starting transfers between devices, on_device(): lax.all_to_all(sent, 'section', split_axis=0, concat_axis=0, tiled=True)  7.35 us
  transfers between devices with their start and end apart: 37, of which 19 were waited for; matrix products, arithmetic and copies ran while one was open for 2% of the time, Pallas kernels for 30%

profile of v5, /device:TPU:1, one launch (start us, length us, event | category | flops | bytes accessed | tf_op | source)
XLA Modules:
  0.0 189.2 jit_solution(15565719452878440515)
XLA Ops:
  0.6 1.8 maximum_bitcast_fusion.after_ref
  2.4 7.3 %all-to-all-start = ((bf16[16,8,1536]{2,1,0:T(8,128)(2,1)}), bf16[16,8,1536]{2,1,0:T(8,128)(2,1)S(1)}, u32[]{:S(2)}, u32[]{:S(2)}) async-start(bf16[16,8,1536]{2,1,0:T(8,128)(2,1)} %maximum_bitcast_fusion.after_ref), calls=%async_computation | async-start | bytes 786432 | tf_op jit(solution)/shard_map/all_to_all | solution.py:469
  10.5 11.1 %all-to-all-done = bf16[16,8,1536]{2,1,0:T(8,128)(2,1)S(1)} async-done(((bf16[16,8,1536]{2,1,0:T(8,128)(2,1)}), bf16[16,8,1536]{2,1,0:T(8,128)(2,1)S(1)}, u32[]{:S(2)}, u32[]{:S(2)}) %all-to-all-start) | async-done | bytes 393248 | tf_op jit(solution)/shard_map/all_to_all | solution.py:469
  21.7 7.7 %join.4 = (f32[2,8,128,256]{3,2,1,0:T(8,128)S(1)}, f32[1,256]{1,0:T(1,128)}, bf16[1536,128]{1,0:T(8,128)(2,1)S(1)}) custom-call(s32[2,16]{1,0:T(2,128)S(1)} %multiply_add_fusion.1.order, bf16[128,1536]{1,0:T(8,128)(2,1)S(1)} %bitcast.133, bf16[3,512,8192]{2,1,0:T(8,128)(2,1)} %w_ref.6, bf16[16,8,1536]{2,1,0:T(8,128)(2,1)} %maximum_bitcast_fusion.after_ref), custom_call_target="tpu_custom_call" | custom-call | flops 1610612736 | bytes 12582912 | tf_op jit(solution)/shard_map/join/pallas_call | solution.py:133
  29.9 4.8 %join.3 = (f32[2,4,128,256]{3,2,1,0:T(8,128)S(1)}, f32[1,256]{1,0:T(1,128)}) custom-call(s32[2,16]{1,0:T(2,128)S(1)} %multiply_add_fusion.1.order, bf16[128,1536]{1,0:T(8,128)(2,1)S(1)} %bitcast.134, bf16[3,512,8192]{2,1,0:T(8,128)(2,1)} %w_ref.6, bf16[16,8,1536]{2,1,0:T(8,128)(2,1)} %maximum_bitcast_fusion.after_ref), custom_call_target="tpu_custom_call" | custom-call | flops 805306368 | bytes 6291456 | tf_op jit(solution)/shard_map/join/pallas_call | solution.py:133
  36.3 4.8 %join.5 = (f32[2,4,128,256]{3,2,1,0:T(8,128)S(1)}, f32[1,256]{1,0:T(1,128)}) custom-call(s32[2,16]{1,0:T(2,128)S(1)} %multiply_add_fusion.1.order, bf16[128,1536]{1,0:T(8,128)(2,1)S(1)} %bitcast.135, bf16[3,512,8192]{2,1,0:T(8,128)(2,1)} %w_ref.6, f32[2,4,128,256]{3,2,1,0:T(8,128)S(1)} %slice_add_fusion.3.after_ref), custom_call_target="tpu_custom_call" | custom-call | flops 805306368 | bytes 6291456 | tf_op jit(solution)/shard_map/join/pallas_call | solution.py:133
  41.1 5.9 %stage.1 = (bf16[8192,1024]{1,0:T(8,128)(2,1)S(1)}, f32[1,256]{1,0:T(1,128)S(1)}) custom-call(bf16[8192,1024]{1,0:T(8,128)(2,1)} %w_ref.7, f32[2,4,128,256]{3,2,1,0:T(8,128)S(1)} %get-tuple-element.33.after_ref), custom_call_target="tpu_custom_call" | custom-call | bytes 16777216 | tf_op jit(solution)/shard_map/stage/pallas_call | solution.py:86
  50.1 5.6 %collective-permute-done.3 = f32[2,128,256]{2,1,0:T(8,128)S(1)} collective-permute-done((f32[2,128,256]{2,1,0:T(8,128)S(1)}, f32[2,128,256]{2,1,0:T(8,128)S(1)}, u32[]{:S(2)}, u32[]{:S(2)}) %collective-permute-start.3) | collective-permute-done | bytes 262176 | tf_op jit(solution)/shard_map/ppermute | solution.py:48
  55.8 1.9 collective-permute-start.5
  58.2 22.7 %collective-permute-done.5 = f32[2,2,128,256]{3,2,1,0:T(8,128)S(1)} collective-permute-done((f32[2,2,128,256]{3,2,1,0:T(8,128)S(1)}, f32[2,2,128,256]{3,2,1,0:T(8,128)S(1)}, u32[]{:S(2)}, u32[]{:S(2)}) %collective-permute-start.5) | collective-permute-done | bytes 524320 | tf_op jit(solution)/shard_map/ppermute | solution.py:48
  85.7 3.2 %collective-permute-start.9 = (f32[128]{0:T(128)S(1)}, f32[128]{0:T(128)S(1)}, u32[]{:S(2)}, u32[]{:S(2)}) collective-permute-start(f32[128]{0:T(128)S(1)} %add_add_fusion.3), channel_id=1, source_target_pairs={{0,1},{1,0},{2,3},{3,2},{4,5},{5,4},{6,7},{7,6},{8,9},{9,8},{10,11... | collective-permute-start | bytes 1544 | tf_op jit(solution)/shard_map/ppermute | solution.py:48
  98.2 3.4 %head.5 = (f32[128,1024]{1,0:T(8,128)S(1)}, f32[1,256]{1,0:T(1,128)S(1)}) custom-call(s32[33]{0:T(128)S(1)} %pad_add_fusion.starts, bf16[8192,1024]{1,0:T(8,128)(2,1)S(1)} %get-tuple-element.34.w_ref, f32[128,1024]{1,0:T(8,128)S(1)} %get-tuple-element.36.before_ref, s32[1,128]{1,0:T(1,128)S(1)} %bitcast.147, bf16[4,128,256]{2,1,0:T(8,128)(2,1)S(1)} %bitcast.141, ...), custom_call_target="tpu_custom_call" | custom-call | flops 805306368 | bytes 1048576 | tf_op jit(solution)/shard_map/head/pallas_call | solution.py:192
  101.6 2.5 %collective-permute-done.15 = bf16[4,128,256]{2,1,0:T(8,128)(2,1)S(1)} collective-permute-done((bf16[4,128,256]{2,1,0:T(8,128)(2,1)S(1)}, bf16[4,128,256]{2,1,0:T(8,128)(2,1)S(1)}, u32[]{:S(2)}, u32[]{:S(2)}) %collective-permute-start.15) | collective-permute-done | bytes 262176 | tf_op jit(solution)/shard_map/ppermute | solution.py:48
  106.2 3.0 %head.6 = (f32[128,1024]{1,0:T(8,128)S(1)}, f32[1,256]{1,0:T(1,128)}) custom-call(s32[33]{0:T(128)S(1)} %pad_add_fusion.starts, bf16[8192,1024]{1,0:T(8,128)(2,1)S(1)} %get-tuple-element.34.w_ref, f32[128,1024]{1,0:T(8,128)S(1)} %get-tuple-element.38.before_ref, s32[1,128]{1,0:T(1,128)S(1)} %bitcast.148, bf16[8,128,256]{2,1,0:T(8,128)(2,1)S(1)} %fusion.3.rest_0_.rest_2_), custom_call_target="tpu_custom_call" | custom-call | flops 536870912 | bytes 1048576 | tf_op jit(solution)/shard_map/head/pallas_call | solution.py:192
  109.2 2.8 %head.7 = (f32[128,1024]{1,0:T(8,128)S(1)}, f32[8,128]{1,0:T(8,128)S(1)}) custom-call(s32[33]{0:T(128)S(1)} %pad_add_fusion.starts, bf16[8192,1024]{1,0:T(8,128)(2,1)S(1)} %get-tuple-element.34.w_ref, f32[128,1024]{1,0:T(8,128)S(1)} %get-tuple-element.40.before_ref, s32[1,128]{1,0:T(1,128)S(1)} %bitcast.149, bf16[8,128,256]{2,1,0:T(8,128)(2,1)S(1)} %bitcast.137), custom_call_target="tpu_custom_call" | custom-call | flops 536870912 | bytes 1048576 | tf_op jit(solution)/shard_map/head/pallas_call | solution.py:192
  112.1 2.5 %collective-permute-start.18 = (f32[4,128]{1,0:T(4,128)S(1)}, f32[4,128]{1,0:T(4,128)S(1)}, u32[]{:S(2)}, u32[]{:S(2)}) collective-permute-start(f32[4,128]{1,0:T(4,128)S(1)} %slice.203), channel_id=1, source_target_pairs={{0,8},{1,9},{2,10},{3,11},{4,12},{5,13},{6,14},{7,15},{8,0},{9,1},... | collective-permute-start | bytes 6152 | tf_op jit(solution)/shard_map/ppermute | solution.py:48
  115.6 1.6 collective-permute-start.21
  120.1 2.7 %collective-permute-start.22 = (f32[4,128]{1,0:T(4,128)S(1)}, f32[4,128]{1,0:T(4,128)S(1)}, u32[]{:S(2)}, u32[]{:S(2)}) collective-permute-start(f32[4,128]{1,0:T(4,128)S(1)} %pad_maximum_fusion.3), channel_id=1, source_target_pairs={{0,1},{1,0},{2,3},{3,2},{4,5},{5,4},{6,7},{7,6},{8,9},{9,8},{10,11... | collective-permute-start | bytes 6152 | tf_op jit(solution)/shard_map/ppermute | solution.py:48
  123.7 4.7 %back_first.1 = (f32[2,8,128,256]{3,2,1,0:T(8,128)S(1)}, bf16[128,1024]{1,0:T(8,128)(2,1)S(1)}) custom-call(s32[2,16]{1,0:T(2,128)S(1)} %multiply_add_fusion.1.order, s32[33]{0:T(128)S(1)} %pad_add_fusion.starts, f32[128,1024]{1,0:T(8,128)S(1)} %get-tuple-element.43.logits_ref, f32[8,128]{1,0:T(8,128)S(1)} %broadcast_in_dim.11.stats_ref, ...), custom_call_target="tpu_custom_call" | custom-call | flops 1073741824 | bytes 2097152 | tf_op jit(solution)/shard_map/back_first/pallas_call | solution.py:228
  129.1 2.8 %back_rest.2 = (f32[2,4,128,256]{3,2,1,0:T(8,128)S(1)}, f32[1,256]{1,0:T(1,128)}) custom-call(s32[2,16]{1,0:T(2,128)S(1)} %multiply_add_fusion.1.order, bf16[128,1024]{1,0:T(8,128)(2,1)S(1)} %get-tuple-element.44.d_ref, bf16[8192,1024]{1,0:T(8,128)(2,1)S(1)} %get-tuple-element.34.w_ref, f32[2,8,128,256]{3,2,1,0:T(8,128)S(1)} %get-tuple-element.45.after_ref), custom_call_target="tpu_custom_call" | custom-call | flops 536870912 | bytes 1048576 | tf_op jit(solution)/shard_map/back_rest/pallas_call | solution.py:245
  134.3 2.8 %back_rest.3 = (f32[2,4,128,256]{3,2,1,0:T(8,128)S(1)}, f32[1,256]{1,0:T(1,128)}) custom-call(s32[2,16]{1,0:T(2,128)S(1)} %multiply_add_fusion.1.order, bf16[128,1024]{1,0:T(8,128)(2,1)S(1)} %get-tuple-element.44.d_ref, bf16[8192,1024]{1,0:T(8,128)(2,1)S(1)} %get-tuple-element.34.w_ref, f32[2,4,128,256]{3,2,1,0:T(8,128)S(1)} %slice_add_fusion.1.after_ref), custom_call_target="tpu_custom_call" | custom-call | flops 536870912 | bytes 1048576 | tf_op jit(solution)/shard_map/back_rest/pallas_call | solution.py:245
  137.2 5.3 %head_grad.2 = (bf16[8192,1024]{1,0:T(8,128)(2,1)}, f32[1,256]{1,0:T(1,128)S(1)}) custom-call(s32[33]{0:T(128)S(1)} %pad_add_fusion.starts, bf16[128,1024]{1,0:T(8,128)(2,1)S(1)} %get-tuple-element.44.d_ref, f32[2,4,128,256]{3,2,1,0:T(8,128)S(1)} %get-tuple-element.47.after_ref, bf16[4,128,256]{2,1,0:T(8,128)(2,1)S(1)} %bitcast.132, ...), custom_call_target="tpu_custom_call" | custom-call | flops 1024 | bytes 1024 | tf_op jit(solution)/shard_map/head_grad/pallas_call | solution.py:293
  144.0 3.2 %collective-permute-done.26 = f16[2,128,256]{2,1,0:T(8,128)(2,1)S(1)} collective-permute-done((f16[2,128,256]{2,1,0:T(8,128)(2,1)S(1)}, f16[2,128,256]{2,1,0:T(8,128)(2,1)S(1)}, u32[]{:S(2)}, u32[]{:S(2)}) %collective-permute-start.26) | collective-permute-done | bytes 131104 | tf_op jit(solution)/shard_map/ppermute | solution.py:48
  147.6 2.6 %collective-permute-start.28 = (f16[2,2,128,256]{3,2,1,0:T(8,128)(2,1)S(1)}, f16[2,2,128,256]{3,2,1,0:T(8,128)(2,1)S(1)}, u32[]{:S(2)}, u32[]{:S(2)}) collective-permute-start(f16[2,2,128,256]{3,2,1,0:T(8,128)(2,1)S(1)} %get-tuple-element.62), channel_id=1, source_target_pairs={{0,8},{1,9},{2,10},{3,11},{4,12},{5,13},{6,14},{7,15},{8,0},{9,1},... | collective-permute-start | bytes 786440 | tf_op jit(solution)/shard_map/ppermute | solution.py:48
  150.1 8.1 %head_grad.3 = (bf16[8192,1024]{1,0:T(8,128)(2,1)}, f32[1,256]{1,0:T(1,128)S(1)}) custom-call(s32[33]{0:T(128)S(1)} %pad_add_fusion.starts, bf16[128,1024]{1,0:T(8,128)(2,1)S(1)} %get-tuple-element.44.d_ref, f32[2,2,128,256]{3,2,1,0:T(8,128)S(1)} %get-tuple-element.63.after_ref, ...), custom_call_target="tpu_custom_call", output_to_operand_aliasing={{0}: (3, {})} | custom-call | flops 1024 | bytes 1024 | tf_op jit(solution)/shard_map/head_grad/pallas_call | solution.py:293
  158.2 3.6 %collective-permute-done.28 = f16[2,2,128,256]{3,2,1,0:T(8,128)(2,1)S(1)} collective-permute-done((f16[2,2,128,256]{3,2,1,0:T(8,128)(2,1)S(1)}, f16[2,2,128,256]{3,2,1,0:T(8,128)(2,1)S(1)}, u32[]{:S(2)}, u32[]{:S(2)}) %collective-permute-start.28) | collective-permute-done | bytes 262176 | tf_op jit(solution)/shard_map/ppermute | solution.py:48
  163.3 1.6 collective-permute-start.29
  165.0 2.9 %join_grad.4 = (bf16[3,512,8192]{2,1,0:T(8,128)(2,1)}, f32[1,256]{1,0:T(1,128)S(1)}) custom-call(s32[33]{0:T(128)S(1)} %pad_add_fusion.starts, bf16[1536,128]{1,0:T(8,128)(2,1)S(1)} %get-tuple-element.42.x_ref, bf16[4,128,256]{2,1,0:T(8,128)(2,1)S(1)} %bitcast.136), custom_call_target="tpu_custom_call" | custom-call | flops 402653184 | bytes 3145728 | tf_op jit(solution)/shard_map/join_grad/pallas_call | solution.py:344
  169.4 1.7 collective-permute-start.34
  171.2 5.8 %join_grad.5 = (bf16[3,512,8192]{2,1,0:T(8,128)(2,1)}, f32[1,256]{1,0:T(1,128)S(1)}) custom-call(s32[33]{0:T(128)S(1)} %pad_add_fusion.starts, bf16[1536,128]{1,0:T(8,128)(2,1)S(1)} %get-tuple-element.42.x_ref, bf16[3,512,8192]{2,1,0:T(8,128)(2,1)} %get-tuple-element.51.rest_0_, bf16[4,128,256]{2,1,0:T(8,128)(2,1)S(1)} %bitcast.144, ...), custom_call_target="tpu_custom_call", output_to_operand_aliasing={{0}: (2, {})} | custom-call | flops 1207959552 | bytes 9437184 | tf_op jit(solution)/shard_map/join_grad/pallas_call | solution.py:344
  179.4 4.9 %join_grad.6 = (bf16[3,512,8192]{2,1,0:T(8,128)(2,1)}, f32[1,256]{1,0:T(1,128)}) custom-call(s32[33]{0:T(128)S(1)} %pad_add_fusion.starts, bf16[1536,128]{1,0:T(8,128)(2,1)S(1)} %get-tuple-element.42.x_ref, bf16[3,512,8192]{2,1,0:T(8,128)(2,1)} %get-tuple-element.53.rest_0_, bf16[8,128,256]{2,1,0:T(8,128)(2,1)S(1)} %fusion.2.rest_1_), custom_call_target="tpu_custom_call", output_to_operand_aliasing={{0}: (2, {})} | custom-call | flops 805306368 | bytes 6291456 | tf_op jit(solution)/shard_map/join_grad/pallas_call | solution.py:344
  184.3 4.9 %join_grad.7 = (bf16[3,512,8192]{2,1,0:T(8,128)(2,1)}, f32[1,256]{1,0:T(1,128)}) custom-call(s32[33]{0:T(128)S(1)} %pad_add_fusion.starts, bf16[1536,128]{1,0:T(8,128)(2,1)S(1)} %get-tuple-element.42.x_ref, bf16[3,512,8192]{2,1,0:T(8,128)(2,1)} %get-tuple-element.55.rest_0_, bf16[8,128,256]{2,1,0:T(8,128)(2,1)S(1)} %bitcast.143), custom_call_target="tpu_custom_call", output_to_operand_aliasing={{0}: (2, {})} | custom-call | flops 805306368 | bytes 6291456 | tf_op jit(solution)/shard_map/join_grad/pallas_call | solution.py:344
  (125 shorter events, 37.6 us)
Async XLA Ops:
  2.4 19.3 %all-to-all-start = ((bf16[16,8,1536]{2,1,0:T(8,128)(2,1)}), bf16[16,8,1536]{2,1,0:T(8,128)(2,1)S(1)}, u32[]{:S(2)}, u32[]{:S(2)}) async-start(bf16[16,8,1536]{2,1,0:T(8,128)(2,1)} %maximum_bitcast_fusion.after_ref), calls=%async_computation | async-start | bytes 786432 | tf_op jit(solution)/shard_map/all_to_all | solution.py:469
  29.4 5.3 %collective-permute-start = (f32[2,8,128,256]{3,2,1,0:T(8,128)S(1)}, f32[2,8,128,256]{3,2,1,0:T(8,128)S(1)}, u32[]{:S(2)}, u32[]{:S(2)}) collective-permute-start(f32[2,8,128,256]{3,2,1,0:T(8,128)S(1)} %get-tuple-element.32), channel_id=1, source_target_pairs={{0,1},{1,0},{2,3},{3,2},{4,5},{5,4},{6,7},{7,6},{8,9},{9,8},{10,11... | collective-permute-start | bytes 6291464 | tf_op jit(solution)/shard_map/ppermute | solution.py:48
  34.9 13.6 %collective-permute-start.1 = (f32[4,128,256]{2,1,0:T(8,128)S(1)}, f32[4,128,256]{2,1,0:T(8,128)S(1)}, u32[]{:S(2)}, u32[]{:S(2)}) collective-permute-start(f32[4,128,256]{2,1,0:T(8,128)S(1)} %get-tuple-element.76), channel_id=1, source_target_pairs={{0,2},{1,3},{2,0},{3,1},{4,6},{5,7},{6,4},{7,5},{8,10},{9,11},{10,... | collective-permute-start | bytes 1572872 | tf_op jit(solution)/shard_map/ppermute | solution.py:48
  35.2 13.3 %collective-permute-start.2 = (f32[4,128,256]{2,1,0:T(8,128)S(1)}, f32[4,128,256]{2,1,0:T(8,128)S(1)}, u32[]{:S(2)}, u32[]{:S(2)}) collective-permute-start(f32[4,128,256]{2,1,0:T(8,128)S(1)} %get-tuple-element.77), channel_id=1, source_target_pairs={{0,4},{1,5},{2,6},{3,7},{4,0},{5,1},{6,2},{7,3},{8,12},{9,13},{10,... | collective-permute-start | bytes 1572872 | tf_op jit(solution)/shard_map/ppermute | solution.py:48
  48.8 6.8 %collective-permute-start.3 = (f32[2,128,256]{2,1,0:T(8,128)S(1)}, f32[2,128,256]{2,1,0:T(8,128)S(1)}, u32[]{:S(2)}, u32[]{:S(2)}) collective-permute-start(f32[2,128,256]{2,1,0:T(8,128)S(1)} %get-tuple-element.74), channel_id=1, source_target_pairs={{0,4},{1,5},{2,6},{3,7},{4,0},{5,1},{6,2},{7,3},{8,12},{9,13},{10,... | collective-permute-start | bytes 786440 | tf_op jit(solution)/shard_map/ppermute | solution.py:48
  49.5 6.1 %collective-permute-start.4 = (f32[2,128,256]{2,1,0:T(8,128)S(1)}, f32[2,128,256]{2,1,0:T(8,128)S(1)}, u32[]{:S(2)}, u32[]{:S(2)}) collective-permute-start(f32[2,128,256]{2,1,0:T(8,128)S(1)} %get-tuple-element.75), channel_id=1, source_target_pairs={{0,2},{1,3},{2,0},{3,1},{4,6},{5,7},{6,4},{7,5},{8,10},{9,11},{10,... | collective-permute-start | bytes 786440 | tf_op jit(solution)/shard_map/ppermute | solution.py:48
  55.8 25.1 %collective-permute-start.5 = (f32[2,2,128,256]{3,2,1,0:T(8,128)S(1)}, f32[2,2,128,256]{3,2,1,0:T(8,128)S(1)}, u32[]{:S(2)}, u32[]{:S(2)}) collective-permute-start(f32[2,2,128,256]{3,2,1,0:T(8,128)S(1)} %slice_add_fusion.5), channel_id=1, source_target_pairs={{0,8},{1,9},{2,10},{3,11},{4,12},{5,13},{6,14},{7,15},{8,0},{9,1},... | collective-permute-start | bytes 1572872 | tf_op jit(solution)/shard_map/ppermute | solution.py:48
  57.6 31.3 %collective-permute-start.10 = (f32[512]{0:T(512)S(1)}, f32[512]{0:T(512)S(1)}, u32[]{:S(2)}, u32[]{:S(2)}) collective-permute-start(f32[512]{0:T(512)S(1)} %copy-done.1), channel_id=1, source_target_pairs={{0,8},{1,9},{2,10},{3,11},{4,12},{5,13},{6,14},{7,15},{8,0},{9,1},... | collective-permute-start | bytes 6152 | tf_op jit(solution)/shard_map/ppermute | solution.py:48
  82.0 3.3 %collective-permute-start.8 = (f32[128]{0:T(128)S(1)}, f32[128]{0:T(128)S(1)}, u32[]{:S(2)}, u32[]{:S(2)}) collective-permute-start(f32[128]{0:T(128)S(1)} %add_bitcast_fusion.1), channel_id=1, source_target_pairs={{0,6},{1,7},{2,4},{3,5},{4,2},{5,3},{6,0},{7,1},{8,14},{9,15},{10,... | collective-permute-start | bytes 1544 | tf_op jit(solution)/shard_map/ppermute | solution.py:48
  85.7 4.0 %collective-permute-start.9 = (f32[128]{0:T(128)S(1)}, f32[128]{0:T(128)S(1)}, u32[]{:S(2)}, u32[]{:S(2)}) collective-permute-start(f32[128]{0:T(128)S(1)} %add_add_fusion.3), channel_id=1, source_target_pairs={{0,1},{1,0},{2,3},{3,2},{4,5},{5,4},{6,7},{7,6},{8,9},{9,8},{10,11... | collective-permute-start | bytes 1544 | tf_op jit(solution)/shard_map/ppermute | solution.py:48
  89.9 4.8 %collective-permute-start.12 = (bf16[2,128,256]{2,1,0:T(8,128)(2,1)S(1)}, bf16[2,128,256]{2,1,0:T(8,128)(2,1)S(1)}, u32[]{:S(2)}, u32[]{:S(2)}) collective-permute-start(bf16[2,128,256]{2,1,0:T(8,128)(2,1)S(1)} %get-tuple-element.88), channel_id=1, source_target_pairs={{0,4},{1,5},{2,6},{3,7},{4,0},{5,1},{6,2},{7,3},{8,12},{9,13},{10,... | collective-permute-start | bytes 393224 | tf_op jit(solution)/shard_map/ppermute | solution.py:48
  90.0 4.8 %collective-permute-start.13 = (bf16[2,128,256]{2,1,0:T(8,128)(2,1)S(1)}, bf16[2,128,256]{2,1,0:T(8,128)(2,1)S(1)}, u32[]{:S(2)}, u32[]{:S(2)}) collective-permute-start(bf16[2,128,256]{2,1,0:T(8,128)(2,1)S(1)} %get-tuple-element.89), channel_id=1, source_target_pairs={{0,2},{1,3},{2,0},{3,1},{4,6},{5,7},{6,4},{7,5},{8,10},{9,11},{10,... | collective-permute-start | bytes 393224 | tf_op jit(solution)/shard_map/ppermute | solution.py:48
  91.0 7.1 %collective-permute-start.11 = (bf16[2,2,128,256]{3,2,1,0:T(8,128)(2,1)S(1)}, bf16[2,2,128,256]{3,2,1,0:T(8,128)(2,1)S(1)}, u32[]{:S(2)}, u32[]{:S(2)}) collective-permute-start(bf16[2,2,128,256]{3,2,1,0:T(8,128)(2,1)S(1)} %multiply_convert_fusion.6), channel_id=1, source_target_pairs={{0,1},{1,0},{2,3},{3,2},{4,5},{5,4},{6,7},{7,6},{8,9},{9,8},{10,11... | collective-permute-start | bytes 786440 | tf_op jit(solution)/shard_map/ppermute | solution.py:48
  94.9 3.3 %collective-permute-start.14 = (bf16[2,2,128,256]{3,2,1,0:T(8,128)(2,1)S(1)}, bf16[2,2,128,256]{3,2,1,0:T(8,128)(2,1)S(1)}, u32[]{:S(2)}, u32[]{:S(2)}) collective-permute-start(bf16[2,2,128,256]{3,2,1,0:T(8,128)(2,1)S(1)} %multiply_convert_fusion.5), channel_id=1, source_target_pairs={{0,1},{1,0},{2,3},{3,2},{4,5},{5,4},{6,7},{7,6},{8,9},{9,8},{10,11... | collective-permute-start | bytes 786440 | tf_op jit(solution)/shard_map/ppermute | solution.py:48
  96.2 8.0 %collective-permute-start.15 = (bf16[4,128,256]{2,1,0:T(8,128)(2,1)S(1)}, bf16[4,128,256]{2,1,0:T(8,128)(2,1)S(1)}, u32[]{:S(2)}, u32[]{:S(2)}) collective-permute-start(bf16[4,128,256]{2,1,0:T(8,128)(2,1)S(1)} %get-tuple-element.80), channel_id=1, source_target_pairs={{0,2},{1,3},{2,0},{3,1},{4,6},{5,7},{6,4},{7,5},{8,10},{9,11},{10,... | collective-permute-start | bytes 786440 | tf_op jit(solution)/shard_map/ppermute | solution.py:48
  97.1 7.6 %collective-permute-start.16 = (bf16[4,128,256]{2,1,0:T(8,128)(2,1)S(1)}, bf16[4,128,256]{2,1,0:T(8,128)(2,1)S(1)}, u32[]{:S(2)}, u32[]{:S(2)}) collective-permute-start(bf16[4,128,256]{2,1,0:T(8,128)(2,1)S(1)} %get-tuple-element.81), channel_id=1, source_target_pairs={{0,4},{1,5},{2,6},{3,7},{4,0},{5,1},{6,2},{7,3},{8,12},{9,13},{10,... | collective-permute-start | bytes 786440 | tf_op jit(solution)/shard_map/ppermute | solution.py:48
  104.8 4.4 %collective-permute-start.17 = (bf16[2,4,128,256]{3,2,1,0:T(8,128)(2,1)S(1)}, bf16[2,4,128,256]{3,2,1,0:T(8,128)(2,1)S(1)}, u32[]{:S(2)}, u32[]{:S(2)}) collective-permute-start(bf16[2,4,128,256]{3,2,1,0:T(8,128)(2,1)S(1)} %multiply_convert_fusion.2), channel_id=1, source_target_pairs={{0,1},{1,0},{2,3},{3,2},{4,5},{5,4},{6,7},{7,6},{8,9},{9,8},{10,11... | collective-permute-start | bytes 1572872 | tf_op jit(solution)/shard_map/ppermute | solution.py:48
  112.1 3.5 %collective-permute-start.18 = (f32[4,128]{1,0:T(4,128)S(1)}, f32[4,128]{1,0:T(4,128)S(1)}, u32[]{:S(2)}, u32[]{:S(2)}) collective-permute-start(f32[4,128]{1,0:T(4,128)S(1)} %slice.203), channel_id=1, source_target_pairs={{0,8},{1,9},{2,10},{3,11},{4,12},{5,13},{6,14},{7,15},{8,0},{9,1},... | collective-permute-start | bytes 6152 | tf_op jit(solution)/shard_map/ppermute | solution.py:48
  115.6 3.4 %collective-permute-start.21 = (f32[4,128]{1,0:T(4,128)S(1)}, f32[4,128]{1,0:T(4,128)S(1)}, u32[]{:S(2)}, u32[]{:S(2)}) collective-permute-start(f32[4,128]{1,0:T(4,128)S(1)} %pad_maximum_fusion.2), channel_id=1, source_target_pairs={{0,6},{1,7},{2,4},{3,5},{4,2},{5,3},{6,0},{7,1},{8,14},{9,15},{10,... | collective-permute-start | bytes 6152 | tf_op jit(solution)/shard_map/ppermute | solution.py:48
  120.1 3.5 %collective-permute-start.22 = (f32[4,128]{1,0:T(4,128)S(1)}, f32[4,128]{1,0:T(4,128)S(1)}, u32[]{:S(2)}, u32[]{:S(2)}) collective-permute-start(f32[4,128]{1,0:T(4,128)S(1)} %pad_maximum_fusion.3), channel_id=1, source_target_pairs={{0,1},{1,0},{2,3},{3,2},{4,5},{5,4},{6,7},{7,6},{8,9},{9,8},{10,11... | collective-permute-start | bytes 6152 | tf_op jit(solution)/shard_map/ppermute | solution.py:48
  128.7 3.2 %collective-permute-start.23 = (f16[2,8,128,256]{3,2,1,0:T(8,128)(2,1)S(1)}, f16[2,8,128,256]{3,2,1,0:T(8,128)(2,1)S(1)}, u32[]{:S(2)}, u32[]{:S(2)}) collective-permute-start(f16[2,8,128,256]{3,2,1,0:T(8,128)(2,1)S(1)} %multiply_convert_fusion), channel_id=1, source_target_pairs={{0,1},{1,0},{2,3},{3,2},{4,5},{5,4},{6,7},{7,6},{8,9},{9,8},{10,11... | collective-permute-start | bytes 3145736 | tf_op jit(solution)/shard_map/ppermute | solution.py:48
  132.4 10.1 %collective-permute-start.24 = (f16[4,128,256]{2,1,0:T(8,128)(2,1)S(1)}, f16[4,128,256]{2,1,0:T(8,128)(2,1)S(1)}, u32[]{:S(2)}, u32[]{:S(2)}) collective-permute-start(f16[4,128,256]{2,1,0:T(8,128)(2,1)S(1)} %get-tuple-element.72), channel_id=1, source_target_pairs={{0,2},{1,3},{2,0},{3,1},{4,6},{5,7},{6,4},{7,5},{8,10},{9,11},{10,... | collective-permute-start | bytes 786440 | tf_op jit(solution)/shard_map/ppermute | solution.py:48
  133.3 9.2 %collective-permute-start.25 = (f16[4,128,256]{2,1,0:T(8,128)(2,1)S(1)}, f16[4,128,256]{2,1,0:T(8,128)(2,1)S(1)}, u32[]{:S(2)}, u32[]{:S(2)}) collective-permute-start(f16[4,128,256]{2,1,0:T(8,128)(2,1)S(1)} %get-tuple-element.73), channel_id=1, source_target_pairs={{0,4},{1,5},{2,6},{3,7},{4,0},{5,1},{6,2},{7,3},{8,12},{9,13},{10,... | collective-permute-start | bytes 786440 | tf_op jit(solution)/shard_map/ppermute | solution.py:48
  142.8 4.4 %collective-permute-start.26 = (f16[2,128,256]{2,1,0:T(8,128)(2,1)S(1)}, f16[2,128,256]{2,1,0:T(8,128)(2,1)S(1)}, u32[]{:S(2)}, u32[]{:S(2)}) collective-permute-start(f16[2,128,256]{2,1,0:T(8,128)(2,1)S(1)} %get-tuple-element.70), channel_id=1, source_target_pairs={{0,4},{1,5},{2,6},{3,7},{4,0},{5,1},{6,2},{7,3},{8,12},{9,13},{10,... | collective-permute-start | bytes 393224 | tf_op jit(solution)/shard_map/ppermute | solution.py:48
  143.4 4.1 %collective-permute-start.27 = (f16[2,128,256]{2,1,0:T(8,128)(2,1)S(1)}, f16[2,128,256]{2,1,0:T(8,128)(2,1)S(1)}, u32[]{:S(2)}, u32[]{:S(2)}) collective-permute-start(f16[2,128,256]{2,1,0:T(8,128)(2,1)S(1)} %get-tuple-element.71), channel_id=1, source_target_pairs={{0,2},{1,3},{2,0},{3,1},{4,6},{5,7},{6,4},{7,5},{8,10},{9,11},{10,... | collective-permute-start | bytes 393224 | tf_op jit(solution)/shard_map/ppermute | solution.py:48
  147.6 14.3 %collective-permute-start.28 = (f16[2,2,128,256]{3,2,1,0:T(8,128)(2,1)S(1)}, f16[2,2,128,256]{3,2,1,0:T(8,128)(2,1)S(1)}, u32[]{:S(2)}, u32[]{:S(2)}) collective-permute-start(f16[2,2,128,256]{3,2,1,0:T(8,128)(2,1)S(1)} %get-tuple-element.62), channel_id=1, source_target_pairs={{0,8},{1,9},{2,10},{3,11},{4,12},{5,13},{6,14},{7,15},{8,0},{9,1},... | collective-permute-start | bytes 786440 | tf_op jit(solution)/shard_map/ppermute | solution.py:48
  162.2 5.7 %collective-permute-start.30 = (bf16[2,128,256]{2,1,0:T(8,128)(2,1)S(1)}, bf16[2,128,256]{2,1,0:T(8,128)(2,1)S(1)}, u32[]{:S(2)}, u32[]{:S(2)}) collective-permute-start(bf16[2,128,256]{2,1,0:T(8,128)(2,1)S(1)} %get-tuple-element.84), channel_id=1, source_target_pairs={{0,4},{1,5},{2,6},{3,7},{4,0},{5,1},{6,2},{7,3},{8,12},{9,13},{10,... | collective-permute-start | bytes 393224 | tf_op jit(solution)/shard_map/ppermute | solution.py:48
  162.2 5.6 %collective-permute-start.31 = (bf16[2,128,256]{2,1,0:T(8,128)(2,1)S(1)}, bf16[2,128,256]{2,1,0:T(8,128)(2,1)S(1)}, u32[]{:S(2)}, u32[]{:S(2)}) collective-permute-start(bf16[2,128,256]{2,1,0:T(8,128)(2,1)S(1)} %get-tuple-element.85), channel_id=1, source_target_pairs={{0,2},{1,3},{2,0},{3,1},{4,6},{5,7},{6,4},{7,5},{8,10},{9,11},{10,... | collective-permute-start | bytes 393224 | tf_op jit(solution)/shard_map/ppermute | solution.py:48
  163.3 7.8 %collective-permute-start.29 = (bf16[2,2,128,256]{3,2,1,0:T(8,128)(2,1)S(1)}, bf16[2,2,128,256]{3,2,1,0:T(8,128)(2,1)S(1)}, u32[]{:S(2)}, u32[]{:S(2)}) collective-permute-start(bf16[2,2,128,256]{3,2,1,0:T(8,128)(2,1)S(1)} %get-tuple-element.58), channel_id=1, source_target_pairs={{0,1},{1,0},{2,3},{3,2},{4,5},{5,4},{6,7},{7,6},{8,9},{9,8},{10,11... | collective-permute-start | bytes 786440 | tf_op jit(solution)/shard_map/ppermute | solution.py:48
  168.6 8.3 %collective-permute-start.33 = (bf16[4,128,256]{2,1,0:T(8,128)(2,1)S(1)}, bf16[4,128,256]{2,1,0:T(8,128)(2,1)S(1)}, u32[]{:S(2)}, u32[]{:S(2)}) collective-permute-start(bf16[4,128,256]{2,1,0:T(8,128)(2,1)S(1)} %get-tuple-element.78), channel_id=1, source_target_pairs={{0,2},{1,3},{2,0},{3,1},{4,6},{5,7},{6,4},{7,5},{8,10},{9,11},{10,... | collective-permute-start | bytes 786440 | tf_op jit(solution)/shard_map/ppermute | solution.py:48
  169.4 8.0 %collective-permute-start.34 = (bf16[4,128,256]{2,1,0:T(8,128)(2,1)S(1)}, bf16[4,128,256]{2,1,0:T(8,128)(2,1)S(1)}, u32[]{:S(2)}, u32[]{:S(2)}) collective-permute-start(bf16[4,128,256]{2,1,0:T(8,128)(2,1)S(1)} %get-tuple-element.79), channel_id=1, source_target_pairs={{0,4},{1,5},{2,6},{3,7},{4,0},{5,1},{6,2},{7,3},{8,12},{9,13},{10,... | collective-permute-start | bytes 786440 | tf_op jit(solution)/shard_map/ppermute | solution.py:48
  177.6 6.7 %collective-permute-start.35 = (bf16[2,4,128,256]{3,2,1,0:T(8,128)(2,1)S(1)}, bf16[2,4,128,256]{3,2,1,0:T(8,128)(2,1)S(1)}, u32[]{:S(2)}, u32[]{:S(2)}) collective-permute-start(bf16[2,4,128,256]{3,2,1,0:T(8,128)(2,1)S(1)} %multiply_convert_fusion.1), channel_id=1, source_target_pairs={{0,1},{1,0},{2,3},{3,2},{4,5},{5,4},{6,7},{7,6},{8,9},{9,8},{10,11... | collective-permute-start | bytes 1572872 | tf_op jit(solution)/shard_map/ppermute | solution.py:48
  (9 other events, 89.4 us)

commit v6 on v5

--- a/solution.py
+++ b/solution.py
@@ -14,14 +14,21 @@
 TILE = 256
 
 
-def reduce_places(bits, order):
-    return [
-        sum(((q >> (bits - 2 - k)) & 1) << bit for k, bit in enumerate(order)) for q in range(1 << (bits - 1))
-    ]
+def reduce_places(bits):
+    out = []
+    for stream, order in enumerate(([1, 2], [2, 1])):
+        order = order + list(range(3, bits - 1))
+        spread = [
+            sum(((q >> (len(order) - 1 - k)) & 1) << bit for k, bit in enumerate(order))
+            for q in range(1 << len(order))
+        ]
+        spread = [p | (stream << (bits - 1)) for p in spread]
+        out.append(spread + [p + 1 for p in spread])
+    return np.array(out, np.int32)
 
 
 def gather_places(bits):
-    held = fresh = np.array([[0, 1 << (bits - 1)]] * 2, np.int32)
+    held = fresh = np.array([[0], [1 << (bits - 1)]], np.int32)
     out, across = [held], []
     for bit in range(bits - 2, 2, -1):
         across.append(fresh ^ 1)
@@ -31,9 +38,7 @@
     first = held ^ np.array([[4], [2]], np.int32)
     second = np.concatenate([held, first], axis=1) ^ np.array([[2], [4]], np.int32)
     out += [*across, fresh ^ 1, first, first ^ 1, second, second ^ 1]
-    places = np.concatenate([p.reshape(-1) for p in out])
-    streams = np.concatenate([np.repeat(np.arange(2), p.shape[1]) for p in out])
-    return places.astype(np.int32), streams.astype(np.int32)
+    return np.concatenate([p.reshape(-1) for p in out]).astype(np.int32)
 
 
 def masks_of(group):
@@ -115,18 +120,23 @@
     def _(q):
         for s in range(2):
             copy(q, s).wait()
-            total = jnp.dot(x_ref[:, :rows], slots[2 * q + s, 0], preferred_element_type=jnp.float32)
-            for j in (1, 2):
-                total += jnp.dot(
-                    x_ref[:, j * rows : (j + 1) * rows], slots[2 * q + s, j], preferred_element_type=jnp.float32
+            for at in range(0, width, TILE):
+                total = jnp.dot(
+                    x_ref[:, :rows], slots[2 * q + s, 0, :, at : at + TILE], preferred_element_type=jnp.float32
                 )
-            out_ref[s, q] = total
+                for j in (1, 2):
+                    total += jnp.dot(
+                        x_ref[:, j * rows : (j + 1) * rows],
+                        slots[2 * q + s, j, :, at : at + TILE],
+                        preferred_element_type=jnp.float32,
+                    )
+                out_ref[s, q, :, at : at + TILE] = total
 
 
 def join(order, first, count, x, w_fc, after, turn):
     tokens = x.shape[0]
     rows = w_fc.shape[1]
-    width = rows // 2
+    width = rows
     shapes = [vmem_out((2, count, tokens, width), jnp.float32), vmem_out((1, width), jnp.float32)]
     if turn:
         shapes.append(jax.ShapeDtypeStruct(x.shape[::-1], x.dtype))
@@ -140,7 +150,7 @@
             pltpu.SemaphoreType.DMA((2 * count,)),
         ],
         name="join",
-        **settings(6 * tokens * rows * rows * count, 6 * rows * rows * count, 20 * MIB),
+        **settings(12 * tokens * rows * rows * count, 12 * rows * rows * count, 20 * MIB),
     )(order, near(x), far(w_fc), after)
 
 
@@ -206,12 +216,13 @@
     def _(q):
         for s in range(2):
             row = pl.multiple_of(order[s, first + q], 128)
-            out_ref[s, q] = lax.dot_general(
-                d_ref[...],
-                w_ref[pl.ds(row, width), :],
-                (((1,), (1,)), ((), ())),
-                preferred_element_type=jnp.float32,
-            )
+            for at in range(0, width, TILE):
+                out_ref[s, q, :, at : at + TILE] = lax.dot_general(
+                    d_ref[...],
+                    w_ref[pl.ds(row + at, TILE), :],
+                    (((1,), (1,)), ((), ())),
+                    preferred_element_type=jnp.float32,
+                )
 
 
 def back_first_kernel(first, count, order, starts, logits_ref, stats_ref, targets_ref, w_ref, out_ref, d_ref):
@@ -320,13 +331,14 @@
 
         @pl.loop(0, count)
         def _(q):
-            for j in range(3):
-                for row in range(0, rows, TILE):
-                    slots[offset + q, j, row : row + TILE, :] = jnp.dot(
-                        x_ref[j * rows + row : j * rows + row + TILE, :],
-                        piece_ref[q],
-                        preferred_element_type=jnp.float32,
-                    ).astype(slots.dtype)
+            for at in range(0, width, TILE):
+                for j in range(3):
+                    for row in range(0, rows, TILE):
+                        slots[offset + q, j, row : row + TILE, at : at + TILE] = jnp.dot(
+                            x_ref[j * rows + row : j * rows + row + TILE, :],
+                            piece_ref[q, :, at : at + TILE],
+                            preferred_element_type=jnp.float32,
+                        ).astype(slots.dtype)
             copy(offset + q).start()
 
         offset += count
@@ -417,7 +429,7 @@
         total = total[:, :half] + unpack(exchange(pack(total[:, half:]), 1 << bit, size))
     passed = exchange(pack(total), 1 << (bits - 1), size)
     token = work(bits - 1, total, None)
-    return total + with_token(unpack(jnp.stack([passed[:, 1], passed[:, 0]], axis=1)), token)
+    return total + with_token(unpack(jnp.stack([passed[1], passed[0]])), token)
 
 
 def gather(held, bits, size, work):
@@ -451,16 +463,11 @@
     rows, full_width = w_fc.shape[1], w_fc.shape[2]
     share = w_lm.shape[1]
     tokens = targets.shape[0]
-    half = rows // 2
     bits = size.bit_length() - 1
-    count = size // 2
-    last = list(range(3, bits))
-    orders = np.array([reduce_places(bits, [1, 2] + last), reduce_places(bits, [2, 1] + last)], np.int32)
-    orders = np.concatenate([orders, orders + 1], axis=1)
-    order = (jnp.asarray(orders) ^ me) * rows + jnp.asarray(np.array([[0], [half]], np.int32))
-    places, streams = gather_places(bits)
-    starts = jnp.concatenate([(jnp.asarray(places) ^ me) * rows + jnp.asarray(streams * half), me[None]])
-    kernels = half % TILE == 0
+    count, quarter = size // 4, size // 8
+    order = (jnp.asarray(reduce_places(bits)) ^ me) * rows
+    starts = jnp.concatenate([(jnp.asarray(gather_places(bits)) ^ me) * rows, me[None]])
+    kernels = rows % TILE == 0
     target_row = targets.reshape(1, tokens)
 
     sent = jnp.concatenate(
@@ -469,31 +476,29 @@
     x = lax.all_to_all(sent, "section", split_axis=0, concat_axis=0, tiled=True).reshape(tokens, 3 * rows)
 
     held = {"logits": jnp.zeros((tokens, share), jnp.float32), "grad_lm": None, "grad_fc": None}
-    quarter = size // 4
     if kernels:
         high, _, held["x"] = join(order, count, count, x, w_fc, sent, True)
         low, _ = join(order, quarter, quarter, x, w_fc, sent, False)
     else:
         total = jnp.dot(x, w_fc.reshape(3 * rows, full_width), preferred_element_type=jnp.float32)
-        remaining, low, high = cut(total, order, half)
+        remaining, low, high = cut(total, order, rows)
 
     def join_rest(after):
         return join(order, 0, quarter, x, w_fc, after, False) if kernels else (remaining, None)
 
     def bring_head(k, after, token):
         if kernels and k == 1:
-            held["lm"], token = stage(w_lm, after, half)
+            held["lm"], token = stage(w_lm, after, rows)
         return token
 
     joined = reduce_halves(low, high, join_rest, bits, size, lambda x: x, lambda x: x, bring_head)
 
-    squares = jnp.sum(joined * joined, axis=(0, 3))
+    squares = jnp.sum(joined * joined, axis=(1, 3))
     squares = squares[0] + squares[1]
     for group in sum_rounds(bits - 1):
         squares = tree_sum(contributions(squares, group, size))
     inv_rms = lax.rsqrt(squares / full_width + epsilon)[:, None]
-    gains = gain.reshape(2, 1, 1, half)
-    gains = jnp.concatenate([gains, exchange(gain, 1 << (bits - 1), size).reshape(2, 1, 1, half)], axis=1)
+    gains = jnp.stack([gain, exchange(gain, 1 << (bits - 1), size)])[:, None, None, :]
     normed = (joined * inv_rms * gains).astype(jnp.bfloat16)
 
     all_normed, all_dfused = [], []
@@ -535,8 +540,8 @@
 
     if kernels:
         spread = jnp.broadcast_to(log_total[None], (8, tokens))
-        high, dlogits = back_first(order, starts, count, count, logits, spread, target_row, held["lm"], half)
-        low, _ = back_rest(order, quarter, quarter, dlogits, held["lm"], half, high)
+        high, dlogits = back_first(order, starts, count, count, logits, spread, target_row, held["lm"], rows)
+        low, _ = back_rest(order, quarter, quarter, dlogits, held["lm"], rows, high)
     else:
         dlogits = (
             (jnp.exp(logits - log_total[:, None]) - is_target.astype(jnp.float32)) / tokens
@@ -544,14 +549,14 @@
         total = lax.dot_general(
             dlogits, w_lm, (((1,), (1,)), ((), ())), preferred_element_type=jnp.float32
         )
-        left, low, high = cut(total, order, half)
+        left, low, high = cut(total, order, rows)
 
     def back_last(after):
-        return back_rest(order, 0, quarter, dlogits, held["lm"], half, after) if kernels else (left, None)
+        return back_rest(order, 0, quarter, dlogits, held["lm"], rows, after) if kernels else (left, None)
 
     def fill_grad_lm(k, after, token):
         if kernels and k != 2:
-            middle = len(all_normed) - 3
+            middle = len(all_normed) - 4
             pieces = all_normed[:middle] if k == 1 else all_normed[middle:]
             first = 0 if k == 1 else sum(p.shape[0] for p in all_normed[:middle])
             held["grad_lm"], token = head_grad(
@@ -575,7 +580,7 @@
             normed_all, dlogits, (((0,), (0,)), ((), ())), preferred_element_type=jnp.float32
         ).astype(jnp.bfloat16)
 
-    grad_gain = jnp.sum(dnormed[:, 0] * joined[:, 0] * inv_rms, axis=1).reshape(rows)
+    grad_gain = jnp.sum(dnormed[0, 0] * joined[0, 0] * inv_rms, axis=0)
     dfused = (
         inv_rms * (dnormed * gains) - joined * (inv_rms * inv_rms * inv_rms * rowdot / full_width)
     ).astype(jnp.bfloat16)

time: 189 us -> 184 us (0.974)
  Pallas kernels: 76.3 us -> 65.6 us
  waiting for transfers between devices: 59.2 us -> 64.9 us
    ppermute x36, waiting for transfers between devices: 48 us -> 53.7 us  [exchange(): return lax.ppermute(x, 'section', [(i, i ^ mask) for i in range(size)])]
    pallas_call x3, Pallas kernels: 17.3 us -> 14 us  [join(): pl.pallas_call(functools.partial(join_kernel, first, count), out_shape=tu...]
    pallas_call x2, Pallas kernels: 13.4 us -> 10.8 us  [head_grad(): pl.pallas_call(functools.partial(head_grad_kernel, first, counts, len(ext...]
    pallas_call x4, Pallas kernels: 10.8 us -> 8.47 us  [head(): pl.pallas_call(functools.partial(head_kernel, first, counts, last), out_s...]
  transfers between devices with their start and end apart: 37 -> 37, of which waited for: 19 -> 22; matrix products, arithmetic and copies ran while one was open for 2% -> 2% of each run, Pallas kernels for 30% -> 26%
where the time goes in v6:
time: 184 us
  Pallas kernels  65.6 us (36%)
  waiting for transfers between devices  64.9 us (35%)
  starting transfers between devices  44.3 us (24%)
  other arithmetic  7.59 us (4%)
    ppermute x36, waiting for transfers between devices, exchange(): return lax.ppermute(x, 'section', [(i, i ^ mask) for i in range(size)])  53.7 us
    ppermute x36, starting transfers between devices, exchange(): return lax.ppermute(x, 'section', [(i, i ^ mask) for i in range(size)])  37 us
    pallas_call x4, Pallas kernels, join_grad(): pl.pallas_call(functools.partial(join_grad_kernel, first, counts, len(ext...  17 us
    pallas_call x3, Pallas kernels, join(): pl.pallas_call(functools.partial(join_kernel, first, count), out_shape=tu...  14 us
    all_to_all x1, waiting for transfers between devices, on_device(): lax.all_to_all(sent, 'section', split_axis=0, concat_axis=0, tiled=True)  11.2 us
    pallas_call x2, Pallas kernels, head_grad(): pl.pallas_call(functools.partial(head_grad_kernel, first, counts, len(ext...  10.8 us
    pallas_call x4, Pallas kernels, head(): pl.pallas_call(functools.partial(head_kernel, first, counts, last), out_s...  8.47 us
    all_to_all x1, starting transfers between devices, on_device(): lax.all_to_all(sent, 'section', split_axis=0, concat_axis=0, tiled=True)  7.35 us
  transfers between devices with their start and end apart: 37, of which 22 were waited for; matrix products, arithmetic and copies ran while one was open for 2% of the time, Pallas kernels for 26%

profile of v6, /device:TPU:1, one launch (start us, length us, event | category | flops | bytes accessed | tf_op | source)
XLA Modules:
  0.0 184.0 jit_solution(9154848674266154484)
XLA Ops:
  0.6 1.8 maximum_bitcast_fusion.after_ref
  2.4 7.3 %all-to-all-start = ((bf16[16,8,1536]{2,1,0:T(8,128)(2,1)}), bf16[16,8,1536]{2,1,0:T(8,128)(2,1)S(1)}, u32[]{:S(2)}, u32[]{:S(2)}) async-start(bf16[16,8,1536]{2,1,0:T(8,128)(2,1)} %maximum_bitcast_fusion.after_ref), calls=%async_computation | async-start | bytes 786432 | tf_op jit(solution)/shard_map/all_to_all | solution.py:476
  10.5 11.2 %all-to-all-done = bf16[16,8,1536]{2,1,0:T(8,128)(2,1)S(1)} async-done(((bf16[16,8,1536]{2,1,0:T(8,128)(2,1)}), bf16[16,8,1536]{2,1,0:T(8,128)(2,1)S(1)}, u32[]{:S(2)}, u32[]{:S(2)}) %all-to-all-start) | async-done | bytes 393248 | tf_op jit(solution)/shard_map/all_to_all | solution.py:476
  21.7 5.9 %join.4 = (f32[2,4,128,512]{3,2,1,0:T(8,128)S(1)}, f32[1,512]{1,0:T(1,128)}, bf16[1536,128]{1,0:T(8,128)(2,1)S(1)}) custom-call(s32[2,8]{1,0:T(2,128)S(1)} %xor_multiply_fusion.order, bf16[128,1536]{1,0:T(8,128)(2,1)S(1)} %bitcast.154, bf16[3,512,8192]{2,1,0:T(8,128)(2,1)} %w_ref.6, bf16[16,8,1536]{2,1,0:T(8,128)(2,1)} %maximum_bitcast_fusion.after_ref), custom_call_target="tpu_custom_call" | custom-call | flops 1610612736 | bytes 12582912 | tf_op jit(solution)/shard_map/join/pallas_call | solution.py:143
  28.1 4.0 %join.3 = (f32[2,2,128,512]{3,2,1,0:T(8,128)S(1)}, f32[1,512]{1,0:T(1,128)}) custom-call(s32[2,8]{1,0:T(2,128)S(1)} %xor_multiply_fusion.order, bf16[128,1536]{1,0:T(8,128)(2,1)S(1)} %bitcast.155, bf16[3,512,8192]{2,1,0:T(8,128)(2,1)} %w_ref.6, bf16[16,8,1536]{2,1,0:T(8,128)(2,1)} %maximum_bitcast_fusion.after_ref), custom_call_target="tpu_custom_call" | custom-call | flops 805306368 | bytes 6291456 | tf_op jit(solution)/shard_map/join/pallas_call | solution.py:143
  33.8 4.0 %join.5 = (f32[2,2,128,512]{3,2,1,0:T(8,128)S(1)}, f32[1,512]{1,0:T(1,128)}) custom-call(s32[2,8]{1,0:T(2,128)S(1)} %xor_multiply_fusion.order, bf16[128,1536]{1,0:T(8,128)(2,1)S(1)} %bitcast.156, bf16[3,512,8192]{2,1,0:T(8,128)(2,1)} %w_ref.6, f32[2,2,128,512]{3,2,1,0:T(8,128)S(1)} %slice_add_fusion.3.after_ref), custom_call_target="tpu_custom_call" | custom-call | flops 805306368 | bytes 6291456 | tf_op jit(solution)/shard_map/join/pallas_call | solution.py:143
  37.8 5.9 %stage.1 = (bf16[8192,1024]{1,0:T(8,128)(2,1)S(1)}, f32[1,512]{1,0:T(1,128)S(1)}) custom-call(bf16[8192,1024]{1,0:T(8,128)(2,1)} %w_ref.7, f32[2,2,128,512]{3,2,1,0:T(8,128)S(1)} %get-tuple-element.33.after_ref), custom_call_target="tpu_custom_call" | custom-call | bytes 16777216 | tf_op jit(solution)/shard_map/stage/pallas_call | solution.py:91
  43.8 2.3 %collective-permute-done.1 = f32[2,128,512]{2,1,0:T(8,128)S(1)} collective-permute-done((f32[2,128,512]{2,1,0:T(8,128)S(1)}, f32[2,128,512]{2,1,0:T(8,128)S(1)}, u32[]{:S(2)}, u32[]{:S(2)}) %collective-permute-start.1) | collective-permute-done | bytes 524320 | tf_op jit(solution)/shard_map/ppermute | solution.py:53
  47.8 5.4 %collective-permute-done.3 = f32[1,128,512]{2,1,0:T(8,128)S(1)} collective-permute-done((f32[1,128,512]{2,1,0:T(8,128)S(1)}, f32[1,128,512]{2,1,0:T(8,128)S(1)}, u32[]{:S(2)}, u32[]{:S(2)}) %collective-permute-start.3) | collective-permute-done | bytes 262176 | tf_op jit(solution)/shard_map/ppermute | solution.py:53
  53.3 1.8 collective-permute-start.5
  55.8 22.7 %collective-permute-done.5 = f32[2,1,128,512]{3,2,0,1:T(8,128)S(1)} collective-permute-done((f32[2,1,128,512]{3,2,0,1:T(8,128)S(1)}, f32[2,1,128,512]{3,2,0,1:T(8,128)S(1)}, u32[]{:S(2)}, u32[]{:S(2)}) %collective-permute-start.5) | collective-permute-done | bytes 524320 | tf_op jit(solution)/shard_map/ppermute | solution.py:53
  83.4 3.2 %collective-permute-start.9 = (f32[128]{0:T(128)S(1)}, f32[128]{0:T(128)S(1)}, u32[]{:S(2)}, u32[]{:S(2)}) collective-permute-start(f32[128]{0:T(128)S(1)} %add_add_fusion.3), channel_id=1, source_target_pairs={{0,1},{1,0},{2,3},{3,2},{4,5},{5,4},{6,7},{7,6},{8,9},{9,8},{10,11... | collective-permute-start | bytes 1544 | tf_op jit(solution)/shard_map/ppermute | solution.py:53
  95.9 2.5 %head.5 = (f32[128,1024]{1,0:T(8,128)S(1)}, f32[1,512]{1,0:T(1,128)S(1)}) custom-call(s32[17]{0:T(128)S(1)} %pad_add_fusion.starts, bf16[8192,1024]{1,0:T(8,128)(2,1)S(1)} %get-tuple-element.34.w_ref, f32[128,1024]{1,0:T(8,128)S(1)} %get-tuple-element.36.before_ref, s32[1,128]{1,0:T(1,128)S(1)} %bitcast.169, bf16[2,128,512]{2,1,0:T(8,128)(2,1)S(1)} %bitcast.163, ...), custom_call_target="tpu_custom_call" | custom-call | flops 805306368 | bytes 1048576 | tf_op jit(solution)/shard_map/head/pallas_call | solution.py:202
  98.4 3.5 %collective-permute-done.15 = bf16[2,128,512]{2,1,0:T(8,128)(2,1)S(1)} collective-permute-done((bf16[2,128,512]{2,1,0:T(8,128)(2,1)S(1)}, bf16[2,128,512]{2,1,0:T(8,128)(2,1)S(1)}, u32[]{:S(2)}, u32[]{:S(2)}) %collective-permute-start.15) | collective-permute-done | bytes 262176 | tf_op jit(solution)/shard_map/ppermute | solution.py:53
  104.0 2.5 %head.6 = (f32[128,1024]{1,0:T(8,128)S(1)}, f32[1,512]{1,0:T(1,128)}) custom-call(s32[17]{0:T(128)S(1)} %pad_add_fusion.starts, bf16[8192,1024]{1,0:T(8,128)(2,1)S(1)} %get-tuple-element.34.w_ref, f32[128,1024]{1,0:T(8,128)S(1)} %get-tuple-element.38.before_ref, s32[1,128]{1,0:T(1,128)S(1)} %bitcast.170, bf16[4,128,512]{2,1,0:T(8,128)(2,1)S(1)} %fusion.3.rest_0_.rest_3_), custom_call_target="tpu_custom_call" | custom-call | flops 536870912 | bytes 1048576 | tf_op jit(solution)/shard_map/head/pallas_call | solution.py:202
  106.4 2.3 %head.7 = (f32[128,1024]{1,0:T(8,128)S(1)}, f32[8,128]{1,0:T(8,128)S(1)}) custom-call(s32[17]{0:T(128)S(1)} %pad_add_fusion.starts, bf16[8192,1024]{1,0:T(8,128)(2,1)S(1)} %get-tuple-element.34.w_ref, f32[128,1024]{1,0:T(8,128)S(1)} %get-tuple-element.40.before_ref, s32[1,128]{1,0:T(1,128)S(1)} %bitcast.171, bf16[4,128,512]{2,1,0:T(8,128)(2,1)S(1)} %bitcast.159), custom_call_target="tpu_custom_call" | custom-call | flops 536870912 | bytes 1048576 | tf_op jit(solution)/shard_map/head/pallas_call | solution.py:202
  108.7 2.4 %collective-permute-start.18 = (f32[4,128]{1,0:T(4,128)S(1)}, f32[4,128]{1,0:T(4,128)S(1)}, u32[]{:S(2)}, u32[]{:S(2)}) collective-permute-start(f32[4,128]{1,0:T(4,128)S(1)} %slice.203), channel_id=1, source_target_pairs={{0,8},{1,9},{2,10},{3,11},{4,12},{5,13},{6,14},{7,15},{8,0},{9,1},... | collective-permute-start | bytes 6152 | tf_op jit(solution)/shard_map/ppermute | solution.py:53
  112.1 1.7 collective-permute-start.21
  116.6 2.8 %collective-permute-start.22 = (f32[4,128]{1,0:T(4,128)S(1)}, f32[4,128]{1,0:T(4,128)S(1)}, u32[]{:S(2)}, u32[]{:S(2)}) collective-permute-start(f32[4,128]{1,0:T(4,128)S(1)} %pad_maximum_fusion.4), channel_id=1, source_target_pairs={{0,1},{1,0},{2,3},{3,2},{4,5},{5,4},{6,7},{7,6},{8,9},{9,8},{10,11... | collective-permute-start | bytes 6152 | tf_op jit(solution)/shard_map/ppermute | solution.py:53
  120.2 4.2 %back_first.1 = (f32[2,4,128,512]{3,2,1,0:T(8,128)S(1)}, bf16[128,1024]{1,0:T(8,128)(2,1)S(1)}) custom-call(s32[2,8]{1,0:T(2,128)S(1)} %xor_multiply_fusion.order, s32[17]{0:T(128)S(1)} %pad_add_fusion.starts, f32[128,1024]{1,0:T(8,128)S(1)} %get-tuple-element.43.logits_ref, f32[8,128]{1,0:T(8,128)S(1)} %broadcast_in_dim.11.stats_ref, ...), custom_call_target="tpu_custom_call" | custom-call | flops 1073741824 | bytes 2097152 | tf_op jit(solution)/shard_map/back_first/pallas_call | solution.py:239
  125.1 2.6 %back_rest.2 = (f32[2,2,128,512]{3,2,1,0:T(8,128)S(1)}, f32[1,512]{1,0:T(1,128)}) custom-call(s32[2,8]{1,0:T(2,128)S(1)} %xor_multiply_fusion.order, bf16[128,1024]{1,0:T(8,128)(2,1)S(1)} %get-tuple-element.44.d_ref, bf16[8192,1024]{1,0:T(8,128)(2,1)S(1)} %get-tuple-element.34.w_ref, f32[2,4,128,512]{3,2,1,0:T(8,128)S(1)} %get-tuple-element.45.after_ref), custom_call_target="tpu_custom_call" | custom-call | flops 536870912 | bytes 1048576 | tf_op jit(solution)/shard_map/back_rest/pallas_call | solution.py:256
  130.2 2.6 %back_rest.3 = (f32[2,2,128,512]{3,2,1,0:T(8,128)S(1)}, f32[1,512]{1,0:T(1,128)}) custom-call(s32[2,8]{1,0:T(2,128)S(1)} %xor_multiply_fusion.order, bf16[128,1024]{1,0:T(8,128)(2,1)S(1)} %get-tuple-element.44.d_ref, bf16[8192,1024]{1,0:T(8,128)(2,1)S(1)} %get-tuple-element.34.w_ref, f32[2,2,128,512]{3,2,1,0:T(8,128)S(1)} %slice_add_fusion.1.after_ref), custom_call_target="tpu_custom_call" | custom-call | flops 536870912 | bytes 1048576 | tf_op jit(solution)/shard_map/back_rest/pallas_call | solution.py:256
  132.8 3.4 %head_grad.2 = (bf16[8192,1024]{1,0:T(8,128)(2,1)}, f32[1,512]{1,0:T(1,128)S(1)}) custom-call(s32[17]{0:T(128)S(1)} %pad_add_fusion.starts, bf16[128,1024]{1,0:T(8,128)(2,1)S(1)} %get-tuple-element.44.d_ref, f32[2,2,128,512]{3,2,1,0:T(8,128)S(1)} %get-tuple-element.47.after_ref, bf16[2,128,512]{2,1,0:T(8,128)(2,1)S(1)} %fusion.31.rest_0_, ...), custom_call_target="tpu_custom_call" | custom-call | flops 1024 | bytes 1024 | tf_op jit(solution)/shard_map/head_grad/pallas_call | solution.py:304
  139.1 1.9 %collective-permute-done.26 = f16[1,128,512]{2,1,0:T(8,128)(2,1)S(1)} collective-permute-done((f16[1,128,512]{2,1,0:T(8,128)(2,1)S(1)}, f16[1,128,512]{2,1,0:T(8,128)(2,1)S(1)}, u32[]{:S(2)}, u32[]{:S(2)}) %collective-permute-start.26) | collective-permute-done | bytes 131104 | tf_op jit(solution)/shard_map/ppermute | solution.py:53
  143.8 7.4 %head_grad.3 = (bf16[8192,1024]{1,0:T(8,128)(2,1)}, f32[1,512]{1,0:T(1,128)S(1)}) custom-call(s32[17]{0:T(128)S(1)} %pad_add_fusion.starts, bf16[128,1024]{1,0:T(8,128)(2,1)S(1)} %get-tuple-element.44.d_ref, f32[2,1,128,512]{3,2,1,0:T(8,128)S(1)} %get-tuple-element.69.after_ref, ...), custom_call_target="tpu_custom_call", output_to_operand_aliasing={{0}: (3, {})} | custom-call | flops 1024 | bytes 1024 | tf_op jit(solution)/shard_map/head_grad/pallas_call | solution.py:304
  151.2 5.6 %collective-permute-done.28 = f16[2,1,128,512]{3,2,0,1:T(8,128)(2,1)S(1)} collective-permute-done((f16[2,1,128,512]{3,2,0,1:T(8,128)(2,1)S(1)}, f16[2,1,128,512]{3,2,0,1:T(8,128)(2,1)S(1)}, u32[]{:S(2)}, u32[]{:S(2)}) %collective-permute-start.28) | collective-permute-done | bytes 262176 | tf_op jit(solution)/shard_map/ppermute | solution.py:53
  159.8 2.8 %join_grad.4 = (bf16[3,512,8192]{2,1,0:T(8,128)(2,1)}, f32[1,512]{1,0:T(1,128)S(1)}) custom-call(s32[17]{0:T(128)S(1)} %pad_add_fusion.starts, bf16[1536,128]{1,0:T(8,128)(2,1)S(1)} %get-tuple-element.42.x_ref, bf16[2,128,512]{2,1,0:T(8,128)(2,1)S(1)} %bitcast.158), custom_call_target="tpu_custom_call" | custom-call | flops 402653184 | bytes 3145728 | tf_op jit(solution)/shard_map/join_grad/pallas_call | solution.py:356
  162.8 1.7 collective-permute-start.32
  165.7 5.1 %join_grad.5 = (bf16[3,512,8192]{2,1,0:T(8,128)(2,1)}, f32[1,512]{1,0:T(1,128)S(1)}) custom-call(s32[17]{0:T(128)S(1)} %pad_add_fusion.starts, bf16[1536,128]{1,0:T(8,128)(2,1)S(1)} %get-tuple-element.42.x_ref, bf16[3,512,8192]{2,1,0:T(8,128)(2,1)} %get-tuple-element.51.rest_0_, bf16[2,128,512]{2,1,0:T(8,128)(2,1)S(1)} %bitcast.166, ...), custom_call_target="tpu_custom_call", output_to_operand_aliasing={{0}: (2, {})} | custom-call | flops 1207959552 | bytes 9437184 | tf_op jit(solution)/shard_map/join_grad/pallas_call | solution.py:356
  170.8 1.8 collective-permute-done.33
  174.7 4.5 %join_grad.6 = (bf16[3,512,8192]{2,1,0:T(8,128)(2,1)}, f32[1,512]{1,0:T(1,128)}) custom-call(s32[17]{0:T(128)S(1)} %pad_add_fusion.starts, bf16[1536,128]{1,0:T(8,128)(2,1)S(1)} %get-tuple-element.42.x_ref, bf16[3,512,8192]{2,1,0:T(8,128)(2,1)} %get-tuple-element.53.rest_0_, bf16[4,128,512]{2,1,0:T(8,128)(2,1)S(1)} %fusion.2.rest_1_), custom_call_target="tpu_custom_call", output_to_operand_aliasing={{0}: (2, {})} | custom-call | flops 805306368 | bytes 6291456 | tf_op jit(solution)/shard_map/join_grad/pallas_call | solution.py:356
  179.3 4.5 %join_grad.7 = (bf16[3,512,8192]{2,1,0:T(8,128)(2,1)}, f32[1,512]{1,0:T(1,128)}) custom-call(s32[17]{0:T(128)S(1)} %pad_add_fusion.starts, bf16[1536,128]{1,0:T(8,128)(2,1)S(1)} %get-tuple-element.42.x_ref, bf16[3,512,8192]{2,1,0:T(8,128)(2,1)} %get-tuple-element.55.rest_0_, bf16[4,128,512]{2,1,0:T(8,128)(2,1)S(1)} %bitcast.165), custom_call_target="tpu_custom_call", output_to_operand_aliasing={{0}: (2, {})} | custom-call | flops 805306368 | bytes 6291456 | tf_op jit(solution)/shard_map/join_grad/pallas_call | solution.py:356
  (122 shorter events, 41.3 us)
Async XLA Ops:
  2.4 19.3 %all-to-all-start = ((bf16[16,8,1536]{2,1,0:T(8,128)(2,1)}), bf16[16,8,1536]{2,1,0:T(8,128)(2,1)S(1)}, u32[]{:S(2)}, u32[]{:S(2)}) async-start(bf16[16,8,1536]{2,1,0:T(8,128)(2,1)} %maximum_bitcast_fusion.after_ref), calls=%async_computation | async-start | bytes 786432 | tf_op jit(solution)/shard_map/all_to_all | solution.py:476
  27.6 4.5 %collective-permute-start = (f32[2,4,128,512]{3,2,1,0:T(8,128)S(1)}, f32[2,4,128,512]{3,2,1,0:T(8,128)S(1)}, u32[]{:S(2)}, u32[]{:S(2)}) collective-permute-start(f32[2,4,128,512]{3,2,1,0:T(8,128)S(1)} %get-tuple-element.32), channel_id=1, source_target_pairs={{0,1},{1,0},{2,3},{3,2},{4,5},{5,4},{6,7},{7,6},{8,9},{9,8},{10,11... | collective-permute-start | bytes 6291464 | tf_op jit(solution)/shard_map/ppermute | solution.py:53
  32.5 13.6 %collective-permute-start.1 = (f32[2,128,512]{2,1,0:T(8,128)S(1)}, f32[2,128,512]{2,1,0:T(8,128)S(1)}, u32[]{:S(2)}, u32[]{:S(2)}) collective-permute-start(f32[2,128,512]{2,1,0:T(8,128)S(1)} %get-tuple-element.76), channel_id=1, source_target_pairs={{0,2},{1,3},{2,0},{3,1},{4,6},{5,7},{6,4},{7,5},{8,10},{9,11},{10,... | collective-permute-start | bytes 1572872 | tf_op jit(solution)/shard_map/ppermute | solution.py:53
  32.8 13.2 %collective-permute-start.2 = (f32[2,128,512]{2,1,0:T(8,128)S(1)}, f32[2,128,512]{2,1,0:T(8,128)S(1)}, u32[]{:S(2)}, u32[]{:S(2)}) collective-permute-start(f32[2,128,512]{2,1,0:T(8,128)S(1)} %get-tuple-element.77), channel_id=1, source_target_pairs={{0,4},{1,5},{2,6},{3,7},{4,0},{5,1},{6,2},{7,3},{8,12},{9,13},{10,... | collective-permute-start | bytes 1572872 | tf_op jit(solution)/shard_map/ppermute | solution.py:53
  46.5 6.8 %collective-permute-start.3 = (f32[1,128,512]{2,1,0:T(8,128)S(1)}, f32[1,128,512]{2,1,0:T(8,128)S(1)}, u32[]{:S(2)}, u32[]{:S(2)}) collective-permute-start(f32[1,128,512]{2,1,0:T(8,128)S(1)} %get-tuple-element.74), channel_id=1, source_target_pairs={{0,4},{1,5},{2,6},{3,7},{4,0},{5,1},{6,2},{7,3},{8,12},{9,13},{10,... | collective-permute-start | bytes 786440 | tf_op jit(solution)/shard_map/ppermute | solution.py:53
  47.2 6.1 %collective-permute-start.4 = (f32[1,128,512]{2,1,0:T(8,128)S(1)}, f32[1,128,512]{2,1,0:T(8,128)S(1)}, u32[]{:S(2)}, u32[]{:S(2)}) collective-permute-start(f32[1,128,512]{2,1,0:T(8,128)S(1)} %get-tuple-element.75), channel_id=1, source_target_pairs={{0,2},{1,3},{2,0},{3,1},{4,6},{5,7},{6,4},{7,5},{8,10},{9,11},{10,... | collective-permute-start | bytes 786440 | tf_op jit(solution)/shard_map/ppermute | solution.py:53
  53.3 25.1 %collective-permute-start.5 = (f32[2,1,128,512]{3,2,0,1:T(8,128)S(1)}, f32[2,1,128,512]{3,2,0,1:T(8,128)S(1)}, u32[]{:S(2)}, u32[]{:S(2)}) collective-permute-start(f32[2,1,128,512]{3,2,0,1:T(8,128)S(1)} %fusion.7), channel_id=1, source_target_pairs={{0,8},{1,9},{2,10},{3,11},{4,12},{5,13},{6,14},{7,15},{8,0},{9,1},... | collective-permute-start | bytes 1572872 | tf_op jit(solution)/shard_map/ppermute | solution.py:53
  55.1 31.4 %collective-permute-start.10 = (f32[512]{0:T(512)S(1)}, f32[512]{0:T(512)S(1)}, u32[]{:S(2)}, u32[]{:S(2)}) collective-permute-start(f32[512]{0:T(512)S(1)} %copy-done.1), channel_id=1, source_target_pairs={{0,8},{1,9},{2,10},{3,11},{4,12},{5,13},{6,14},{7,15},{8,0},{9,1},... | collective-permute-start | bytes 6152 | tf_op jit(solution)/shard_map/ppermute | solution.py:53
  79.5 3.3 %collective-permute-start.8 = (f32[128]{0:T(128)S(1)}, f32[128]{0:T(128)S(1)}, u32[]{:S(2)}, u32[]{:S(2)}) collective-permute-start(f32[128]{0:T(128)S(1)} %add_bitcast_fusion.1), channel_id=1, source_target_pairs={{0,6},{1,7},{2,4},{3,5},{4,2},{5,3},{6,0},{7,1},{8,14},{9,15},{10,... | collective-permute-start | bytes 1544 | tf_op jit(solution)/shard_map/ppermute | solution.py:53
  83.4 4.0 %collective-permute-start.9 = (f32[128]{0:T(128)S(1)}, f32[128]{0:T(128)S(1)}, u32[]{:S(2)}, u32[]{:S(2)}) collective-permute-start(f32[128]{0:T(128)S(1)} %add_add_fusion.3), channel_id=1, source_target_pairs={{0,1},{1,0},{2,3},{3,2},{4,5},{5,4},{6,7},{7,6},{8,9},{9,8},{10,11... | collective-permute-start | bytes 1544 | tf_op jit(solution)/shard_map/ppermute | solution.py:53
  87.7 4.8 %collective-permute-start.12 = (bf16[1,128,512]{2,1,0:T(8,128)(2,1)S(1)}, bf16[1,128,512]{2,1,0:T(8,128)(2,1)S(1)}, u32[]{:S(2)}, u32[]{:S(2)}) collective-permute-start(bf16[1,128,512]{2,1,0:T(8,128)(2,1)S(1)} %get-tuple-element.86), channel_id=1, source_target_pairs={{0,4},{1,5},{2,6},{3,7},{4,0},{5,1},{6,2},{7,3},{8,12},{9,13},{10,... | collective-permute-start | bytes 393224 | tf_op jit(solution)/shard_map/ppermute | solution.py:53
  87.8 4.8 %collective-permute-start.13 = (bf16[1,128,512]{2,1,0:T(8,128)(2,1)S(1)}, bf16[1,128,512]{2,1,0:T(8,128)(2,1)S(1)}, u32[]{:S(2)}, u32[]{:S(2)}) collective-permute-start(bf16[1,128,512]{2,1,0:T(8,128)(2,1)S(1)} %get-tuple-element.87), channel_id=1, source_target_pairs={{0,2},{1,3},{2,0},{3,1},{4,6},{5,7},{6,4},{7,5},{8,10},{9,11},{10,... | collective-permute-start | bytes 393224 | tf_op jit(solution)/shard_map/ppermute | solution.py:53
  88.8 7.0 %collective-permute-start.11 = (bf16[2,1,128,512]{3,2,0,1:T(8,128)(2,1)S(1)}, bf16[2,1,128,512]{3,2,0,1:T(8,128)(2,1)S(1)}, u32[]{:S(2)}, u32[]{:S(2)}) collective-permute-start(bf16[2,1,128,512]{3,2,0,1:T(8,128)(2,1)S(1)} %multiply_convert_fusion.7), channel_id=1, source_target_pairs={{0,1},{1,0},{2,3},{3,2},{4,5},{5,4},{6,7},{7,6},{8,9},{9,8},{10,11... | collective-permute-start | bytes 786440 | tf_op jit(solution)/shard_map/ppermute | solution.py:53
  92.6 3.3 %collective-permute-start.14 = (bf16[2,1,128,512]{3,2,0,1:T(8,128)(2,1)S(1)}, bf16[2,1,128,512]{3,2,0,1:T(8,128)(2,1)S(1)}, u32[]{:S(2)}, u32[]{:S(2)}) collective-permute-start(bf16[2,1,128,512]{3,2,0,1:T(8,128)(2,1)S(1)} %multiply_convert_fusion.5), channel_id=1, source_target_pairs={{0,1},{1,0},{2,3},{3,2},{4,5},{5,4},{6,7},{7,6},{8,9},{9,8},{10,11... | collective-permute-start | bytes 786440 | tf_op jit(solution)/shard_map/ppermute | solution.py:53
  93.9 8.0 %collective-permute-start.15 = (bf16[2,128,512]{2,1,0:T(8,128)(2,1)S(1)}, bf16[2,128,512]{2,1,0:T(8,128)(2,1)S(1)}, u32[]{:S(2)}, u32[]{:S(2)}) collective-permute-start(bf16[2,128,512]{2,1,0:T(8,128)(2,1)S(1)} %get-tuple-element.80), channel_id=1, source_target_pairs={{0,2},{1,3},{2,0},{3,1},{4,6},{5,7},{6,4},{7,5},{8,10},{9,11},{10,... | collective-permute-start | bytes 786440 | tf_op jit(solution)/shard_map/ppermute | solution.py:53
  94.9 7.6 %collective-permute-start.16 = (bf16[2,128,512]{2,1,0:T(8,128)(2,1)S(1)}, bf16[2,128,512]{2,1,0:T(8,128)(2,1)S(1)}, u32[]{:S(2)}, u32[]{:S(2)}) collective-permute-start(bf16[2,128,512]{2,1,0:T(8,128)(2,1)S(1)} %get-tuple-element.81), channel_id=1, source_target_pairs={{0,4},{1,5},{2,6},{3,7},{4,0},{5,1},{6,2},{7,3},{8,12},{9,13},{10,... | collective-permute-start | bytes 786440 | tf_op jit(solution)/shard_map/ppermute | solution.py:53
  102.6 3.8 %collective-permute-start.17 = (bf16[2,2,128,512]{3,2,1,0:T(8,128)(2,1)S(1)}, bf16[2,2,128,512]{3,2,1,0:T(8,128)(2,1)S(1)}, u32[]{:S(2)}, u32[]{:S(2)}) collective-permute-start(bf16[2,2,128,512]{3,2,1,0:T(8,128)(2,1)S(1)} %multiply_convert_fusion.2), channel_id=1, source_target_pairs={{0,1},{1,0},{2,3},{3,2},{4,5},{5,4},{6,7},{7,6},{8,9},{9,8},{10,11... | collective-permute-start | bytes 1572872 | tf_op jit(solution)/shard_map/ppermute | solution.py:53
  108.7 3.4 %collective-permute-start.18 = (f32[4,128]{1,0:T(4,128)S(1)}, f32[4,128]{1,0:T(4,128)S(1)}, u32[]{:S(2)}, u32[]{:S(2)}) collective-permute-start(f32[4,128]{1,0:T(4,128)S(1)} %slice.203), channel_id=1, source_target_pairs={{0,8},{1,9},{2,10},{3,11},{4,12},{5,13},{6,14},{7,15},{8,0},{9,1},... | collective-permute-start | bytes 6152 | tf_op jit(solution)/shard_map/ppermute | solution.py:53
  112.1 3.4 %collective-permute-start.21 = (f32[4,128]{1,0:T(4,128)S(1)}, f32[4,128]{1,0:T(4,128)S(1)}, u32[]{:S(2)}, u32[]{:S(2)}) collective-permute-start(f32[4,128]{1,0:T(4,128)S(1)} %pad_maximum_fusion.3), channel_id=1, source_target_pairs={{0,6},{1,7},{2,4},{3,5},{4,2},{5,3},{6,0},{7,1},{8,14},{9,15},{10,... | collective-permute-start | bytes 6152 | tf_op jit(solution)/shard_map/ppermute | solution.py:53
  116.6 3.6 %collective-permute-start.22 = (f32[4,128]{1,0:T(4,128)S(1)}, f32[4,128]{1,0:T(4,128)S(1)}, u32[]{:S(2)}, u32[]{:S(2)}) collective-permute-start(f32[4,128]{1,0:T(4,128)S(1)} %pad_maximum_fusion.4), channel_id=1, source_target_pairs={{0,1},{1,0},{2,3},{3,2},{4,5},{5,4},{6,7},{7,6},{8,9},{9,8},{10,11... | collective-permute-start | bytes 6152 | tf_op jit(solution)/shard_map/ppermute | solution.py:53
  124.7 3.0 %collective-permute-start.23 = (f16[2,4,128,512]{3,2,1,0:T(8,128)(2,1)S(1)}, f16[2,4,128,512]{3,2,1,0:T(8,128)(2,1)S(1)}, u32[]{:S(2)}, u32[]{:S(2)}) collective-permute-start(f16[2,4,128,512]{3,2,1,0:T(8,128)(2,1)S(1)} %multiply_convert_fusion), channel_id=1, source_target_pairs={{0,1},{1,0},{2,3},{3,2},{4,5},{5,4},{6,7},{7,6},{8,9},{9,8},{10,11... | collective-permute-start | bytes 3145736 | tf_op jit(solution)/shard_map/ppermute | solution.py:53
  128.3 7.9 %collective-permute-start.24 = (f16[2,128,512]{2,1,0:T(8,128)(2,1)S(1)}, f16[2,128,512]{2,1,0:T(8,128)(2,1)S(1)}, u32[]{:S(2)}, u32[]{:S(2)}) collective-permute-start(f16[2,128,512]{2,1,0:T(8,128)(2,1)S(1)} %get-tuple-element.72), channel_id=1, source_target_pairs={{0,2},{1,3},{2,0},{3,1},{4,6},{5,7},{6,4},{7,5},{8,10},{9,11},{10,... | collective-permute-start | bytes 786440 | tf_op jit(solution)/shard_map/ppermute | solution.py:53
  129.3 7.4 %collective-permute-start.25 = (f16[2,128,512]{2,1,0:T(8,128)(2,1)S(1)}, f16[2,128,512]{2,1,0:T(8,128)(2,1)S(1)}, u32[]{:S(2)}, u32[]{:S(2)}) collective-permute-start(f16[2,128,512]{2,1,0:T(8,128)(2,1)S(1)} %get-tuple-element.73), channel_id=1, source_target_pairs={{0,4},{1,5},{2,6},{3,7},{4,0},{5,1},{6,2},{7,3},{8,12},{9,13},{10,... | collective-permute-start | bytes 786440 | tf_op jit(solution)/shard_map/ppermute | solution.py:53
  137.1 3.9 %collective-permute-start.26 = (f16[1,128,512]{2,1,0:T(8,128)(2,1)S(1)}, f16[1,128,512]{2,1,0:T(8,128)(2,1)S(1)}, u32[]{:S(2)}, u32[]{:S(2)}) collective-permute-start(f16[1,128,512]{2,1,0:T(8,128)(2,1)S(1)} %get-tuple-element.70), channel_id=1, source_target_pairs={{0,4},{1,5},{2,6},{3,7},{4,0},{5,1},{6,2},{7,3},{8,12},{9,13},{10,... | collective-permute-start | bytes 393224 | tf_op jit(solution)/shard_map/ppermute | solution.py:53
  138.1 4.1 %collective-permute-start.27 = (f16[1,128,512]{2,1,0:T(8,128)(2,1)S(1)}, f16[1,128,512]{2,1,0:T(8,128)(2,1)S(1)}, u32[]{:S(2)}, u32[]{:S(2)}) collective-permute-start(f16[1,128,512]{2,1,0:T(8,128)(2,1)S(1)} %get-tuple-element.71), channel_id=1, source_target_pairs={{0,2},{1,3},{2,0},{3,1},{4,6},{5,7},{6,4},{7,5},{8,10},{9,11},{10,... | collective-permute-start | bytes 393224 | tf_op jit(solution)/shard_map/ppermute | solution.py:53
  142.3 14.5 %collective-permute-start.28 = (f16[2,1,128,512]{3,2,0,1:T(8,128)(2,1)S(1)}, f16[2,1,128,512]{3,2,0,1:T(8,128)(2,1)S(1)}, u32[]{:S(2)}, u32[]{:S(2)}) collective-permute-start(f16[2,1,128,512]{3,2,0,1:T(8,128)(2,1)S(1)} %get-tuple-element.68), channel_id=1, source_target_pairs={{0,8},{1,9},{2,10},{3,11},{4,12},{5,13},{6,14},{7,15},{8,0},{9,1},... | collective-permute-start | bytes 786440 | tf_op jit(solution)/shard_map/ppermute | solution.py:53
  157.1 5.5 %collective-permute-start.31 = (bf16[1,128,512]{2,1,0:T(8,128)(2,1)S(1)}, bf16[1,128,512]{2,1,0:T(8,128)(2,1)S(1)}, u32[]{:S(2)}, u32[]{:S(2)}) collective-permute-start(bf16[1,128,512]{2,1,0:T(8,128)(2,1)S(1)} %slice_bitcast_fusion.6), channel_id=1, source_target_pairs={{0,2},{1,3},{2,0},{3,1},{4,6},{5,7},{6,4},{7,5},{8,10},{9,11},{10,... | collective-permute-start | bytes 393224 | tf_op jit(solution)/shard_map/ppermute | solution.py:53
  158.5 4.2 %collective-permute-start.30 = (bf16[1,128,512]{2,1,0:T(8,128)(2,1)S(1)}, bf16[1,128,512]{2,1,0:T(8,128)(2,1)S(1)}, u32[]{:S(2)}, u32[]{:S(2)}) collective-permute-start(bf16[1,128,512]{2,1,0:T(8,128)(2,1)S(1)} %slice_bitcast_fusion.7), channel_id=1, source_target_pairs={{0,4},{1,5},{2,6},{3,7},{4,0},{5,1},{6,2},{7,3},{8,12},{9,13},{10,... | collective-permute-start | bytes 393224 | tf_op jit(solution)/shard_map/ppermute | solution.py:53
  159.0 6.1 %collective-permute-start.29 = (bf16[2,1,128,512]{3,2,0,1:T(8,128)(2,1)S(1)}, bf16[2,1,128,512]{3,2,0,1:T(8,128)(2,1)S(1)}, u32[]{:S(2)}, u32[]{:S(2)}) collective-permute-start(bf16[2,1,128,512]{3,2,0,1:T(8,128)(2,1)S(1)} %get-tuple-element.58), channel_id=1, source_target_pairs={{0,1},{1,0},{2,3},{3,2},{4,5},{5,4},{6,7},{7,6},{8,9},{9,8},{10,11... | collective-permute-start | bytes 786440 | tf_op jit(solution)/shard_map/ppermute | solution.py:53
  164.6 8.0 %collective-permute-start.33 = (bf16[2,128,512]{2,1,0:T(8,128)(2,1)S(1)}, bf16[2,128,512]{2,1,0:T(8,128)(2,1)S(1)}, u32[]{:S(2)}, u32[]{:S(2)}) collective-permute-start(bf16[2,128,512]{2,1,0:T(8,128)(2,1)S(1)} %get-tuple-element.78), channel_id=1, source_target_pairs={{0,2},{1,3},{2,0},{3,1},{4,6},{5,7},{6,4},{7,5},{8,10},{9,11},{10,... | collective-permute-start | bytes 786440 | tf_op jit(solution)/shard_map/ppermute | solution.py:53
  165.0 7.6 %collective-permute-start.34 = (bf16[2,128,512]{2,1,0:T(8,128)(2,1)S(1)}, bf16[2,128,512]{2,1,0:T(8,128)(2,1)S(1)}, u32[]{:S(2)}, u32[]{:S(2)}) collective-permute-start(bf16[2,128,512]{2,1,0:T(8,128)(2,1)S(1)} %get-tuple-element.79), channel_id=1, source_target_pairs={{0,4},{1,5},{2,6},{3,7},{4,0},{5,1},{6,2},{7,3},{8,12},{9,13},{10,... | collective-permute-start | bytes 786440 | tf_op jit(solution)/shard_map/ppermute | solution.py:53
  172.7 6.6 %collective-permute-start.35 = (bf16[2,2,128,512]{3,2,1,0:T(8,128)(2,1)S(1)}, bf16[2,2,128,512]{3,2,1,0:T(8,128)(2,1)S(1)}, u32[]{:S(2)}, u32[]{:S(2)}) collective-permute-start(bf16[2,2,128,512]{3,2,1,0:T(8,128)(2,1)S(1)} %multiply_convert_fusion.1), channel_id=1, source_target_pairs={{0,1},{1,0},{2,3},{3,2},{4,5},{5,4},{6,7},{7,6},{8,9},{9,8},{10,11... | collective-permute-start | bytes 1572872 | tf_op jit(solution)/shard_map/ppermute | solution.py:53
  (8 other events, 42.2 us)

commit v7 on v6

--- a/solution.py
+++ b/solution.py
@@ -263,15 +263,15 @@
     )(order, near(dlogits), near(w_lm), after)
 
 
-def head_grad_kernel(first, counts, aliased, starts, d_ref, after_ref, *rest):
-    pieces = rest[aliased : aliased + len(counts)]
+def head_grad_kernel(counts, starts, d_ref, after_ref, *rest):
+    pieces = rest[: len(counts)]
     out_ref, token_ref, slots, sems = rest[-4:]
     width = pieces[0].shape[2]
     share = d_ref.shape[1]
     token_ref[...] = jnp.ones_like(token_ref)
 
     def copy(at):
-        row = pl.multiple_of(starts[first + at], 128)
+        row = pl.multiple_of(starts[at], 128)
         return pltpu.make_async_copy(slots.at[at], out_ref.at[pl.ds(row, width), :], sems.at[at])
 
     offset = 0
@@ -295,25 +295,23 @@
         copy(at).wait()
 
 
-def head_grad(starts, first, pieces, dlogits, full_width, after, into):
+def head_grad(starts, pieces, dlogits, full_width, after):
     tokens, width = pieces[0].shape[1:]
     counts = tuple(p.shape[0] for p in pieces)
     share = dlogits.shape[1]
-    extra = () if into is None else (into,)
     blocks = sum(counts)
     return pl.pallas_call(
-        functools.partial(head_grad_kernel, first, counts, len(extra)),
+        functools.partial(head_grad_kernel, counts),
         out_shape=(
             jax.ShapeDtypeStruct((full_width, share), jnp.bfloat16),
             vmem_out((1, width), jnp.float32),
         ),
-        in_specs=[IN_SMEM, IN_VMEM, ANYWHERE] + [ANYWHERE] * len(extra) + [IN_VMEM] * len(pieces),
+        in_specs=[IN_SMEM, IN_VMEM, ANYWHERE] + [IN_VMEM] * len(pieces),
         out_specs=(ANYWHERE, IN_VMEM),
         scratch_shapes=[pltpu.VMEM((blocks, width, share), jnp.bfloat16), pltpu.SemaphoreType.DMA((blocks,))],
-        input_output_aliases={3: 0} if extra else {},
         name="head_grad",
-        **settings(1024, 1024, 14 * MIB),
-    )(starts, near(dlogits), after, *extra, *[near(p) for p in pieces])
+        **settings(2 * tokens * width * share * blocks, 2 * width * share * blocks, 22 * MIB),
+    )(starts, near(dlogits), after, *[near(p) for p in pieces])
 
 
 def join_grad_kernel(first, counts, aliased, starts, x_ref, *rest):
@@ -322,29 +320,32 @@
     rows, width = slots.shape[2:]
     token_ref[...] = jnp.ones_like(token_ref)
 
-    def copy(at):
+    def copy(at, j):
         column = pl.multiple_of(starts[first + at], 128)
-        return pltpu.make_async_copy(slots.at[at], out_ref.at[:, :, pl.ds(column, width)], sems.at[at])
+        return pltpu.make_async_copy(
+            slots.at[at, j], out_ref.at[j, :, pl.ds(column, width)], sems.at[3 * at + j]
+        )
 
     offset = 0
     for piece_ref, count in zip(pieces, counts):
 
         @pl.loop(0, count)
         def _(q):
-            for at in range(0, width, TILE):
-                for j in range(3):
+            for j in range(3):
+                for at in range(0, width, TILE):
                     for row in range(0, rows, TILE):
                         slots[offset + q, j, row : row + TILE, at : at + TILE] = jnp.dot(
                             x_ref[j * rows + row : j * rows + row + TILE, :],
                             piece_ref[q, :, at : at + TILE],
                             preferred_element_type=jnp.float32,
                         ).astype(slots.dtype)
-            copy(offset + q).start()
+                copy(offset + q, j).start()
 
         offset += count
 
     for at in range(sum(counts)):
-        copy(at).wait()
+        for j in range(3):
+            copy(at, j).wait()
 
 
 def join_grad(starts, first, pieces, x_turned, full_width, into):
@@ -361,7 +362,10 @@
         ),
         in_specs=[IN_SMEM, IN_VMEM] + [ANYWHERE] * len(extra) + [IN_VMEM] * len(pieces),
         out_specs=(ANYWHERE, IN_VMEM),
-        scratch_shapes=[pltpu.VMEM((blocks, 3, rows, width), jnp.bfloat16), pltpu.SemaphoreType.DMA((blocks,))],
+        scratch_shapes=[
+            pltpu.VMEM((blocks, 3, rows, width), jnp.bfloat16),
+            pltpu.SemaphoreType.DMA((3 * blocks,)),
+        ],
         input_output_aliases={2: 0} if extra else {},
         name="join_grad",
         **settings(6 * tokens * rows * width * blocks, 6 * rows * width * blocks, 14 * MIB),
@@ -427,9 +431,7 @@
     for bit in range(3, bits - 1):
         half = total.shape[1] // 2
         total = total[:, :half] + unpack(exchange(pack(total[:, half:]), 1 << bit, size))
-    passed = exchange(pack(total), 1 << (bits - 1), size)
-    token = work(bits - 1, total, None)
-    return total + with_token(unpack(jnp.stack([passed[1], passed[0]])), token)
+    return total
 
 
 def gather(held, bits, size, work):
@@ -491,14 +493,21 @@
             held["lm"], token = stage(w_lm, after, rows)
         return token
 
-    joined = reduce_halves(low, high, join_rest, bits, size, lambda x: x, lambda x: x, bring_head)
+    total = reduce_halves(low, high, join_rest, bits, size, lambda x: x, lambda x: x, bring_head)
+    partner = 1 << (bits - 1)
+
+    def finish(total, pack, unpack, beside):
+        passed = unpack(exchange(pack(total), partner, size))
+        return total + with_token(jnp.stack([passed[1], passed[0]]), beside(total))
+
+    joined = finish(total, lambda x: x, lambda x: x, lambda after: None)
 
     squares = jnp.sum(joined * joined, axis=(1, 3))
     squares = squares[0] + squares[1]
     for group in sum_rounds(bits - 1):
         squares = tree_sum(contributions(squares, group, size))
     inv_rms = lax.rsqrt(squares / full_width + epsilon)[:, None]
-    gains = jnp.stack([gain, exchange(gain, 1 << (bits - 1), size)])[:, None, None, :]
+    gains = jnp.stack([gain, exchange(gain, partner, size)])[:, None, None, :]
     normed = (joined * inv_rms * gains).astype(jnp.bfloat16)
 
     all_normed, all_dfused = [], []
@@ -554,16 +563,6 @@
     def back_last(after):
         return back_rest(order, 0, quarter, dlogits, held["lm"], rows, after) if kernels else (left, None)
 
-    def fill_grad_lm(k, after, token):
-        if kernels and k != 2:
-            middle = len(all_normed) - 4
-            pieces = all_normed[:middle] if k == 1 else all_normed[middle:]
-            first = 0 if k == 1 else sum(p.shape[0] for p in all_normed[:middle])
-            held["grad_lm"], token = head_grad(
-                starts, first, pieces, dlogits, full_width, after, held["grad_lm"]
-            )
-        return token
-
     scale = HALF_SCALE * (tokens / 128)
 
     def pack_half(x):
@@ -572,7 +571,17 @@
     def unpack_half(x):
         return x.astype(jnp.float32) * (1.0 / scale)
 
-    dnormed = reduce_halves(low, high, back_last, bits, size, pack_half, unpack_half, fill_grad_lm)
+    def nothing(k, after, token):
+        return token
+
+    total = reduce_halves(low, high, back_last, bits, size, pack_half, unpack_half, nothing)
+
+    def fill_grad_lm(after):
+        if kernels:
+            held["grad_lm"], token = head_grad(starts, all_normed, dlogits, full_width, after)
+            return token
+
+    dnormed = finish(total, pack_half, unpack_half, fill_grad_lm)
     if kernels:
         grad_lm = held["grad_lm"]
     else:

time: 184 us -> 184 us (level)
  Pallas kernels: 65.6 us -> 62.7 us
  waiting for transfers between devices: 64.9 us -> 67.4 us
    ppermute x36, waiting for transfers between devices: 53.7 us -> 56.2 us  [exchange(): return lax.ppermute(x, 'section', [(i, i ^ mask) for i in range(size)])]
    pallas_call x2 -> x1, Pallas kernels: 10.8 us -> 9.35 us  [head_grad(): pl.pallas_call(functools.partial(head_grad_kernel, counts), out_shape=(ja...]
  transfers between devices with their start and end apart: 37 -> 37, of which waited for: 22 -> 23; matrix products, arithmetic and copies ran while one was open for 2% -> 2% of each run, Pallas kernels for 26% -> 25%
where the time goes in v7:
time: 184 us; the launch traced here: 183 us
  waiting for transfers between devices  67.4 us (37%)
  Pallas kernels  62.7 us (34%)
  starting transfers between devices  44.2 us (24%)
  other arithmetic  7.59 us (4%)
    ppermute x36, waiting for transfers between devices, exchange(): return lax.ppermute(x, 'section', [(i, i ^ mask) for i in range(size)])  56.2 us
    ppermute x36, starting transfers between devices, exchange(): return lax.ppermute(x, 'section', [(i, i ^ mask) for i in range(size)])  36.8 us
    pallas_call x4, Pallas kernels, join_grad(): pl.pallas_call(functools.partial(join_grad_kernel, first, counts, len(ext...  16 us
    pallas_call x3, Pallas kernels, join(): pl.pallas_call(functools.partial(join_kernel, first, count), out_shape=tu...  14 us
    all_to_all x1, waiting for transfers between devices, on_device(): lax.all_to_all(sent, 'section', split_axis=0, concat_axis=0, tiled=True)  11.2 us
    pallas_call x1, Pallas kernels, head_grad(): pl.pallas_call(functools.partial(head_grad_kernel, counts), out_shape=(ja...  9.35 us
    pallas_call x4, Pallas kernels, head(): pl.pallas_call(functools.partial(head_kernel, first, counts, last), out_s...  8.35 us
    all_to_all x1, starting transfers between devices, on_device(): lax.all_to_all(sent, 'section', split_axis=0, concat_axis=0, tiled=True)  7.35 us
  transfers between devices with their start and end apart: 37, of which 23 were waited for; matrix products, arithmetic and copies ran while one was open for 2% of the time, Pallas kernels for 25%

profile of v7, /device:TPU:1, one launch (start us, length us, event | category | flops | bytes accessed | tf_op | source)
XLA Modules:
  0.0 183.5 jit_solution(15896402815912267686)
XLA Ops:
  0.6 1.8 maximum_bitcast_fusion.after_ref
  2.4 7.3 %all-to-all-start = ((bf16[16,8,1536]{2,1,0:T(8,128)(2,1)}), bf16[16,8,1536]{2,1,0:T(8,128)(2,1)S(1)}, u32[]{:S(2)}, u32[]{:S(2)}) async-start(bf16[16,8,1536]{2,1,0:T(8,128)(2,1)} %maximum_bitcast_fusion.after_ref), calls=%async_computation | async-start | bytes 786432 | tf_op jit(solution)/shard_map/all_to_all | solution.py:478
  10.5 11.2 %all-to-all-done = bf16[16,8,1536]{2,1,0:T(8,128)(2,1)S(1)} async-done(((bf16[16,8,1536]{2,1,0:T(8,128)(2,1)}), bf16[16,8,1536]{2,1,0:T(8,128)(2,1)S(1)}, u32[]{:S(2)}, u32[]{:S(2)}) %all-to-all-start) | async-done | bytes 393248 | tf_op jit(solution)/shard_map/all_to_all | solution.py:478
  21.7 5.9 %join.4 = (f32[2,4,128,512]{3,2,1,0:T(8,128)S(1)}, f32[1,512]{1,0:T(1,128)}, bf16[1536,128]{1,0:T(8,128)(2,1)S(1)}) custom-call(s32[2,8]{1,0:T(2,128)S(1)} %xor_multiply_fusion.order, bf16[128,1536]{1,0:T(8,128)(2,1)S(1)} %bitcast.164, bf16[3,512,8192]{2,1,0:T(8,128)(2,1)} %w_ref.6, bf16[16,8,1536]{2,1,0:T(8,128)(2,1)} %maximum_bitcast_fusion.after_ref), custom_call_target="tpu_custom_call" | custom-call | flops 1610612736 | bytes 12582912 | tf_op jit(solution)/shard_map/join/pallas_call | solution.py:143
  28.1 4.0 %join.3 = (f32[2,2,128,512]{3,2,1,0:T(8,128)S(1)}, f32[1,512]{1,0:T(1,128)}) custom-call(s32[2,8]{1,0:T(2,128)S(1)} %xor_multiply_fusion.order, bf16[128,1536]{1,0:T(8,128)(2,1)S(1)} %bitcast.165, bf16[3,512,8192]{2,1,0:T(8,128)(2,1)} %w_ref.6, bf16[16,8,1536]{2,1,0:T(8,128)(2,1)} %maximum_bitcast_fusion.after_ref), custom_call_target="tpu_custom_call" | custom-call | flops 805306368 | bytes 6291456 | tf_op jit(solution)/shard_map/join/pallas_call | solution.py:143
  33.8 4.0 %join.5 = (f32[2,2,128,512]{3,2,1,0:T(8,128)S(1)}, f32[1,512]{1,0:T(1,128)}) custom-call(s32[2,8]{1,0:T(2,128)S(1)} %xor_multiply_fusion.order, bf16[128,1536]{1,0:T(8,128)(2,1)S(1)} %bitcast.166, bf16[3,512,8192]{2,1,0:T(8,128)(2,1)} %w_ref.6, f32[2,2,128,512]{3,2,1,0:T(8,128)S(1)} %slice_add_fusion.3.after_ref), custom_call_target="tpu_custom_call" | custom-call | flops 805306368 | bytes 6291456 | tf_op jit(solution)/shard_map/join/pallas_call | solution.py:143
  37.8 5.9 %stage.1 = (bf16[8192,1024]{1,0:T(8,128)(2,1)S(1)}, f32[1,512]{1,0:T(1,128)S(1)}) custom-call(bf16[8192,1024]{1,0:T(8,128)(2,1)} %w_ref.7, f32[2,2,128,512]{3,2,1,0:T(8,128)S(1)} %get-tuple-element.32.after_ref), custom_call_target="tpu_custom_call" | custom-call | bytes 16777216 | tf_op jit(solution)/shard_map/stage/pallas_call | solution.py:91
  43.8 2.3 %collective-permute-done.1 = f32[2,128,512]{2,1,0:T(8,128)S(1)} collective-permute-done((f32[2,128,512]{2,1,0:T(8,128)S(1)}, f32[2,128,512]{2,1,0:T(8,128)S(1)}, u32[]{:S(2)}, u32[]{:S(2)}) %collective-permute-start.1) | collective-permute-done | bytes 524320 | tf_op jit(solution)/shard_map/ppermute | solution.py:53
  47.8 5.4 %collective-permute-done.3 = f32[1,128,512]{2,1,0:T(8,128)S(1)} collective-permute-done((f32[1,128,512]{2,1,0:T(8,128)S(1)}, f32[1,128,512]{2,1,0:T(8,128)S(1)}, u32[]{:S(2)}, u32[]{:S(2)}) %collective-permute-start.3) | collective-permute-done | bytes 262176 | tf_op jit(solution)/shard_map/ppermute | solution.py:53
  53.3 1.8 collective-permute-start.5
  55.8 22.7 %collective-permute-done.5 = f32[2,1,128,512]{3,2,0,1:T(8,128)S(1)} collective-permute-done((f32[2,1,128,512]{3,2,0,1:T(8,128)S(1)}, f32[2,1,128,512]{3,2,0,1:T(8,128)S(1)}, u32[]{:S(2)}, u32[]{:S(2)}) %collective-permute-start.5) | collective-permute-done | bytes 524320 | tf_op jit(solution)/shard_map/ppermute | solution.py:53
  83.4 3.2 %collective-permute-start.9 = (f32[128]{0:T(128)S(1)}, f32[128]{0:T(128)S(1)}, u32[]{:S(2)}, u32[]{:S(2)}) collective-permute-start(f32[128]{0:T(128)S(1)} %add_add_fusion.3), channel_id=1, source_target_pairs={{0,1},{1,0},{2,3},{3,2},{4,5},{5,4},{6,7},{7,6},{8,9},{9,8},{10,11... | collective-permute-start | bytes 1544 | tf_op jit(solution)/shard_map/ppermute | solution.py:53
  95.8 2.5 %head.5 = (f32[128,1024]{1,0:T(8,128)S(1)}, f32[1,512]{1,0:T(1,128)S(1)}) custom-call(s32[17]{0:T(128)S(1)} %pad_add_fusion.starts, bf16[8192,1024]{1,0:T(8,128)(2,1)S(1)} %get-tuple-element.33.w_ref, f32[128,1024]{1,0:T(8,128)S(1)} %get-tuple-element.35.before_ref, s32[1,128]{1,0:T(1,128)S(1)} %bitcast.179, bf16[2,128,512]{2,1,0:T(8,128)(2,1)S(1)} %bitcast.172, ...), custom_call_target="tpu_custom_call" | custom-call | flops 805306368 | bytes 1048576 | tf_op jit(solution)/shard_map/head/pallas_call | solution.py:202
  98.3 3.5 %collective-permute-done.15 = bf16[2,128,512]{2,1,0:T(8,128)(2,1)S(1)} collective-permute-done((bf16[2,128,512]{2,1,0:T(8,128)(2,1)S(1)}, bf16[2,128,512]{2,1,0:T(8,128)(2,1)S(1)}, u32[]{:S(2)}, u32[]{:S(2)}) %collective-permute-start.15) | collective-permute-done | bytes 262176 | tf_op jit(solution)/shard_map/ppermute | solution.py:53
  103.9 2.4 %head.6 = (f32[128,1024]{1,0:T(8,128)S(1)}, f32[1,512]{1,0:T(1,128)}) custom-call(s32[17]{0:T(128)S(1)} %pad_add_fusion.starts, bf16[8192,1024]{1,0:T(8,128)(2,1)S(1)} %get-tuple-element.33.w_ref, f32[128,1024]{1,0:T(8,128)S(1)} %get-tuple-element.37.before_ref, s32[1,128]{1,0:T(1,128)S(1)} %bitcast.180, bf16[4,128,512]{2,1,0:T(8,128)(2,1)S(1)} %fusion.2.rest_0_.rest_4_), custom_call_target="tpu_custom_call" | custom-call | flops 536870912 | bytes 1048576 | tf_op jit(solution)/shard_map/head/pallas_call | solution.py:202
  106.4 2.2 %head.7 = (f32[128,1024]{1,0:T(8,128)S(1)}, f32[8,128]{1,0:T(8,128)S(1)}) custom-call(s32[17]{0:T(128)S(1)} %pad_add_fusion.starts, bf16[8192,1024]{1,0:T(8,128)(2,1)S(1)} %get-tuple-element.33.w_ref, f32[128,1024]{1,0:T(8,128)S(1)} %get-tuple-element.39.before_ref, s32[1,128]{1,0:T(1,128)S(1)} %bitcast.181, bf16[4,128,512]{2,1,0:T(8,128)(2,1)S(1)} %bitcast.169), custom_call_target="tpu_custom_call" | custom-call | flops 536870912 | bytes 1048576 | tf_op jit(solution)/shard_map/head/pallas_call | solution.py:202
  108.6 2.4 %collective-permute-start.18 = (f32[4,128]{1,0:T(4,128)S(1)}, f32[4,128]{1,0:T(4,128)S(1)}, u32[]{:S(2)}, u32[]{:S(2)}) collective-permute-start(f32[4,128]{1,0:T(4,128)S(1)} %slice.203), channel_id=1, source_target_pairs={{0,8},{1,9},{2,10},{3,11},{4,12},{5,13},{6,14},{7,15},{8,0},{9,1},... | collective-permute-start | bytes 6152 | tf_op jit(solution)/shard_map/ppermute | solution.py:53
  112.0 1.7 collective-permute-start.21
  116.5 2.8 %collective-permute-start.22 = (f32[4,128]{1,0:T(4,128)S(1)}, f32[4,128]{1,0:T(4,128)S(1)}, u32[]{:S(2)}, u32[]{:S(2)}) collective-permute-start(f32[4,128]{1,0:T(4,128)S(1)} %pad_maximum_fusion.4), channel_id=1, source_target_pairs={{0,1},{1,0},{2,3},{3,2},{4,5},{5,4},{6,7},{7,6},{8,9},{9,8},{10,11... | collective-permute-start | bytes 6152 | tf_op jit(solution)/shard_map/ppermute | solution.py:53
  120.1 4.2 %back_first.1 = (f32[2,4,128,512]{3,2,1,0:T(8,128)S(1)}, bf16[128,1024]{1,0:T(8,128)(2,1)S(1)}) custom-call(s32[2,8]{1,0:T(2,128)S(1)} %xor_multiply_fusion.order, s32[17]{0:T(128)S(1)} %pad_add_fusion.starts, f32[128,1024]{1,0:T(8,128)S(1)} %get-tuple-element.42.logits_ref, f32[8,128]{1,0:T(8,128)S(1)} %broadcast_in_dim.11.stats_ref, ...), custom_call_target="tpu_custom_call" | custom-call | flops 1073741824 | bytes 2097152 | tf_op jit(solution)/shard_map/back_first/pallas_call | solution.py:239
  125.0 2.6 %back_rest.2 = (f32[2,2,128,512]{3,2,1,0:T(8,128)S(1)}, f32[1,512]{1,0:T(1,128)}) custom-call(s32[2,8]{1,0:T(2,128)S(1)} %xor_multiply_fusion.order, bf16[128,1024]{1,0:T(8,128)(2,1)S(1)} %get-tuple-element.43.d_ref, bf16[8192,1024]{1,0:T(8,128)(2,1)S(1)} %get-tuple-element.33.w_ref, f32[2,4,128,512]{3,2,1,0:T(8,128)S(1)} %get-tuple-element.44.after_ref), custom_call_target="tpu_custom_call" | custom-call | flops 536870912 | bytes 1048576 | tf_op jit(solution)/shard_map/back_rest/pallas_call | solution.py:256
  130.2 2.2 %back_rest.3 = (f32[2,2,128,512]{3,2,1,0:T(8,128)S(1)}, f32[1,512]{1,0:T(1,128)S(1)}) custom-call(s32[2,8]{1,0:T(2,128)S(1)} %xor_multiply_fusion.order, bf16[128,1024]{1,0:T(8,128)(2,1)S(1)} %get-tuple-element.43.d_ref, bf16[8192,1024]{1,0:T(8,128)(2,1)S(1)} %get-tuple-element.33.w_ref, f32[2,2,128,512]{3,2,1,0:T(8,128)S(1)} %slice_add_fusion.1.after_ref), custom_call_target="tpu_custom_call" | custom-call | flops 536870912 | bytes 1048576 | tf_op jit(solution)/shard_map/back_rest/pallas_call | solution.py:256
  132.4 3.7 %collective-permute-done.24 = f16[2,128,512]{2,1,0:T(8,128)(2,1)S(1)} collective-permute-done((f16[2,128,512]{2,1,0:T(8,128)(2,1)S(1)}, f16[2,128,512]{2,1,0:T(8,128)(2,1)S(1)}, u32[]{:S(2)}, u32[]{:S(2)}) %collective-permute-start.24) | collective-permute-done | bytes 262176 | tf_op jit(solution)/shard_map/ppermute | solution.py:53
  139.0 1.9 %collective-permute-done.26 = f16[1,128,512]{2,1,0:T(8,128)(2,1)S(1)} collective-permute-done((f16[1,128,512]{2,1,0:T(8,128)(2,1)S(1)}, f16[1,128,512]{2,1,0:T(8,128)(2,1)S(1)}, u32[]{:S(2)}, u32[]{:S(2)}) %collective-permute-start.26) | collective-permute-done | bytes 131104 | tf_op jit(solution)/shard_map/ppermute | solution.py:53
  143.7 9.4 %head_grad.1 = (bf16[8192,1024]{1,0:T(8,128)(2,1)}, f32[1,512]{1,0:T(1,128)S(1)}) custom-call(s32[17]{0:T(128)S(1)} %pad_add_fusion.starts, bf16[128,1024]{1,0:T(8,128)(2,1)S(1)} %get-tuple-element.43.d_ref, f32[2,1,128,512]{3,2,1,0:T(8,128)S(1)} %get-tuple-element.67.after_ref, bf16[2,128,512]{2,1,0:T(8,128)(2,1)S(1)} %fusion.32.rest_0_, ...), custom_call_target="tpu_custom_call" | custom-call | flops 2147483648 | bytes 16777216 | tf_op jit(solution)/shard_map/head_grad/pallas_call | solution.py:303
  153.0 3.6 %collective-permute-done.28 = f16[2,1,128,512]{3,2,0,1:T(8,128)(2,1)S(1)} collective-permute-done((f16[2,1,128,512]{3,2,0,1:T(8,128)(2,1)S(1)}, f16[2,1,128,512]{3,2,0,1:T(8,128)(2,1)S(1)}, u32[]{:S(2)}, u32[]{:S(2)}) %collective-permute-start.28) | collective-permute-done | bytes 262176 | tf_op jit(solution)/shard_map/ppermute | solution.py:53
  159.8 2.6 %join_grad.4 = (bf16[3,512,8192]{2,1,0:T(8,128)(2,1)}, f32[1,512]{1,0:T(1,128)S(1)}) custom-call(s32[17]{0:T(128)S(1)} %pad_add_fusion.starts, bf16[1536,128]{1,0:T(8,128)(2,1)S(1)} %get-tuple-element.41.x_ref, bf16[2,128,512]{2,1,0:T(8,128)(2,1)S(1)} %bitcast.168), custom_call_target="tpu_custom_call" | custom-call | flops 402653184 | bytes 3145728 | tf_op jit(solution)/shard_map/join_grad/pallas_call | solution.py:357
  162.8 1.7 collective-permute-start.32
  165.7 4.9 %join_grad.5 = (bf16[3,512,8192]{2,1,0:T(8,128)(2,1)}, f32[1,512]{1,0:T(1,128)S(1)}) custom-call(s32[17]{0:T(128)S(1)} %pad_add_fusion.starts, bf16[1536,128]{1,0:T(8,128)(2,1)S(1)} %get-tuple-element.41.x_ref, bf16[3,512,8192]{2,1,0:T(8,128)(2,1)} %get-tuple-element.49.rest_0_, bf16[2,128,512]{2,1,0:T(8,128)(2,1)S(1)} %bitcast.176, ...), custom_call_target="tpu_custom_call", output_to_operand_aliasing={{0}: (2, {})} | custom-call | flops 1207959552 | bytes 9437184 | tf_op jit(solution)/shard_map/join_grad/pallas_call | solution.py:357
  170.6 2.0 %collective-permute-done.33 = bf16[2,128,512]{2,1,0:T(8,128)(2,1)S(1)} collective-permute-done((bf16[2,128,512]{2,1,0:T(8,128)(2,1)S(1)}, bf16[2,128,512]{2,1,0:T(8,128)(2,1)S(1)}, u32[]{:S(2)}, u32[]{:S(2)}) %collective-permute-start.33) | collective-permute-done | bytes 262176 | tf_op jit(solution)/shard_map/ppermute | solution.py:53
  174.7 4.3 %join_grad.6 = (bf16[3,512,8192]{2,1,0:T(8,128)(2,1)}, f32[1,512]{1,0:T(1,128)}) custom-call(s32[17]{0:T(128)S(1)} %pad_add_fusion.starts, bf16[1536,128]{1,0:T(8,128)(2,1)S(1)} %get-tuple-element.41.x_ref, bf16[3,512,8192]{2,1,0:T(8,128)(2,1)} %get-tuple-element.51.rest_0_, bf16[4,128,512]{2,1,0:T(8,128)(2,1)S(1)} %fusion.1.rest_1_), custom_call_target="tpu_custom_call", output_to_operand_aliasing={{0}: (2, {})} | custom-call | flops 805306368 | bytes 6291456 | tf_op jit(solution)/shard_map/join_grad/pallas_call | solution.py:357
  179.0 4.3 %join_grad.7 = (bf16[3,512,8192]{2,1,0:T(8,128)(2,1)}, f32[1,512]{1,0:T(1,128)}) custom-call(s32[17]{0:T(128)S(1)} %pad_add_fusion.starts, bf16[1536,128]{1,0:T(8,128)(2,1)S(1)} %get-tuple-element.41.x_ref, bf16[3,512,8192]{2,1,0:T(8,128)(2,1)} %get-tuple-element.53.rest_0_, bf16[4,128,512]{2,1,0:T(8,128)(2,1)S(1)} %bitcast.171), custom_call_target="tpu_custom_call", output_to_operand_aliasing={{0}: (2, {})} | custom-call | flops 805306368 | bytes 6291456 | tf_op jit(solution)/shard_map/join_grad/pallas_call | solution.py:357
  (122 shorter events, 41.6 us)
Async XLA Ops:
  2.4 19.3 %all-to-all-start = ((bf16[16,8,1536]{2,1,0:T(8,128)(2,1)}), bf16[16,8,1536]{2,1,0:T(8,128)(2,1)S(1)}, u32[]{:S(2)}, u32[]{:S(2)}) async-start(bf16[16,8,1536]{2,1,0:T(8,128)(2,1)} %maximum_bitcast_fusion.after_ref), calls=%async_computation | async-start | bytes 786432 | tf_op jit(solution)/shard_map/all_to_all | solution.py:478
  27.6 4.5 %collective-permute-start = (f32[2,4,128,512]{3,2,1,0:T(8,128)S(1)}, f32[2,4,128,512]{3,2,1,0:T(8,128)S(1)}, u32[]{:S(2)}, u32[]{:S(2)}) collective-permute-start(f32[2,4,128,512]{3,2,1,0:T(8,128)S(1)} %get-tuple-element.31), channel_id=1, source_target_pairs={{0,1},{1,0},{2,3},{3,2},{4,5},{5,4},{6,7},{7,6},{8,9},{9,8},{10,11... | collective-permute-start | bytes 6291464 | tf_op jit(solution)/shard_map/ppermute | solution.py:53
  32.5 13.6 %collective-permute-start.1 = (f32[2,128,512]{2,1,0:T(8,128)S(1)}, f32[2,128,512]{2,1,0:T(8,128)S(1)}, u32[]{:S(2)}, u32[]{:S(2)}) collective-permute-start(f32[2,128,512]{2,1,0:T(8,128)S(1)} %get-tuple-element.72), channel_id=1, source_target_pairs={{0,2},{1,3},{2,0},{3,1},{4,6},{5,7},{6,4},{7,5},{8,10},{9,11},{10,... | collective-permute-start | bytes 1572872 | tf_op jit(solution)/shard_map/ppermute | solution.py:53
  32.8 13.2 %collective-permute-start.2 = (f32[2,128,512]{2,1,0:T(8,128)S(1)}, f32[2,128,512]{2,1,0:T(8,128)S(1)}, u32[]{:S(2)}, u32[]{:S(2)}) collective-permute-start(f32[2,128,512]{2,1,0:T(8,128)S(1)} %get-tuple-element.73), channel_id=1, source_target_pairs={{0,4},{1,5},{2,6},{3,7},{4,0},{5,1},{6,2},{7,3},{8,12},{9,13},{10,... | collective-permute-start | bytes 1572872 | tf_op jit(solution)/shard_map/ppermute | solution.py:53
  46.5 6.8 %collective-permute-start.3 = (f32[1,128,512]{2,1,0:T(8,128)S(1)}, f32[1,128,512]{2,1,0:T(8,128)S(1)}, u32[]{:S(2)}, u32[]{:S(2)}) collective-permute-start(f32[1,128,512]{2,1,0:T(8,128)S(1)} %get-tuple-element.70), channel_id=1, source_target_pairs={{0,4},{1,5},{2,6},{3,7},{4,0},{5,1},{6,2},{7,3},{8,12},{9,13},{10,... | collective-permute-start | bytes 786440 | tf_op jit(solution)/shard_map/ppermute | solution.py:53
  47.2 6.1 %collective-permute-start.4 = (f32[1,128,512]{2,1,0:T(8,128)S(1)}, f32[1,128,512]{2,1,0:T(8,128)S(1)}, u32[]{:S(2)}, u32[]{:S(2)}) collective-permute-start(f32[1,128,512]{2,1,0:T(8,128)S(1)} %get-tuple-element.71), channel_id=1, source_target_pairs={{0,2},{1,3},{2,0},{3,1},{4,6},{5,7},{6,4},{7,5},{8,10},{9,11},{10,... | collective-permute-start | bytes 786440 | tf_op jit(solution)/shard_map/ppermute | solution.py:53
  53.3 25.1 %collective-permute-start.5 = (f32[2,1,128,512]{3,2,0,1:T(8,128)S(1)}, f32[2,1,128,512]{3,2,0,1:T(8,128)S(1)}, u32[]{:S(2)}, u32[]{:S(2)}) collective-permute-start(f32[2,1,128,512]{3,2,0,1:T(8,128)S(1)} %fusion.5), channel_id=1, source_target_pairs={{0,8},{1,9},{2,10},{3,11},{4,12},{5,13},{6,14},{7,15},{8,0},{9,1},... | collective-permute-start | bytes 1572872 | tf_op jit(solution)/shard_map/ppermute | solution.py:53
  55.1 31.4 %collective-permute-start.10 = (f32[512]{0:T(512)S(1)}, f32[512]{0:T(512)S(1)}, u32[]{:S(2)}, u32[]{:S(2)}) collective-permute-start(f32[512]{0:T(512)S(1)} %copy-done.1), channel_id=1, source_target_pairs={{0,8},{1,9},{2,10},{3,11},{4,12},{5,13},{6,14},{7,15},{8,0},{9,1},... | collective-permute-start | bytes 6152 | tf_op jit(solution)/shard_map/ppermute | solution.py:53
  79.5 3.3 %collective-permute-start.8 = (f32[128]{0:T(128)S(1)}, f32[128]{0:T(128)S(1)}, u32[]{:S(2)}, u32[]{:S(2)}) collective-permute-start(f32[128]{0:T(128)S(1)} %add_bitcast_fusion.1), channel_id=1, source_target_pairs={{0,6},{1,7},{2,4},{3,5},{4,2},{5,3},{6,0},{7,1},{8,14},{9,15},{10,... | collective-permute-start | bytes 1544 | tf_op jit(solution)/shard_map/ppermute | solution.py:53
  83.4 4.0 %collective-permute-start.9 = (f32[128]{0:T(128)S(1)}, f32[128]{0:T(128)S(1)}, u32[]{:S(2)}, u32[]{:S(2)}) collective-permute-start(f32[128]{0:T(128)S(1)} %add_add_fusion.3), channel_id=1, source_target_pairs={{0,1},{1,0},{2,3},{3,2},{4,5},{5,4},{6,7},{7,6},{8,9},{9,8},{10,11... | collective-permute-start | bytes 1544 | tf_op jit(solution)/shard_map/ppermute | solution.py:53
  87.7 4.8 %collective-permute-start.12 = (bf16[1,128,512]{2,1,0:T(8,128)(2,1)S(1)}, bf16[1,128,512]{2,1,0:T(8,128)(2,1)S(1)}, u32[]{:S(2)}, u32[]{:S(2)}) collective-permute-start(bf16[1,128,512]{2,1,0:T(8,128)(2,1)S(1)} %get-tuple-element.82), channel_id=1, source_target_pairs={{0,4},{1,5},{2,6},{3,7},{4,0},{5,1},{6,2},{7,3},{8,12},{9,13},{10,... | collective-permute-start | bytes 393224 | tf_op jit(solution)/shard_map/ppermute | solution.py:53
  87.7 4.8 %collective-permute-start.13 = (bf16[1,128,512]{2,1,0:T(8,128)(2,1)S(1)}, bf16[1,128,512]{2,1,0:T(8,128)(2,1)S(1)}, u32[]{:S(2)}, u32[]{:S(2)}) collective-permute-start(bf16[1,128,512]{2,1,0:T(8,128)(2,1)S(1)} %get-tuple-element.83), channel_id=1, source_target_pairs={{0,2},{1,3},{2,0},{3,1},{4,6},{5,7},{6,4},{7,5},{8,10},{9,11},{10,... | collective-permute-start | bytes 393224 | tf_op jit(solution)/shard_map/ppermute | solution.py:53
  88.8 7.0 %collective-permute-start.11 = (bf16[2,1,128,512]{3,2,0,1:T(8,128)(2,1)S(1)}, bf16[2,1,128,512]{3,2,0,1:T(8,128)(2,1)S(1)}, u32[]{:S(2)}, u32[]{:S(2)}) collective-permute-start(bf16[2,1,128,512]{3,2,0,1:T(8,128)(2,1)S(1)} %multiply_convert_fusion.7), channel_id=1, source_target_pairs={{0,1},{1,0},{2,3},{3,2},{4,5},{5,4},{6,7},{7,6},{8,9},{9,8},{10,11... | collective-permute-start | bytes 786440 | tf_op jit(solution)/shard_map/ppermute | solution.py:53
  92.6 3.3 %collective-permute-start.14 = (bf16[2,1,128,512]{3,2,0,1:T(8,128)(2,1)S(1)}, bf16[2,1,128,512]{3,2,0,1:T(8,128)(2,1)S(1)}, u32[]{:S(2)}, u32[]{:S(2)}) collective-permute-start(bf16[2,1,128,512]{3,2,0,1:T(8,128)(2,1)S(1)} %multiply_convert_fusion.5), channel_id=1, source_target_pairs={{0,1},{1,0},{2,3},{3,2},{4,5},{5,4},{6,7},{7,6},{8,9},{9,8},{10,11... | collective-permute-start | bytes 786440 | tf_op jit(solution)/shard_map/ppermute | solution.py:53
  93.9 8.0 %collective-permute-start.15 = (bf16[2,128,512]{2,1,0:T(8,128)(2,1)S(1)}, bf16[2,128,512]{2,1,0:T(8,128)(2,1)S(1)}, u32[]{:S(2)}, u32[]{:S(2)}) collective-permute-start(bf16[2,128,512]{2,1,0:T(8,128)(2,1)S(1)} %get-tuple-element.78), channel_id=1, source_target_pairs={{0,2},{1,3},{2,0},{3,1},{4,6},{5,7},{6,4},{7,5},{8,10},{9,11},{10,... | collective-permute-start | bytes 786440 | tf_op jit(solution)/shard_map/ppermute | solution.py:53
  94.8 7.6 %collective-permute-start.16 = (bf16[2,128,512]{2,1,0:T(8,128)(2,1)S(1)}, bf16[2,128,512]{2,1,0:T(8,128)(2,1)S(1)}, u32[]{:S(2)}, u32[]{:S(2)}) collective-permute-start(bf16[2,128,512]{2,1,0:T(8,128)(2,1)S(1)} %get-tuple-element.79), channel_id=1, source_target_pairs={{0,4},{1,5},{2,6},{3,7},{4,0},{5,1},{6,2},{7,3},{8,12},{9,13},{10,... | collective-permute-start | bytes 786440 | tf_op jit(solution)/shard_map/ppermute | solution.py:53
  102.5 3.8 %collective-permute-start.17 = (bf16[2,2,128,512]{3,2,1,0:T(8,128)(2,1)S(1)}, bf16[2,2,128,512]{3,2,1,0:T(8,128)(2,1)S(1)}, u32[]{:S(2)}, u32[]{:S(2)}) collective-permute-start(bf16[2,2,128,512]{3,2,1,0:T(8,128)(2,1)S(1)} %multiply_convert_fusion.2), channel_id=1, source_target_pairs={{0,1},{1,0},{2,3},{3,2},{4,5},{5,4},{6,7},{7,6},{8,9},{9,8},{10,11... | collective-permute-start | bytes 1572872 | tf_op jit(solution)/shard_map/ppermute | solution.py:53
  108.6 3.4 %collective-permute-start.18 = (f32[4,128]{1,0:T(4,128)S(1)}, f32[4,128]{1,0:T(4,128)S(1)}, u32[]{:S(2)}, u32[]{:S(2)}) collective-permute-start(f32[4,128]{1,0:T(4,128)S(1)} %slice.203), channel_id=1, source_target_pairs={{0,8},{1,9},{2,10},{3,11},{4,12},{5,13},{6,14},{7,15},{8,0},{9,1},... | collective-permute-start | bytes 6152 | tf_op jit(solution)/shard_map/ppermute | solution.py:53
  112.0 3.4 %collective-permute-start.21 = (f32[4,128]{1,0:T(4,128)S(1)}, f32[4,128]{1,0:T(4,128)S(1)}, u32[]{:S(2)}, u32[]{:S(2)}) collective-permute-start(f32[4,128]{1,0:T(4,128)S(1)} %pad_maximum_fusion.3), channel_id=1, source_target_pairs={{0,6},{1,7},{2,4},{3,5},{4,2},{5,3},{6,0},{7,1},{8,14},{9,15},{10,... | collective-permute-start | bytes 6152 | tf_op jit(solution)/shard_map/ppermute | solution.py:53
  116.5 3.6 %collective-permute-start.22 = (f32[4,128]{1,0:T(4,128)S(1)}, f32[4,128]{1,0:T(4,128)S(1)}, u32[]{:S(2)}, u32[]{:S(2)}) collective-permute-start(f32[4,128]{1,0:T(4,128)S(1)} %pad_maximum_fusion.4), channel_id=1, source_target_pairs={{0,1},{1,0},{2,3},{3,2},{4,5},{5,4},{6,7},{7,6},{8,9},{9,8},{10,11... | collective-permute-start | bytes 6152 | tf_op jit(solution)/shard_map/ppermute | solution.py:53
  124.6 3.0 %collective-permute-start.23 = (f16[2,4,128,512]{3,2,1,0:T(8,128)(2,1)S(1)}, f16[2,4,128,512]{3,2,1,0:T(8,128)(2,1)S(1)}, u32[]{:S(2)}, u32[]{:S(2)}) collective-permute-start(f16[2,4,128,512]{3,2,1,0:T(8,128)(2,1)S(1)} %multiply_convert_fusion), channel_id=1, source_target_pairs={{0,1},{1,0},{2,3},{3,2},{4,5},{5,4},{6,7},{7,6},{8,9},{9,8},{10,11... | collective-permute-start | bytes 3145736 | tf_op jit(solution)/shard_map/ppermute | solution.py:53
  128.3 7.8 %collective-permute-start.24 = (f16[2,128,512]{2,1,0:T(8,128)(2,1)S(1)}, f16[2,128,512]{2,1,0:T(8,128)(2,1)S(1)}, u32[]{:S(2)}, u32[]{:S(2)}) collective-permute-start(f16[2,128,512]{2,1,0:T(8,128)(2,1)S(1)} %get-tuple-element.68), channel_id=1, source_target_pairs={{0,2},{1,3},{2,0},{3,1},{4,6},{5,7},{6,4},{7,5},{8,10},{9,11},{10,... | collective-permute-start | bytes 786440 | tf_op jit(solution)/shard_map/ppermute | solution.py:53
  129.2 7.4 %collective-permute-start.25 = (f16[2,128,512]{2,1,0:T(8,128)(2,1)S(1)}, f16[2,128,512]{2,1,0:T(8,128)(2,1)S(1)}, u32[]{:S(2)}, u32[]{:S(2)}) collective-permute-start(f16[2,128,512]{2,1,0:T(8,128)(2,1)S(1)} %get-tuple-element.69), channel_id=1, source_target_pairs={{0,4},{1,5},{2,6},{3,7},{4,0},{5,1},{6,2},{7,3},{8,12},{9,13},{10,... | collective-permute-start | bytes 786440 | tf_op jit(solution)/shard_map/ppermute | solution.py:53
  137.0 3.9 %collective-permute-start.26 = (f16[1,128,512]{2,1,0:T(8,128)(2,1)S(1)}, f16[1,128,512]{2,1,0:T(8,128)(2,1)S(1)}, u32[]{:S(2)}, u32[]{:S(2)}) collective-permute-start(f16[1,128,512]{2,1,0:T(8,128)(2,1)S(1)} %fusion.21), channel_id=1, source_target_pairs={{0,4},{1,5},{2,6},{3,7},{4,0},{5,1},{6,2},{7,3},{8,12},{9,13},{10,... | collective-permute-start | bytes 393224 | tf_op jit(solution)/shard_map/ppermute | solution.py:53
  138.0 4.1 %collective-permute-start.27 = (f16[1,128,512]{2,1,0:T(8,128)(2,1)S(1)}, f16[1,128,512]{2,1,0:T(8,128)(2,1)S(1)}, u32[]{:S(2)}, u32[]{:S(2)}) collective-permute-start(f16[1,128,512]{2,1,0:T(8,128)(2,1)S(1)} %fusion.22), channel_id=1, source_target_pairs={{0,2},{1,3},{2,0},{3,1},{4,6},{5,7},{6,4},{7,5},{8,10},{9,11},{10,... | collective-permute-start | bytes 393224 | tf_op jit(solution)/shard_map/ppermute | solution.py:53
  142.2 14.5 %collective-permute-start.28 = (f16[2,1,128,512]{3,2,0,1:T(8,128)(2,1)S(1)}, f16[2,1,128,512]{3,2,0,1:T(8,128)(2,1)S(1)}, u32[]{:S(2)}, u32[]{:S(2)}) collective-permute-start(f16[2,1,128,512]{3,2,0,1:T(8,128)(2,1)S(1)} %get-tuple-element.66), channel_id=1, source_target_pairs={{0,8},{1,9},{2,10},{3,11},{4,12},{5,13},{6,14},{7,15},{8,0},{9,1},... | collective-permute-start | bytes 786440 | tf_op jit(solution)/shard_map/ppermute | solution.py:53
  157.1 5.3 %collective-permute-start.31 = (bf16[1,128,512]{2,1,0:T(8,128)(2,1)S(1)}, bf16[1,128,512]{2,1,0:T(8,128)(2,1)S(1)}, u32[]{:S(2)}, u32[]{:S(2)}) collective-permute-start(bf16[1,128,512]{2,1,0:T(8,128)(2,1)S(1)} %slice_bitcast_fusion.6), channel_id=1, source_target_pairs={{0,2},{1,3},{2,0},{3,1},{4,6},{5,7},{6,4},{7,5},{8,10},{9,11},{10,... | collective-permute-start | bytes 393224 | tf_op jit(solution)/shard_map/ppermute | solution.py:53
  158.5 4.2 %collective-permute-start.30 = (bf16[1,128,512]{2,1,0:T(8,128)(2,1)S(1)}, bf16[1,128,512]{2,1,0:T(8,128)(2,1)S(1)}, u32[]{:S(2)}, u32[]{:S(2)}) collective-permute-start(bf16[1,128,512]{2,1,0:T(8,128)(2,1)S(1)} %slice_bitcast_fusion.7), channel_id=1, source_target_pairs={{0,4},{1,5},{2,6},{3,7},{4,0},{5,1},{6,2},{7,3},{8,12},{9,13},{10,... | collective-permute-start | bytes 393224 | tf_op jit(solution)/shard_map/ppermute | solution.py:53
  159.0 5.9 %collective-permute-start.29 = (bf16[2,1,128,512]{3,2,0,1:T(8,128)(2,1)S(1)}, bf16[2,1,128,512]{3,2,0,1:T(8,128)(2,1)S(1)}, u32[]{:S(2)}, u32[]{:S(2)}) collective-permute-start(bf16[2,1,128,512]{3,2,0,1:T(8,128)(2,1)S(1)} %get-tuple-element.56), channel_id=1, source_target_pairs={{0,1},{1,0},{2,3},{3,2},{4,5},{5,4},{6,7},{7,6},{8,9},{9,8},{10,11... | collective-permute-start | bytes 786440 | tf_op jit(solution)/shard_map/ppermute | solution.py:53
  164.6 8.0 %collective-permute-start.33 = (bf16[2,128,512]{2,1,0:T(8,128)(2,1)S(1)}, bf16[2,128,512]{2,1,0:T(8,128)(2,1)S(1)}, u32[]{:S(2)}, u32[]{:S(2)}) collective-permute-start(bf16[2,128,512]{2,1,0:T(8,128)(2,1)S(1)} %get-tuple-element.74), channel_id=1, source_target_pairs={{0,2},{1,3},{2,0},{3,1},{4,6},{5,7},{6,4},{7,5},{8,10},{9,11},{10,... | collective-permute-start | bytes 786440 | tf_op jit(solution)/shard_map/ppermute | solution.py:53
  164.9 7.7 %collective-permute-start.34 = (bf16[2,128,512]{2,1,0:T(8,128)(2,1)S(1)}, bf16[2,128,512]{2,1,0:T(8,128)(2,1)S(1)}, u32[]{:S(2)}, u32[]{:S(2)}) collective-permute-start(bf16[2,128,512]{2,1,0:T(8,128)(2,1)S(1)} %get-tuple-element.75), channel_id=1, source_target_pairs={{0,4},{1,5},{2,6},{3,7},{4,0},{5,1},{6,2},{7,3},{8,12},{9,13},{10,... | collective-permute-start | bytes 786440 | tf_op jit(solution)/shard_map/ppermute | solution.py:53
  172.7 6.3 %collective-permute-start.35 = (bf16[2,2,128,512]{3,2,1,0:T(8,128)(2,1)S(1)}, bf16[2,2,128,512]{3,2,1,0:T(8,128)(2,1)S(1)}, u32[]{:S(2)}, u32[]{:S(2)}) collective-permute-start(bf16[2,2,128,512]{3,2,1,0:T(8,128)(2,1)S(1)} %multiply_convert_fusion.1), channel_id=1, source_target_pairs={{0,1},{1,0},{2,3},{3,2},{4,5},{5,4},{6,7},{7,6},{8,9},{9,8},{10,11... | collective-permute-start | bytes 1572872 | tf_op jit(solution)/shard_map/ppermute | solution.py:53
  (8 other events, 42.2 us)

commit v8 on v7

--- a/solution.py
+++ b/solution.py
@@ -35,9 +35,9 @@
         fresh = held ^ (1 << bit)
         held = np.concatenate([held, fresh], axis=1)
         out.append(fresh)
-    first = held ^ np.array([[4], [2]], np.int32)
-    second = np.concatenate([held, first], axis=1) ^ np.array([[2], [4]], np.int32)
-    out += [*across, fresh ^ 1, first, first ^ 1, second, second ^ 1]
+    over_y, over_z = held ^ 2, held ^ 4
+    second = np.stack([over_z[0] ^ 2, over_y[1] ^ 4])
+    out += [*across, fresh ^ 1, over_y, over_z, over_y ^ 1, over_z ^ 1, second, second ^ 1]
     return np.concatenate([p.reshape(-1) for p in out]).astype(np.int32)
 
 
@@ -281,12 +281,9 @@
         def _(q):
             turned = piece_ref[q].T
             for column in range(0, share, TILE):
-                for row in range(0, width, TILE):
-                    slots[offset + q, row : row + TILE, column : column + TILE] = jnp.dot(
-                        turned[row : row + TILE],
-                        d_ref[:, column : column + TILE],
-                        preferred_element_type=jnp.float32,
-                    ).astype(slots.dtype)
+                slots[offset + q, :, column : column + TILE] = jnp.dot(
+                    turned, d_ref[:, column : column + TILE], preferred_element_type=jnp.float32
+                ).astype(slots.dtype)
             copy(offset + q).start()
 
         offset += count
@@ -333,12 +330,11 @@
         def _(q):
             for j in range(3):
                 for at in range(0, width, TILE):
-                    for row in range(0, rows, TILE):
-                        slots[offset + q, j, row : row + TILE, at : at + TILE] = jnp.dot(
-                            x_ref[j * rows + row : j * rows + row + TILE, :],
-                            piece_ref[q, :, at : at + TILE],
-                            preferred_element_type=jnp.float32,
-                        ).astype(slots.dtype)
+                    slots[offset + q, j, :, at : at + TILE] = jnp.dot(
+                        x_ref[j * rows : (j + 1) * rows, :],
+                        piece_ref[q, :, at : at + TILE],
+                        preferred_element_type=jnp.float32,
+                    ).astype(slots.dtype)
                 copy(offset + q, j).start()
 
         offset += count
@@ -446,17 +442,16 @@
         token = work([flat(fresh)], False)
         fresh = with_token(arrived, token)
         held = jnp.concatenate([held, fresh], axis=1)
-    first = [exchange(held[0], 4, size), exchange(held[1], 2, size)]
+    over_y, over_z = exchange(held, 2, size), exchange(held, 4, size)
     across.append(exchange(fresh, 1, size))
-    token = work([flat(fresh)], False)
-    first = with_token(jnp.stack(first), token)
-    across += [first, exchange(first, 1, size)]
-    both = jnp.concatenate([held, first], axis=1)
-    second = [exchange(both[0], 2, size), exchange(both[1], 4, size)]
-    token = work([flat(a) for a in across], False)
-    second = with_token(jnp.stack(second), token)
-    across = exchange(second, 1, size)
-    work([flat(second)], False)
+    token = work([flat(fresh)] + [flat(a) for a in across], False)
+    over_y, over_z = with_token(over_y, token), with_token(over_z, token)
+    second = [exchange(over_z[0], 2, size), exchange(over_y[1], 4, size)]
+    across = [exchange(over_y, 1, size), exchange(over_z, 1, size)]
+    token = work([flat(x) for x in (over_y, over_z, *across)], False)
+    second = [with_token(x, token) for x in second]
+    across = exchange(jnp.stack(second), 1, size)
+    work(second, False)
     work([flat(across)], True)
 
 

time: 184 us -> 183 us (level)
    ppermute x36 -> x38, starting transfers between devices: 36.8 us -> 37.3 us  [exchange(): return lax.ppermute(x, 'section', [(i, i ^ mask) for i in range(size)])]
    ppermute x36 -> x38, waiting for transfers between devices: 56.2 us -> 56.6 us  [exchange(): return lax.ppermute(x, 'section', [(i, i ^ mask) for i in range(size)])]
  transfers between devices with their start and end apart: 37 -> 39, of which waited for: 23 -> 25; matrix products, arithmetic and copies ran while one was open for 2% -> 1% of each run, Pallas kernels for 25% -> 26%
where the time goes in v8:
time: 183 us
  waiting for transfers between devices  67.8 us (37%)
  Pallas kernels  61.9 us (34%)
  starting transfers between devices  44.7 us (24%)
  other arithmetic  6.98 us (4%)
    ppermute x38, waiting for transfers between devices, exchange(): return lax.ppermute(x, 'section', [(i, i ^ mask) for i in range(size)])  56.6 us
    ppermute x38, starting transfers between devices, exchange(): return lax.ppermute(x, 'section', [(i, i ^ mask) for i in range(size)])  37.3 us
    pallas_call x4, Pallas kernels, join_grad(): pl.pallas_call(functools.partial(join_grad_kernel, first, counts, len(ext...  16 us
    pallas_call x3, Pallas kernels, join(): pl.pallas_call(functools.partial(join_kernel, first, count), out_shape=tu...  14 us
    all_to_all x1, waiting for transfers between devices, on_device(): lax.all_to_all(sent, 'section', split_axis=0, concat_axis=0, tiled=True)  11.2 us
    pallas_call x1, Pallas kernels, head_grad(): pl.pallas_call(functools.partial(head_grad_kernel, counts), out_shape=(ja...  8.97 us
    pallas_call x4, Pallas kernels, head(): pl.pallas_call(functools.partial(head_kernel, first, counts, last), out_s...  8.07 us
    all_to_all x1, starting transfers between devices, on_device(): lax.all_to_all(sent, 'section', split_axis=0, concat_axis=0, tiled=True)  7.35 us
  transfers between devices with their start and end apart: 39, of which 25 were waited for; matrix products, arithmetic and copies ran while one was open for 1% of the time, Pallas kernels for 26%

profile of v8, /device:TPU:1, one launch (start us, length us, event | category | flops | bytes accessed | tf_op | source)
XLA Modules:
  0.0 182.9 jit_solution(5300177157045830993)
XLA Ops:
  0.6 1.8 maximum_bitcast_fusion.after_ref
  2.4 7.3 %all-to-all-start = ((bf16[16,8,1536]{2,1,0:T(8,128)(2,1)}), bf16[16,8,1536]{2,1,0:T(8,128)(2,1)S(1)}, u32[]{:S(2)}, u32[]{:S(2)}) async-start(bf16[16,8,1536]{2,1,0:T(8,128)(2,1)} %maximum_bitcast_fusion.after_ref), calls=%async_computation | async-start | bytes 786432 | tf_op jit(solution)/shard_map/all_to_all | solution.py:473
  10.5 11.2 %all-to-all-done = bf16[16,8,1536]{2,1,0:T(8,128)(2,1)S(1)} async-done(((bf16[16,8,1536]{2,1,0:T(8,128)(2,1)}), bf16[16,8,1536]{2,1,0:T(8,128)(2,1)S(1)}, u32[]{:S(2)}, u32[]{:S(2)}) %all-to-all-start) | async-done | bytes 393248 | tf_op jit(solution)/shard_map/all_to_all | solution.py:473
  21.7 5.9 %join.4 = (f32[2,4,128,512]{3,2,1,0:T(8,128)S(1)}, f32[1,512]{1,0:T(1,128)}, bf16[1536,128]{1,0:T(8,128)(2,1)S(1)}) custom-call(s32[2,8]{1,0:T(2,128)S(1)} %xor_multiply_fusion.order, bf16[128,1536]{1,0:T(8,128)(2,1)S(1)} %bitcast.108, bf16[3,512,8192]{2,1,0:T(8,128)(2,1)} %w_ref.6, bf16[16,8,1536]{2,1,0:T(8,128)(2,1)} %maximum_bitcast_fusion.after_ref), custom_call_target="tpu_custom_call" | custom-call | flops 1610612736 | bytes 12582912 | tf_op jit(solution)/shard_map/join/pallas_call | solution.py:143
  28.1 4.0 %join.3 = (f32[2,2,128,512]{3,2,1,0:T(8,128)S(1)}, f32[1,512]{1,0:T(1,128)}) custom-call(s32[2,8]{1,0:T(2,128)S(1)} %xor_multiply_fusion.order, bf16[128,1536]{1,0:T(8,128)(2,1)S(1)} %bitcast.109, bf16[3,512,8192]{2,1,0:T(8,128)(2,1)} %w_ref.6, bf16[16,8,1536]{2,1,0:T(8,128)(2,1)} %maximum_bitcast_fusion.after_ref), custom_call_target="tpu_custom_call" | custom-call | flops 805306368 | bytes 6291456 | tf_op jit(solution)/shard_map/join/pallas_call | solution.py:143
  33.8 4.0 %join.5 = (f32[2,2,128,512]{3,2,1,0:T(8,128)S(1)}, f32[1,512]{1,0:T(1,128)}) custom-call(s32[2,8]{1,0:T(2,128)S(1)} %xor_multiply_fusion.order, bf16[128,1536]{1,0:T(8,128)(2,1)S(1)} %bitcast.110, bf16[3,512,8192]{2,1,0:T(8,128)(2,1)} %w_ref.6, f32[2,2,128,512]{3,2,1,0:T(8,128)S(1)} %slice_add_fusion.3.after_ref), custom_call_target="tpu_custom_call" | custom-call | flops 805306368 | bytes 6291456 | tf_op jit(solution)/shard_map/join/pallas_call | solution.py:143
  37.8 5.9 %stage.1 = (bf16[8192,1024]{1,0:T(8,128)(2,1)S(1)}, f32[1,512]{1,0:T(1,128)S(1)}) custom-call(bf16[8192,1024]{1,0:T(8,128)(2,1)} %w_ref.7, f32[2,2,128,512]{3,2,1,0:T(8,128)S(1)} %get-tuple-element.32.after_ref), custom_call_target="tpu_custom_call" | custom-call | bytes 16777216 | tf_op jit(solution)/shard_map/stage/pallas_call | solution.py:91
  43.8 2.3 %collective-permute-done.1 = f32[2,128,512]{2,1,0:T(8,128)S(1)} collective-permute-done((f32[2,128,512]{2,1,0:T(8,128)S(1)}, f32[2,128,512]{2,1,0:T(8,128)S(1)}, u32[]{:S(2)}, u32[]{:S(2)}) %collective-permute-start.1) | collective-permute-done | bytes 524320 | tf_op jit(solution)/shard_map/ppermute | solution.py:53
  47.8 5.4 %collective-permute-done.3 = f32[1,128,512]{2,1,0:T(8,128)S(1)} collective-permute-done((f32[1,128,512]{2,1,0:T(8,128)S(1)}, f32[1,128,512]{2,1,0:T(8,128)S(1)}, u32[]{:S(2)}, u32[]{:S(2)}) %collective-permute-start.3) | collective-permute-done | bytes 262176 | tf_op jit(solution)/shard_map/ppermute | solution.py:53
  53.3 1.8 collective-permute-start.5
  55.8 22.7 %collective-permute-done.5 = f32[2,1,128,512]{3,2,1,0:T(8,128)S(1)} collective-permute-done((f32[2,1,128,512]{3,2,1,0:T(8,128)S(1)}, f32[2,1,128,512]{3,2,1,0:T(8,128)S(1)}, u32[]{:S(2)}, u32[]{:S(2)}) %collective-permute-start.5) | collective-permute-done | bytes 524320 | tf_op jit(solution)/shard_map/ppermute | solution.py:53
  83.4 3.2 %collective-permute-start.9 = (f32[128]{0:T(128)S(1)}, f32[128]{0:T(128)S(1)}, u32[]{:S(2)}, u32[]{:S(2)}) collective-permute-start(f32[128]{0:T(128)S(1)} %add_add_fusion.3), channel_id=1, source_target_pairs={{0,1},{1,0},{2,3},{3,2},{4,5},{5,4},{6,7},{7,6},{8,9},{9,8},{10,11... | collective-permute-start | bytes 1544 | tf_op jit(solution)/shard_map/ppermute | solution.py:53
  89.2 1.9 %head.4 = (f32[128,1024]{1,0:T(8,128)S(1)}, f32[1,512]{1,0:T(1,128)S(1)}) custom-call(s32[17]{0:T(128)S(1)} %pad_add_fusion.starts, bf16[8192,1024]{1,0:T(8,128)(2,1)S(1)} %get-tuple-element.33.w_ref, f32[128,1024]{1,0:T(8,128)S(1)} %broadcast_in_dim.9.before_ref, s32[1,128]{1,0:T(1,128)S(1)} %bitcast.133, bf16[2,128,512]{2,1,0:T(8,128)(2,1)S(1)} %fusion.21.rest_0_, ...), custom_call_target="tpu_custom_call" | custom-call | flops 536870912 | bytes 1048576 | tf_op jit(solution)/shard_map/head/pallas_call | solution.py:202
  91.0 4.6 %collective-permute-done.12 = bf16[2,1,128,512]{3,2,1,0:T(8,128)(2,1)S(1)} collective-permute-done((bf16[2,1,128,512]{3,2,1,0:T(8,128)(2,1)S(1)}, bf16[2,1,128,512]{3,2,1,0:T(8,128)(2,1)S(1)}, u32[]{:S(2)}, u32[]{:S(2)}) %collective-permute-start.12) | collective-permute-done | bytes 262176 | tf_op jit(solution)/shard_map/ppermute | solution.py:53
  98.8 3.1 %head.5 = (f32[128,1024]{1,0:T(8,128)S(1)}, f32[1,512]{1,0:T(1,128)S(1)}) custom-call(s32[17]{0:T(128)S(1)} %pad_add_fusion.starts, bf16[8192,1024]{1,0:T(8,128)(2,1)S(1)} %get-tuple-element.33.w_ref, f32[128,1024]{1,0:T(8,128)S(1)} %get-tuple-element.35.before_ref, s32[1,128]{1,0:T(1,128)S(1)} %bitcast.134, bf16[2,128,512]{2,1,0:T(8,128)(2,1)S(1)} %bitcast.113, ...), custom_call_target="tpu_custom_call" | custom-call | flops 1073741824 | bytes 1048576 | tf_op jit(solution)/shard_map/head/pallas_call | solution.py:202
  102.4 1.7 collective-permute-start.18
  105.6 1.6 head.7
  107.2 2.4 %collective-permute-start.19 = (f32[4,128]{1,0:T(4,128)S(1)}, f32[4,128]{1,0:T(4,128)S(1)}, u32[]{:S(2)}, u32[]{:S(2)}) collective-permute-start(f32[4,128]{1,0:T(4,128)S(1)} %slice.189), channel_id=1, source_target_pairs={{0,8},{1,9},{2,10},{3,11},{4,12},{5,13},{6,14},{7,15},{8,0},{9,1},... | collective-permute-start | bytes 6152 | tf_op jit(solution)/shard_map/ppermute | solution.py:53
  110.6 1.7 collective-permute-start.22
  115.1 2.8 %collective-permute-start.23 = (f32[4,128]{1,0:T(4,128)S(1)}, f32[4,128]{1,0:T(4,128)S(1)}, u32[]{:S(2)}, u32[]{:S(2)}) collective-permute-start(f32[4,128]{1,0:T(4,128)S(1)} %pad_maximum_fusion.4), channel_id=1, source_target_pairs={{0,1},{1,0},{2,3},{3,2},{4,5},{5,4},{6,7},{7,6},{8,9},{9,8},{10,11... | collective-permute-start | bytes 6152 | tf_op jit(solution)/shard_map/ppermute | solution.py:53
  118.7 4.2 %back_first.1 = (f32[2,4,128,512]{3,2,1,0:T(8,128)S(1)}, bf16[128,1024]{1,0:T(8,128)(2,1)S(1)}) custom-call(s32[2,8]{1,0:T(2,128)S(1)} %xor_multiply_fusion.order, s32[17]{0:T(128)S(1)} %pad_add_fusion.starts, f32[128,1024]{1,0:T(8,128)S(1)} %get-tuple-element.42.logits_ref, f32[8,128]{1,0:T(8,128)S(1)} %broadcast_in_dim.11.stats_ref, ...), custom_call_target="tpu_custom_call" | custom-call | flops 1073741824 | bytes 2097152 | tf_op jit(solution)/shard_map/back_first/pallas_call | solution.py:239
  123.6 2.6 %back_rest.2 = (f32[2,2,128,512]{3,2,1,0:T(8,128)S(1)}, f32[1,512]{1,0:T(1,128)}) custom-call(s32[2,8]{1,0:T(2,128)S(1)} %xor_multiply_fusion.order, bf16[128,1024]{1,0:T(8,128)(2,1)S(1)} %get-tuple-element.43.d_ref, bf16[8192,1024]{1,0:T(8,128)(2,1)S(1)} %get-tuple-element.33.w_ref, f32[2,4,128,512]{3,2,1,0:T(8,128)S(1)} %get-tuple-element.44.after_ref), custom_call_target="tpu_custom_call" | custom-call | flops 536870912 | bytes 1048576 | tf_op jit(solution)/shard_map/back_rest/pallas_call | solution.py:256
  128.7 2.2 %back_rest.3 = (f32[2,2,128,512]{3,2,1,0:T(8,128)S(1)}, f32[1,512]{1,0:T(1,128)S(1)}) custom-call(s32[2,8]{1,0:T(2,128)S(1)} %xor_multiply_fusion.order, bf16[128,1024]{1,0:T(8,128)(2,1)S(1)} %get-tuple-element.43.d_ref, bf16[8192,1024]{1,0:T(8,128)(2,1)S(1)} %get-tuple-element.33.w_ref, f32[2,2,128,512]{3,2,1,0:T(8,128)S(1)} %slice_add_fusion.1.after_ref), custom_call_target="tpu_custom_call" | custom-call | flops 536870912 | bytes 1048576 | tf_op jit(solution)/shard_map/back_rest/pallas_call | solution.py:256
  130.9 3.7 %collective-permute-done.25 = f16[2,128,512]{2,1,0:T(8,128)(2,1)S(1)} collective-permute-done((f16[2,128,512]{2,1,0:T(8,128)(2,1)S(1)}, f16[2,128,512]{2,1,0:T(8,128)(2,1)S(1)}, u32[]{:S(2)}, u32[]{:S(2)}) %collective-permute-start.25) | collective-permute-done | bytes 262176 | tf_op jit(solution)/shard_map/ppermute | solution.py:53
  137.6 1.9 %collective-permute-done.27 = f16[1,128,512]{2,1,0:T(8,128)(2,1)S(1)} collective-permute-done((f16[1,128,512]{2,1,0:T(8,128)(2,1)S(1)}, f16[1,128,512]{2,1,0:T(8,128)(2,1)S(1)}, u32[]{:S(2)}, u32[]{:S(2)}) %collective-permute-start.27) | collective-permute-done | bytes 131104 | tf_op jit(solution)/shard_map/ppermute | solution.py:53
  142.3 9.0 %head_grad.1 = (bf16[8192,1024]{1,0:T(8,128)(2,1)}, f32[1,512]{1,0:T(1,128)S(1)}) custom-call(s32[17]{0:T(128)S(1)} %pad_add_fusion.starts, bf16[128,1024]{1,0:T(8,128)(2,1)S(1)} %get-tuple-element.43.d_ref, f32[2,1,128,512]{3,2,1,0:T(8,128)S(1)} %get-tuple-element.61.after_ref, bf16[2,128,512]{2,1,0:T(8,128)(2,1)S(1)} %fusion.21.rest_0_, ...), custom_call_target="tpu_custom_call" | custom-call | flops 2147483648 | bytes 16777216 | tf_op jit(solution)/shard_map/head_grad/pallas_call | solution.py:300
  151.2 4.0 %collective-permute-done.29 = f16[2,1,128,512]{3,2,1,0:T(8,128)(2,1)S(1)} collective-permute-done((f16[2,1,128,512]{3,2,1,0:T(8,128)(2,1)S(1)}, f16[2,1,128,512]{3,2,1,0:T(8,128)(2,1)S(1)}, u32[]{:S(2)}, u32[]{:S(2)}) %collective-permute-start.29) | collective-permute-done | bytes 262176 | tf_op jit(solution)/shard_map/ppermute | solution.py:53
  157.6 3.7 %join_grad.4 = (bf16[3,512,8192]{2,1,0:T(8,128)(2,1)}, f32[1,512]{1,0:T(1,128)S(1)}) custom-call(s32[17]{0:T(128)S(1)} %pad_add_fusion.starts, bf16[1536,128]{1,0:T(8,128)(2,1)S(1)} %get-tuple-element.41.x_ref, bf16[2,128,512]{2,1,0:T(8,128)(2,1)S(1)} %bitcast.132, bf16[2,128,512]{2,1,0:T(8,128)(2,1)S(1)} %bitcast.144), custom_call_target="tpu_custom_call" | custom-call | flops 805306368 | bytes 6291456 | tf_op jit(solution)/shard_map/join_grad/pallas_call | solution.py:353
  161.4 3.0 %collective-permute-done.32 = bf16[2,1,128,512]{3,2,1,0:T(8,128)(2,1)S(1)} collective-permute-done((bf16[2,1,128,512]{3,2,1,0:T(8,128)(2,1)S(1)}, bf16[2,1,128,512]{3,2,1,0:T(8,128)(2,1)S(1)}, u32[]{:S(2)}, u32[]{:S(2)}) %collective-permute-start.32) | collective-permute-done | bytes 262176 | tf_op jit(solution)/shard_map/ppermute | solution.py:53
  168.1 6.0 %join_grad.5 = (bf16[3,512,8192]{2,1,0:T(8,128)(2,1)}, f32[1,512]{1,0:T(1,128)S(1)}) custom-call(s32[17]{0:T(128)S(1)} %pad_add_fusion.starts, bf16[1536,128]{1,0:T(8,128)(2,1)S(1)} %get-tuple-element.41.x_ref, bf16[3,512,8192]{2,1,0:T(8,128)(2,1)} %get-tuple-element.49.rest_0_, bf16[2,128,512]{2,1,0:T(8,128)(2,1)S(1)} %bitcast.116, ...), custom_call_target="tpu_custom_call", output_to_operand_aliasing={{0}: (2, {})} | custom-call | flops 1610612736 | bytes 12582912 | tf_op jit(solution)/shard_map/join_grad/pallas_call | solution.py:353
  176.5 3.1 %join_grad.6 = (bf16[3,512,8192]{2,1,0:T(8,128)(2,1)}, f32[1,512]{1,0:T(1,128)}) custom-call(s32[17]{0:T(128)S(1)} %pad_add_fusion.starts, bf16[1536,128]{1,0:T(8,128)(2,1)S(1)} %get-tuple-element.41.x_ref, bf16[3,512,8192]{2,1,0:T(8,128)(2,1)} %get-tuple-element.51.rest_0_, ...), custom_call_target="tpu_custom_call", output_to_operand_aliasing={{0}: (2, {})} | custom-call | flops 402653184 | bytes 3145728 | tf_op jit(solution)/shard_map/join_grad/pallas_call | solution.py:353
  179.6 3.1 %join_grad.7 = (bf16[3,512,8192]{2,1,0:T(8,128)(2,1)}, f32[1,512]{1,0:T(1,128)}) custom-call(s32[17]{0:T(128)S(1)} %pad_add_fusion.starts, bf16[1536,128]{1,0:T(8,128)(2,1)S(1)} %get-tuple-element.41.x_ref, bf16[3,512,8192]{2,1,0:T(8,128)(2,1)} %get-tuple-element.53.rest_0_, bf16[2,128,512]{2,1,0:T(8,128)(2,1)S(1)} %bitcast.130), custom_call_target="tpu_custom_call", output_to_operand_aliasing={{0}: (2, {})} | custom-call | flops 402653184 | bytes 3145728 | tf_op jit(solution)/shard_map/join_grad/pallas_call | solution.py:353
  (119 shorter events, 39.8 us)
Async XLA Ops:
  2.4 19.3 %all-to-all-start = ((bf16[16,8,1536]{2,1,0:T(8,128)(2,1)}), bf16[16,8,1536]{2,1,0:T(8,128)(2,1)S(1)}, u32[]{:S(2)}, u32[]{:S(2)}) async-start(bf16[16,8,1536]{2,1,0:T(8,128)(2,1)} %maximum_bitcast_fusion.after_ref), calls=%async_computation | async-start | bytes 786432 | tf_op jit(solution)/shard_map/all_to_all | solution.py:473
  27.6 4.5 %collective-permute-start = (f32[2,4,128,512]{3,2,1,0:T(8,128)S(1)}, f32[2,4,128,512]{3,2,1,0:T(8,128)S(1)}, u32[]{:S(2)}, u32[]{:S(2)}) collective-permute-start(f32[2,4,128,512]{3,2,1,0:T(8,128)S(1)} %get-tuple-element.31), channel_id=1, source_target_pairs={{0,1},{1,0},{2,3},{3,2},{4,5},{5,4},{6,7},{7,6},{8,9},{9,8},{10,11... | collective-permute-start | bytes 6291464 | tf_op jit(solution)/shard_map/ppermute | solution.py:53
  32.5 13.6 %collective-permute-start.1 = (f32[2,128,512]{2,1,0:T(8,128)S(1)}, f32[2,128,512]{2,1,0:T(8,128)S(1)}, u32[]{:S(2)}, u32[]{:S(2)}) collective-permute-start(f32[2,128,512]{2,1,0:T(8,128)S(1)} %get-tuple-element.74), channel_id=1, source_target_pairs={{0,2},{1,3},{2,0},{3,1},{4,6},{5,7},{6,4},{7,5},{8,10},{9,11},{10,... | collective-permute-start | bytes 1572872 | tf_op jit(solution)/shard_map/ppermute | solution.py:53
  32.8 13.2 %collective-permute-start.2 = (f32[2,128,512]{2,1,0:T(8,128)S(1)}, f32[2,128,512]{2,1,0:T(8,128)S(1)}, u32[]{:S(2)}, u32[]{:S(2)}) collective-permute-start(f32[2,128,512]{2,1,0:T(8,128)S(1)} %get-tuple-element.75), channel_id=1, source_target_pairs={{0,4},{1,5},{2,6},{3,7},{4,0},{5,1},{6,2},{7,3},{8,12},{9,13},{10,... | collective-permute-start | bytes 1572872 | tf_op jit(solution)/shard_map/ppermute | solution.py:53
  46.5 6.8 %collective-permute-start.3 = (f32[1,128,512]{2,1,0:T(8,128)S(1)}, f32[1,128,512]{2,1,0:T(8,128)S(1)}, u32[]{:S(2)}, u32[]{:S(2)}) collective-permute-start(f32[1,128,512]{2,1,0:T(8,128)S(1)} %get-tuple-element.72), channel_id=1, source_target_pairs={{0,4},{1,5},{2,6},{3,7},{4,0},{5,1},{6,2},{7,3},{8,12},{9,13},{10,... | collective-permute-start | bytes 786440 | tf_op jit(solution)/shard_map/ppermute | solution.py:53
  47.2 6.1 %collective-permute-start.4 = (f32[1,128,512]{2,1,0:T(8,128)S(1)}, f32[1,128,512]{2,1,0:T(8,128)S(1)}, u32[]{:S(2)}, u32[]{:S(2)}) collective-permute-start(f32[1,128,512]{2,1,0:T(8,128)S(1)} %get-tuple-element.73), channel_id=1, source_target_pairs={{0,2},{1,3},{2,0},{3,1},{4,6},{5,7},{6,4},{7,5},{8,10},{9,11},{10,... | collective-permute-start | bytes 786440 | tf_op jit(solution)/shard_map/ppermute | solution.py:53
  53.3 25.1 %collective-permute-start.5 = (f32[2,1,128,512]{3,2,1,0:T(8,128)S(1)}, f32[2,1,128,512]{3,2,1,0:T(8,128)S(1)}, u32[]{:S(2)}, u32[]{:S(2)}) collective-permute-start(f32[2,1,128,512]{3,2,1,0:T(8,128)S(1)} %slice_add_fusion.5), channel_id=1, source_target_pairs={{0,8},{1,9},{2,10},{3,11},{4,12},{5,13},{6,14},{7,15},{8,0},{9,1},... | collective-permute-start | bytes 1572872 | tf_op jit(solution)/shard_map/ppermute | solution.py:53
  55.1 31.4 %collective-permute-start.10 = (f32[512]{0:T(512)S(1)}, f32[512]{0:T(512)S(1)}, u32[]{:S(2)}, u32[]{:S(2)}) collective-permute-start(f32[512]{0:T(512)S(1)} %copy-done.1), channel_id=1, source_target_pairs={{0,8},{1,9},{2,10},{3,11},{4,12},{5,13},{6,14},{7,15},{8,0},{9,1},... | collective-permute-start | bytes 6152 | tf_op jit(solution)/shard_map/ppermute | solution.py:53
  78.7 2.7 %collective-permute-start.7 = (f32[128]{0:T(128)S(1)}, f32[128]{0:T(128)S(1)}, u32[]{:S(2)}, u32[]{:S(2)}) collective-permute-start(f32[128]{0:T(128)S(1)} %add_bitcast_fusion.1), channel_id=1, source_target_pairs={{0,4},{1,5},{2,6},{3,7},{4,0},{5,1},{6,2},{7,3},{8,12},{9,13},{10,... | collective-permute-start | bytes 1544 | tf_op jit(solution)/shard_map/ppermute | solution.py:53
  79.5 3.3 %collective-permute-start.8 = (f32[128]{0:T(128)S(1)}, f32[128]{0:T(128)S(1)}, u32[]{:S(2)}, u32[]{:S(2)}) collective-permute-start(f32[128]{0:T(128)S(1)} %add_bitcast_fusion.1), channel_id=1, source_target_pairs={{0,6},{1,7},{2,4},{3,5},{4,2},{5,3},{6,0},{7,1},{8,14},{9,15},{10,... | collective-permute-start | bytes 1544 | tf_op jit(solution)/shard_map/ppermute | solution.py:53
  83.4 4.0 %collective-permute-start.9 = (f32[128]{0:T(128)S(1)}, f32[128]{0:T(128)S(1)}, u32[]{:S(2)}, u32[]{:S(2)}) collective-permute-start(f32[128]{0:T(128)S(1)} %add_add_fusion.3), channel_id=1, source_target_pairs={{0,1},{1,0},{2,3},{3,2},{4,5},{5,4},{6,7},{7,6},{8,9},{9,8},{10,11... | collective-permute-start | bytes 1544 | tf_op jit(solution)/shard_map/ppermute | solution.py:53
  88.0 7.7 %collective-permute-start.12 = (bf16[2,1,128,512]{3,2,1,0:T(8,128)(2,1)S(1)}, bf16[2,1,128,512]{3,2,1,0:T(8,128)(2,1)S(1)}, u32[]{:S(2)}, u32[]{:S(2)}) collective-permute-start(bf16[2,1,128,512]{3,2,1,0:T(8,128)(2,1)S(1)} %multiply_convert_fusion.6), channel_id=1, source_target_pairs={{0,2},{1,3},{2,0},{3,1},{4,6},{5,7},{6,4},{7,5},{8,10},{9,11},{10,... | collective-permute-start | bytes 786440 | tf_op jit(solution)/shard_map/ppermute | solution.py:53
  88.4 7.4 %collective-permute-start.13 = (bf16[2,1,128,512]{3,2,1,0:T(8,128)(2,1)S(1)}, bf16[2,1,128,512]{3,2,1,0:T(8,128)(2,1)S(1)}, u32[]{:S(2)}, u32[]{:S(2)}) collective-permute-start(bf16[2,1,128,512]{3,2,1,0:T(8,128)(2,1)S(1)} %multiply_convert_fusion.6), channel_id=1, source_target_pairs={{0,4},{1,5},{2,6},{3,7},{4,0},{5,1},{6,2},{7,3},{8,12},{9,13},{10,... | collective-permute-start | bytes 786440 | tf_op jit(solution)/shard_map/ppermute | solution.py:53
  97.4 4.7 %collective-permute-start.17 = (bf16[1,128,512]{2,1,0:T(8,128)(2,1)S(1)}, bf16[1,128,512]{2,1,0:T(8,128)(2,1)S(1)}, u32[]{:S(2)}, u32[]{:S(2)}) collective-permute-start(bf16[1,128,512]{2,1,0:T(8,128)(2,1)S(1)} %slice_bitcast_fusion.6), channel_id=1, source_target_pairs={{0,4},{1,5},{2,6},{3,7},{4,0},{5,1},{6,2},{7,3},{8,12},{9,13},{10,... | collective-permute-start | bytes 393224 | tf_op jit(solution)/shard_map/ppermute | solution.py:53
  98.0 4.3 %collective-permute-start.16 = (bf16[1,128,512]{2,1,0:T(8,128)(2,1)S(1)}, bf16[1,128,512]{2,1,0:T(8,128)(2,1)S(1)}, u32[]{:S(2)}, u32[]{:S(2)}) collective-permute-start(bf16[1,128,512]{2,1,0:T(8,128)(2,1)S(1)} %slice_bitcast_fusion.7), channel_id=1, source_target_pairs={{0,2},{1,3},{2,0},{3,1},{4,6},{5,7},{6,4},{7,5},{8,10},{9,11},{10,... | collective-permute-start | bytes 393224 | tf_op jit(solution)/shard_map/ppermute | solution.py:53
  102.4 3.2 %collective-permute-start.18 = (bf16[2,1,128,512]{3,2,1,0:T(8,128)(2,1)S(1)}, bf16[2,1,128,512]{3,2,1,0:T(8,128)(2,1)S(1)}, u32[]{:S(2)}, u32[]{:S(2)}) collective-permute-start(bf16[2,1,128,512]{3,2,1,0:T(8,128)(2,1)S(1)} %pad_maximum_fusion), channel_id=1, source_target_pairs={{0,1},{1,0},{2,3},{3,2},{4,5},{5,4},{6,7},{7,6},{8,9},{9,8},{10,11... | collective-permute-start | bytes 786440 | tf_op jit(solution)/shard_map/ppermute | solution.py:53
  107.2 3.4 %collective-permute-start.19 = (f32[4,128]{1,0:T(4,128)S(1)}, f32[4,128]{1,0:T(4,128)S(1)}, u32[]{:S(2)}, u32[]{:S(2)}) collective-permute-start(f32[4,128]{1,0:T(4,128)S(1)} %slice.189), channel_id=1, source_target_pairs={{0,8},{1,9},{2,10},{3,11},{4,12},{5,13},{6,14},{7,15},{8,0},{9,1},... | collective-permute-start | bytes 6152 | tf_op jit(solution)/shard_map/ppermute | solution.py:53
  110.6 3.4 %collective-permute-start.22 = (f32[4,128]{1,0:T(4,128)S(1)}, f32[4,128]{1,0:T(4,128)S(1)}, u32[]{:S(2)}, u32[]{:S(2)}) collective-permute-start(f32[4,128]{1,0:T(4,128)S(1)} %pad_maximum_fusion.3), channel_id=1, source_target_pairs={{0,6},{1,7},{2,4},{3,5},{4,2},{5,3},{6,0},{7,1},{8,14},{9,15},{10,... | collective-permute-start | bytes 6152 | tf_op jit(solution)/shard_map/ppermute | solution.py:53
  115.1 3.6 %collective-permute-start.23 = (f32[4,128]{1,0:T(4,128)S(1)}, f32[4,128]{1,0:T(4,128)S(1)}, u32[]{:S(2)}, u32[]{:S(2)}) collective-permute-start(f32[4,128]{1,0:T(4,128)S(1)} %pad_maximum_fusion.4), channel_id=1, source_target_pairs={{0,1},{1,0},{2,3},{3,2},{4,5},{5,4},{6,7},{7,6},{8,9},{9,8},{10,11... | collective-permute-start | bytes 6152 | tf_op jit(solution)/shard_map/ppermute | solution.py:53
  123.2 3.0 %collective-permute-start.24 = (f16[2,4,128,512]{3,2,1,0:T(8,128)(2,1)S(1)}, f16[2,4,128,512]{3,2,1,0:T(8,128)(2,1)S(1)}, u32[]{:S(2)}, u32[]{:S(2)}) collective-permute-start(f16[2,4,128,512]{3,2,1,0:T(8,128)(2,1)S(1)} %multiply_convert_fusion), channel_id=1, source_target_pairs={{0,1},{1,0},{2,3},{3,2},{4,5},{5,4},{6,7},{7,6},{8,9},{9,8},{10,11... | collective-permute-start | bytes 3145736 | tf_op jit(solution)/shard_map/ppermute | solution.py:53
  126.8 7.8 %collective-permute-start.25 = (f16[2,128,512]{2,1,0:T(8,128)(2,1)S(1)}, f16[2,128,512]{2,1,0:T(8,128)(2,1)S(1)}, u32[]{:S(2)}, u32[]{:S(2)}) collective-permute-start(f16[2,128,512]{2,1,0:T(8,128)(2,1)S(1)} %get-tuple-element.70), channel_id=1, source_target_pairs={{0,2},{1,3},{2,0},{3,1},{4,6},{5,7},{6,4},{7,5},{8,10},{9,11},{10,... | collective-permute-start | bytes 786440 | tf_op jit(solution)/shard_map/ppermute | solution.py:53
  127.8 7.4 %collective-permute-start.26 = (f16[2,128,512]{2,1,0:T(8,128)(2,1)S(1)}, f16[2,128,512]{2,1,0:T(8,128)(2,1)S(1)}, u32[]{:S(2)}, u32[]{:S(2)}) collective-permute-start(f16[2,128,512]{2,1,0:T(8,128)(2,1)S(1)} %get-tuple-element.71), channel_id=1, source_target_pairs={{0,4},{1,5},{2,6},{3,7},{4,0},{5,1},{6,2},{7,3},{8,12},{9,13},{10,... | collective-permute-start | bytes 786440 | tf_op jit(solution)/shard_map/ppermute | solution.py:53
  135.6 3.9 %collective-permute-start.27 = (f16[1,128,512]{2,1,0:T(8,128)(2,1)S(1)}, f16[1,128,512]{2,1,0:T(8,128)(2,1)S(1)}, u32[]{:S(2)}, u32[]{:S(2)}) collective-permute-start(f16[1,128,512]{2,1,0:T(8,128)(2,1)S(1)} %get-tuple-element.68), channel_id=1, source_target_pairs={{0,4},{1,5},{2,6},{3,7},{4,0},{5,1},{6,2},{7,3},{8,12},{9,13},{10,... | collective-permute-start | bytes 393224 | tf_op jit(solution)/shard_map/ppermute | solution.py:53
  136.6 4.1 %collective-permute-start.28 = (f16[1,128,512]{2,1,0:T(8,128)(2,1)S(1)}, f16[1,128,512]{2,1,0:T(8,128)(2,1)S(1)}, u32[]{:S(2)}, u32[]{:S(2)}) collective-permute-start(f16[1,128,512]{2,1,0:T(8,128)(2,1)S(1)} %get-tuple-element.69), channel_id=1, source_target_pairs={{0,2},{1,3},{2,0},{3,1},{4,6},{5,7},{6,4},{7,5},{8,10},{9,11},{10,... | collective-permute-start | bytes 393224 | tf_op jit(solution)/shard_map/ppermute | solution.py:53
  140.8 14.5 %collective-permute-start.29 = (f16[2,1,128,512]{3,2,1,0:T(8,128)(2,1)S(1)}, f16[2,1,128,512]{3,2,1,0:T(8,128)(2,1)S(1)}, u32[]{:S(2)}, u32[]{:S(2)}) collective-permute-start(f16[2,1,128,512]{3,2,1,0:T(8,128)(2,1)S(1)} %get-tuple-element.60), channel_id=1, source_target_pairs={{0,8},{1,9},{2,10},{3,11},{4,12},{5,13},{6,14},{7,15},{8,0},{9,1},... | collective-permute-start | bytes 786440 | tf_op jit(solution)/shard_map/ppermute | solution.py:53
  156.5 7.9 %collective-permute-start.32 = (bf16[2,1,128,512]{3,2,1,0:T(8,128)(2,1)S(1)}, bf16[2,1,128,512]{3,2,1,0:T(8,128)(2,1)S(1)}, u32[]{:S(2)}, u32[]{:S(2)}) collective-permute-start(bf16[2,1,128,512]{3,2,1,0:T(8,128)(2,1)S(1)} %get-tuple-element.56), channel_id=1, source_target_pairs={{0,4},{1,5},{2,6},{3,7},{4,0},{5,1},{6,2},{7,3},{8,12},{9,13},{10,... | collective-permute-start | bytes 786440 | tf_op jit(solution)/shard_map/ppermute | solution.py:53
  156.5 7.9 %collective-permute-start.31 = (bf16[2,1,128,512]{3,2,1,0:T(8,128)(2,1)S(1)}, bf16[2,1,128,512]{3,2,1,0:T(8,128)(2,1)S(1)}, u32[]{:S(2)}, u32[]{:S(2)}) collective-permute-start(bf16[2,1,128,512]{3,2,1,0:T(8,128)(2,1)S(1)} %get-tuple-element.56), channel_id=1, source_target_pairs={{0,2},{1,3},{2,0},{3,1},{4,6},{5,7},{6,4},{7,5},{8,10},{9,11},{10,... | collective-permute-start | bytes 786440 | tf_op jit(solution)/shard_map/ppermute | solution.py:53
  164.5 3.6 %collective-permute-start.34 = (bf16[2,1,128,512]{3,2,1,0:T(8,128)(2,1)S(1)}, bf16[2,1,128,512]{3,2,1,0:T(8,128)(2,1)S(1)}, u32[]{:S(2)}, u32[]{:S(2)}) collective-permute-start(bf16[2,1,128,512]{3,2,1,0:T(8,128)(2,1)S(1)} %get-tuple-element.86), channel_id=1, source_target_pairs={{0,1},{1,0},{2,3},{3,2},{4,5},{5,4},{6,7},{7,6},{8,9},{9,8},{10,11... | collective-permute-start | bytes 786440 | tf_op jit(solution)/shard_map/ppermute | solution.py:53
  165.4 2.7 %collective-permute-start.33 = (bf16[2,1,128,512]{3,2,1,0:T(8,128)(2,1)S(1)}, bf16[2,1,128,512]{3,2,1,0:T(8,128)(2,1)S(1)}, u32[]{:S(2)}, u32[]{:S(2)}) collective-permute-start(bf16[2,1,128,512]{3,2,1,0:T(8,128)(2,1)S(1)} %get-tuple-element.87), channel_id=1, source_target_pairs={{0,1},{1,0},{2,3},{3,2},{4,5},{5,4},{6,7},{7,6},{8,9},{9,8},{10,11... | collective-permute-start | bytes 786440 | tf_op jit(solution)/shard_map/ppermute | solution.py:53
  165.5 8.7 %collective-permute-start.36 = (bf16[1,128,512]{2,1,0:T(8,128)(2,1)S(1)}, bf16[1,128,512]{2,1,0:T(8,128)(2,1)S(1)}, u32[]{:S(2)}, u32[]{:S(2)}) collective-permute-start(bf16[1,128,512]{2,1,0:T(8,128)(2,1)S(1)} %slice_bitcast_fusion.4), channel_id=1, source_target_pairs={{0,4},{1,5},{2,6},{3,7},{4,0},{5,1},{6,2},{7,3},{8,12},{9,13},{10,... | collective-permute-start | bytes 393224 | tf_op jit(solution)/shard_map/ppermute | solution.py:53
  167.0 7.1 %collective-permute-start.35 = (bf16[1,128,512]{2,1,0:T(8,128)(2,1)S(1)}, bf16[1,128,512]{2,1,0:T(8,128)(2,1)S(1)}, u32[]{:S(2)}, u32[]{:S(2)}) collective-permute-start(bf16[1,128,512]{2,1,0:T(8,128)(2,1)S(1)} %slice_bitcast_fusion.5), channel_id=1, source_target_pairs={{0,2},{1,3},{2,0},{3,1},{4,6},{5,7},{6,4},{7,5},{8,10},{9,11},{10,... | collective-permute-start | bytes 393224 | tf_op jit(solution)/shard_map/ppermute | solution.py:53
  174.3 5.4 %collective-permute-start.37 = (bf16[2,1,128,512]{3,2,0,1:T(8,128)(2,1)S(1)}, bf16[2,1,128,512]{3,2,0,1:T(8,128)(2,1)S(1)}, u32[]{:S(2)}, u32[]{:S(2)}) collective-permute-start(bf16[2,1,128,512]{3,2,0,1:T(8,128)(2,1)S(1)} %pad_maximum_fusion.1), channel_id=1, source_target_pairs={{0,1},{1,0},{2,3},{3,2},{4,5},{5,4},{6,7},{7,6},{8,9},{9,8},{10,11... | collective-permute-start | bytes 786440 | tf_op jit(solution)/shard_map/ppermute | solution.py:53
  (10 other events, 62.7 us)

commit v9 on v8

--- a/solution.py
+++ b/solution.py
@@ -495,11 +495,15 @@
         passed = unpack(exchange(pack(total), partner, size))
         return total + with_token(jnp.stack([passed[1], passed[0]]), beside(total))
 
-    joined = finish(total, lambda x: x, lambda x: x, lambda after: None)
-
-    squares = jnp.sum(joined * joined, axis=(1, 3))
-    squares = squares[0] + squares[1]
-    for group in sum_rounds(bits - 1):
+    own = total[0] + exchange(total[1], partner, size)
+    other = exchange(own, partner, size)
+    joined = jnp.stack([own, other])
+
+    squares = jnp.sum(own * own, axis=(0, 2))
+    rounds = sum_rounds(bits)
+    for group in rounds:
+        if group is rounds[-1]:
+            squares = squares * (other[0, 0, :1] * 0.0 + 1.0)
         squares = tree_sum(contributions(squares, group, size))
     inv_rms = lax.rsqrt(squares / full_width + epsilon)[:, None]
     gains = jnp.stack([gain, exchange(gain, partner, size)])[:, None, None, :]

time: 183 us -> 185 us (1.011)
  waiting for transfers between devices: 67.8 us -> 70.5 us
  starting transfers between devices: 44.7 us -> 42.2 us
    ppermute x38 -> x40, waiting for transfers between devices: 56.6 us -> 59.3 us  [exchange(): return lax.ppermute(x, 'section', [(i, i ^ mask) for i in range(size)])]
    ppermute x38 -> x40, starting transfers between devices: 37.3 us -> 34.8 us  [exchange(): return lax.ppermute(x, 'section', [(i, i ^ mask) for i in range(size)])]
  transfers between devices with their start and end apart: 39 -> 41, of which waited for: 25 -> 22; matrix products, arithmetic and copies ran while one was open for 1% -> 1% of each run, Pallas kernels for 26% -> 26%
where the time goes in v9:
time: 185 us; the launch traced here: 184 us
  waiting for transfers between devices  70.5 us (38%)
  Pallas kernels  61.9 us (33%)
  starting transfers between devices  42.2 us (23%)
  other arithmetic  6.93 us (4%)
  between operations  1.92 us (1%)
    ppermute x40, waiting for transfers between devices, exchange(): return lax.ppermute(x, 'section', [(i, i ^ mask) for i in range(size)])  59.3 us
    ppermute x40, starting transfers between devices, exchange(): return lax.ppermute(x, 'section', [(i, i ^ mask) for i in range(size)])  34.8 us
    pallas_call x4, Pallas kernels, join_grad(): pl.pallas_call(functools.partial(join_grad_kernel, first, counts, len(ext...  16 us
    pallas_call x3, Pallas kernels, join(): pl.pallas_call(functools.partial(join_kernel, first, count), out_shape=tu...  14 us
    all_to_all x1, waiting for transfers between devices, on_device(): lax.all_to_all(sent, 'section', split_axis=0, concat_axis=0, tiled=True)  11.2 us
    pallas_call x1, Pallas kernels, head_grad(): pl.pallas_call(functools.partial(head_grad_kernel, counts), out_shape=(ja...  8.97 us
    pallas_call x4, Pallas kernels, head(): pl.pallas_call(functools.partial(head_kernel, first, counts, last), out_s...  8.06 us
    all_to_all x1, starting transfers between devices, on_device(): lax.all_to_all(sent, 'section', split_axis=0, concat_axis=0, tiled=True)  7.35 us
  transfers between devices with their start and end apart: 41, of which 22 were waited for; matrix products, arithmetic and copies ran while one was open for 1% of the time, Pallas kernels for 26%

profile of v9, /device:TPU:1, one launch (start us, length us, event | category | flops | bytes accessed | tf_op | source)
XLA Modules:
  0.0 184.3 jit_solution(8366815839832927096)
XLA Ops:
  2.4 7.3 %all-to-all-start = ((bf16[16,8,1536]{2,1,0:T(8,128)(2,1)}), bf16[16,8,1536]{2,1,0:T(8,128)(2,1)S(1)}, u32[]{:S(2)}, u32[]{:S(2)}) async-start(bf16[16,8,1536]{2,1,0:T(8,128)(2,1)} %maximum_bitcast_fusion.after_ref), calls=%async_computation | async-start | bytes 786432 | tf_op jit(solution)/shard_map/all_to_all | solution.py:473
  10.5 11.2 %all-to-all-done = bf16[16,8,1536]{2,1,0:T(8,128)(2,1)S(1)} async-done(((bf16[16,8,1536]{2,1,0:T(8,128)(2,1)}), bf16[16,8,1536]{2,1,0:T(8,128)(2,1)S(1)}, u32[]{:S(2)}, u32[]{:S(2)}) %all-to-all-start) | async-done | bytes 393248 | tf_op jit(solution)/shard_map/all_to_all | solution.py:473
  21.7 5.9 %join.4 = (f32[2,4,128,512]{3,2,1,0:T(8,128)S(1)}, f32[1,512]{1,0:T(1,128)}, bf16[1536,128]{1,0:T(8,128)(2,1)S(1)}) custom-call(s32[2,8]{1,0:T(2,128)S(1)} %xor_multiply_fusion.order, bf16[128,1536]{1,0:T(8,128)(2,1)S(1)} %bitcast.116, bf16[3,512,8192]{2,1,0:T(8,128)(2,1)} %w_ref.6, bf16[16,8,1536]{2,1,0:T(8,128)(2,1)} %maximum_bitcast_fusion.after_ref), custom_call_target="tpu_custom_call" | custom-call | flops 1610612736 | bytes 12582912 | tf_op jit(solution)/shard_map/join/pallas_call | solution.py:143
  28.1 4.0 %join.3 = (f32[2,2,128,512]{3,2,1,0:T(8,128)S(1)}, f32[1,512]{1,0:T(1,128)}) custom-call(s32[2,8]{1,0:T(2,128)S(1)} %xor_multiply_fusion.order, bf16[128,1536]{1,0:T(8,128)(2,1)S(1)} %bitcast.117, bf16[3,512,8192]{2,1,0:T(8,128)(2,1)} %w_ref.6, bf16[16,8,1536]{2,1,0:T(8,128)(2,1)} %maximum_bitcast_fusion.after_ref), custom_call_target="tpu_custom_call" | custom-call | flops 805306368 | bytes 6291456 | tf_op jit(solution)/shard_map/join/pallas_call | solution.py:143
  33.8 4.0 %join.5 = (f32[2,2,128,512]{3,2,1,0:T(8,128)S(1)}, f32[1,512]{1,0:T(1,128)}) custom-call(s32[2,8]{1,0:T(2,128)S(1)} %xor_multiply_fusion.order, bf16[128,1536]{1,0:T(8,128)(2,1)S(1)} %bitcast.118, bf16[3,512,8192]{2,1,0:T(8,128)(2,1)} %w_ref.6, f32[2,2,128,512]{3,2,1,0:T(8,128)S(1)} %slice_add_fusion.3.after_ref), custom_call_target="tpu_custom_call" | custom-call | flops 805306368 | bytes 6291456 | tf_op jit(solution)/shard_map/join/pallas_call | solution.py:143
  37.8 5.9 %stage.1 = (bf16[8192,1024]{1,0:T(8,128)(2,1)S(1)}, f32[1,512]{1,0:T(1,128)S(1)}) custom-call(bf16[8192,1024]{1,0:T(8,128)(2,1)} %w_ref.7, f32[2,2,128,512]{3,2,1,0:T(8,128)S(1)} %get-tuple-element.32.after_ref), custom_call_target="tpu_custom_call" | custom-call | bytes 16777216 | tf_op jit(solution)/shard_map/stage/pallas_call | solution.py:91
  43.8 2.3 %collective-permute-done.1 = f32[2,128,512]{2,1,0:T(8,128)S(1)} collective-permute-done((f32[2,128,512]{2,1,0:T(8,128)S(1)}, f32[2,128,512]{2,1,0:T(8,128)S(1)}, u32[]{:S(2)}, u32[]{:S(2)}) %collective-permute-start.1) | collective-permute-done | bytes 524320 | tf_op jit(solution)/shard_map/ppermute | solution.py:53
  47.8 5.4 %collective-permute-done.3 = f32[1,128,512]{2,1,0:T(8,128)S(1)} collective-permute-done((f32[1,128,512]{2,1,0:T(8,128)S(1)}, f32[1,128,512]{2,1,0:T(8,128)S(1)}, u32[]{:S(2)}, u32[]{:S(2)}) %collective-permute-start.3) | collective-permute-done | bytes 262176 | tf_op jit(solution)/shard_map/ppermute | solution.py:53
  53.4 1.8 collective-permute-start.5
  55.2 12.0 %collective-permute-done.5 = f32[1,128,512]{2,1,0:T(8,128)S(1)} collective-permute-done((f32[1,128,512]{2,1,0:T(8,128)S(1)}, f32[1,128,512]{2,1,0:T(8,128)S(1)}, u32[]{:S(2)}, u32[]{:S(2)}) %collective-permute-start.5) | collective-permute-done | bytes 262176 | tf_op jit(solution)/shard_map/ppermute | solution.py:53
  67.4 2.4 %collective-permute-start.7 = (f32[128]{0:T(128)S(1)}, f32[128]{0:T(128)S(1)}, u32[]{:S(2)}, u32[]{:S(2)}) collective-permute-start(f32[128]{0:T(128)S(1)} %get-tuple-element.66), channel_id=1, source_target_pairs={{0,8},{1,9},{2,10},{3,11},{4,12},{5,13},{6,14},{7,15},{8,0},{9,1},... | collective-permute-start | bytes 1544 | tf_op jit(solution)/shard_map/ppermute | solution.py:53
  69.9 11.1 %collective-permute-done.7 = f32[128]{0:T(128)S(1)} collective-permute-done((f32[128]{0:T(128)S(1)}, f32[128]{0:T(128)S(1)}, u32[]{:S(2)}, u32[]{:S(2)}) %collective-permute-start.7) | collective-permute-done | bytes 544 | tf_op jit(solution)/shard_map/ppermute | solution.py:53
  81.1 2.3 %collective-permute-start.9 = (f32[128]{0:T(128)S(1)}, f32[128]{0:T(128)S(1)}, u32[]{:S(2)}, u32[]{:S(2)}) collective-permute-start(f32[128]{0:T(128)S(1)} %add.135), channel_id=1, source_target_pairs={{0,4},{1,5},{2,6},{3,7},{4,0},{5,1},{6,2},{7,3},{8,12},{9,13},{10,... | collective-permute-start | bytes 1544 | tf_op jit(solution)/shard_map/ppermute | solution.py:53
  85.8 3.3 %collective-permute-start.11 = (f32[128]{0:T(128)S(1)}, f32[128]{0:T(128)S(1)}, u32[]{:S(2)}, u32[]{:S(2)}) collective-permute-start(f32[128]{0:T(128)S(1)} %add_multiply_fusion), channel_id=1, source_target_pairs={{0,1},{1,0},{2,3},{3,2},{4,5},{5,4},{6,7},{7,6},{8,9},{9,8},{10,11... | collective-permute-start | bytes 1544 | tf_op jit(solution)/shard_map/ppermute | solution.py:53
  91.7 1.9 %head.4 = (f32[128,1024]{1,0:T(8,128)S(1)}, f32[1,512]{1,0:T(1,128)S(1)}) custom-call(s32[17]{0:T(128)S(1)} %pad_add_fusion.starts, bf16[8192,1024]{1,0:T(8,128)(2,1)S(1)} %get-tuple-element.33.w_ref, f32[128,1024]{1,0:T(8,128)S(1)} %broadcast_in_dim.9.before_ref, s32[1,128]{1,0:T(1,128)S(1)} %bitcast.141, bf16[2,128,512]{2,1,0:T(8,128)(2,1)S(1)} %fusion.5.rest_0_, ...), custom_call_target="tpu_custom_call" | custom-call | flops 536870912 | bytes 1048576 | tf_op jit(solution)/shard_map/head/pallas_call | solution.py:202
  93.6 4.6 %collective-permute-done.15 = bf16[2,1,128,512]{3,2,1,0:T(8,128)(2,1)S(1)} collective-permute-done((bf16[2,1,128,512]{3,2,1,0:T(8,128)(2,1)S(1)}, bf16[2,1,128,512]{3,2,1,0:T(8,128)(2,1)S(1)}, u32[]{:S(2)}, u32[]{:S(2)}) %collective-permute-start.15) | collective-permute-done | bytes 262176 | tf_op jit(solution)/shard_map/ppermute | solution.py:53
  101.5 3.1 %head.5 = (f32[128,1024]{1,0:T(8,128)S(1)}, f32[1,512]{1,0:T(1,128)S(1)}) custom-call(s32[17]{0:T(128)S(1)} %pad_add_fusion.starts, bf16[8192,1024]{1,0:T(8,128)(2,1)S(1)} %get-tuple-element.33.w_ref, f32[128,1024]{1,0:T(8,128)S(1)} %get-tuple-element.35.before_ref, s32[1,128]{1,0:T(1,128)S(1)} %bitcast.142, bf16[2,128,512]{2,1,0:T(8,128)(2,1)S(1)} %bitcast.121, ...), custom_call_target="tpu_custom_call" | custom-call | flops 1073741824 | bytes 1048576 | tf_op jit(solution)/shard_map/head/pallas_call | solution.py:202
  110.3 3.3 %collective-permute-done.21 = f32[4,128]{1,0:T(4,128)S(1)} collective-permute-done((f32[4,128]{1,0:T(4,128)S(1)}, f32[4,128]{1,0:T(4,128)S(1)}, u32[]{:S(2)}, u32[]{:S(2)}) %collective-permute-start.21) | collective-permute-done | bytes 2080 | tf_op jit(solution)/shard_map/ppermute | solution.py:53
  117.8 3.0 %collective-permute-start.25 = (f32[4,128]{1,0:T(4,128)S(1)}, f32[4,128]{1,0:T(4,128)S(1)}, u32[]{:S(2)}, u32[]{:S(2)}) collective-permute-start(f32[4,128]{1,0:T(4,128)S(1)} %pad_maximum_fusion.5), channel_id=1, source_target_pairs={{0,1},{1,0},{2,3},{3,2},{4,5},{5,4},{6,7},{7,6},{8,9},{9,8},{10,11... | collective-permute-start | bytes 6152 | tf_op jit(solution)/shard_map/ppermute | solution.py:53
  121.6 4.2 %back_first.1 = (f32[2,4,128,512]{3,2,1,0:T(8,128)S(1)}, bf16[128,1024]{1,0:T(8,128)(2,1)S(1)}) custom-call(s32[2,8]{1,0:T(2,128)S(1)} %xor_multiply_fusion.order, s32[17]{0:T(128)S(1)} %pad_add_fusion.starts, f32[128,1024]{1,0:T(8,128)S(1)} %get-tuple-element.42.logits_ref, f32[8,128]{1,0:T(8,128)S(1)} %broadcast_in_dim.11.stats_ref, ...), custom_call_target="tpu_custom_call" | custom-call | flops 1073741824 | bytes 2097152 | tf_op jit(solution)/shard_map/back_first/pallas_call | solution.py:239
  126.5 2.6 %back_rest.2 = (f32[2,2,128,512]{3,2,1,0:T(8,128)S(1)}, f32[1,512]{1,0:T(1,128)}) custom-call(s32[2,8]{1,0:T(2,128)S(1)} %xor_multiply_fusion.order, bf16[128,1024]{1,0:T(8,128)(2,1)S(1)} %get-tuple-element.43.d_ref, bf16[8192,1024]{1,0:T(8,128)(2,1)S(1)} %get-tuple-element.33.w_ref, f32[2,4,128,512]{3,2,1,0:T(8,128)S(1)} %get-tuple-element.44.after_ref), custom_call_target="tpu_custom_call" | custom-call | flops 536870912 | bytes 1048576 | tf_op jit(solution)/shard_map/back_rest/pallas_call | solution.py:256
  130.9 2.2 %back_rest.3 = (f32[2,2,128,512]{3,2,1,0:T(8,128)S(1)}, f32[1,512]{1,0:T(1,128)S(1)}) custom-call(s32[2,8]{1,0:T(2,128)S(1)} %xor_multiply_fusion.order, bf16[128,1024]{1,0:T(8,128)(2,1)S(1)} %get-tuple-element.43.d_ref, bf16[8192,1024]{1,0:T(8,128)(2,1)S(1)} %get-tuple-element.33.w_ref, f32[2,2,128,512]{3,2,1,0:T(8,128)S(1)} %slice_add_fusion.1.after_ref), custom_call_target="tpu_custom_call" | custom-call | flops 536870912 | bytes 1048576 | tf_op jit(solution)/shard_map/back_rest/pallas_call | solution.py:256
  133.2 4.4 %collective-permute-done.27 = f16[2,128,512]{2,1,0:T(8,128)(2,1)S(1)} collective-permute-done((f16[2,128,512]{2,1,0:T(8,128)(2,1)S(1)}, f16[2,128,512]{2,1,0:T(8,128)(2,1)S(1)}, u32[]{:S(2)}, u32[]{:S(2)}) %collective-permute-start.27) | collective-permute-done | bytes 262176 | tf_op jit(solution)/shard_map/ppermute | solution.py:53
  139.2 3.3 %collective-permute-done.29 = f16[1,128,512]{2,1,0:T(8,128)(2,1)S(1)} collective-permute-done((f16[1,128,512]{2,1,0:T(8,128)(2,1)S(1)}, f16[1,128,512]{2,1,0:T(8,128)(2,1)S(1)}, u32[]{:S(2)}, u32[]{:S(2)}) %collective-permute-start.29) | collective-permute-done | bytes 131104 | tf_op jit(solution)/shard_map/ppermute | solution.py:53
  144.2 9.0 %head_grad.1 = (bf16[8192,1024]{1,0:T(8,128)(2,1)}, f32[1,512]{1,0:T(1,128)S(1)}) custom-call(s32[17]{0:T(128)S(1)} %pad_add_fusion.starts, bf16[128,1024]{1,0:T(8,128)(2,1)S(1)} %get-tuple-element.43.d_ref, f32[2,1,128,512]{3,2,1,0:T(8,128)S(1)} %get-tuple-element.61.after_ref, bf16[2,128,512]{2,1,0:T(8,128)(2,1)S(1)} %fusion.5.rest_0_, ...), custom_call_target="tpu_custom_call" | custom-call | flops 2147483648 | bytes 16777216 | tf_op jit(solution)/shard_map/head_grad/pallas_call | solution.py:300
  153.2 2.9 %collective-permute-done.31 = f16[2,1,128,512]{3,2,1,0:T(8,128)(2,1)S(1)} collective-permute-done((f16[2,1,128,512]{3,2,1,0:T(8,128)(2,1)S(1)}, f16[2,1,128,512]{3,2,1,0:T(8,128)(2,1)S(1)}, u32[]{:S(2)}, u32[]{:S(2)}) %collective-permute-start.31) | collective-permute-done | bytes 262176 | tf_op jit(solution)/shard_map/ppermute | solution.py:53
  156.4 2.0 %collective-permute-start.32 = (bf16[2,1,128,512]{3,2,1,0:T(8,128)(2,1)S(1)}, bf16[2,1,128,512]{3,2,1,0:T(8,128)(2,1)S(1)}, u32[]{:S(2)}, u32[]{:S(2)}) collective-permute-start(bf16[2,1,128,512]{3,2,1,0:T(8,128)(2,1)S(1)} %get-tuple-element.56), channel_id=1, source_target_pairs={{0,1},{1,0},{2,3},{3,2},{4,5},{5,4},{6,7},{7,6},{8,9},{9,8},{10,11... | collective-permute-start | bytes 786440 | tf_op jit(solution)/shard_map/ppermute | solution.py:53
  159.6 3.7 %join_grad.4 = (bf16[3,512,8192]{2,1,0:T(8,128)(2,1)}, f32[1,512]{1,0:T(1,128)S(1)}) custom-call(s32[17]{0:T(128)S(1)} %pad_add_fusion.starts, bf16[1536,128]{1,0:T(8,128)(2,1)S(1)} %get-tuple-element.41.x_ref, bf16[2,128,512]{2,1,0:T(8,128)(2,1)S(1)} %bitcast.140, bf16[2,128,512]{2,1,0:T(8,128)(2,1)S(1)} %bitcast.152), custom_call_target="tpu_custom_call" | custom-call | flops 805306368 | bytes 6291456 | tf_op jit(solution)/shard_map/join_grad/pallas_call | solution.py:353
  163.3 3.0 %collective-permute-done.34 = bf16[2,1,128,512]{3,2,1,0:T(8,128)(2,1)S(1)} collective-permute-done((bf16[2,1,128,512]{3,2,1,0:T(8,128)(2,1)S(1)}, bf16[2,1,128,512]{3,2,1,0:T(8,128)(2,1)S(1)}, u32[]{:S(2)}, u32[]{:S(2)}) %collective-permute-start.34) | collective-permute-done | bytes 262176 | tf_op jit(solution)/shard_map/ppermute | solution.py:53
  169.4 6.0 %join_grad.5 = (bf16[3,512,8192]{2,1,0:T(8,128)(2,1)}, f32[1,512]{1,0:T(1,128)S(1)}) custom-call(s32[17]{0:T(128)S(1)} %pad_add_fusion.starts, bf16[1536,128]{1,0:T(8,128)(2,1)S(1)} %get-tuple-element.41.x_ref, bf16[3,512,8192]{2,1,0:T(8,128)(2,1)} %get-tuple-element.49.rest_0_, bf16[2,128,512]{2,1,0:T(8,128)(2,1)S(1)} %bitcast.124, ...), custom_call_target="tpu_custom_call", output_to_operand_aliasing={{0}: (2, {})} | custom-call | flops 1610612736 | bytes 12582912 | tf_op jit(solution)/shard_map/join_grad/pallas_call | solution.py:353
  177.9 3.1 %join_grad.6 = (bf16[3,512,8192]{2,1,0:T(8,128)(2,1)}, f32[1,512]{1,0:T(1,128)}) custom-call(s32[17]{0:T(128)S(1)} %pad_add_fusion.starts, bf16[1536,128]{1,0:T(8,128)(2,1)S(1)} %get-tuple-element.41.x_ref, bf16[3,512,8192]{2,1,0:T(8,128)(2,1)} %get-tuple-element.51.rest_0_, ...), custom_call_target="tpu_custom_call", output_to_operand_aliasing={{0}: (2, {})} | custom-call | flops 402653184 | bytes 3145728 | tf_op jit(solution)/shard_map/join_grad/pallas_call | solution.py:353
  181.0 3.1 %join_grad.7 = (bf16[3,512,8192]{2,1,0:T(8,128)(2,1)}, f32[1,512]{1,0:T(1,128)}) custom-call(s32[17]{0:T(128)S(1)} %pad_add_fusion.starts, bf16[1536,128]{1,0:T(8,128)(2,1)S(1)} %get-tuple-element.41.x_ref, bf16[3,512,8192]{2,1,0:T(8,128)(2,1)} %get-tuple-element.53.rest_0_, bf16[2,128,512]{2,1,0:T(8,128)(2,1)S(1)} %bitcast.138), custom_call_target="tpu_custom_call", output_to_operand_aliasing={{0}: (2, {})} | custom-call | flops 402653184 | bytes 3145728 | tf_op jit(solution)/shard_map/join_grad/pallas_call | solution.py:353
  (124 shorter events, 37.8 us)
Async XLA Ops:
  2.4 19.3 %all-to-all-start = ((bf16[16,8,1536]{2,1,0:T(8,128)(2,1)}), bf16[16,8,1536]{2,1,0:T(8,128)(2,1)S(1)}, u32[]{:S(2)}, u32[]{:S(2)}) async-start(bf16[16,8,1536]{2,1,0:T(8,128)(2,1)} %maximum_bitcast_fusion.after_ref), calls=%async_computation | async-start | bytes 786432 | tf_op jit(solution)/shard_map/all_to_all | solution.py:473
  27.6 4.5 %collective-permute-start = (f32[2,4,128,512]{3,2,1,0:T(8,128)S(1)}, f32[2,4,128,512]{3,2,1,0:T(8,128)S(1)}, u32[]{:S(2)}, u32[]{:S(2)}) collective-permute-start(f32[2,4,128,512]{3,2,1,0:T(8,128)S(1)} %get-tuple-element.31), channel_id=1, source_target_pairs={{0,1},{1,0},{2,3},{3,2},{4,5},{5,4},{6,7},{7,6},{8,9},{9,8},{10,11... | collective-permute-start | bytes 6291464 | tf_op jit(solution)/shard_map/ppermute | solution.py:53
  32.5 13.6 %collective-permute-start.1 = (f32[2,128,512]{2,1,0:T(8,128)S(1)}, f32[2,128,512]{2,1,0:T(8,128)S(1)}, u32[]{:S(2)}, u32[]{:S(2)}) collective-permute-start(f32[2,128,512]{2,1,0:T(8,128)S(1)} %get-tuple-element.74), channel_id=1, source_target_pairs={{0,2},{1,3},{2,0},{3,1},{4,6},{5,7},{6,4},{7,5},{8,10},{9,11},{10,... | collective-permute-start | bytes 1572872 | tf_op jit(solution)/shard_map/ppermute | solution.py:53
  32.8 13.2 %collective-permute-start.2 = (f32[2,128,512]{2,1,0:T(8,128)S(1)}, f32[2,128,512]{2,1,0:T(8,128)S(1)}, u32[]{:S(2)}, u32[]{:S(2)}) collective-permute-start(f32[2,128,512]{2,1,0:T(8,128)S(1)} %get-tuple-element.75), channel_id=1, source_target_pairs={{0,4},{1,5},{2,6},{3,7},{4,0},{5,1},{6,2},{7,3},{8,12},{9,13},{10,... | collective-permute-start | bytes 1572872 | tf_op jit(solution)/shard_map/ppermute | solution.py:53
  46.5 6.8 %collective-permute-start.3 = (f32[1,128,512]{2,1,0:T(8,128)S(1)}, f32[1,128,512]{2,1,0:T(8,128)S(1)}, u32[]{:S(2)}, u32[]{:S(2)}) collective-permute-start(f32[1,128,512]{2,1,0:T(8,128)S(1)} %get-tuple-element.72), channel_id=1, source_target_pairs={{0,4},{1,5},{2,6},{3,7},{4,0},{5,1},{6,2},{7,3},{8,12},{9,13},{10,... | collective-permute-start | bytes 786440 | tf_op jit(solution)/shard_map/ppermute | solution.py:53
  47.2 6.1 %collective-permute-start.4 = (f32[1,128,512]{2,1,0:T(8,128)S(1)}, f32[1,128,512]{2,1,0:T(8,128)S(1)}, u32[]{:S(2)}, u32[]{:S(2)}) collective-permute-start(f32[1,128,512]{2,1,0:T(8,128)S(1)} %get-tuple-element.73), channel_id=1, source_target_pairs={{0,2},{1,3},{2,0},{3,1},{4,6},{5,7},{6,4},{7,5},{8,10},{9,11},{10,... | collective-permute-start | bytes 786440 | tf_op jit(solution)/shard_map/ppermute | solution.py:53
  53.4 13.9 %collective-permute-start.5 = (f32[1,128,512]{2,1,0:T(8,128)S(1)}, f32[1,128,512]{2,1,0:T(8,128)S(1)}, u32[]{:S(2)}, u32[]{:S(2)}) collective-permute-start(f32[1,128,512]{2,1,0:T(8,128)S(1)} %slice_bitcast_fusion.3), channel_id=1, source_target_pairs={{0,8},{1,9},{2,10},{3,11},{4,12},{5,13},{6,14},{7,15},{8,0},{9,1},... | collective-permute-start | bytes 786440 | tf_op jit(solution)/shard_map/ppermute | solution.py:53
  67.3 16.3 %collective-permute-start.6 = (f32[1,128,512]{2,1,0:T(8,128)S(1)}, f32[1,128,512]{2,1,0:T(8,128)S(1)}, u32[]{:S(2)}, u32[]{:S(2)}) collective-permute-start(f32[1,128,512]{2,1,0:T(8,128)S(1)} %get-tuple-element.67), channel_id=1, source_target_pairs={{0,8},{1,9},{2,10},{3,11},{4,12},{5,13},{6,14},{7,15},{8,0},{9,1},... | collective-permute-start | bytes 786440 | tf_op jit(solution)/shard_map/ppermute | solution.py:53
  67.4 13.5 %collective-permute-start.7 = (f32[128]{0:T(128)S(1)}, f32[128]{0:T(128)S(1)}, u32[]{:S(2)}, u32[]{:S(2)}) collective-permute-start(f32[128]{0:T(128)S(1)} %get-tuple-element.66), channel_id=1, source_target_pairs={{0,8},{1,9},{2,10},{3,11},{4,12},{5,13},{6,14},{7,15},{8,0},{9,1},... | collective-permute-start | bytes 1544 | tf_op jit(solution)/shard_map/ppermute | solution.py:53
  69.8 19.3 %collective-permute-start.12 = (f32[512]{0:T(512)S(1)}, f32[512]{0:T(512)S(1)}, u32[]{:S(2)}, u32[]{:S(2)}) collective-permute-start(f32[512]{0:T(512)S(1)} %copy-done.1), channel_id=1, source_target_pairs={{0,8},{1,9},{2,10},{3,11},{4,12},{5,13},{6,14},{7,15},{8,0},{9,1},... | collective-permute-start | bytes 6152 | tf_op jit(solution)/shard_map/ppermute | solution.py:53
  81.0 3.8 %collective-permute-start.10 = (f32[128]{0:T(128)S(1)}, f32[128]{0:T(128)S(1)}, u32[]{:S(2)}, u32[]{:S(2)}) collective-permute-start(f32[128]{0:T(128)S(1)} %add.135), channel_id=1, source_target_pairs={{0,6},{1,7},{2,4},{3,5},{4,2},{5,3},{6,0},{7,1},{8,14},{9,15},{10,... | collective-permute-start | bytes 1544 | tf_op jit(solution)/shard_map/ppermute | solution.py:53
  81.1 3.7 %collective-permute-start.9 = (f32[128]{0:T(128)S(1)}, f32[128]{0:T(128)S(1)}, u32[]{:S(2)}, u32[]{:S(2)}) collective-permute-start(f32[128]{0:T(128)S(1)} %add.135), channel_id=1, source_target_pairs={{0,4},{1,5},{2,6},{3,7},{4,0},{5,1},{6,2},{7,3},{8,12},{9,13},{10,... | collective-permute-start | bytes 1544 | tf_op jit(solution)/shard_map/ppermute | solution.py:53
  85.8 4.1 %collective-permute-start.11 = (f32[128]{0:T(128)S(1)}, f32[128]{0:T(128)S(1)}, u32[]{:S(2)}, u32[]{:S(2)}) collective-permute-start(f32[128]{0:T(128)S(1)} %add_multiply_fusion), channel_id=1, source_target_pairs={{0,1},{1,0},{2,3},{3,2},{4,5},{5,4},{6,7},{7,6},{8,9},{9,8},{10,11... | collective-permute-start | bytes 1544 | tf_op jit(solution)/shard_map/ppermute | solution.py:53
  90.5 7.7 %collective-permute-start.15 = (bf16[2,1,128,512]{3,2,1,0:T(8,128)(2,1)S(1)}, bf16[2,1,128,512]{3,2,1,0:T(8,128)(2,1)S(1)}, u32[]{:S(2)}, u32[]{:S(2)}) collective-permute-start(bf16[2,1,128,512]{3,2,1,0:T(8,128)(2,1)S(1)} %multiply_convert_fusion.6), channel_id=1, source_target_pairs={{0,4},{1,5},{2,6},{3,7},{4,0},{5,1},{6,2},{7,3},{8,12},{9,13},{10,... | collective-permute-start | bytes 786440 | tf_op jit(solution)/shard_map/ppermute | solution.py:53
  90.5 7.8 %collective-permute-start.14 = (bf16[2,1,128,512]{3,2,1,0:T(8,128)(2,1)S(1)}, bf16[2,1,128,512]{3,2,1,0:T(8,128)(2,1)S(1)}, u32[]{:S(2)}, u32[]{:S(2)}) collective-permute-start(bf16[2,1,128,512]{3,2,1,0:T(8,128)(2,1)S(1)} %multiply_convert_fusion.6), channel_id=1, source_target_pairs={{0,2},{1,3},{2,0},{3,1},{4,6},{5,7},{6,4},{7,5},{8,10},{9,11},{10,... | collective-permute-start | bytes 786440 | tf_op jit(solution)/shard_map/ppermute | solution.py:53
  99.6 5.1 %collective-permute-start.19 = (bf16[1,128,512]{2,1,0:T(8,128)(2,1)S(1)}, bf16[1,128,512]{2,1,0:T(8,128)(2,1)S(1)}, u32[]{:S(2)}, u32[]{:S(2)}) collective-permute-start(bf16[1,128,512]{2,1,0:T(8,128)(2,1)S(1)} %slice_bitcast_fusion.9), channel_id=1, source_target_pairs={{0,4},{1,5},{2,6},{3,7},{4,0},{5,1},{6,2},{7,3},{8,12},{9,13},{10,... | collective-permute-start | bytes 393224 | tf_op jit(solution)/shard_map/ppermute | solution.py:53
  101.1 4.3 %collective-permute-start.18 = (bf16[1,128,512]{2,1,0:T(8,128)(2,1)S(1)}, bf16[1,128,512]{2,1,0:T(8,128)(2,1)S(1)}, u32[]{:S(2)}, u32[]{:S(2)}) collective-permute-start(bf16[1,128,512]{2,1,0:T(8,128)(2,1)S(1)} %slice_bitcast_fusion.10), channel_id=1, source_target_pairs={{0,2},{1,3},{2,0},{3,1},{4,6},{5,7},{6,4},{7,5},{8,10},{9,11},{10,... | collective-permute-start | bytes 393224 | tf_op jit(solution)/shard_map/ppermute | solution.py:53
  105.5 3.1 %collective-permute-start.20 = (bf16[2,1,128,512]{3,2,1,0:T(8,128)(2,1)S(1)}, bf16[2,1,128,512]{3,2,1,0:T(8,128)(2,1)S(1)}, u32[]{:S(2)}, u32[]{:S(2)}) collective-permute-start(bf16[2,1,128,512]{3,2,1,0:T(8,128)(2,1)S(1)} %pad_maximum_fusion.1), channel_id=1, source_target_pairs={{0,1},{1,0},{2,3},{3,2},{4,5},{5,4},{6,7},{7,6},{8,9},{9,8},{10,11... | collective-permute-start | bytes 786440 | tf_op jit(solution)/shard_map/ppermute | solution.py:53
  110.2 3.4 %collective-permute-start.21 = (f32[4,128]{1,0:T(4,128)S(1)}, f32[4,128]{1,0:T(4,128)S(1)}, u32[]{:S(2)}, u32[]{:S(2)}) collective-permute-start(f32[4,128]{1,0:T(4,128)S(1)} %slice.182), channel_id=1, source_target_pairs={{0,8},{1,9},{2,10},{3,11},{4,12},{5,13},{6,14},{7,15},{8,0},{9,1},... | collective-permute-start | bytes 6152 | tf_op jit(solution)/shard_map/ppermute | solution.py:53
  113.6 3.4 %collective-permute-start.24 = (f32[4,128]{1,0:T(4,128)S(1)}, f32[4,128]{1,0:T(4,128)S(1)}, u32[]{:S(2)}, u32[]{:S(2)}) collective-permute-start(f32[4,128]{1,0:T(4,128)S(1)} %pad_maximum_fusion.4), channel_id=1, source_target_pairs={{0,6},{1,7},{2,4},{3,5},{4,2},{5,3},{6,0},{7,1},{8,14},{9,15},{10,... | collective-permute-start | bytes 6152 | tf_op jit(solution)/shard_map/ppermute | solution.py:53
  117.8 3.8 %collective-permute-start.25 = (f32[4,128]{1,0:T(4,128)S(1)}, f32[4,128]{1,0:T(4,128)S(1)}, u32[]{:S(2)}, u32[]{:S(2)}) collective-permute-start(f32[4,128]{1,0:T(4,128)S(1)} %pad_maximum_fusion.5), channel_id=1, source_target_pairs={{0,1},{1,0},{2,3},{3,2},{4,5},{5,4},{6,7},{7,6},{8,9},{9,8},{10,11... | collective-permute-start | bytes 6152 | tf_op jit(solution)/shard_map/ppermute | solution.py:53
  129.8 7.8 %collective-permute-start.27 = (f16[2,128,512]{2,1,0:T(8,128)(2,1)S(1)}, f16[2,128,512]{2,1,0:T(8,128)(2,1)S(1)}, u32[]{:S(2)}, u32[]{:S(2)}) collective-permute-start(f16[2,128,512]{2,1,0:T(8,128)(2,1)S(1)} %get-tuple-element.70), channel_id=1, source_target_pairs={{0,2},{1,3},{2,0},{3,1},{4,6},{5,7},{6,4},{7,5},{8,10},{9,11},{10,... | collective-permute-start | bytes 786440 | tf_op jit(solution)/shard_map/ppermute | solution.py:53
  130.8 7.4 %collective-permute-start.28 = (f16[2,128,512]{2,1,0:T(8,128)(2,1)S(1)}, f16[2,128,512]{2,1,0:T(8,128)(2,1)S(1)}, u32[]{:S(2)}, u32[]{:S(2)}) collective-permute-start(f16[2,128,512]{2,1,0:T(8,128)(2,1)S(1)} %get-tuple-element.71), channel_id=1, source_target_pairs={{0,4},{1,5},{2,6},{3,7},{4,0},{5,1},{6,2},{7,3},{8,12},{9,13},{10,... | collective-permute-start | bytes 786440 | tf_op jit(solution)/shard_map/ppermute | solution.py:53
  138.6 3.9 %collective-permute-start.29 = (f16[1,128,512]{2,1,0:T(8,128)(2,1)S(1)}, f16[1,128,512]{2,1,0:T(8,128)(2,1)S(1)}, u32[]{:S(2)}, u32[]{:S(2)}) collective-permute-start(f16[1,128,512]{2,1,0:T(8,128)(2,1)S(1)} %get-tuple-element.68), channel_id=1, source_target_pairs={{0,4},{1,5},{2,6},{3,7},{4,0},{5,1},{6,2},{7,3},{8,12},{9,13},{10,... | collective-permute-start | bytes 393224 | tf_op jit(solution)/shard_map/ppermute | solution.py:53
  138.8 3.8 %collective-permute-start.30 = (f16[1,128,512]{2,1,0:T(8,128)(2,1)S(1)}, f16[1,128,512]{2,1,0:T(8,128)(2,1)S(1)}, u32[]{:S(2)}, u32[]{:S(2)}) collective-permute-start(f16[1,128,512]{2,1,0:T(8,128)(2,1)S(1)} %get-tuple-element.69), channel_id=1, source_target_pairs={{0,2},{1,3},{2,0},{3,1},{4,6},{5,7},{6,4},{7,5},{8,10},{9,11},{10,... | collective-permute-start | bytes 393224 | tf_op jit(solution)/shard_map/ppermute | solution.py:53
  142.7 13.3 %collective-permute-start.31 = (f16[2,1,128,512]{3,2,1,0:T(8,128)(2,1)S(1)}, f16[2,1,128,512]{3,2,1,0:T(8,128)(2,1)S(1)}, u32[]{:S(2)}, u32[]{:S(2)}) collective-permute-start(f16[2,1,128,512]{3,2,1,0:T(8,128)(2,1)S(1)} %get-tuple-element.60), channel_id=1, source_target_pairs={{0,8},{1,9},{2,10},{3,11},{4,12},{5,13},{6,14},{7,15},{8,0},{9,1},... | collective-permute-start | bytes 786440 | tf_op jit(solution)/shard_map/ppermute | solution.py:53
  156.4 3.2 %collective-permute-start.32 = (bf16[2,1,128,512]{3,2,1,0:T(8,128)(2,1)S(1)}, bf16[2,1,128,512]{3,2,1,0:T(8,128)(2,1)S(1)}, u32[]{:S(2)}, u32[]{:S(2)}) collective-permute-start(bf16[2,1,128,512]{3,2,1,0:T(8,128)(2,1)S(1)} %get-tuple-element.56), channel_id=1, source_target_pairs={{0,1},{1,0},{2,3},{3,2},{4,5},{5,4},{6,7},{7,6},{8,9},{9,8},{10,11... | collective-permute-start | bytes 786440 | tf_op jit(solution)/shard_map/ppermute | solution.py:53
  158.4 7.9 %collective-permute-start.34 = (bf16[2,1,128,512]{3,2,1,0:T(8,128)(2,1)S(1)}, bf16[2,1,128,512]{3,2,1,0:T(8,128)(2,1)S(1)}, u32[]{:S(2)}, u32[]{:S(2)}) collective-permute-start(bf16[2,1,128,512]{3,2,1,0:T(8,128)(2,1)S(1)} %get-tuple-element.56), channel_id=1, source_target_pairs={{0,4},{1,5},{2,6},{3,7},{4,0},{5,1},{6,2},{7,3},{8,12},{9,13},{10,... | collective-permute-start | bytes 786440 | tf_op jit(solution)/shard_map/ppermute | solution.py:53
  158.4 7.9 %collective-permute-start.33 = (bf16[2,1,128,512]{3,2,1,0:T(8,128)(2,1)S(1)}, bf16[2,1,128,512]{3,2,1,0:T(8,128)(2,1)S(1)}, u32[]{:S(2)}, u32[]{:S(2)}) collective-permute-start(bf16[2,1,128,512]{3,2,1,0:T(8,128)(2,1)S(1)} %get-tuple-element.56), channel_id=1, source_target_pairs={{0,2},{1,3},{2,0},{3,1},{4,6},{5,7},{6,4},{7,5},{8,10},{9,11},{10,... | collective-permute-start | bytes 786440 | tf_op jit(solution)/shard_map/ppermute | solution.py:53
  167.4 8.1 %collective-permute-start.38 = (bf16[1,128,512]{2,1,0:T(8,128)(2,1)S(1)}, bf16[1,128,512]{2,1,0:T(8,128)(2,1)S(1)}, u32[]{:S(2)}, u32[]{:S(2)}) collective-permute-start(bf16[1,128,512]{2,1,0:T(8,128)(2,1)S(1)} %slice_bitcast_fusion.7), channel_id=1, source_target_pairs={{0,4},{1,5},{2,6},{3,7},{4,0},{5,1},{6,2},{7,3},{8,12},{9,13},{10,... | collective-permute-start | bytes 393224 | tf_op jit(solution)/shard_map/ppermute | solution.py:53
  168.9 6.6 %collective-permute-start.37 = (bf16[1,128,512]{2,1,0:T(8,128)(2,1)S(1)}, bf16[1,128,512]{2,1,0:T(8,128)(2,1)S(1)}, u32[]{:S(2)}, u32[]{:S(2)}) collective-permute-start(bf16[1,128,512]{2,1,0:T(8,128)(2,1)S(1)} %slice_bitcast_fusion.8), channel_id=1, source_target_pairs={{0,2},{1,3},{2,0},{3,1},{4,6},{5,7},{6,4},{7,5},{8,10},{9,11},{10,... | collective-permute-start | bytes 393224 | tf_op jit(solution)/shard_map/ppermute | solution.py:53
  175.6 5.4 %collective-permute-start.39 = (bf16[2,1,128,512]{3,2,0,1:T(8,128)(2,1)S(1)}, bf16[2,1,128,512]{3,2,0,1:T(8,128)(2,1)S(1)}, u32[]{:S(2)}, u32[]{:S(2)}) collective-permute-start(bf16[2,1,128,512]{3,2,0,1:T(8,128)(2,1)S(1)} %pad_maximum_fusion.2), channel_id=1, source_target_pairs={{0,1},{1,0},{2,3},{3,2},{4,5},{5,4},{6,7},{7,6},{8,9},{9,8},{10,11... | collective-permute-start | bytes 786440 | tf_op jit(solution)/shard_map/ppermute | solution.py:53
  (12 other events, 121.8 us)

commit v10 on v8

--- a/solution.py
+++ b/solution.py
@@ -38,6 +38,20 @@
     over_y, over_z = held ^ 2, held ^ 4
     second = np.stack([over_z[0] ^ 2, over_y[1] ^ 4])
     out += [*across, fresh ^ 1, over_y, over_z, over_y ^ 1, over_z ^ 1, second, second ^ 1]
+    return np.concatenate([p.reshape(-1) for p in out]).astype(np.int32)
+
+
+def gather_crossing_places(bits):
+    held = fresh = np.array([[0], [1 << (bits - 1)]], np.int32)
+    out, across = [held], []
+    for bit in range(bits - 2, 2, -1):
+        across.append(fresh ^ 1)
+        fresh = held ^ (1 << bit)
+        held = np.concatenate([held, fresh], axis=1)
+        out.append(fresh)
+    first = held ^ np.array([[4], [2]], np.int32)
+    second = np.concatenate([held, first], axis=1) ^ np.array([[2], [4]], np.int32)
+    out += [*across, fresh ^ 1, first, first ^ 1, second, second ^ 1]
     return np.concatenate([p.reshape(-1) for p in out]).astype(np.int32)
 
 
@@ -455,6 +469,32 @@
     work([flat(across)], True)
 
 
+def gather_crossing(held, bits, size, work):
+    def flat(x):
+        return x.reshape((-1,) + x.shape[2:])
+
+    fresh = held
+    across = []
+    for bit in range(bits - 2, 2, -1):
+        arrived = exchange(held, 1 << bit, size)
+        across.append(exchange(fresh, 1, size))
+        token = work([flat(fresh)], False)
+        fresh = with_token(arrived, token)
+        held = jnp.concatenate([held, fresh], axis=1)
+    first = [exchange(held[0], 4, size), exchange(held[1], 2, size)]
+    across.append(exchange(fresh, 1, size))
+    token = work([flat(fresh)], False)
+    first = with_token(jnp.stack(first), token)
+    across += [first, exchange(first, 1, size)]
+    both = jnp.concatenate([held, first], axis=1)
+    second = [exchange(both[0], 2, size), exchange(both[1], 4, size)]
+    token = work([flat(a) for a in across], False)
+    second = with_token(jnp.stack(second), token)
+    across = exchange(second, 1, size)
+    work([flat(second)], False)
+    work([flat(across)], True)
+
+
 def on_device(size, low_feat, mid_feat, high_feat, w_fc, gain, w_lm, targets):
     me = lax.axis_index("section")
     rows, full_width = w_fc.shape[1], w_fc.shape[2]
@@ -464,6 +504,7 @@
     count, quarter = size // 4, size // 8
     order = (jnp.asarray(reduce_places(bits)) ^ me) * rows
     starts = jnp.concatenate([(jnp.asarray(gather_places(bits)) ^ me) * rows, me[None]])
+    crossing_starts = jnp.concatenate([(jnp.asarray(gather_crossing_places(bits)) ^ me) * rows, me[None]])
     kernels = rows % TILE == 0
     target_row = targets.reshape(1, tokens)
 
@@ -593,14 +634,14 @@
         first = sum(p.shape[0] for p in all_dfused)
         all_dfused.extend(pieces)
         if kernels:
-            held["grad_fc"], token = join_grad(starts, first, pieces, held["x"], full_width, held["grad_fc"])
+            held["grad_fc"], token = join_grad(crossing_starts, first, pieces, held["x"], full_width, held["grad_fc"])
             return token
 
-    gather(dfused, bits, size, fill_grad_fc)
+    gather_crossing(dfused, bits, size, fill_grad_fc)
     if kernels:
         grad_fc = held["grad_fc"]
     else:
-        grad_fc = jnp.dot(x.T, whole(all_dfused, starts), preferred_element_type=jnp.float32)
+        grad_fc = jnp.dot(x.T, whole(all_dfused, crossing_starts), preferred_element_type=jnp.float32)
         grad_fc = grad_fc.astype(jnp.bfloat16).reshape(3, rows, full_width)
     return (token_loss, grad_fc, grad_gain, grad_lm)
 

time: 183 us -> 182 us (level)
    ppermute x38 -> x37, waiting for transfers between devices: 56.6 us -> 55.5 us  [exchange(): return lax.ppermute(x, 'section', [(i, i ^ mask) for i in range(size)])]
    ppermute x38 -> x37, starting transfers between devices: 37.3 us -> 36.8 us  [exchange(): return lax.ppermute(x, 'section', [(i, i ^ mask) for i in range(size)])]
  transfers between devices with their start and end apart: 39 -> 38, of which waited for: 25 -> 21; matrix products, arithmetic and copies ran while one was open for 1% -> 2% of each run, Pallas kernels for 26% -> 25%
where the time goes in v10:
time: 182 us
  waiting for transfers between devices  66.7 us (37%)
  Pallas kernels  62 us (34%)
  starting transfers between devices  44.1 us (24%)
  other arithmetic  7.51 us (4%)
    ppermute x37, waiting for transfers between devices, exchange(): return lax.ppermute(x, 'section', [(i, i ^ mask) for i in range(size)])  55.5 us
    ppermute x37, starting transfers between devices, exchange(): return lax.ppermute(x, 'section', [(i, i ^ mask) for i in range(size)])  36.8 us
    pallas_call x4, Pallas kernels, join_grad(): pl.pallas_call(functools.partial(join_grad_kernel, first, counts, len(ext...  16 us
    pallas_call x3, Pallas kernels, join(): pl.pallas_call(functools.partial(join_kernel, first, count), out_shape=tu...  14 us
    all_to_all x1, waiting for transfers between devices, on_device(): lax.all_to_all(sent, 'section', split_axis=0, concat_axis=0, tiled=True)  11.2 us
    pallas_call x1, Pallas kernels, head_grad(): pl.pallas_call(functools.partial(head_grad_kernel, counts), out_shape=(ja...  8.97 us
    pallas_call x4, Pallas kernels, head(): pl.pallas_call(functools.partial(head_kernel, first, counts, last), out_s...  8.06 us
    all_to_all x1, starting transfers between devices, on_device(): lax.all_to_all(sent, 'section', split_axis=0, concat_axis=0, tiled=True)  7.35 us
  transfers between devices with their start and end apart: 38, of which 21 were waited for; matrix products, arithmetic and copies ran while one was open for 2% of the time, Pallas kernels for 25%

profile of v10, /device:TPU:1, one launch (start us, length us, event | category | flops | bytes accessed | tf_op | source)
XLA Modules:
  0.0 182.0 jit_solution(5502268203072644154)
XLA Ops:
  0.6 1.8 maximum_bitcast_fusion.after_ref
  2.4 7.3 %all-to-all-start = ((bf16[16,8,1536]{2,1,0:T(8,128)(2,1)}), bf16[16,8,1536]{2,1,0:T(8,128)(2,1)S(1)}, u32[]{:S(2)}, u32[]{:S(2)}) async-start(bf16[16,8,1536]{2,1,0:T(8,128)(2,1)} %maximum_bitcast_fusion.after_ref), calls=%async_computation | async-start | bytes 786432 | tf_op jit(solution)/shard_map/all_to_all | solution.py:514
  10.5 11.2 %all-to-all-done = bf16[16,8,1536]{2,1,0:T(8,128)(2,1)S(1)} async-done(((bf16[16,8,1536]{2,1,0:T(8,128)(2,1)}), bf16[16,8,1536]{2,1,0:T(8,128)(2,1)S(1)}, u32[]{:S(2)}, u32[]{:S(2)}) %all-to-all-start) | async-done | bytes 393248 | tf_op jit(solution)/shard_map/all_to_all | solution.py:514
  21.7 5.9 %join.4 = (f32[2,4,128,512]{3,2,1,0:T(8,128)S(1)}, f32[1,512]{1,0:T(1,128)}, bf16[1536,128]{1,0:T(8,128)(2,1)S(1)}) custom-call(s32[2,8]{1,0:T(2,128)S(1)} %xor_multiply_fusion.order, bf16[128,1536]{1,0:T(8,128)(2,1)S(1)} %bitcast.161, bf16[3,512,8192]{2,1,0:T(8,128)(2,1)} %w_ref.6, bf16[16,8,1536]{2,1,0:T(8,128)(2,1)} %maximum_bitcast_fusion.after_ref), custom_call_target="tpu_custom_call" | custom-call | flops 1610612736 | bytes 12582912 | tf_op jit(solution)/shard_map/join/pallas_call | solution.py:157
  28.1 4.0 %join.3 = (f32[2,2,128,512]{3,2,1,0:T(8,128)S(1)}, f32[1,512]{1,0:T(1,128)}) custom-call(s32[2,8]{1,0:T(2,128)S(1)} %xor_multiply_fusion.order, bf16[128,1536]{1,0:T(8,128)(2,1)S(1)} %bitcast.162, bf16[3,512,8192]{2,1,0:T(8,128)(2,1)} %w_ref.6, bf16[16,8,1536]{2,1,0:T(8,128)(2,1)} %maximum_bitcast_fusion.after_ref), custom_call_target="tpu_custom_call" | custom-call | flops 805306368 | bytes 6291456 | tf_op jit(solution)/shard_map/join/pallas_call | solution.py:157
  33.8 4.0 %join.5 = (f32[2,2,128,512]{3,2,1,0:T(8,128)S(1)}, f32[1,512]{1,0:T(1,128)}) custom-call(s32[2,8]{1,0:T(2,128)S(1)} %xor_multiply_fusion.order, bf16[128,1536]{1,0:T(8,128)(2,1)S(1)} %bitcast.163, bf16[3,512,8192]{2,1,0:T(8,128)(2,1)} %w_ref.6, f32[2,2,128,512]{3,2,1,0:T(8,128)S(1)} %slice_add_fusion.3.after_ref), custom_call_target="tpu_custom_call" | custom-call | flops 805306368 | bytes 6291456 | tf_op jit(solution)/shard_map/join/pallas_call | solution.py:157
  37.8 5.9 %stage.1 = (bf16[8192,1024]{1,0:T(8,128)(2,1)S(1)}, f32[1,512]{1,0:T(1,128)S(1)}) custom-call(bf16[8192,1024]{1,0:T(8,128)(2,1)} %w_ref.7, f32[2,2,128,512]{3,2,1,0:T(8,128)S(1)} %get-tuple-element.32.after_ref), custom_call_target="tpu_custom_call" | custom-call | bytes 16777216 | tf_op jit(solution)/shard_map/stage/pallas_call | solution.py:105
  43.8 2.3 %collective-permute-done.1 = f32[2,128,512]{2,1,0:T(8,128)S(1)} collective-permute-done((f32[2,128,512]{2,1,0:T(8,128)S(1)}, f32[2,128,512]{2,1,0:T(8,128)S(1)}, u32[]{:S(2)}, u32[]{:S(2)}) %collective-permute-start.1) | collective-permute-done | bytes 524320 | tf_op jit(solution)/shard_map/ppermute | solution.py:67
  47.8 5.4 %collective-permute-done.3 = f32[1,128,512]{2,1,0:T(8,128)S(1)} collective-permute-done((f32[1,128,512]{2,1,0:T(8,128)S(1)}, f32[1,128,512]{2,1,0:T(8,128)S(1)}, u32[]{:S(2)}, u32[]{:S(2)}) %collective-permute-start.3) | collective-permute-done | bytes 262176 | tf_op jit(solution)/shard_map/ppermute | solution.py:67
  53.3 1.8 collective-permute-start.5
  55.8 22.7 %collective-permute-done.5 = f32[2,1,128,512]{3,2,0,1:T(8,128)S(1)} collective-permute-done((f32[2,1,128,512]{3,2,0,1:T(8,128)S(1)}, f32[2,1,128,512]{3,2,0,1:T(8,128)S(1)}, u32[]{:S(2)}, u32[]{:S(2)}) %collective-permute-start.5) | collective-permute-done | bytes 524320 | tf_op jit(solution)/shard_map/ppermute | solution.py:67
  83.4 3.2 %collective-permute-start.9 = (f32[128]{0:T(128)S(1)}, f32[128]{0:T(128)S(1)}, u32[]{:S(2)}, u32[]{:S(2)}) collective-permute-start(f32[128]{0:T(128)S(1)} %add_add_fusion.3), channel_id=1, source_target_pairs={{0,1},{1,0},{2,3},{3,2},{4,5},{5,4},{6,7},{7,6},{8,9},{9,8},{10,11... | collective-permute-start | bytes 1544 | tf_op jit(solution)/shard_map/ppermute | solution.py:67
  89.2 1.8 %head.4 = (f32[128,1024]{1,0:T(8,128)S(1)}, f32[1,512]{1,0:T(1,128)S(1)}) custom-call(s32[17]{0:T(128)S(1)} %pad_add_fusion.starts, bf16[8192,1024]{1,0:T(8,128)(2,1)S(1)} %get-tuple-element.33.w_ref, f32[128,1024]{1,0:T(8,128)S(1)} %broadcast_in_dim.9.before_ref, s32[1,128]{1,0:T(1,128)S(1)} %bitcast.183, bf16[2,128,512]{2,1,0:T(8,128)(2,1)S(1)} %fusion.31.rest_0_, ...), custom_call_target="tpu_custom_call" | custom-call | flops 536870912 | bytes 1048576 | tf_op jit(solution)/shard_map/head/pallas_call | solution.py:216
  91.1 4.6 %collective-permute-done.12 = bf16[2,1,128,512]{3,2,1,0:T(8,128)(2,1)S(1)} collective-permute-done((bf16[2,1,128,512]{3,2,1,0:T(8,128)(2,1)S(1)}, bf16[2,1,128,512]{3,2,1,0:T(8,128)(2,1)S(1)}, u32[]{:S(2)}, u32[]{:S(2)}) %collective-permute-start.12) | collective-permute-done | bytes 262176 | tf_op jit(solution)/shard_map/ppermute | solution.py:67
  99.2 3.1 %head.5 = (f32[128,1024]{1,0:T(8,128)S(1)}, f32[1,512]{1,0:T(1,128)S(1)}) custom-call(s32[17]{0:T(128)S(1)} %pad_add_fusion.starts, bf16[8192,1024]{1,0:T(8,128)(2,1)S(1)} %get-tuple-element.33.w_ref, f32[128,1024]{1,0:T(8,128)S(1)} %get-tuple-element.35.before_ref, s32[1,128]{1,0:T(1,128)S(1)} %bitcast.184, ...), custom_call_target="tpu_custom_call" | custom-call | flops 1073741824 | bytes 1048576 | tf_op jit(solution)/shard_map/head/pallas_call | solution.py:216
  103.0 1.7 collective-permute-start.18
  109.2 2.0 %collective-permute-done.19 = f32[4,128]{1,0:T(4,128)S(1)} collective-permute-done((f32[4,128]{1,0:T(4,128)S(1)}, f32[4,128]{1,0:T(4,128)S(1)}, u32[]{:S(2)}, u32[]{:S(2)}) %collective-permute-start.19) | collective-permute-done | bytes 2080 | tf_op jit(solution)/shard_map/ppermute | solution.py:67
  115.4 3.0 %collective-permute-start.23 = (f32[4,128]{1,0:T(4,128)S(1)}, f32[4,128]{1,0:T(4,128)S(1)}, u32[]{:S(2)}, u32[]{:S(2)}) collective-permute-start(f32[4,128]{1,0:T(4,128)S(1)} %pad_maximum_fusion.4), channel_id=1, source_target_pairs={{0,1},{1,0},{2,3},{3,2},{4,5},{5,4},{6,7},{7,6},{8,9},{9,8},{10,11... | collective-permute-start | bytes 6152 | tf_op jit(solution)/shard_map/ppermute | solution.py:67
  119.2 4.2 %back_first.1 = (f32[2,4,128,512]{3,2,1,0:T(8,128)S(1)}, bf16[128,1024]{1,0:T(8,128)(2,1)S(1)}) custom-call(s32[2,8]{1,0:T(2,128)S(1)} %xor_multiply_fusion.order, s32[17]{0:T(128)S(1)} %pad_add_fusion.starts, f32[128,1024]{1,0:T(8,128)S(1)} %get-tuple-element.42.logits_ref, f32[8,128]{1,0:T(8,128)S(1)} %broadcast_in_dim.11.stats_ref, ...), custom_call_target="tpu_custom_call" | custom-call | flops 1073741824 | bytes 2097152 | tf_op jit(solution)/shard_map/back_first/pallas_call | solution.py:253
  124.1 2.6 %back_rest.2 = (f32[2,2,128,512]{3,2,1,0:T(8,128)S(1)}, f32[1,512]{1,0:T(1,128)}) custom-call(s32[2,8]{1,0:T(2,128)S(1)} %xor_multiply_fusion.order, bf16[128,1024]{1,0:T(8,128)(2,1)S(1)} %get-tuple-element.43.d_ref, bf16[8192,1024]{1,0:T(8,128)(2,1)S(1)} %get-tuple-element.33.w_ref, f32[2,4,128,512]{3,2,1,0:T(8,128)S(1)} %get-tuple-element.44.after_ref), custom_call_target="tpu_custom_call" | custom-call | flops 536870912 | bytes 1048576 | tf_op jit(solution)/shard_map/back_rest/pallas_call | solution.py:270
  128.5 2.2 %back_rest.3 = (f32[2,2,128,512]{3,2,1,0:T(8,128)S(1)}, f32[1,512]{1,0:T(1,128)S(1)}) custom-call(s32[2,8]{1,0:T(2,128)S(1)} %xor_multiply_fusion.order, bf16[128,1024]{1,0:T(8,128)(2,1)S(1)} %get-tuple-element.43.d_ref, bf16[8192,1024]{1,0:T(8,128)(2,1)S(1)} %get-tuple-element.33.w_ref, f32[2,2,128,512]{3,2,1,0:T(8,128)S(1)} %slice_add_fusion.1.after_ref), custom_call_target="tpu_custom_call" | custom-call | flops 536870912 | bytes 1048576 | tf_op jit(solution)/shard_map/back_rest/pallas_call | solution.py:270
  130.7 4.4 %collective-permute-done.25 = f16[2,128,512]{2,1,0:T(8,128)(2,1)S(1)} collective-permute-done((f16[2,128,512]{2,1,0:T(8,128)(2,1)S(1)}, f16[2,128,512]{2,1,0:T(8,128)(2,1)S(1)}, u32[]{:S(2)}, u32[]{:S(2)}) %collective-permute-start.25) | collective-permute-done | bytes 262176 | tf_op jit(solution)/shard_map/ppermute | solution.py:67
  137.2 2.8 %collective-permute-done.27 = f16[1,128,512]{2,1,0:T(8,128)(2,1)S(1)} collective-permute-done((f16[1,128,512]{2,1,0:T(8,128)(2,1)S(1)}, f16[1,128,512]{2,1,0:T(8,128)(2,1)S(1)}, u32[]{:S(2)}, u32[]{:S(2)}) %collective-permute-start.27) | collective-permute-done | bytes 131104 | tf_op jit(solution)/shard_map/ppermute | solution.py:67
  140.3 2.9 %collective-permute-start.29 = (f16[2,1,128,512]{3,2,0,1:T(8,128)(2,1)S(1)}, f16[2,1,128,512]{3,2,0,1:T(8,128)(2,1)S(1)}, u32[]{:S(2)}, u32[]{:S(2)}) collective-permute-start(f16[2,1,128,512]{3,2,0,1:T(8,128)(2,1)S(1)} %get-tuple-element.66), channel_id=1, source_target_pairs={{0,8},{1,9},{2,10},{3,11},{4,12},{5,13},{6,14},{7,15},{8,0},{9,1},... | collective-permute-start | bytes 786440 | tf_op jit(solution)/shard_map/ppermute | solution.py:67
  143.3 9.0 %head_grad.1 = (bf16[8192,1024]{1,0:T(8,128)(2,1)}, f32[1,512]{1,0:T(1,128)S(1)}) custom-call(s32[17]{0:T(128)S(1)} %pad_add_fusion.starts, bf16[128,1024]{1,0:T(8,128)(2,1)S(1)} %get-tuple-element.43.d_ref, f32[2,1,128,512]{3,2,1,0:T(8,128)S(1)} %get-tuple-element.67.after_ref, bf16[2,128,512]{2,1,0:T(8,128)(2,1)S(1)} %fusion.31.rest_0_, ...), custom_call_target="tpu_custom_call" | custom-call | flops 2147483648 | bytes 16777216 | tf_op jit(solution)/shard_map/head_grad/pallas_call | solution.py:314
  152.2 2.3 %collective-permute-done.29 = f16[2,1,128,512]{3,2,0,1:T(8,128)(2,1)S(1)} collective-permute-done((f16[2,1,128,512]{3,2,0,1:T(8,128)(2,1)S(1)}, f16[2,1,128,512]{3,2,0,1:T(8,128)(2,1)S(1)}, u32[]{:S(2)}, u32[]{:S(2)}) %collective-permute-start.29) | collective-permute-done | bytes 262176 | tf_op jit(solution)/shard_map/ppermute | solution.py:67
  158.0 2.6 %join_grad.4 = (bf16[3,512,8192]{2,1,0:T(8,128)(2,1)}, f32[1,512]{1,0:T(1,128)S(1)}) custom-call(s32[17]{0:T(128)S(1)} %pad_add_fusion.1.starts, bf16[1536,128]{1,0:T(8,128)(2,1)S(1)} %get-tuple-element.41.x_ref, bf16[2,128,512]{2,1,0:T(8,128)(2,1)S(1)} %bitcast.165), custom_call_target="tpu_custom_call" | custom-call | flops 402653184 | bytes 3145728 | tf_op jit(solution)/shard_map/join_grad/pallas_call | solution.py:367
  160.7 1.9 %collective-permute-start.33 = (bf16[2,1,128,512]{3,2,0,1:T(8,128)(2,1)S(1)}, bf16[2,1,128,512]{3,2,0,1:T(8,128)(2,1)S(1)}, u32[]{:S(2)}, u32[]{:S(2)}) collective-permute-start(bf16[2,1,128,512]{3,2,0,1:T(8,128)(2,1)S(1)} %bitcast_convert_fusion), channel_id=1, source_target_pairs={{0,1},{1,0},{2,3},{3,2},{4,5},{5,4},{6,7},{7,6},{8,9},{9,8},{10,11... | collective-permute-start | bytes 786440 | tf_op jit(solution)/shard_map/ppermute | solution.py:67
  163.8 4.9 %join_grad.5 = (bf16[3,512,8192]{2,1,0:T(8,128)(2,1)}, f32[1,512]{1,0:T(1,128)S(1)}) custom-call(s32[17]{0:T(128)S(1)} %pad_add_fusion.1.starts, bf16[1536,128]{1,0:T(8,128)(2,1)S(1)} %get-tuple-element.41.x_ref, bf16[3,512,8192]{2,1,0:T(8,128)(2,1)} %get-tuple-element.49.rest_0_, ...), custom_call_target="tpu_custom_call", output_to_operand_aliasing={{0}: (2, {})} | custom-call | flops 1207959552 | bytes 9437184 | tf_op jit(solution)/shard_map/join_grad/pallas_call | solution.py:367
  168.6 2.0 %collective-permute-done.34 = bf16[2,128,512]{2,1,0:T(8,128)(2,1)S(1)} collective-permute-done((bf16[2,128,512]{2,1,0:T(8,128)(2,1)S(1)}, bf16[2,128,512]{2,1,0:T(8,128)(2,1)S(1)}, u32[]{:S(2)}, u32[]{:S(2)}) %collective-permute-start.34) | collective-permute-done | bytes 262176 | tf_op jit(solution)/shard_map/ppermute | solution.py:67
  173.2 4.3 %join_grad.6 = (bf16[3,512,8192]{2,1,0:T(8,128)(2,1)}, f32[1,512]{1,0:T(1,128)}) custom-call(s32[17]{0:T(128)S(1)} %pad_add_fusion.1.starts, bf16[1536,128]{1,0:T(8,128)(2,1)S(1)} %get-tuple-element.41.x_ref, bf16[3,512,8192]{2,1,0:T(8,128)(2,1)} %get-tuple-element.51.rest_0_, bf16[4,128,512]{2,1,0:T(8,128)(2,1)S(1)} %fusion.1.rest_1_), custom_call_target="tpu_custom_call", output_to_operand_aliasing={{0}: (2, {})} | custom-call | flops 805306368 | bytes 6291456 | tf_op jit(solution)/shard_map/join_grad/pallas_call | solution.py:367
  177.5 4.3 %join_grad.7 = (bf16[3,512,8192]{2,1,0:T(8,128)(2,1)}, f32[1,512]{1,0:T(1,128)}) custom-call(s32[17]{0:T(128)S(1)} %pad_add_fusion.1.starts, bf16[1536,128]{1,0:T(8,128)(2,1)S(1)} %get-tuple-element.41.x_ref, bf16[3,512,8192]{2,1,0:T(8,128)(2,1)} %get-tuple-element.53.rest_0_, bf16[4,128,512]{2,1,0:T(8,128)(2,1)S(1)} %bitcast.168), custom_call_target="tpu_custom_call", output_to_operand_aliasing={{0}: (2, {})} | custom-call | flops 805306368 | bytes 6291456 | tf_op jit(solution)/shard_map/join_grad/pallas_call | solution.py:367
  (129 shorter events, 38.5 us)
Async XLA Ops:
  2.4 19.3 %all-to-all-start = ((bf16[16,8,1536]{2,1,0:T(8,128)(2,1)}), bf16[16,8,1536]{2,1,0:T(8,128)(2,1)S(1)}, u32[]{:S(2)}, u32[]{:S(2)}) async-start(bf16[16,8,1536]{2,1,0:T(8,128)(2,1)} %maximum_bitcast_fusion.after_ref), calls=%async_computation | async-start | bytes 786432 | tf_op jit(solution)/shard_map/all_to_all | solution.py:514
  27.6 4.5 %collective-permute-start = (f32[2,4,128,512]{3,2,1,0:T(8,128)S(1)}, f32[2,4,128,512]{3,2,1,0:T(8,128)S(1)}, u32[]{:S(2)}, u32[]{:S(2)}) collective-permute-start(f32[2,4,128,512]{3,2,1,0:T(8,128)S(1)} %get-tuple-element.31), channel_id=1, source_target_pairs={{0,1},{1,0},{2,3},{3,2},{4,5},{5,4},{6,7},{7,6},{8,9},{9,8},{10,11... | collective-permute-start | bytes 6291464 | tf_op jit(solution)/shard_map/ppermute | solution.py:67
  32.5 13.6 %collective-permute-start.1 = (f32[2,128,512]{2,1,0:T(8,128)S(1)}, f32[2,128,512]{2,1,0:T(8,128)S(1)}, u32[]{:S(2)}, u32[]{:S(2)}) collective-permute-start(f32[2,128,512]{2,1,0:T(8,128)S(1)} %get-tuple-element.72), channel_id=1, source_target_pairs={{0,2},{1,3},{2,0},{3,1},{4,6},{5,7},{6,4},{7,5},{8,10},{9,11},{10,... | collective-permute-start | bytes 1572872 | tf_op jit(solution)/shard_map/ppermute | solution.py:67
  32.8 13.2 %collective-permute-start.2 = (f32[2,128,512]{2,1,0:T(8,128)S(1)}, f32[2,128,512]{2,1,0:T(8,128)S(1)}, u32[]{:S(2)}, u32[]{:S(2)}) collective-permute-start(f32[2,128,512]{2,1,0:T(8,128)S(1)} %get-tuple-element.73), channel_id=1, source_target_pairs={{0,4},{1,5},{2,6},{3,7},{4,0},{5,1},{6,2},{7,3},{8,12},{9,13},{10,... | collective-permute-start | bytes 1572872 | tf_op jit(solution)/shard_map/ppermute | solution.py:67
  46.5 6.8 %collective-permute-start.3 = (f32[1,128,512]{2,1,0:T(8,128)S(1)}, f32[1,128,512]{2,1,0:T(8,128)S(1)}, u32[]{:S(2)}, u32[]{:S(2)}) collective-permute-start(f32[1,128,512]{2,1,0:T(8,128)S(1)} %get-tuple-element.70), channel_id=1, source_target_pairs={{0,4},{1,5},{2,6},{3,7},{4,0},{5,1},{6,2},{7,3},{8,12},{9,13},{10,... | collective-permute-start | bytes 786440 | tf_op jit(solution)/shard_map/ppermute | solution.py:67
  47.2 6.1 %collective-permute-start.4 = (f32[1,128,512]{2,1,0:T(8,128)S(1)}, f32[1,128,512]{2,1,0:T(8,128)S(1)}, u32[]{:S(2)}, u32[]{:S(2)}) collective-permute-start(f32[1,128,512]{2,1,0:T(8,128)S(1)} %get-tuple-element.71), channel_id=1, source_target_pairs={{0,2},{1,3},{2,0},{3,1},{4,6},{5,7},{6,4},{7,5},{8,10},{9,11},{10,... | collective-permute-start | bytes 786440 | tf_op jit(solution)/shard_map/ppermute | solution.py:67
  53.3 25.1 %collective-permute-start.5 = (f32[2,1,128,512]{3,2,0,1:T(8,128)S(1)}, f32[2,1,128,512]{3,2,0,1:T(8,128)S(1)}, u32[]{:S(2)}, u32[]{:S(2)}) collective-permute-start(f32[2,1,128,512]{3,2,0,1:T(8,128)S(1)} %fusion.4), channel_id=1, source_target_pairs={{0,8},{1,9},{2,10},{3,11},{4,12},{5,13},{6,14},{7,15},{8,0},{9,1},... | collective-permute-start | bytes 1572872 | tf_op jit(solution)/shard_map/ppermute | solution.py:67
  55.1 31.4 %collective-permute-start.10 = (f32[512]{0:T(512)S(1)}, f32[512]{0:T(512)S(1)}, u32[]{:S(2)}, u32[]{:S(2)}) collective-permute-start(f32[512]{0:T(512)S(1)} %copy-done.1), channel_id=1, source_target_pairs={{0,8},{1,9},{2,10},{3,11},{4,12},{5,13},{6,14},{7,15},{8,0},{9,1},... | collective-permute-start | bytes 6152 | tf_op jit(solution)/shard_map/ppermute | solution.py:67
  79.5 3.3 %collective-permute-start.8 = (f32[128]{0:T(128)S(1)}, f32[128]{0:T(128)S(1)}, u32[]{:S(2)}, u32[]{:S(2)}) collective-permute-start(f32[128]{0:T(128)S(1)} %add_bitcast_fusion.1), channel_id=1, source_target_pairs={{0,6},{1,7},{2,4},{3,5},{4,2},{5,3},{6,0},{7,1},{8,14},{9,15},{10,... | collective-permute-start | bytes 1544 | tf_op jit(solution)/shard_map/ppermute | solution.py:67
  83.4 4.0 %collective-permute-start.9 = (f32[128]{0:T(128)S(1)}, f32[128]{0:T(128)S(1)}, u32[]{:S(2)}, u32[]{:S(2)}) collective-permute-start(f32[128]{0:T(128)S(1)} %add_add_fusion.3), channel_id=1, source_target_pairs={{0,1},{1,0},{2,3},{3,2},{4,5},{5,4},{6,7},{7,6},{8,9},{9,8},{10,11... | collective-permute-start | bytes 1544 | tf_op jit(solution)/shard_map/ppermute | solution.py:67
  88.0 9.0 %collective-permute-start.13 = (bf16[2,1,128,512]{3,2,0,1:T(8,128)(2,1)S(1)}, bf16[2,1,128,512]{3,2,0,1:T(8,128)(2,1)S(1)}, u32[]{:S(2)}, u32[]{:S(2)}) collective-permute-start(bf16[2,1,128,512]{3,2,0,1:T(8,128)(2,1)S(1)} %multiply_convert_fusion.5), channel_id=1, source_target_pairs={{0,4},{1,5},{2,6},{3,7},{4,0},{5,1},{6,2},{7,3},{8,12},{9,13},{10,... | collective-permute-start | bytes 786440 | tf_op jit(solution)/shard_map/ppermute | solution.py:67
  88.1 7.6 %collective-permute-start.12 = (bf16[2,1,128,512]{3,2,1,0:T(8,128)(2,1)S(1)}, bf16[2,1,128,512]{3,2,1,0:T(8,128)(2,1)S(1)}, u32[]{:S(2)}, u32[]{:S(2)}) collective-permute-start(bf16[2,1,128,512]{3,2,1,0:T(8,128)(2,1)S(1)} %fusion.30), channel_id=1, source_target_pairs={{0,2},{1,3},{2,0},{3,1},{4,6},{5,7},{6,4},{7,5},{8,10},{9,11},{10,... | collective-permute-start | bytes 786440 | tf_op jit(solution)/shard_map/ppermute | solution.py:67
  95.8 3.4 %collective-permute-start.14 = (bf16[2,1,128,512]{3,2,1,0:T(8,128)(2,1)S(1)}, bf16[2,1,128,512]{3,2,1,0:T(8,128)(2,1)S(1)}, u32[]{:S(2)}, u32[]{:S(2)}) collective-permute-start(bf16[2,1,128,512]{3,2,1,0:T(8,128)(2,1)S(1)} %multiply_convert_fusion.4), channel_id=1, source_target_pairs={{0,1},{1,0},{2,3},{3,2},{4,5},{5,4},{6,7},{7,6},{8,9},{9,8},{10,11... | collective-permute-start | bytes 786440 | tf_op jit(solution)/shard_map/ppermute | solution.py:67
  97.2 5.1 %collective-permute-start.17 = (bf16[1,128,512]{2,1,0:T(8,128)(2,1)S(1)}, bf16[1,128,512]{2,1,0:T(8,128)(2,1)S(1)}, u32[]{:S(2)}, u32[]{:S(2)}) collective-permute-start(bf16[1,128,512]{2,1,0:T(8,128)(2,1)S(1)} %slice_bitcast_fusion.8), channel_id=1, source_target_pairs={{0,4},{1,5},{2,6},{3,7},{4,0},{5,1},{6,2},{7,3},{8,12},{9,13},{10,... | collective-permute-start | bytes 393224 | tf_op jit(solution)/shard_map/ppermute | solution.py:67
  98.6 4.3 %collective-permute-start.16 = (bf16[1,128,512]{2,1,0:T(8,128)(2,1)S(1)}, bf16[1,128,512]{2,1,0:T(8,128)(2,1)S(1)}, u32[]{:S(2)}, u32[]{:S(2)}) collective-permute-start(bf16[1,128,512]{2,1,0:T(8,128)(2,1)S(1)} %slice_bitcast_fusion.9), channel_id=1, source_target_pairs={{0,2},{1,3},{2,0},{3,1},{4,6},{5,7},{6,4},{7,5},{8,10},{9,11},{10,... | collective-permute-start | bytes 393224 | tf_op jit(solution)/shard_map/ppermute | solution.py:67
  103.0 3.2 %collective-permute-start.18 = (bf16[2,1,128,512]{3,2,1,0:T(8,128)(2,1)S(1)}, bf16[2,1,128,512]{3,2,1,0:T(8,128)(2,1)S(1)}, u32[]{:S(2)}, u32[]{:S(2)}) collective-permute-start(bf16[2,1,128,512]{3,2,1,0:T(8,128)(2,1)S(1)} %pad_maximum_fusion.1), channel_id=1, source_target_pairs={{0,1},{1,0},{2,3},{3,2},{4,5},{5,4},{6,7},{7,6},{8,9},{9,8},{10,11... | collective-permute-start | bytes 786440 | tf_op jit(solution)/shard_map/ppermute | solution.py:67
  107.8 3.4 %collective-permute-start.19 = (f32[4,128]{1,0:T(4,128)S(1)}, f32[4,128]{1,0:T(4,128)S(1)}, u32[]{:S(2)}, u32[]{:S(2)}) collective-permute-start(f32[4,128]{1,0:T(4,128)S(1)} %slice.195), channel_id=1, source_target_pairs={{0,8},{1,9},{2,10},{3,11},{4,12},{5,13},{6,14},{7,15},{8,0},{9,1},... | collective-permute-start | bytes 6152 | tf_op jit(solution)/shard_map/ppermute | solution.py:67
  111.2 3.4 %collective-permute-start.22 = (f32[4,128]{1,0:T(4,128)S(1)}, f32[4,128]{1,0:T(4,128)S(1)}, u32[]{:S(2)}, u32[]{:S(2)}) collective-permute-start(f32[4,128]{1,0:T(4,128)S(1)} %pad_maximum_fusion.3), channel_id=1, source_target_pairs={{0,6},{1,7},{2,4},{3,5},{4,2},{5,3},{6,0},{7,1},{8,14},{9,15},{10,... | collective-permute-start | bytes 6152 | tf_op jit(solution)/shard_map/ppermute | solution.py:67
  115.4 3.8 %collective-permute-start.23 = (f32[4,128]{1,0:T(4,128)S(1)}, f32[4,128]{1,0:T(4,128)S(1)}, u32[]{:S(2)}, u32[]{:S(2)}) collective-permute-start(f32[4,128]{1,0:T(4,128)S(1)} %pad_maximum_fusion.4), channel_id=1, source_target_pairs={{0,1},{1,0},{2,3},{3,2},{4,5},{5,4},{6,7},{7,6},{8,9},{9,8},{10,11... | collective-permute-start | bytes 6152 | tf_op jit(solution)/shard_map/ppermute | solution.py:67
  123.7 3.0 %collective-permute-start.24 = (f16[2,4,128,512]{3,2,1,0:T(8,128)(2,1)S(1)}, f16[2,4,128,512]{3,2,1,0:T(8,128)(2,1)S(1)}, u32[]{:S(2)}, u32[]{:S(2)}) collective-permute-start(f16[2,4,128,512]{3,2,1,0:T(8,128)(2,1)S(1)} %multiply_convert_fusion), channel_id=1, source_target_pairs={{0,1},{1,0},{2,3},{3,2},{4,5},{5,4},{6,7},{7,6},{8,9},{9,8},{10,11... | collective-permute-start | bytes 3145736 | tf_op jit(solution)/shard_map/ppermute | solution.py:67
  127.3 7.8 %collective-permute-start.25 = (f16[2,128,512]{2,1,0:T(8,128)(2,1)S(1)}, f16[2,128,512]{2,1,0:T(8,128)(2,1)S(1)}, u32[]{:S(2)}, u32[]{:S(2)}) collective-permute-start(f16[2,128,512]{2,1,0:T(8,128)(2,1)S(1)} %get-tuple-element.68), channel_id=1, source_target_pairs={{0,2},{1,3},{2,0},{3,1},{4,6},{5,7},{6,4},{7,5},{8,10},{9,11},{10,... | collective-permute-start | bytes 786440 | tf_op jit(solution)/shard_map/ppermute | solution.py:67
  128.4 7.4 %collective-permute-start.26 = (f16[2,128,512]{2,1,0:T(8,128)(2,1)S(1)}, f16[2,128,512]{2,1,0:T(8,128)(2,1)S(1)}, u32[]{:S(2)}, u32[]{:S(2)}) collective-permute-start(f16[2,128,512]{2,1,0:T(8,128)(2,1)S(1)} %get-tuple-element.69), channel_id=1, source_target_pairs={{0,4},{1,5},{2,6},{3,7},{4,0},{5,1},{6,2},{7,3},{8,12},{9,13},{10,... | collective-permute-start | bytes 786440 | tf_op jit(solution)/shard_map/ppermute | solution.py:67
  136.2 3.9 %collective-permute-start.27 = (f16[1,128,512]{2,1,0:T(8,128)(2,1)S(1)}, f16[1,128,512]{2,1,0:T(8,128)(2,1)S(1)}, u32[]{:S(2)}, u32[]{:S(2)}) collective-permute-start(f16[1,128,512]{2,1,0:T(8,128)(2,1)S(1)} %fusion.18), channel_id=1, source_target_pairs={{0,4},{1,5},{2,6},{3,7},{4,0},{5,1},{6,2},{7,3},{8,12},{9,13},{10,... | collective-permute-start | bytes 393224 | tf_op jit(solution)/shard_map/ppermute | solution.py:67
  136.3 3.8 %collective-permute-start.28 = (f16[1,128,512]{2,1,0:T(8,128)(2,1)S(1)}, f16[1,128,512]{2,1,0:T(8,128)(2,1)S(1)}, u32[]{:S(2)}, u32[]{:S(2)}) collective-permute-start(f16[1,128,512]{2,1,0:T(8,128)(2,1)S(1)} %fusion.19), channel_id=1, source_target_pairs={{0,2},{1,3},{2,0},{3,1},{4,6},{5,7},{6,4},{7,5},{8,10},{9,11},{10,... | collective-permute-start | bytes 393224 | tf_op jit(solution)/shard_map/ppermute | solution.py:67
  140.3 14.3 %collective-permute-start.29 = (f16[2,1,128,512]{3,2,0,1:T(8,128)(2,1)S(1)}, f16[2,1,128,512]{3,2,0,1:T(8,128)(2,1)S(1)}, u32[]{:S(2)}, u32[]{:S(2)}) collective-permute-start(f16[2,1,128,512]{3,2,0,1:T(8,128)(2,1)S(1)} %get-tuple-element.66), channel_id=1, source_target_pairs={{0,8},{1,9},{2,10},{3,11},{4,12},{5,13},{6,14},{7,15},{8,0},{9,1},... | collective-permute-start | bytes 786440 | tf_op jit(solution)/shard_map/ppermute | solution.py:67
  154.9 5.7 %collective-permute-start.32 = (bf16[1,128,512]{2,1,0:T(8,128)(2,1)S(1)}, bf16[1,128,512]{2,1,0:T(8,128)(2,1)S(1)}, u32[]{:S(2)}, u32[]{:S(2)}) collective-permute-start(bf16[1,128,512]{2,1,0:T(8,128)(2,1)S(1)} %slice_bitcast_fusion.6), channel_id=1, source_target_pairs={{0,2},{1,3},{2,0},{3,1},{4,6},{5,7},{6,4},{7,5},{8,10},{9,11},{10,... | collective-permute-start | bytes 393224 | tf_op jit(solution)/shard_map/ppermute | solution.py:67
  156.0 4.6 %collective-permute-start.31 = (bf16[1,128,512]{2,1,0:T(8,128)(2,1)S(1)}, bf16[1,128,512]{2,1,0:T(8,128)(2,1)S(1)}, u32[]{:S(2)}, u32[]{:S(2)}) collective-permute-start(bf16[1,128,512]{2,1,0:T(8,128)(2,1)S(1)} %slice_bitcast_fusion.7), channel_id=1, source_target_pairs={{0,4},{1,5},{2,6},{3,7},{4,0},{5,1},{6,2},{7,3},{8,12},{9,13},{10,... | collective-permute-start | bytes 393224 | tf_op jit(solution)/shard_map/ppermute | solution.py:67
  156.6 7.0 %collective-permute-start.30 = (bf16[2,1,128,512]{3,2,0,1:T(8,128)(2,1)S(1)}, bf16[2,1,128,512]{3,2,0,1:T(8,128)(2,1)S(1)}, u32[]{:S(2)}, u32[]{:S(2)}) collective-permute-start(bf16[2,1,128,512]{3,2,0,1:T(8,128)(2,1)S(1)} %get-tuple-element.56), channel_id=1, source_target_pairs={{0,1},{1,0},{2,3},{3,2},{4,5},{5,4},{6,7},{7,6},{8,9},{9,8},{10,11... | collective-permute-start | bytes 786440 | tf_op jit(solution)/shard_map/ppermute | solution.py:67
  160.7 3.1 %collective-permute-start.33 = (bf16[2,1,128,512]{3,2,0,1:T(8,128)(2,1)S(1)}, bf16[2,1,128,512]{3,2,0,1:T(8,128)(2,1)S(1)}, u32[]{:S(2)}, u32[]{:S(2)}) collective-permute-start(bf16[2,1,128,512]{3,2,0,1:T(8,128)(2,1)S(1)} %bitcast_convert_fusion), channel_id=1, source_target_pairs={{0,1},{1,0},{2,3},{3,2},{4,5},{5,4},{6,7},{7,6},{8,9},{9,8},{10,11... | collective-permute-start | bytes 786440 | tf_op jit(solution)/shard_map/ppermute | solution.py:67
  162.6 8.0 %collective-permute-start.34 = (bf16[2,128,512]{2,1,0:T(8,128)(2,1)S(1)}, bf16[2,128,512]{2,1,0:T(8,128)(2,1)S(1)}, u32[]{:S(2)}, u32[]{:S(2)}) collective-permute-start(bf16[2,128,512]{2,1,0:T(8,128)(2,1)S(1)} %get-tuple-element.74), channel_id=1, source_target_pairs={{0,2},{1,3},{2,0},{3,1},{4,6},{5,7},{6,4},{7,5},{8,10},{9,11},{10,... | collective-permute-start | bytes 786440 | tf_op jit(solution)/shard_map/ppermute | solution.py:67
  163.4 7.6 %collective-permute-start.35 = (bf16[2,128,512]{2,1,0:T(8,128)(2,1)S(1)}, bf16[2,128,512]{2,1,0:T(8,128)(2,1)S(1)}, u32[]{:S(2)}, u32[]{:S(2)}) collective-permute-start(bf16[2,128,512]{2,1,0:T(8,128)(2,1)S(1)} %get-tuple-element.75), channel_id=1, source_target_pairs={{0,4},{1,5},{2,6},{3,7},{4,0},{5,1},{6,2},{7,3},{8,12},{9,13},{10,... | collective-permute-start | bytes 786440 | tf_op jit(solution)/shard_map/ppermute | solution.py:67
  171.2 6.4 %collective-permute-start.36 = (bf16[2,2,128,512]{3,2,1,0:T(8,128)(2,1)S(1)}, bf16[2,2,128,512]{3,2,1,0:T(8,128)(2,1)S(1)}, u32[]{:S(2)}, u32[]{:S(2)}) collective-permute-start(bf16[2,2,128,512]{3,2,1,0:T(8,128)(2,1)S(1)} %multiply_convert_fusion.1), channel_id=1, source_target_pairs={{0,1},{1,0},{2,3},{3,2},{4,5},{5,4},{6,7},{7,6},{8,9},{9,8},{10,11... | collective-permute-start | bytes 1572872 | tf_op jit(solution)/shard_map/ppermute | solution.py:67
  (10 other events, 44.2 us)

commit v11 on v10

--- a/solution.py
+++ b/solution.py
@@ -489,10 +489,10 @@
     both = jnp.concatenate([held, first], axis=1)
     second = [exchange(both[0], 2, size), exchange(both[1], 4, size)]
     token = work([flat(a) for a in across], False)
-    second = with_token(jnp.stack(second), token)
-    across = exchange(second, 1, size)
-    work([flat(second)], False)
-    work([flat(across)], True)
+    second = [with_token(x, token) for x in second]
+    across = [exchange(x, 1, size) for x in second]
+    work(second, False)
+    work(across, True)
 
 
 def on_device(size, low_feat, mid_feat, high_feat, w_fc, gain, w_lm, targets):
@@ -580,7 +580,7 @@
         stats = merge_sums(contributions(stats, group, size))
     peak, exp_total, exp_moment, picked = stats[0], stats[1], stats[2], stats[3]
     log_total = peak + jnp.log(exp_total)
-    token_loss = log_total - picked
+    log_total, token_loss = lax.optimization_barrier((log_total, log_total - picked))
     rowdot = ((exp_moment / exp_total - (picked - peak)) / tokens)[:, None] / inv_rms
 
     if kernels:

time: 182 us -> 183 us (level)
    ppermute x37 -> x38, starting transfers between devices: 36.8 us -> 38.3 us  [exchange(): return lax.ppermute(x, 'section', [(i, i ^ mask) for i in range(size)])]
    ppermute x37 -> x38, waiting for transfers between devices: 55.5 us -> 54.9 us  [exchange(): return lax.ppermute(x, 'section', [(i, i ^ mask) for i in range(size)])]
  transfers between devices with their start and end apart: 38 -> 39, of which waited for: 21 -> 25; matrix products, arithmetic and copies ran while one was open for 2% -> 1% of each run, Pallas kernels for 25% -> 25%
where the time goes in v11:
time: 183 us; the launch traced here: 182 us
  waiting for transfers between devices  66.1 us (36%)
  Pallas kernels  61.9 us (34%)
  starting transfers between devices  45.7 us (25%)
  other arithmetic  7.08 us (4%)
    ppermute x38, waiting for transfers between devices, exchange(): return lax.ppermute(x, 'section', [(i, i ^ mask) for i in range(size)])  54.9 us
    ppermute x38, starting transfers between devices, exchange(): return lax.ppermute(x, 'section', [(i, i ^ mask) for i in range(size)])  38.3 us
    pallas_call x4, Pallas kernels, join_grad(): pl.pallas_call(functools.partial(join_grad_kernel, first, counts, len(ext...  16 us
    pallas_call x3, Pallas kernels, join(): pl.pallas_call(functools.partial(join_kernel, first, count), out_shape=tu...  14 us
    all_to_all x1, waiting for transfers between devices, on_device(): lax.all_to_all(sent, 'section', split_axis=0, concat_axis=0, tiled=True)  11.2 us
    pallas_call x1, Pallas kernels, head_grad(): pl.pallas_call(functools.partial(head_grad_kernel, counts), out_shape=(ja...  8.96 us
    pallas_call x4, Pallas kernels, head(): pl.pallas_call(functools.partial(head_kernel, first, counts, last), out_s...  8.06 us
    all_to_all x1, starting transfers between devices, on_device(): lax.all_to_all(sent, 'section', split_axis=0, concat_axis=0, tiled=True)  7.35 us
  transfers between devices with their start and end apart: 39, of which 25 were waited for; matrix products, arithmetic and copies ran while one was open for 1% of the time, Pallas kernels for 25%

profile of v11, /device:TPU:1, one launch (start us, length us, event | category | flops | bytes accessed | tf_op | source)
XLA Modules:
  0.0 182.3 jit_solution(18008428595058663871)
XLA Ops:
  0.6 1.8 maximum_bitcast_fusion.after_ref
  2.4 7.3 %all-to-all-start = ((bf16[16,8,1536]{2,1,0:T(8,128)(2,1)}), bf16[16,8,1536]{2,1,0:T(8,128)(2,1)S(1)}, u32[]{:S(2)}, u32[]{:S(2)}) async-start(bf16[16,8,1536]{2,1,0:T(8,128)(2,1)} %maximum_bitcast_fusion.after_ref), calls=%async_computation | async-start | bytes 786432 | tf_op jit(solution)/shard_map/all_to_all | solution.py:514
  10.5 11.2 %all-to-all-done = bf16[16,8,1536]{2,1,0:T(8,128)(2,1)S(1)} async-done(((bf16[16,8,1536]{2,1,0:T(8,128)(2,1)}), bf16[16,8,1536]{2,1,0:T(8,128)(2,1)S(1)}, u32[]{:S(2)}, u32[]{:S(2)}) %all-to-all-start) | async-done | bytes 393248 | tf_op jit(solution)/shard_map/all_to_all | solution.py:514
  21.7 5.9 %join.4 = (f32[2,4,128,512]{3,2,1,0:T(8,128)S(1)}, f32[1,512]{1,0:T(1,128)}, bf16[1536,128]{1,0:T(8,128)(2,1)S(1)}) custom-call(s32[2,8]{1,0:T(2,128)S(1)} %xor_multiply_fusion.order, bf16[128,1536]{1,0:T(8,128)(2,1)S(1)} %bitcast.104, bf16[3,512,8192]{2,1,0:T(8,128)(2,1)} %w_ref.6, bf16[16,8,1536]{2,1,0:T(8,128)(2,1)} %maximum_bitcast_fusion.after_ref), custom_call_target="tpu_custom_call" | custom-call | flops 1610612736 | bytes 12582912 | tf_op jit(solution)/shard_map/join/pallas_call | solution.py:157
  28.1 4.0 %join.3 = (f32[2,2,128,512]{3,2,1,0:T(8,128)S(1)}, f32[1,512]{1,0:T(1,128)}) custom-call(s32[2,8]{1,0:T(2,128)S(1)} %xor_multiply_fusion.order, bf16[128,1536]{1,0:T(8,128)(2,1)S(1)} %bitcast.105, bf16[3,512,8192]{2,1,0:T(8,128)(2,1)} %w_ref.6, bf16[16,8,1536]{2,1,0:T(8,128)(2,1)} %maximum_bitcast_fusion.after_ref), custom_call_target="tpu_custom_call" | custom-call | flops 805306368 | bytes 6291456 | tf_op jit(solution)/shard_map/join/pallas_call | solution.py:157
  33.8 4.0 %join.5 = (f32[2,2,128,512]{3,2,1,0:T(8,128)S(1)}, f32[1,512]{1,0:T(1,128)}) custom-call(s32[2,8]{1,0:T(2,128)S(1)} %xor_multiply_fusion.order, bf16[128,1536]{1,0:T(8,128)(2,1)S(1)} %bitcast.106, bf16[3,512,8192]{2,1,0:T(8,128)(2,1)} %w_ref.6, f32[2,2,128,512]{3,2,1,0:T(8,128)S(1)} %slice_add_fusion.3.after_ref), custom_call_target="tpu_custom_call" | custom-call | flops 805306368 | bytes 6291456 | tf_op jit(solution)/shard_map/join/pallas_call | solution.py:157
  37.8 5.9 %stage.1 = (bf16[8192,1024]{1,0:T(8,128)(2,1)S(1)}, f32[1,512]{1,0:T(1,128)S(1)}) custom-call(bf16[8192,1024]{1,0:T(8,128)(2,1)} %w_ref.7, f32[2,2,128,512]{3,2,1,0:T(8,128)S(1)} %get-tuple-element.34.after_ref), custom_call_target="tpu_custom_call" | custom-call | bytes 16777216 | tf_op jit(solution)/shard_map/stage/pallas_call | solution.py:105
  43.8 2.3 %collective-permute-done.1 = f32[2,128,512]{2,1,0:T(8,128)S(1)} collective-permute-done((f32[2,128,512]{2,1,0:T(8,128)S(1)}, f32[2,128,512]{2,1,0:T(8,128)S(1)}, u32[]{:S(2)}, u32[]{:S(2)}) %collective-permute-start.1) | collective-permute-done | bytes 524320 | tf_op jit(solution)/shard_map/ppermute | solution.py:67
  47.8 5.4 %collective-permute-done.3 = f32[1,128,512]{2,1,0:T(8,128)S(1)} collective-permute-done((f32[1,128,512]{2,1,0:T(8,128)S(1)}, f32[1,128,512]{2,1,0:T(8,128)S(1)}, u32[]{:S(2)}, u32[]{:S(2)}) %collective-permute-start.3) | collective-permute-done | bytes 262176 | tf_op jit(solution)/shard_map/ppermute | solution.py:67
  53.3 1.8 collective-permute-start.5
  55.8 22.7 %collective-permute-done.5 = f32[2,1,128,512]{3,2,1,0:T(8,128)S(1)} collective-permute-done((f32[2,1,128,512]{3,2,1,0:T(8,128)S(1)}, f32[2,1,128,512]{3,2,1,0:T(8,128)S(1)}, u32[]{:S(2)}, u32[]{:S(2)}) %collective-permute-start.5) | collective-permute-done | bytes 524320 | tf_op jit(solution)/shard_map/ppermute | solution.py:67
  83.4 3.2 %collective-permute-start.9 = (f32[128]{0:T(128)S(1)}, f32[128]{0:T(128)S(1)}, u32[]{:S(2)}, u32[]{:S(2)}) collective-permute-start(f32[128]{0:T(128)S(1)} %add_add_fusion.3), channel_id=1, source_target_pairs={{0,1},{1,0},{2,3},{3,2},{4,5},{5,4},{6,7},{7,6},{8,9},{9,8},{10,11... | collective-permute-start | bytes 1544 | tf_op jit(solution)/shard_map/ppermute | solution.py:67
  89.2 1.9 %head.4 = (f32[128,1024]{1,0:T(8,128)S(1)}, f32[1,512]{1,0:T(1,128)S(1)}) custom-call(s32[17]{0:T(128)S(1)} %pad_add_fusion.starts, bf16[8192,1024]{1,0:T(8,128)(2,1)S(1)} %get-tuple-element.35.w_ref, f32[128,1024]{1,0:T(8,128)S(1)} %broadcast_in_dim.7.before_ref, s32[1,128]{1,0:T(1,128)S(1)} %bitcast.124, bf16[2,128,512]{2,1,0:T(8,128)(2,1)S(1)} %fusion.24.rest_0_, ...), custom_call_target="tpu_custom_call" | custom-call | flops 536870912 | bytes 1048576 | tf_op jit(solution)/shard_map/head/pallas_call | solution.py:216
  91.0 4.6 %collective-permute-done.12 = bf16[2,1,128,512]{3,2,1,0:T(8,128)(2,1)S(1)} collective-permute-done((bf16[2,1,128,512]{3,2,1,0:T(8,128)(2,1)S(1)}, bf16[2,1,128,512]{3,2,1,0:T(8,128)(2,1)S(1)}, u32[]{:S(2)}, u32[]{:S(2)}) %collective-permute-start.12) | collective-permute-done | bytes 262176 | tf_op jit(solution)/shard_map/ppermute | solution.py:67
  98.8 3.1 %head.5 = (f32[128,1024]{1,0:T(8,128)S(1)}, f32[1,512]{1,0:T(1,128)S(1)}) custom-call(s32[17]{0:T(128)S(1)} %pad_add_fusion.starts, bf16[8192,1024]{1,0:T(8,128)(2,1)S(1)} %get-tuple-element.35.w_ref, f32[128,1024]{1,0:T(8,128)S(1)} %get-tuple-element.37.before_ref, s32[1,128]{1,0:T(1,128)S(1)} %bitcast.125, bf16[2,128,512]{2,1,0:T(8,128)(2,1)S(1)} %bitcast.110, ...), custom_call_target="tpu_custom_call" | custom-call | flops 1073741824 | bytes 1048576 | tf_op jit(solution)/shard_map/head/pallas_call | solution.py:216
  102.4 1.7 collective-permute-start.18
  105.5 1.6 head.7
  107.1 2.4 %collective-permute-start.19 = (f32[4,128]{1,0:T(4,128)S(1)}, f32[4,128]{1,0:T(4,128)S(1)}, u32[]{:S(2)}, u32[]{:S(2)}) collective-permute-start(f32[4,128]{1,0:T(4,128)S(1)} %slice.195), channel_id=1, source_target_pairs={{0,8},{1,9},{2,10},{3,11},{4,12},{5,13},{6,14},{7,15},{8,0},{9,1},... | collective-permute-start | bytes 6152 | tf_op jit(solution)/shard_map/ppermute | solution.py:67
  110.6 1.7 collective-permute-start.22
  115.0 2.8 %collective-permute-start.23 = (f32[4,128]{1,0:T(4,128)S(1)}, f32[4,128]{1,0:T(4,128)S(1)}, u32[]{:S(2)}, u32[]{:S(2)}) collective-permute-start(f32[4,128]{1,0:T(4,128)S(1)} %pad_maximum_fusion.4), channel_id=1, source_target_pairs={{0,1},{1,0},{2,3},{3,2},{4,5},{5,4},{6,7},{7,6},{8,9},{9,8},{10,11... | collective-permute-start | bytes 6152 | tf_op jit(solution)/shard_map/ppermute | solution.py:67
  119.2 4.2 %back_first.1 = (f32[2,4,128,512]{3,2,1,0:T(8,128)S(1)}, bf16[128,1024]{1,0:T(8,128)(2,1)S(1)}) custom-call(s32[2,8]{1,0:T(2,128)S(1)} %xor_multiply_fusion.order, s32[17]{0:T(128)S(1)} %pad_add_fusion.starts, f32[128,1024]{1,0:T(8,128)S(1)} %get-tuple-element.45.logits_ref, f32[8,128]{1,0:T(8,128)S(1)} %broadcast_in_dim.8.stats_ref, ...), custom_call_target="tpu_custom_call" | custom-call | flops 1073741824 | bytes 2097152 | tf_op jit(solution)/shard_map/back_first/pallas_call | solution.py:253
  124.1 2.6 %back_rest.2 = (f32[2,2,128,512]{3,2,1,0:T(8,128)S(1)}, f32[1,512]{1,0:T(1,128)}) custom-call(s32[2,8]{1,0:T(2,128)S(1)} %xor_multiply_fusion.order, bf16[128,1024]{1,0:T(8,128)(2,1)S(1)} %get-tuple-element.47.d_ref, bf16[8192,1024]{1,0:T(8,128)(2,1)S(1)} %get-tuple-element.35.w_ref, f32[2,4,128,512]{3,2,1,0:T(8,128)S(1)} %get-tuple-element.48.after_ref), custom_call_target="tpu_custom_call" | custom-call | flops 536870912 | bytes 1048576 | tf_op jit(solution)/shard_map/back_rest/pallas_call | solution.py:270
  129.2 2.2 %back_rest.3 = (f32[2,2,128,512]{3,2,1,0:T(8,128)S(1)}, f32[1,512]{1,0:T(1,128)S(1)}) custom-call(s32[2,8]{1,0:T(2,128)S(1)} %xor_multiply_fusion.order, bf16[128,1024]{1,0:T(8,128)(2,1)S(1)} %get-tuple-element.47.d_ref, bf16[8192,1024]{1,0:T(8,128)(2,1)S(1)} %get-tuple-element.35.w_ref, f32[2,2,128,512]{3,2,1,0:T(8,128)S(1)} %slice_add_fusion.1.after_ref), custom_call_target="tpu_custom_call" | custom-call | flops 536870912 | bytes 1048576 | tf_op jit(solution)/shard_map/back_rest/pallas_call | solution.py:270
  131.4 3.7 %collective-permute-done.25 = f16[2,128,512]{2,1,0:T(8,128)(2,1)S(1)} collective-permute-done((f16[2,128,512]{2,1,0:T(8,128)(2,1)S(1)}, f16[2,128,512]{2,1,0:T(8,128)(2,1)S(1)}, u32[]{:S(2)}, u32[]{:S(2)}) %collective-permute-start.25) | collective-permute-done | bytes 262176 | tf_op jit(solution)/shard_map/ppermute | solution.py:67
  138.1 1.9 %collective-permute-done.27 = f16[1,128,512]{2,1,0:T(8,128)(2,1)S(1)} collective-permute-done((f16[1,128,512]{2,1,0:T(8,128)(2,1)S(1)}, f16[1,128,512]{2,1,0:T(8,128)(2,1)S(1)}, u32[]{:S(2)}, u32[]{:S(2)}) %collective-permute-start.27) | collective-permute-done | bytes 131104 | tf_op jit(solution)/shard_map/ppermute | solution.py:67
  142.8 9.0 %head_grad.1 = (bf16[8192,1024]{1,0:T(8,128)(2,1)}, f32[1,512]{1,0:T(1,128)S(1)}) custom-call(s32[17]{0:T(128)S(1)} %pad_add_fusion.starts, bf16[128,1024]{1,0:T(8,128)(2,1)S(1)} %get-tuple-element.47.d_ref, f32[2,1,128,512]{3,2,1,0:T(8,128)S(1)} %get-tuple-element.63.after_ref, bf16[2,128,512]{2,1,0:T(8,128)(2,1)S(1)} %fusion.24.rest_0_, ...), custom_call_target="tpu_custom_call" | custom-call | flops 2147483648 | bytes 16777216 | tf_op jit(solution)/shard_map/head_grad/pallas_call | solution.py:314
  151.8 4.0 %collective-permute-done.29 = f16[2,1,128,512]{3,2,1,0:T(8,128)(2,1)S(1)} collective-permute-done((f16[2,1,128,512]{3,2,1,0:T(8,128)(2,1)S(1)}, f16[2,1,128,512]{3,2,1,0:T(8,128)(2,1)S(1)}, u32[]{:S(2)}, u32[]{:S(2)}) %collective-permute-start.29) | collective-permute-done | bytes 262176 | tf_op jit(solution)/shard_map/ppermute | solution.py:67
  158.4 2.6 %join_grad.4 = (bf16[3,512,8192]{2,1,0:T(8,128)(2,1)}, f32[1,512]{1,0:T(1,128)S(1)}) custom-call(s32[17]{0:T(128)S(1)} %pad_add_fusion.1.starts, bf16[1536,128]{1,0:T(8,128)(2,1)S(1)} %get-tuple-element.44.x_ref, bf16[2,128,512]{2,1,0:T(8,128)(2,1)S(1)} %bitcast.107), custom_call_target="tpu_custom_call" | custom-call | flops 402653184 | bytes 3145728 | tf_op jit(solution)/shard_map/join_grad/pallas_call | solution.py:367
  162.3 1.6 collective-permute-start.35
  165.2 4.9 %join_grad.5 = (bf16[3,512,8192]{2,1,0:T(8,128)(2,1)}, f32[1,512]{1,0:T(1,128)S(1)}) custom-call(s32[17]{0:T(128)S(1)} %pad_add_fusion.1.starts, bf16[1536,128]{1,0:T(8,128)(2,1)S(1)} %get-tuple-element.44.x_ref, bf16[3,512,8192]{2,1,0:T(8,128)(2,1)} %get-tuple-element.53.rest_0_, ...), custom_call_target="tpu_custom_call", output_to_operand_aliasing={{0}: (2, {})} | custom-call | flops 1207959552 | bytes 9437184 | tf_op jit(solution)/shard_map/join_grad/pallas_call | solution.py:367
  173.6 4.3 %join_grad.6 = (bf16[3,512,8192]{2,1,0:T(8,128)(2,1)}, f32[1,512]{1,0:T(1,128)}) custom-call(s32[17]{0:T(128)S(1)} %pad_add_fusion.1.starts, bf16[1536,128]{1,0:T(8,128)(2,1)S(1)} %get-tuple-element.44.x_ref, bf16[3,512,8192]{2,1,0:T(8,128)(2,1)} %get-tuple-element.55.rest_0_, ...), custom_call_target="tpu_custom_call", output_to_operand_aliasing={{0}: (2, {})} | custom-call | flops 805306368 | bytes 6291456 | tf_op jit(solution)/shard_map/join_grad/pallas_call | solution.py:367
  177.9 4.3 %join_grad.7 = (bf16[3,512,8192]{2,1,0:T(8,128)(2,1)}, f32[1,512]{1,0:T(1,128)}) custom-call(s32[17]{0:T(128)S(1)} %pad_add_fusion.1.starts, bf16[1536,128]{1,0:T(8,128)(2,1)S(1)} %get-tuple-element.44.x_ref, bf16[3,512,8192]{2,1,0:T(8,128)(2,1)} %get-tuple-element.57.rest_0_, ...), custom_call_target="tpu_custom_call", output_to_operand_aliasing={{0}: (2, {})} | custom-call | flops 805306368 | bytes 6291456 | tf_op jit(solution)/shard_map/join_grad/pallas_call | solution.py:367
  (121 shorter events, 40.5 us)
Async XLA Ops:
  2.4 19.3 %all-to-all-start = ((bf16[16,8,1536]{2,1,0:T(8,128)(2,1)}), bf16[16,8,1536]{2,1,0:T(8,128)(2,1)S(1)}, u32[]{:S(2)}, u32[]{:S(2)}) async-start(bf16[16,8,1536]{2,1,0:T(8,128)(2,1)} %maximum_bitcast_fusion.after_ref), calls=%async_computation | async-start | bytes 786432 | tf_op jit(solution)/shard_map/all_to_all | solution.py:514
  27.6 4.5 %collective-permute-start = (f32[2,4,128,512]{3,2,1,0:T(8,128)S(1)}, f32[2,4,128,512]{3,2,1,0:T(8,128)S(1)}, u32[]{:S(2)}, u32[]{:S(2)}) collective-permute-start(f32[2,4,128,512]{3,2,1,0:T(8,128)S(1)} %get-tuple-element.33), channel_id=1, source_target_pairs={{0,1},{1,0},{2,3},{3,2},{4,5},{5,4},{6,7},{7,6},{8,9},{9,8},{10,11... | collective-permute-start | bytes 6291464 | tf_op jit(solution)/shard_map/ppermute | solution.py:67
  32.5 13.6 %collective-permute-start.1 = (f32[2,128,512]{2,1,0:T(8,128)S(1)}, f32[2,128,512]{2,1,0:T(8,128)S(1)}, u32[]{:S(2)}, u32[]{:S(2)}) collective-permute-start(f32[2,128,512]{2,1,0:T(8,128)S(1)} %get-tuple-element.78), channel_id=1, source_target_pairs={{0,2},{1,3},{2,0},{3,1},{4,6},{5,7},{6,4},{7,5},{8,10},{9,11},{10,... | collective-permute-start | bytes 1572872 | tf_op jit(solution)/shard_map/ppermute | solution.py:67
  32.8 13.2 %collective-permute-start.2 = (f32[2,128,512]{2,1,0:T(8,128)S(1)}, f32[2,128,512]{2,1,0:T(8,128)S(1)}, u32[]{:S(2)}, u32[]{:S(2)}) collective-permute-start(f32[2,128,512]{2,1,0:T(8,128)S(1)} %get-tuple-element.79), channel_id=1, source_target_pairs={{0,4},{1,5},{2,6},{3,7},{4,0},{5,1},{6,2},{7,3},{8,12},{9,13},{10,... | collective-permute-start | bytes 1572872 | tf_op jit(solution)/shard_map/ppermute | solution.py:67
  46.5 6.8 %collective-permute-start.3 = (f32[1,128,512]{2,1,0:T(8,128)S(1)}, f32[1,128,512]{2,1,0:T(8,128)S(1)}, u32[]{:S(2)}, u32[]{:S(2)}) collective-permute-start(f32[1,128,512]{2,1,0:T(8,128)S(1)} %get-tuple-element.76), channel_id=1, source_target_pairs={{0,4},{1,5},{2,6},{3,7},{4,0},{5,1},{6,2},{7,3},{8,12},{9,13},{10,... | collective-permute-start | bytes 786440 | tf_op jit(solution)/shard_map/ppermute | solution.py:67
  47.2 6.1 %collective-permute-start.4 = (f32[1,128,512]{2,1,0:T(8,128)S(1)}, f32[1,128,512]{2,1,0:T(8,128)S(1)}, u32[]{:S(2)}, u32[]{:S(2)}) collective-permute-start(f32[1,128,512]{2,1,0:T(8,128)S(1)} %get-tuple-element.77), channel_id=1, source_target_pairs={{0,2},{1,3},{2,0},{3,1},{4,6},{5,7},{6,4},{7,5},{8,10},{9,11},{10,... | collective-permute-start | bytes 786440 | tf_op jit(solution)/shard_map/ppermute | solution.py:67
  53.3 25.1 %collective-permute-start.5 = (f32[2,1,128,512]{3,2,1,0:T(8,128)S(1)}, f32[2,1,128,512]{3,2,1,0:T(8,128)S(1)}, u32[]{:S(2)}, u32[]{:S(2)}) collective-permute-start(f32[2,1,128,512]{3,2,1,0:T(8,128)S(1)} %slice_add_fusion.5), channel_id=1, source_target_pairs={{0,8},{1,9},{2,10},{3,11},{4,12},{5,13},{6,14},{7,15},{8,0},{9,1},... | collective-permute-start | bytes 1572872 | tf_op jit(solution)/shard_map/ppermute | solution.py:67
  55.1 31.4 %collective-permute-start.10 = (f32[512]{0:T(512)S(1)}, f32[512]{0:T(512)S(1)}, u32[]{:S(2)}, u32[]{:S(2)}) collective-permute-start(f32[512]{0:T(512)S(1)} %copy-done.1), channel_id=1, source_target_pairs={{0,8},{1,9},{2,10},{3,11},{4,12},{5,13},{6,14},{7,15},{8,0},{9,1},... | collective-permute-start | bytes 6152 | tf_op jit(solution)/shard_map/ppermute | solution.py:67
  79.5 3.3 %collective-permute-start.8 = (f32[128]{0:T(128)S(1)}, f32[128]{0:T(128)S(1)}, u32[]{:S(2)}, u32[]{:S(2)}) collective-permute-start(f32[128]{0:T(128)S(1)} %add_bitcast_fusion), channel_id=1, source_target_pairs={{0,6},{1,7},{2,4},{3,5},{4,2},{5,3},{6,0},{7,1},{8,14},{9,15},{10,... | collective-permute-start | bytes 1544 | tf_op jit(solution)/shard_map/ppermute | solution.py:67
  83.4 4.0 %collective-permute-start.9 = (f32[128]{0:T(128)S(1)}, f32[128]{0:T(128)S(1)}, u32[]{:S(2)}, u32[]{:S(2)}) collective-permute-start(f32[128]{0:T(128)S(1)} %add_add_fusion.3), channel_id=1, source_target_pairs={{0,1},{1,0},{2,3},{3,2},{4,5},{5,4},{6,7},{7,6},{8,9},{9,8},{10,11... | collective-permute-start | bytes 1544 | tf_op jit(solution)/shard_map/ppermute | solution.py:67
  88.0 7.7 %collective-permute-start.12 = (bf16[2,1,128,512]{3,2,1,0:T(8,128)(2,1)S(1)}, bf16[2,1,128,512]{3,2,1,0:T(8,128)(2,1)S(1)}, u32[]{:S(2)}, u32[]{:S(2)}) collective-permute-start(bf16[2,1,128,512]{3,2,1,0:T(8,128)(2,1)S(1)} %multiply_convert_fusion.8), channel_id=1, source_target_pairs={{0,2},{1,3},{2,0},{3,1},{4,6},{5,7},{6,4},{7,5},{8,10},{9,11},{10,... | collective-permute-start | bytes 786440 | tf_op jit(solution)/shard_map/ppermute | solution.py:67
  88.4 7.4 %collective-permute-start.13 = (bf16[2,1,128,512]{3,2,1,0:T(8,128)(2,1)S(1)}, bf16[2,1,128,512]{3,2,1,0:T(8,128)(2,1)S(1)}, u32[]{:S(2)}, u32[]{:S(2)}) collective-permute-start(bf16[2,1,128,512]{3,2,1,0:T(8,128)(2,1)S(1)} %multiply_convert_fusion.8), channel_id=1, source_target_pairs={{0,4},{1,5},{2,6},{3,7},{4,0},{5,1},{6,2},{7,3},{8,12},{9,13},{10,... | collective-permute-start | bytes 786440 | tf_op jit(solution)/shard_map/ppermute | solution.py:67
  97.4 4.7 %collective-permute-start.17 = (bf16[1,128,512]{2,1,0:T(8,128)(2,1)S(1)}, bf16[1,128,512]{2,1,0:T(8,128)(2,1)S(1)}, u32[]{:S(2)}, u32[]{:S(2)}) collective-permute-start(bf16[1,128,512]{2,1,0:T(8,128)(2,1)S(1)} %slice_bitcast_fusion.6), channel_id=1, source_target_pairs={{0,4},{1,5},{2,6},{3,7},{4,0},{5,1},{6,2},{7,3},{8,12},{9,13},{10,... | collective-permute-start | bytes 393224 | tf_op jit(solution)/shard_map/ppermute | solution.py:67
  98.0 4.3 %collective-permute-start.16 = (bf16[1,128,512]{2,1,0:T(8,128)(2,1)S(1)}, bf16[1,128,512]{2,1,0:T(8,128)(2,1)S(1)}, u32[]{:S(2)}, u32[]{:S(2)}) collective-permute-start(bf16[1,128,512]{2,1,0:T(8,128)(2,1)S(1)} %slice_bitcast_fusion.7), channel_id=1, source_target_pairs={{0,2},{1,3},{2,0},{3,1},{4,6},{5,7},{6,4},{7,5},{8,10},{9,11},{10,... | collective-permute-start | bytes 393224 | tf_op jit(solution)/shard_map/ppermute | solution.py:67
  102.4 3.2 %collective-permute-start.18 = (bf16[2,1,128,512]{3,2,1,0:T(8,128)(2,1)S(1)}, bf16[2,1,128,512]{3,2,1,0:T(8,128)(2,1)S(1)}, u32[]{:S(2)}, u32[]{:S(2)}) collective-permute-start(bf16[2,1,128,512]{3,2,1,0:T(8,128)(2,1)S(1)} %pad_maximum_fusion.1), channel_id=1, source_target_pairs={{0,1},{1,0},{2,3},{3,2},{4,5},{5,4},{6,7},{7,6},{8,9},{9,8},{10,11... | collective-permute-start | bytes 786440 | tf_op jit(solution)/shard_map/ppermute | solution.py:67
  107.1 3.4 %collective-permute-start.19 = (f32[4,128]{1,0:T(4,128)S(1)}, f32[4,128]{1,0:T(4,128)S(1)}, u32[]{:S(2)}, u32[]{:S(2)}) collective-permute-start(f32[4,128]{1,0:T(4,128)S(1)} %slice.195), channel_id=1, source_target_pairs={{0,8},{1,9},{2,10},{3,11},{4,12},{5,13},{6,14},{7,15},{8,0},{9,1},... | collective-permute-start | bytes 6152 | tf_op jit(solution)/shard_map/ppermute | solution.py:67
  110.6 3.4 %collective-permute-start.22 = (f32[4,128]{1,0:T(4,128)S(1)}, f32[4,128]{1,0:T(4,128)S(1)}, u32[]{:S(2)}, u32[]{:S(2)}) collective-permute-start(f32[4,128]{1,0:T(4,128)S(1)} %pad_maximum_fusion.3), channel_id=1, source_target_pairs={{0,6},{1,7},{2,4},{3,5},{4,2},{5,3},{6,0},{7,1},{8,14},{9,15},{10,... | collective-permute-start | bytes 6152 | tf_op jit(solution)/shard_map/ppermute | solution.py:67
  115.0 3.6 %collective-permute-start.23 = (f32[4,128]{1,0:T(4,128)S(1)}, f32[4,128]{1,0:T(4,128)S(1)}, u32[]{:S(2)}, u32[]{:S(2)}) collective-permute-start(f32[4,128]{1,0:T(4,128)S(1)} %pad_maximum_fusion.4), channel_id=1, source_target_pairs={{0,1},{1,0},{2,3},{3,2},{4,5},{5,4},{6,7},{7,6},{8,9},{9,8},{10,11... | collective-permute-start | bytes 6152 | tf_op jit(solution)/shard_map/ppermute | solution.py:67
  123.7 3.0 %collective-permute-start.24 = (f16[2,4,128,512]{3,2,1,0:T(8,128)(2,1)S(1)}, f16[2,4,128,512]{3,2,1,0:T(8,128)(2,1)S(1)}, u32[]{:S(2)}, u32[]{:S(2)}) collective-permute-start(f16[2,4,128,512]{3,2,1,0:T(8,128)(2,1)S(1)} %multiply_convert_fusion), channel_id=1, source_target_pairs={{0,1},{1,0},{2,3},{3,2},{4,5},{5,4},{6,7},{7,6},{8,9},{9,8},{10,11... | collective-permute-start | bytes 3145736 | tf_op jit(solution)/shard_map/ppermute | solution.py:67
  127.3 7.8 %collective-permute-start.25 = (f16[2,128,512]{2,1,0:T(8,128)(2,1)S(1)}, f16[2,128,512]{2,1,0:T(8,128)(2,1)S(1)}, u32[]{:S(2)}, u32[]{:S(2)}) collective-permute-start(f16[2,128,512]{2,1,0:T(8,128)(2,1)S(1)} %get-tuple-element.74), channel_id=1, source_target_pairs={{0,2},{1,3},{2,0},{3,1},{4,6},{5,7},{6,4},{7,5},{8,10},{9,11},{10,... | collective-permute-start | bytes 786440 | tf_op jit(solution)/shard_map/ppermute | solution.py:67
  128.3 7.4 %collective-permute-start.26 = (f16[2,128,512]{2,1,0:T(8,128)(2,1)S(1)}, f16[2,128,512]{2,1,0:T(8,128)(2,1)S(1)}, u32[]{:S(2)}, u32[]{:S(2)}) collective-permute-start(f16[2,128,512]{2,1,0:T(8,128)(2,1)S(1)} %get-tuple-element.75), channel_id=1, source_target_pairs={{0,4},{1,5},{2,6},{3,7},{4,0},{5,1},{6,2},{7,3},{8,12},{9,13},{10,... | collective-permute-start | bytes 786440 | tf_op jit(solution)/shard_map/ppermute | solution.py:67
  136.1 3.9 %collective-permute-start.27 = (f16[1,128,512]{2,1,0:T(8,128)(2,1)S(1)}, f16[1,128,512]{2,1,0:T(8,128)(2,1)S(1)}, u32[]{:S(2)}, u32[]{:S(2)}) collective-permute-start(f16[1,128,512]{2,1,0:T(8,128)(2,1)S(1)} %get-tuple-element.72), channel_id=1, source_target_pairs={{0,4},{1,5},{2,6},{3,7},{4,0},{5,1},{6,2},{7,3},{8,12},{9,13},{10,... | collective-permute-start | bytes 393224 | tf_op jit(solution)/shard_map/ppermute | solution.py:67
  137.1 4.1 %collective-permute-start.28 = (f16[1,128,512]{2,1,0:T(8,128)(2,1)S(1)}, f16[1,128,512]{2,1,0:T(8,128)(2,1)S(1)}, u32[]{:S(2)}, u32[]{:S(2)}) collective-permute-start(f16[1,128,512]{2,1,0:T(8,128)(2,1)S(1)} %get-tuple-element.73), channel_id=1, source_target_pairs={{0,2},{1,3},{2,0},{3,1},{4,6},{5,7},{6,4},{7,5},{8,10},{9,11},{10,... | collective-permute-start | bytes 393224 | tf_op jit(solution)/shard_map/ppermute | solution.py:67
  141.3 14.5 %collective-permute-start.29 = (f16[2,1,128,512]{3,2,1,0:T(8,128)(2,1)S(1)}, f16[2,1,128,512]{3,2,1,0:T(8,128)(2,1)S(1)}, u32[]{:S(2)}, u32[]{:S(2)}) collective-permute-start(f16[2,1,128,512]{3,2,1,0:T(8,128)(2,1)S(1)} %get-tuple-element.62), channel_id=1, source_target_pairs={{0,8},{1,9},{2,10},{3,11},{4,12},{5,13},{6,14},{7,15},{8,0},{9,1},... | collective-permute-start | bytes 786440 | tf_op jit(solution)/shard_map/ppermute | solution.py:67
  156.1 4.9 %collective-permute-start.31 = (bf16[1,128,512]{2,1,0:T(8,128)(2,1)S(1)}, bf16[1,128,512]{2,1,0:T(8,128)(2,1)S(1)}, u32[]{:S(2)}, u32[]{:S(2)}) collective-permute-start(bf16[1,128,512]{2,1,0:T(8,128)(2,1)S(1)} %get-tuple-element.86), channel_id=1, source_target_pairs={{0,4},{1,5},{2,6},{3,7},{4,0},{5,1},{6,2},{7,3},{8,12},{9,13},{10,... | collective-permute-start | bytes 393224 | tf_op jit(solution)/shard_map/ppermute | solution.py:67
  156.2 4.8 %collective-permute-start.32 = (bf16[1,128,512]{2,1,0:T(8,128)(2,1)S(1)}, bf16[1,128,512]{2,1,0:T(8,128)(2,1)S(1)}, u32[]{:S(2)}, u32[]{:S(2)}) collective-permute-start(bf16[1,128,512]{2,1,0:T(8,128)(2,1)S(1)} %get-tuple-element.87), channel_id=1, source_target_pairs={{0,2},{1,3},{2,0},{3,1},{4,6},{5,7},{6,4},{7,5},{8,10},{9,11},{10,... | collective-permute-start | bytes 393224 | tf_op jit(solution)/shard_map/ppermute | solution.py:67
  157.7 7.5 %collective-permute-start.30 = (bf16[2,1,128,512]{3,2,1,0:T(8,128)(2,1)S(1)}, bf16[2,1,128,512]{3,2,1,0:T(8,128)(2,1)S(1)}, u32[]{:S(2)}, u32[]{:S(2)}) collective-permute-start(bf16[2,1,128,512]{3,2,1,0:T(8,128)(2,1)S(1)} %get-tuple-element.60), channel_id=1, source_target_pairs={{0,1},{1,0},{2,3},{3,2},{4,5},{5,4},{6,7},{7,6},{8,9},{9,8},{10,11... | collective-permute-start | bytes 786440 | tf_op jit(solution)/shard_map/ppermute | solution.py:67
  161.1 4.1 %collective-permute-start.33 = (bf16[2,1,128,512]{3,2,1,0:T(8,128)(2,1)S(1)}, bf16[2,1,128,512]{3,2,1,0:T(8,128)(2,1)S(1)}, u32[]{:S(2)}, u32[]{:S(2)}) collective-permute-start(bf16[2,1,128,512]{3,2,1,0:T(8,128)(2,1)S(1)} %multiply_convert_fusion.3), channel_id=1, source_target_pairs={{0,1},{1,0},{2,3},{3,2},{4,5},{5,4},{6,7},{7,6},{8,9},{9,8},{10,11... | collective-permute-start | bytes 786440 | tf_op jit(solution)/shard_map/ppermute | solution.py:67
  162.3 8.2 %collective-permute-start.35 = (bf16[2,128,512]{2,1,0:T(8,128)(2,1)S(1)}, bf16[2,128,512]{2,1,0:T(8,128)(2,1)S(1)}, u32[]{:S(2)}, u32[]{:S(2)}) collective-permute-start(bf16[2,128,512]{2,1,0:T(8,128)(2,1)S(1)} %get-tuple-element.80), channel_id=1, source_target_pairs={{0,4},{1,5},{2,6},{3,7},{4,0},{5,1},{6,2},{7,3},{8,12},{9,13},{10,... | collective-permute-start | bytes 786440 | tf_op jit(solution)/shard_map/ppermute | solution.py:67
  163.9 7.6 %collective-permute-start.34 = (bf16[2,128,512]{2,1,0:T(8,128)(2,1)S(1)}, bf16[2,128,512]{2,1,0:T(8,128)(2,1)S(1)}, u32[]{:S(2)}, u32[]{:S(2)}) collective-permute-start(bf16[2,128,512]{2,1,0:T(8,128)(2,1)S(1)} %get-tuple-element.81), channel_id=1, source_target_pairs={{0,2},{1,3},{2,0},{3,1},{4,6},{5,7},{6,4},{7,5},{8,10},{9,11},{10,... | collective-permute-start | bytes 786440 | tf_op jit(solution)/shard_map/ppermute | solution.py:67
  171.6 6.2 %collective-permute-start.37 = (bf16[2,128,512]{2,1,0:T(8,128)(2,1)S(1)}, bf16[2,128,512]{2,1,0:T(8,128)(2,1)S(1)}, u32[]{:S(2)}, u32[]{:S(2)}) collective-permute-start(bf16[2,128,512]{2,1,0:T(8,128)(2,1)S(1)} %get-tuple-element.93.rest_2_), channel_id=1, source_target_pairs={{0,1},{1,0},{2,3},{3,2},{4,5},{5,4},{6,7},{7,6},{8,9},{9,8},{10,11... | collective-permute-start | bytes 786440 | tf_op jit(solution)/shard_map/ppermute | solution.py:67
  172.8 5.0 %collective-permute-start.36 = (bf16[2,128,512]{2,1,0:T(8,128)(2,1)S(1)}, bf16[2,128,512]{2,1,0:T(8,128)(2,1)S(1)}, u32[]{:S(2)}, u32[]{:S(2)}) collective-permute-start(bf16[2,128,512]{2,1,0:T(8,128)(2,1)S(1)} %get-tuple-element.94.rest_1_), channel_id=1, source_target_pairs={{0,1},{1,0},{2,3},{3,2},{4,5},{5,4},{6,7},{7,6},{8,9},{9,8},{10,11... | collective-permute-start | bytes 786440 | tf_op jit(solution)/shard_map/ppermute | solution.py:67
  (11 other events, 70.1 us)
